TPU v7x, 32 devices: a whole 2x2x4 slice. The times are simulated.
32 devices in a mesh: lon: 16 (over z, x, core), lat: 2 (over y).
Axes of the slice: x: 2, y: 2, z: 4, core: 2. Of those that a mesh axis runs over, the one named last changes fastest.
Arguments:
- tracers: float32 [3, 10, 128, 2048], P(None, None, 'lat', 'lon'), may hold values from -6 to 6
- offsets: int32 [10, 128, 2048], P(None, 'lat', 'lon'), may hold values from -16 to 15, as said below
- weights: float32 [10, 128, 2048], P(None, 'lat', 'lon'), may hold values from 0 to 1
- diffusion: float32 [9, 128, 2048], P(None, 'lat', 'lon'), may hold values from 0.05 to 5
- send_index: int32 [32, 32, 512], P(('lon', 'lat')), may hold values from 0 to 8191, as said below
- send_count: int32 [32, 32], P(('lon', 'lat')), may hold values from 1 to 512, as said below
Outputs:
- owned_tracers: float32 [3, 10, 262144], P(None, None, ('lon', 'lat'))
Inputs may be any that keep to these rules, and one draw needn't show every extreme that they name: `offsets`: the departure interval of a cell starts this many cells east of it on the same row and level; both ends of the range occur. `send_count`: entry [d, e] counts the columns of device d that device e owns. Every row and every column sums to 8192. A device keeps exactly 511 of its own columns and sends exactly one to the device 32 // 2 further on; some list holds exactly 512 columns. `send_index`: entries [d, e, 0 : send_count[d, e]] are local column indices of device d that device e owns, in owner order; each column of d appears in exactly one list once; entries past the count are valid column indices that carry no meaning.
All inputs are finite; a program needn't handle non-finite values.
Results may differ from a plain program's by a relative error of at most 0.0003.
Values sent between devices are 32-bit elements; how exact they have to be, the bound alone decides.
No kernel may reach another device: no remote copies, remote signals or barrier semaphores. Data moves between devices by JAX's collectives and lax.ppermute only.
A program may use at most 128 MiB of HBM per device.

v0:
```python
import jax
import jax.numpy as jnp
from jax import lax
from jax.sharding import PartitionSpec as P

NTR = 3
LEV = 10
HALO = 16


def shifted(block, axis, distance):
    devices = range(lax.axis_size(axis))
    route = [((i - distance) % len(devices), i) for i in devices]
    return lax.ppermute(block, axis, route)


def solve_columns(values, coef_rows):
    levels = values.shape[1]
    diag = []
    for level in range(levels):
        term = jnp.ones_like(coef_rows[0])
        if level > 0:
            term = term + coef_rows[level - 1]
        if level < levels - 1:
            term = term + coef_rows[level]
        diag.append(term)
    upper = []
    reduced = []
    denom = diag[0]
    upper.append(-coef_rows[0] / denom)
    reduced.append(values[:, 0] / denom)
    for level in range(1, levels):
        denom = diag[level] + coef_rows[level - 1] * upper[level - 1]
        reduced.append((values[:, level] + coef_rows[level - 1] * reduced[level - 1]) / denom)
        if level < levels - 1:
            upper.append(-coef_rows[level] / denom)
    output = [None] * levels
    output[levels - 1] = reduced[levels - 1]
    for level in range(levels - 2, -1, -1):
        output[level] = reduced[level] - upper[level] * output[level + 1]
    return jnp.stack(output, axis=1)


def pick_columns(source, index):
    total = index.shape[0]
    width = source.shape[1]
    block = 512
    blocks = index.reshape(total // block, block)
    column_ids = jnp.arange(width, dtype=jnp.int32)

    def one_block(block_index):
        selector = (column_ids[:, None] == block_index[None, :]).astype(jnp.float32)
        return jnp.dot(
            source, selector, precision=lax.Precision.HIGHEST, preferred_element_type=jnp.float32
        )

    picked = lax.map(one_block, blocks)
    return jnp.moveaxis(picked, 0, 1).reshape(source.shape[0], total)


def place_owned(arrived, counts_in, columns):
    peer_count = lax.axis_size(("lon", "lat"))
    own_index = lax.axis_index(("lon", "lat"))
    slot_width = arrived.shape[1] // peer_count
    by_source = counts_in[0].astype(jnp.int32)
    counts = jnp.roll(by_source[::-1], own_index + 1)
    seg_ends = jnp.cumsum(counts)
    places = jnp.arange(columns, dtype=jnp.int32)
    passed = seg_ends[:, None] <= places[None, :]
    segment = jnp.sum(passed.astype(jnp.int32), axis=0)
    seg_start = jnp.sum(jnp.where(passed, counts[:, None], 0), axis=0)
    source = (own_index - segment) % peer_count
    column = source * slot_width + places - seg_start
    return pick_columns(arrived, column)


def body(tracers, offsets, weights, diffusion, send_index, send_count):
    lon_width = tracers.shape[3]
    from_west = shifted(tracers[..., lon_width - HALO :], "lon", 1)
    from_east = shifted(tracers[..., :HALO], "lon", -1)
    extended = jnp.concatenate([from_west, tracers, from_east], axis=3)
    start_shift = offsets + HALO
    advected = jnp.zeros(tracers.shape, jnp.float32)
    for shift_value in range(2 * HALO + 1):
        west_part = jnp.where(start_shift == shift_value, 1.0 - weights, 0.0)
        east_part = jnp.where(start_shift + 1 == shift_value, weights, 0.0)
        window = extended[..., shift_value : shift_value + lon_width]
        advected = advected + west_part[None] * window
        advected = advected + east_part[None] * window
    columns = tracers.shape[2] * lon_width
    row_block = advected.reshape(NTR * LEV, columns)
    coef_rows = diffusion.reshape(LEV - 1, columns)
    index_flat = send_index[0].reshape(-1)
    counts_out = send_count.astype(jnp.float32)
    stacked = jnp.concatenate([row_block, coef_rows], axis=0)
    packed = pick_columns(stacked, index_flat)
    arrived, counts_in = (
        lax.all_to_all(packed, ("lon", "lat"), split_axis=1, concat_axis=1, tiled=True),
        lax.all_to_all(counts_out, ("lon", "lat"), split_axis=1, concat_axis=1, tiled=True),
    )
    owned = place_owned(arrived, counts_in, columns)
    values = owned[: NTR * LEV].reshape(NTR, LEV, columns)
    result = solve_columns(values, owned[NTR * LEV :])
    return result


def solution(mesh):
    return jax.shard_map(
        body,
        mesh=mesh,
        in_specs=(
            P(None, None, "lat", "lon"),
            P(None, "lat", "lon"),
            P(None, "lat", "lon"),
            P(None, "lat", "lon"),
            P(("lon", "lat"), None, None),
            P(("lon", "lat"), None),
        ),
        out_specs=P(None, None, ("lon", "lat")),
        check_vma=False,
    )
```

profile of v0, /device:TPU:0, one launch (start us, length us, event | category | flops | bytes accessed | tf_op | source)
XLA Modules:
  0.0 546.0 jit_solution(9551341975835855462)
XLA Ops:
  12.3 8.5 %compare_select_fusion.63 = (f32[10,64,128]{2,1,0:T(8,128)}, f32[10,64,128]{2,1,0:T(8,128)}, f32[10,64,128]{2,1,0:T(8,128)}, f32[10,64,128]{2,1,0:T(8,128)}, f32...) fusion(f32[10,64,128]{2,1,0:T(8,128)S(1)} %copy-done.1, ...), kind=kLoop, calls=%fused_computation.197 | loop fusion | flops 11141120 | bytes 21954560 | tf_op jit(solution)/shard_map/jit(_where)/select_n | solution.py:85
  22.8 22.4 %multiply_add_fusion = f32[3,10,64,128]{3,2,1,0:T(8,128)S(1)} fusion(f32[3,10,64,16]{3,2,1,0:T(8,128)S(1)} %copy.36, f32[3,10,64,128]{3,2,1,0:T(8,128)S(1)} %copy-done, f32[3,10,64,16]{3,2,1,0:T(8,128)S(1)} %copy.34, f32[10,64,128]{2,1,0:T(8,128)} %get-tuple-element.205, f32[10,64,128]{2,1,0:T(8,128)} %get-tuple-element.206, ...), kind=kLoop, calls=%fused_computation.132 | loop fusion | flops 39567360 | bytes 23511040 | tf_op jit(solution)/shard_map/add | solution.py:89
  46.1 225.1 %while.22 = (s32[]{:T(128)}, f32[32,39,512]{2,1,0:T(8,128)}, s32[32,512]{1,0:T(8,128)}, f32[39,8192]{1,0:T(8,128)S(1)}, s32[]{:T(128)}) while((s32[]{:T(128)}, f32[32,39,512]{2,1,0:T(8,128)}, s32[32,512]{1,0:T(8,128)}, f32[39,8192]{1,0:T(8,128)S(1)}, s32[]{:T(128)}) %tuple.146), condition=%wide.region_4.5_spmd.clone, body=%wide.region_3.4_spmd.clone.sunk | while | flops 1967128576 | bytes 1366593 | solution.py:57
  89.0 6.3 %fusion.94 = f32[32,39,512]{2,1,0:T(8,128)} fusion(f32[32,39,512]{2,1,0:T(8,128)} %get-tuple-element.268, s32[]{:T(128)} %get-tuple-element.267, f32[39,8192]{1,0:T(8,128)S(1)} %get-tuple-element.275, s32[512]{0:T(512)S(1)} %bitcast.89), kind=kOutput, calls=%fused_computation.6.clone.1 | convolution fusion | flops 1967128576 | bytes 1362432 | tf_op jit(solution)/shard_map/while/body/eval_jaxpr/dot_general | solution.py:53
  103.1 6.3 %fusion.94 = f32[32,39,512]{2,1,0:T(8,128)} fusion(f32[32,39,512]{2,1,0:T(8,128)} %get-tuple-element.268, s32[]{:T(128)} %get-tuple-element.267, f32[39,8192]{1,0:T(8,128)S(1)} %get-tuple-element.275, s32[512]{0:T(512)S(1)} %bitcast.89), kind=kOutput, calls=%fused_computation.6.clone.1 | convolution fusion | flops 1967128576 | bytes 1362432 | tf_op jit(solution)/shard_map/while/body/eval_jaxpr/dot_general | solution.py:53
  110.1 6.3 %fusion.94 = f32[32,39,512]{2,1,0:T(8,128)} fusion(f32[32,39,512]{2,1,0:T(8,128)} %get-tuple-element.268, s32[]{:T(128)} %get-tuple-element.267, f32[39,8192]{1,0:T(8,128)S(1)} %get-tuple-element.275, s32[512]{0:T(512)S(1)} %bitcast.89), kind=kOutput, calls=%fused_computation.6.clone.1 | convolution fusion | flops 1967128576 | bytes 1362432 | tf_op jit(solution)/shard_map/while/body/eval_jaxpr/dot_general | solution.py:53
  117.2 6.3 %fusion.94 = f32[32,39,512]{2,1,0:T(8,128)} fusion(f32[32,39,512]{2,1,0:T(8,128)} %get-tuple-element.268, s32[]{:T(128)} %get-tuple-element.267, f32[39,8192]{1,0:T(8,128)S(1)} %get-tuple-element.275, s32[512]{0:T(512)S(1)} %bitcast.89), kind=kOutput, calls=%fused_computation.6.clone.1 | convolution fusion | flops 1967128576 | bytes 1362432 | tf_op jit(solution)/shard_map/while/body/eval_jaxpr/dot_general | solution.py:53
  124.2 6.3 %fusion.94 = f32[32,39,512]{2,1,0:T(8,128)} fusion(f32[32,39,512]{2,1,0:T(8,128)} %get-tuple-element.268, s32[]{:T(128)} %get-tuple-element.267, f32[39,8192]{1,0:T(8,128)S(1)} %get-tuple-element.275, s32[512]{0:T(512)S(1)} %bitcast.89), kind=kOutput, calls=%fused_computation.6.clone.1 | convolution fusion | flops 1967128576 | bytes 1362432 | tf_op jit(solution)/shard_map/while/body/eval_jaxpr/dot_general | solution.py:53
  145.3 6.3 %fusion.94 = f32[32,39,512]{2,1,0:T(8,128)} fusion(f32[32,39,512]{2,1,0:T(8,128)} %get-tuple-element.268, s32[]{:T(128)} %get-tuple-element.267, f32[39,8192]{1,0:T(8,128)S(1)} %get-tuple-element.275, s32[512]{0:T(512)S(1)} %bitcast.89), kind=kOutput, calls=%fused_computation.6.clone.1 | convolution fusion | flops 1967128576 | bytes 1362432 | tf_op jit(solution)/shard_map/while/body/eval_jaxpr/dot_general | solution.py:53
  173.5 6.3 %fusion.94 = f32[32,39,512]{2,1,0:T(8,128)} fusion(f32[32,39,512]{2,1,0:T(8,128)} %get-tuple-element.268, s32[]{:T(128)} %get-tuple-element.267, f32[39,8192]{1,0:T(8,128)S(1)} %get-tuple-element.275, s32[512]{0:T(512)S(1)} %bitcast.89), kind=kOutput, calls=%fused_computation.6.clone.1 | convolution fusion | flops 1967128576 | bytes 1362432 | tf_op jit(solution)/shard_map/while/body/eval_jaxpr/dot_general | solution.py:53
  201.6 6.3 %fusion.94 = f32[32,39,512]{2,1,0:T(8,128)} fusion(f32[32,39,512]{2,1,0:T(8,128)} %get-tuple-element.268, s32[]{:T(128)} %get-tuple-element.267, f32[39,8192]{1,0:T(8,128)S(1)} %get-tuple-element.275, s32[512]{0:T(512)S(1)} %bitcast.89), kind=kOutput, calls=%fused_computation.6.clone.1 | convolution fusion | flops 1967128576 | bytes 1362432 | tf_op jit(solution)/shard_map/while/body/eval_jaxpr/dot_general | solution.py:53
  215.7 6.3 %fusion.94 = f32[32,39,512]{2,1,0:T(8,128)} fusion(f32[32,39,512]{2,1,0:T(8,128)} %get-tuple-element.268, s32[]{:T(128)} %get-tuple-element.267, f32[39,8192]{1,0:T(8,128)S(1)} %get-tuple-element.275, s32[512]{0:T(512)S(1)} %bitcast.89), kind=kOutput, calls=%fused_computation.6.clone.1 | convolution fusion | flops 1967128576 | bytes 1362432 | tf_op jit(solution)/shard_map/while/body/eval_jaxpr/dot_general | solution.py:53
  222.7 6.3 %fusion.94 = f32[32,39,512]{2,1,0:T(8,128)} fusion(f32[32,39,512]{2,1,0:T(8,128)} %get-tuple-element.268, s32[]{:T(128)} %get-tuple-element.267, f32[39,8192]{1,0:T(8,128)S(1)} %get-tuple-element.275, s32[512]{0:T(512)S(1)} %bitcast.89), kind=kOutput, calls=%fused_computation.6.clone.1 | convolution fusion | flops 1967128576 | bytes 1362432 | tf_op jit(solution)/shard_map/while/body/eval_jaxpr/dot_general | solution.py:53
  257.9 6.3 %fusion.94 = f32[32,39,512]{2,1,0:T(8,128)} fusion(f32[32,39,512]{2,1,0:T(8,128)} %get-tuple-element.268, s32[]{:T(128)} %get-tuple-element.267, f32[39,8192]{1,0:T(8,128)S(1)} %get-tuple-element.275, s32[512]{0:T(512)S(1)} %bitcast.89), kind=kOutput, calls=%fused_computation.6.clone.1 | convolution fusion | flops 1967128576 | bytes 1362432 | tf_op jit(solution)/shard_map/while/body/eval_jaxpr/dot_general | solution.py:53
  278.8 58.2 %all-to-all-done.1 = f32[39,32,512]{2,0,1:T(8,128)S(1)} async-done(((f32[39,32,512]{2,0,1:T(8,128)}), f32[39,32,512]{2,0,1:T(8,128)S(1)}, u32[]{:S(2)}, u32[]{:S(2)}) %all-to-all-start.1) | async-done | bytes 2555936 | tf_op jit(solution)/shard_map/all_to_all | solution.py:98
  340.5 190.3 %while.23 = (s32[]{:T(128)}, f32[16,39,512]{2,1,0:T(8,128)}, s32[16,512]{1,0:T(8,128)S(1)}, f32[39,16384]{1,0:T(8,128)S(1)}, s32[]{:T(128)}) while((s32[]{:T(128)}, f32[16,39,512]{2,1,0:T(8,128)}, s32[16,512]{1,0:T(8,128)S(1)}, f32[39,16384]{1,0:T(8,128)S(1)}, s32[]{:T(128)}) %tuple.145), condition=%wide.region_6.7_spmd.clone, body=%wide.region_5.6_spmd.clone.sunk | while | flops 3934257152 | bytes 2644545 | solution.py:57
  340.5 11.9 %fusion.96 = f32[16,39,512]{2,1,0:T(8,128)} fusion(f32[16,39,512]{2,1,0:T(8,128)} %get-tuple-element.283, s32[]{:T(128)} %get-tuple-element.282, f32[39,16384]{1,0:T(8,128)S(1)} %get-tuple-element.290, s32[512]{0:T(512)S(1)} %bitcast.90), kind=kOutput, calls=%fused_computation.12.clone.1 | convolution fusion | flops 3934257152 | bytes 2640384 | tf_op jit(solution)/shard_map/while/body/eval_jaxpr/dot_general | solution.py:53
  352.4 11.9 %fusion.96 = f32[16,39,512]{2,1,0:T(8,128)} fusion(f32[16,39,512]{2,1,0:T(8,128)} %get-tuple-element.283, s32[]{:T(128)} %get-tuple-element.282, f32[39,16384]{1,0:T(8,128)S(1)} %get-tuple-element.290, s32[512]{0:T(512)S(1)} %bitcast.90), kind=kOutput, calls=%fused_computation.12.clone.1 | convolution fusion | flops 3934257152 | bytes 2640384 | tf_op jit(solution)/shard_map/while/body/eval_jaxpr/dot_general | solution.py:53
  364.3 11.9 %fusion.96 = f32[16,39,512]{2,1,0:T(8,128)} fusion(f32[16,39,512]{2,1,0:T(8,128)} %get-tuple-element.283, s32[]{:T(128)} %get-tuple-element.282, f32[39,16384]{1,0:T(8,128)S(1)} %get-tuple-element.290, s32[512]{0:T(512)S(1)} %bitcast.90), kind=kOutput, calls=%fused_computation.12.clone.1 | convolution fusion | flops 3934257152 | bytes 2640384 | tf_op jit(solution)/shard_map/while/body/eval_jaxpr/dot_general | solution.py:53
  376.2 11.9 %fusion.96 = f32[16,39,512]{2,1,0:T(8,128)} fusion(f32[16,39,512]{2,1,0:T(8,128)} %get-tuple-element.283, s32[]{:T(128)} %get-tuple-element.282, f32[39,16384]{1,0:T(8,128)S(1)} %get-tuple-element.290, s32[512]{0:T(512)S(1)} %bitcast.90), kind=kOutput, calls=%fused_computation.12.clone.1 | convolution fusion | flops 3934257152 | bytes 2640384 | tf_op jit(solution)/shard_map/while/body/eval_jaxpr/dot_general | solution.py:53
  388.1 11.9 %fusion.96 = f32[16,39,512]{2,1,0:T(8,128)} fusion(f32[16,39,512]{2,1,0:T(8,128)} %get-tuple-element.283, s32[]{:T(128)} %get-tuple-element.282, f32[39,16384]{1,0:T(8,128)S(1)} %get-tuple-element.290, s32[512]{0:T(512)S(1)} %bitcast.90), kind=kOutput, calls=%fused_computation.12.clone.1 | convolution fusion | flops 3934257152 | bytes 2640384 | tf_op jit(solution)/shard_map/while/body/eval_jaxpr/dot_general | solution.py:53
  399.9 11.9 %fusion.96 = f32[16,39,512]{2,1,0:T(8,128)} fusion(f32[16,39,512]{2,1,0:T(8,128)} %get-tuple-element.283, s32[]{:T(128)} %get-tuple-element.282, f32[39,16384]{1,0:T(8,128)S(1)} %get-tuple-element.290, s32[512]{0:T(512)S(1)} %bitcast.90), kind=kOutput, calls=%fused_computation.12.clone.1 | convolution fusion | flops 3934257152 | bytes 2640384 | tf_op jit(solution)/shard_map/while/body/eval_jaxpr/dot_general | solution.py:53
  411.8 11.9 %fusion.96 = f32[16,39,512]{2,1,0:T(8,128)} fusion(f32[16,39,512]{2,1,0:T(8,128)} %get-tuple-element.283, s32[]{:T(128)} %get-tuple-element.282, f32[39,16384]{1,0:T(8,128)S(1)} %get-tuple-element.290, s32[512]{0:T(512)S(1)} %bitcast.90), kind=kOutput, calls=%fused_computation.12.clone.1 | convolution fusion | flops 3934257152 | bytes 2640384 | tf_op jit(solution)/shard_map/while/body/eval_jaxpr/dot_general | solution.py:53
  423.7 11.9 %fusion.96 = f32[16,39,512]{2,1,0:T(8,128)} fusion(f32[16,39,512]{2,1,0:T(8,128)} %get-tuple-element.283, s32[]{:T(128)} %get-tuple-element.282, f32[39,16384]{1,0:T(8,128)S(1)} %get-tuple-element.290, s32[512]{0:T(512)S(1)} %bitcast.90), kind=kOutput, calls=%fused_computation.12.clone.1 | convolution fusion | flops 3934257152 | bytes 2640384 | tf_op jit(solution)/shard_map/while/body/eval_jaxpr/dot_general | solution.py:53
  435.6 11.9 %fusion.96 = f32[16,39,512]{2,1,0:T(8,128)} fusion(f32[16,39,512]{2,1,0:T(8,128)} %get-tuple-element.283, s32[]{:T(128)} %get-tuple-element.282, f32[39,16384]{1,0:T(8,128)S(1)} %get-tuple-element.290, s32[512]{0:T(512)S(1)} %bitcast.90), kind=kOutput, calls=%fused_computation.12.clone.1 | convolution fusion | flops 3934257152 | bytes 2640384 | tf_op jit(solution)/shard_map/while/body/eval_jaxpr/dot_general | solution.py:53
  447.5 11.9 %fusion.96 = f32[16,39,512]{2,1,0:T(8,128)} fusion(f32[16,39,512]{2,1,0:T(8,128)} %get-tuple-element.283, s32[]{:T(128)} %get-tuple-element.282, f32[39,16384]{1,0:T(8,128)S(1)} %get-tuple-element.290, s32[512]{0:T(512)S(1)} %bitcast.90), kind=kOutput, calls=%fused_computation.12.clone.1 | convolution fusion | flops 3934257152 | bytes 2640384 | tf_op jit(solution)/shard_map/while/body/eval_jaxpr/dot_general | solution.py:53
  459.4 11.9 %fusion.96 = f32[16,39,512]{2,1,0:T(8,128)} fusion(f32[16,39,512]{2,1,0:T(8,128)} %get-tuple-element.283, s32[]{:T(128)} %get-tuple-element.282, f32[39,16384]{1,0:T(8,128)S(1)} %get-tuple-element.290, s32[512]{0:T(512)S(1)} %bitcast.90), kind=kOutput, calls=%fused_computation.12.clone.1 | convolution fusion | flops 3934257152 | bytes 2640384 | tf_op jit(solution)/shard_map/while/body/eval_jaxpr/dot_general | solution.py:53
  471.3 11.9 %fusion.96 = f32[16,39,512]{2,1,0:T(8,128)} fusion(f32[16,39,512]{2,1,0:T(8,128)} %get-tuple-element.283, s32[]{:T(128)} %get-tuple-element.282, f32[39,16384]{1,0:T(8,128)S(1)} %get-tuple-element.290, s32[512]{0:T(512)S(1)} %bitcast.90), kind=kOutput, calls=%fused_computation.12.clone.1 | convolution fusion | flops 3934257152 | bytes 2640384 | tf_op jit(solution)/shard_map/while/body/eval_jaxpr/dot_general | solution.py:53
  483.2 11.9 %fusion.96 = f32[16,39,512]{2,1,0:T(8,128)} fusion(f32[16,39,512]{2,1,0:T(8,128)} %get-tuple-element.283, s32[]{:T(128)} %get-tuple-element.282, f32[39,16384]{1,0:T(8,128)S(1)} %get-tuple-element.290, s32[512]{0:T(512)S(1)} %bitcast.90), kind=kOutput, calls=%fused_computation.12.clone.1 | convolution fusion | flops 3934257152 | bytes 2640384 | tf_op jit(solution)/shard_map/while/body/eval_jaxpr/dot_general | solution.py:53
  495.1 11.9 %fusion.96 = f32[16,39,512]{2,1,0:T(8,128)} fusion(f32[16,39,512]{2,1,0:T(8,128)} %get-tuple-element.283, s32[]{:T(128)} %get-tuple-element.282, f32[39,16384]{1,0:T(8,128)S(1)} %get-tuple-element.290, s32[512]{0:T(512)S(1)} %bitcast.90), kind=kOutput, calls=%fused_computation.12.clone.1 | convolution fusion | flops 3934257152 | bytes 2640384 | tf_op jit(solution)/shard_map/while/body/eval_jaxpr/dot_general | solution.py:53
  507.0 11.9 %fusion.96 = f32[16,39,512]{2,1,0:T(8,128)} fusion(f32[16,39,512]{2,1,0:T(8,128)} %get-tuple-element.283, s32[]{:T(128)} %get-tuple-element.282, f32[39,16384]{1,0:T(8,128)S(1)} %get-tuple-element.290, s32[512]{0:T(512)S(1)} %bitcast.90), kind=kOutput, calls=%fused_computation.12.clone.1 | convolution fusion | flops 3934257152 | bytes 2640384 | tf_op jit(solution)/shard_map/while/body/eval_jaxpr/dot_general | solution.py:53
  518.9 11.9 %fusion.96 = f32[16,39,512]{2,1,0:T(8,128)} fusion(f32[16,39,512]{2,1,0:T(8,128)} %get-tuple-element.283, s32[]{:T(128)} %get-tuple-element.282, f32[39,16384]{1,0:T(8,128)S(1)} %get-tuple-element.290, s32[512]{0:T(512)S(1)} %bitcast.90), kind=kOutput, calls=%fused_computation.12.clone.1 | convolution fusion | flops 3934257152 | bytes 2640384 | tf_op jit(solution)/shard_map/while/body/eval_jaxpr/dot_general | solution.py:53
  (148 shorter events, 196.7 us)
Async XLA Ops:
  1.9 6.1 %copy-start.12 = (s32[1,32]{1,0:T(1,128)S(1)}, s32[1,32]{1,0:T(1,128)}, u32[]{:S(2)}) copy-start(s32[1,32]{1,0:T(1,128)} %param.15) | copy-start | bytes 388
  1.9 10.4 %copy-start.1 = (f32[10,64,128]{2,1,0:T(8,128)S(1)}, f32[10,64,128]{2,1,0:T(8,128)}, u32[]{:S(2)}) copy-start(f32[10,64,128]{2,1,0:T(8,128)} %param.12) | copy-start | bytes 983044
  1.9 10.4 %copy-start.2 = (s32[10,64,128]{2,1,0:T(8,128)S(1)}, s32[10,64,128]{2,1,0:T(8,128)}, u32[]{:S(2)}) copy-start(s32[10,64,128]{2,1,0:T(8,128)} %param.11) | copy-start | bytes 983044
  2.2 19.0 %collective-permute-start = (f32[3,10,64,16]{2,3,1,0:T(8,128)S(1)}, f32[3,10,64,16]{2,3,1,0:T(8,128)S(1)}, u32[]{:S(2)}, u32[]{:S(2)}) collective-permute-start(f32[3,10,64,16]{2,3,1,0:T(8,128)S(1)} %copy.40), channel_id=1, source_target_pairs={{30,0},{0,2},{2,4},{4,6},{6,8},{8,10},{10,12},{12,14},{14,16},{16,... | collective-permute-start | bytes 368648 | tf_op jit(solution)/shard_map/ppermute | solution.py:14
  3.0 18.6 %collective-permute-start.1 = (f32[3,10,64,16]{2,3,1,0:T(8,128)S(1)}, f32[3,10,64,16]{2,3,1,0:T(8,128)}, u32[]{:S(2)}, u32[]{:S(2)}) collective-permute-start(f32[3,10,64,16]{2,3,1,0:T(8,128)S(1)} %copy.41), channel_id=1, source_target_pairs={{2,0},{4,2},{6,4},{8,6},{10,8},{12,10},{14,12},{16,14},{18,16},{20... | collective-permute-start | bytes 368648 | tf_op jit(solution)/shard_map/ppermute | solution.py:14
  8.7 262.6 %all-to-all-start = ((f32[1,32,1]{2,0,1:T(1,128)}), f32[1,32,1]{2,0,1:T(1,128)S(1)}, u32[]{:S(2)}, u32[]{:S(2)}) async-start(f32[1,32,1]{2,0,1:T(1,128)} %copy.31), calls=%async_computation | async-start | bytes 32768 | tf_op jit(solution)/shard_map/all_to_all | solution.py:99
  12.3 8.5 %copy-start.3 = (f32[9,64,128]{2,1,0:T(8,128)S(1)}, f32[9,64,128]{2,1,0:T(8,128)}, u32[]{:S(2)}) copy-start(f32[9,64,128]{2,1,0:T(8,128)} %param.13) | copy-start | bytes 884740
  20.9 2.0 copy-start
  271.2 65.8 %all-to-all-start.1 = ((f32[39,32,512]{2,0,1:T(8,128)}), f32[39,32,512]{2,0,1:T(8,128)S(1)}, u32[]{:S(2)}, u32[]{:S(2)}) async-start(f32[39,32,512]{2,0,1:T(8,128)} %bitcast.58), calls=%async_computation.1 | async-start | bytes 5242880 | tf_op jit(solution)/shard_map/all_to_all | solution.py:98
  540.4 1.3 copy-start.4
  540.4 1.3 copy-start.5
  540.4 1.3 copy-start.6
  540.4 1.3 copy-start.7
  540.4 1.3 copy-start.8
  540.4 1.3 copy-start.9
  540.5 1.3 copy-start.10
  540.5 1.3 copy-start.11
where the time goes:
time: 549 us; the launch traced here: 546 us
  matrix products  392 us (71%)
  waiting for transfers between devices  58.2 us (11%)
  local copies, waits for them, and re-layouts  40.8 us (7%)
  other arithmetic  39.4 us (7%)
  starting transfers between devices  14.9 us (3%)
    dot_general x48, matrix products, one_block(): jnp.dot(source, selector, precision=lax.Precision.HIGHEST, preferred_elem...  392 us
    all_to_all x1, waiting for transfers between devices, body(): lax.all_to_all(packed, ('lon', 'lat'), split_axis=1, concat_axis=1, tiled...  58.2 us
    dynamic_slice x48, local copies, waits for them, and re-layouts, pick_columns(): picked = lax.map(one_block, blocks)  23.2 us
    add x1, other arithmetic, body(): advected = advected + east_part[None] * window  22.4 us
  transfers between devices with their start and end apart: 4, of which 1 were waited for; matrix products, arithmetic and copies ran while one was open for 48% of the time, Pallas kernels for 0%

commit v1 on v0

v1 whole, which is shorter than its diff:
```python
import functools

import jax
import jax.numpy as jnp
from jax import lax
from jax.experimental import pallas as pl
from jax.experimental.pallas import tpu as pltpu
from jax.sharding import PartitionSpec as P

HALO = 16
LANES = 128
SUB = 8
VMEM_LIMIT = 56 * 1024 * 1024


def take_lanes(block, index):
    return jnp.take_along_axis(block, index, axis=1, mode="promise_in_bounds")


def lane_ids(rows):
    return lax.broadcasted_iota(jnp.int32, (rows, LANES), 1)


def pack_halo_kernel(tracers, west_cells, east_cells):
    ntr, levels, lats, _ = tracers.shape
    per_row = LANES // HALO
    group = lane_ids(SUB) // HALO

    def one_level(level, carry):
        for tracer in range(ntr):
            west = jnp.zeros((SUB, LANES), jnp.float32)
            east = jnp.zeros((SUB, LANES), jnp.float32)
            for part in range(lats // SUB):
                cells = tracers[tracer, level, part * SUB : (part + 1) * SUB, :]
                shift = part * HALO
                rolled_west = pltpu.roll(cells, shift, 1) if shift else cells
                shift = (part * HALO + HALO) % LANES
                rolled_east = pltpu.roll(cells, shift, 1) if shift else cells
                west = jnp.where(group == part, rolled_west, west)
                east = jnp.where(group == part, rolled_east, east)
            west_cells[level, tracer] = west
            east_cells[level, tracer] = east
        return carry

    assert lats == SUB * per_row
    lax.fori_loop(0, levels, one_level, 0)


def pack_halo(tracers):
    ntr, levels, _, _ = tracers.shape
    shape = jax.ShapeDtypeStruct((levels, ntr, SUB, LANES), jnp.float32)
    return pl.pallas_call(
        pack_halo_kernel,
        out_shape=(shape, shape),
        in_specs=[pl.BlockSpec(memory_space=pltpu.VMEM)],
        out_specs=[pl.BlockSpec(memory_space=pltpu.VMEM)] * 2,
        compiler_params=pltpu.CompilerParams(vmem_limit_bytes=VMEM_LIMIT),
        name="pack_halo",
    )(tracers)


def merge_halo(west, east, halo, count):
    lane = lane_ids(SUB)
    cell = lane % (2 * HALO)
    for half in range(2):
        source = (half * 4 + lane // (2 * HALO)) * HALO + cell % HALO

        def one_value(value, carry, half=half, source=source):
            merged = jnp.where(cell < HALO, take_lanes(west[value], source), take_lanes(east[value], source))
            halo[value, half] = merged
            return carry

        lax.fori_loop(0, count, one_value, 0)


def advect_and_solve(tracers, offsets, weights, diffusion, halo, solved):
    ntr, levels, lats, _ = tracers.shape
    lane = lane_ids(SUB)

    def one_part(part, carry):
        rows = pl.ds(pl.multiple_of(part * SUB, SUB), SUB)
        half = part // 4
        base = (part % 4) * (2 * HALO)
        coefs = [diffusion[level, rows, :] for level in range(levels - 1)]
        upper = []
        reduced = [[] for _ in range(ntr)]
        for level in range(levels):
            left = lane + offsets[level, rows, :]
            right = left + 1
            weight = weights[level, rows, :]
            left_in = (left >= 0) & (left < LANES)
            right_in = (right >= 0) & (right < LANES)
            left_main = left & (LANES - 1)
            right_main = right & (LANES - 1)
            left_halo = base + ((left + HALO) & (2 * HALO - 1))
            right_halo = base + ((right + HALO) & (2 * HALO - 1))
            denom = 1.0
            if level > 0:
                denom = denom + coefs[level - 1]
            if level < levels - 1:
                denom = denom + coefs[level]
            if level > 0:
                denom = denom - coefs[level - 1] * upper[level - 1]
            inverse = 1.0 / denom
            if level < levels - 1:
                upper.append(coefs[level] * inverse)
            for tracer in range(ntr):
                cells = tracers[tracer, level, rows, :]
                edge = halo[level * ntr + tracer, half]
                left_value = jnp.where(left_in, take_lanes(cells, left_main), take_lanes(edge, left_halo))
                right_value = jnp.where(right_in, take_lanes(cells, right_main), take_lanes(edge, right_halo))
                value = (1.0 - weight) * left_value + weight * right_value
                if level > 0:
                    value = value + coefs[level - 1] * reduced[tracer][level - 1]
                reduced[tracer].append(value * inverse)
        for tracer in range(ntr):
            x = reduced[tracer][levels - 1]
            solved[(levels - 1) * ntr + tracer, rows, :] = x
            for level in range(levels - 2, -1, -1):
                x = reduced[tracer][level] + upper[level] * x
                solved[level * ntr + tracer, rows, :] = x
        return carry

    lax.fori_loop(0, lats // SUB, one_part, 0)


def build_table(solved, table):
    values, lats, _ = solved.shape
    upper_half = lax.broadcasted_iota(jnp.int32, (SUB, LANES), 0) < 4

    def one_row(row, carry):
        tiles = []
        for pair in range(values // 2):
            first = jnp.broadcast_to(solved[2 * pair, pl.ds(row, 1), :], (SUB, LANES))
            second = jnp.broadcast_to(solved[2 * pair + 1, pl.ds(row, 1), :], (SUB, LANES))
            tiles.append(jnp.where(upper_half, first, second))
        while len(tiles) < LANES // SUB:
            tiles.append(jnp.zeros((SUB, LANES), jnp.float32))
        block = jnp.concatenate(tiles, axis=0)
        table[pl.ds(pl.multiple_of(row * LANES, LANES), LANES), :] = block.T
        return carry

    lax.fori_loop(0, lats, one_row, 0)


def pick_rows(table, index, count, packed, sent):
    blocks, height, _ = sent.shape
    parts = index.shape[2] // LANES
    lists = 4 // parts
    stream = lax.broadcasted_iota(jnp.int32, (1, LANES), 1) % 4

    def one_block(block, carry):
        owners = [block * lists + item for item in range(lists)]
        rows = [(count[0, owner] + (parts - 1)) // parts for owner in owners]
        longest = functools.reduce(jnp.maximum, rows)
        places = [(owners[g // parts], (g % parts) * rows[g // parts]) for g in range(4)]

        def eight_rows(step, inner):
            start = pl.multiple_of(step * SUB, SUB)
            for line in range(SUB):
                picked = [
                    table[pl.ds(index[0, owner, place + start + line], 1), :] for owner, place in places
                ]
                low = jnp.where(stream == 0, picked[0], picked[1])
                high = jnp.where(stream == 2, picked[2], picked[3])
                packed[pl.ds(start + line, 1), :] = jnp.where(stream < 2, low, high)
            return inner

        lax.fori_loop(0, (longest + (SUB - 1)) // SUB, eight_rows, 0)
        sent[block] = packed[...].T[:height, :]
        return carry

    lax.fori_loop(0, blocks, one_block, 0)


def send_kernel(tracers, offsets, weights, diffusion, west, east, index, count, sent, halo, solved, table, packed):
    merge_halo(west, east, halo, solved.shape[0])
    advect_and_solve(tracers, offsets, weights, diffusion, halo, solved)
    build_table(solved, table)
    packed[...] = jnp.zeros_like(packed)
    pick_rows(table, index, count, packed, sent)


def make_sent(tracers, offsets, weights, diffusion, west, east, index, count):
    ntr, levels, lats, lons = tracers.shape
    values = ntr * levels
    lists, cap = index.shape[1:]
    blocks = lists * (cap // LANES) // 4
    vmem = pl.BlockSpec(memory_space=pltpu.VMEM)
    smem = pl.BlockSpec(memory_space=pltpu.SMEM)
    return pl.pallas_call(
        send_kernel,
        out_shape=jax.ShapeDtypeStruct((blocks, 4 * values, LANES), jnp.float32),
        in_specs=[vmem] * 6 + [smem] * 2,
        out_specs=vmem,
        scratch_shapes=[
            pltpu.VMEM((values, 2, SUB, LANES), jnp.float32),
            pltpu.VMEM((values, lats, LANES), jnp.float32),
            pltpu.VMEM((lats * lons, LANES), jnp.float32),
            pltpu.VMEM((LANES, LANES), jnp.float32),
        ],
        compiler_params=pltpu.CompilerParams(vmem_limit_bytes=VMEM_LIMIT),
        name="advect_solve_pick",
    )(
        tracers,
        offsets,
        weights,
        diffusion,
        west.reshape(values, SUB, LANES),
        east.reshape(values, SUB, LANES),
        index,
        count,
    )


def place_kernel(arrived, counts, own, owned, row):
    sources, height, _ = arrived.shape
    levels, ntr, columns = owned.shape
    values = levels * ntr
    parts = height // values
    lane = lane_ids(1)

    def one_source(turn, start):
        source = lax.rem(own[0] - turn + sources, sources)
        total = counts[source, own[0]]
        rows = (total + (parts - 1)) // parts
        for part in range(parts):
            place = start + jnp.minimum(part * rows, total)
            tile = place // LANES
            shift = place % LANES
            piece = arrived[source, pl.ds(part, values, stride=parts), :]
            rolled = pltpu.roll(piece, shift, 1)
            here = pl.ds(pl.multiple_of(tile * LANES, LANES), LANES)
            after = pl.ds(pl.multiple_of(tile * LANES + LANES, LANES), LANES)
            row[:, here] = jnp.where(lane >= shift, rolled, row[:, here])
            row[:, after] = rolled
        return start + total

    lax.fori_loop(0, sources, one_source, 0)
    for level in range(levels):
        owned[level] = row[level * ntr : (level + 1) * ntr, :columns]


def place_owned(arrived, counts, own, levels, ntr, columns):
    vmem = pl.BlockSpec(memory_space=pltpu.VMEM)
    smem = pl.BlockSpec(memory_space=pltpu.SMEM)
    return pl.pallas_call(
        place_kernel,
        out_shape=jax.ShapeDtypeStruct((levels, ntr, columns), jnp.float32),
        in_specs=[vmem, smem, smem],
        out_specs=vmem,
        scratch_shapes=[pltpu.VMEM((levels * ntr, columns + 2 * LANES), jnp.float32)],
        compiler_params=pltpu.CompilerParams(vmem_limit_bytes=VMEM_LIMIT),
        name="place_owned",
    )(arrived, counts, own)


def ring(axis, distance):
    size = lax.axis_size(axis)
    return [(i, (i + distance) % size) for i in range(size)]


def body(tracers, offsets, weights, diffusion, send_index, send_count):
    ntr, levels, lats, lons = tracers.shape
    columns = lats * lons
    lists, cap = send_index.shape[1:]
    parts = cap // LANES
    values = ntr * levels
    west_cells, east_cells = pack_halo(tracers)
    from_west = lax.ppermute(east_cells, "lon", ring("lon", 1))
    from_east = lax.ppermute(west_cells, "lon", ring("lon", -1))
    counts = lax.all_gather(send_count, ("lon", "lat"), axis=0, tiled=True)
    sent = make_sent(tracers, offsets, weights, diffusion, from_west, from_east, send_index, send_count)
    if parts < 4:
        sent = sent.reshape(-1, values, 4 // parts, parts, LANES)
        sent = jnp.transpose(sent, (0, 2, 1, 3, 4)).reshape(lists, values * parts, LANES)
    arrived = lax.all_to_all(sent, ("lon", "lat"), split_axis=0, concat_axis=0, tiled=True)
    own = lax.axis_index(("lon", "lat")).astype(jnp.int32).reshape(1)
    owned = place_owned(arrived, counts, own, levels, ntr, columns)
    return jnp.transpose(owned, (1, 0, 2))


def solution(mesh):
    return jax.shard_map(
        body,
        mesh=mesh,
        in_specs=(
            P(None, None, "lat", "lon"),
            P(None, "lat", "lon"),
            P(None, "lat", "lon"),
            P(None, "lat", "lon"),
            P(("lon", "lat"), None, None),
            P(("lon", "lat"), None),
        ),
        out_specs=P(None, None, ("lon", "lat")),
        check_vma=False,
    )
```

time: 549 us -> 166 us (0.30)
  matrix products: 392 us -> 0 us
  blocking collectives: 0 us -> 96.2 us
  waiting for transfers between devices: 58.2 us -> 2.88 us
  Pallas kernels: 0 us -> 52.8 us
  other arithmetic: 39.4 us -> 0 us
  local copies, waits for them, and re-layouts: 40.8 us -> 2 us
    dot_general x48 -> x0, matrix products: 392 us -> none  [one_block(): jnp.dot(source, selector, precision=lax.Precision.HIGHEST, preferred_elem...]
    all_gather x0 -> x1, blocking collectives: none -> 96.2 us  [body(): counts = lax.all_gather(send_count, ('lon', 'lat'), axis=0, tiled=True)]
    all_to_all x2 -> x1, waiting for transfers between devices: 58.2 us -> 0.01 us  [body(): lax.all_to_all(sent, ('lon', 'lat'), split_axis=0, concat_axis=0, tiled=T...]
    pallas_call x0 -> x3, Pallas kernels: none -> 52.8 us  [the longest x1 43.5 us: make_sent(): pl.pallas_call(send_kernel, out_shape=jax.ShapeDtypeStruct((blocks, 4 * v...]
    dynamic_slice x49 -> x0, local copies, waits for them, and re-layouts: 23.3 us -> none  [the longest x48 23.2 us: pick_columns(): picked = lax.map(one_block, blocks)]
    add x2 -> x0, other arithmetic: 23 us -> none  [the longest x1 22.4 us: body(): advected = advected + east_part[None] * window]
    select_n x1 -> x0, other arithmetic: 8.46 us -> none  [body(): west_part = jnp.where(start_shift == shift_value, 1.0 - weights, 0.0)]
    slice x4 -> x0, local copies, waits for them, and re-layouts: 6.24 us -> none  [the longest x1 2.5 us: solve_columns(): term = term + coef_rows[level]]
  transfers between devices with their start and end apart: 4 -> 3, of which waited for: 1 -> 1; matrix products, arithmetic and copies ran while one was open for 48% -> 0% of each run, Pallas kernels for 0% -> 0%
where the time goes in v1:
time: 166 us
  blocking collectives  96.2 us (58%)
  Pallas kernels  52.8 us (32%)
  starting transfers between devices  11.5 us (7%)
  waiting for transfers between devices  2.88 us (2%)
  local copies, waits for them, and re-layouts  2 us (1%)
    all_gather x1, blocking collectives, body(): counts = lax.all_gather(send_count, ('lon', 'lat'), axis=0, tiled=True)  96.2 us
    pallas_call x1, Pallas kernels, make_sent(): pl.pallas_call(send_kernel, out_shape=jax.ShapeDtypeStruct((blocks, 4 * v...  43.5 us
    pallas_call x1, Pallas kernels, place_owned(): pl.pallas_call(place_kernel, out_shape=jax.ShapeDtypeStruct((levels, ntr,...  6.34 us
    all_to_all x1, starting transfers between devices, body(): lax.all_to_all(sent, ('lon', 'lat'), split_axis=0, concat_axis=0, tiled=T...  6.09 us
    ppermute x1, starting transfers between devices, body(): from_east = lax.ppermute(west_cells, 'lon', ring('lon', -1))  4.97 us
  transfers between devices with their start and end apart: 3, of which 1 were waited for; matrix products, arithmetic and copies ran while one was open for 0% of the time, Pallas kernels for 0%

profile of v1, /device:TPU:0, one launch (start us, length us, event | category | flops | bytes accessed | tf_op | source)
XLA Modules:
  0.0 165.5 jit_solution(6615433817230173693)
XLA Ops:
  0.0 3.0 %pack_halo.1 = (f32[10,3,8,128]{3,2,1,0:T(8,128)}, f32[10,3,8,128]{3,2,1,0:T(8,128)}) custom-call(f32[3,10,64,128]{3,2,1,0:T(8,128)} %tracers.3), custom_call_target="tpu_custom_call" | custom-call | tf_op jit(solution)/shard_map/pack_halo/pallas_call | solution.py:52
  3.0 0.5 collective-permute-start
  3.5 5.0 %collective-permute-start.1 = (f32[10,3,8,128]{3,2,1,0:T(8,128)}, f32[10,3,8,128]{3,2,1,0:T(8,128)S(1)}, u32[]{:S(2)}, u32[]{:S(2)}) collective-permute-start(f32[10,3,8,128]{3,2,1,0:T(8,128)} %get-tuple-element.8), channel_id=1, source_target_pairs={{0,30},{2,0},{4,2},{6,4},{8,6},{10,8},{12,10},{14,12},{16,14},{18,... | collective-permute-start | bytes 368648 | tf_op jit(solution)/shard_map/ppermute | solution.py:271
  8.4 2.9 %collective-permute-done = f32[10,3,8,128]{3,2,1,0:T(8,128)S(1)} collective-permute-done((f32[10,3,8,128]{3,2,1,0:T(8,128)}, f32[10,3,8,128]{3,2,1,0:T(8,128)S(1)}, u32[]{:S(2)}, u32[]{:S(2)}) %collective-permute-start) | collective-permute-done | bytes 122912 | tf_op jit(solution)/shard_map/ppermute | solution.py:270
  11.3 0.0 copy-start.1
  11.3 0.0 collective-permute-done.1
  11.3 0.0 copy-start.2
  11.3 0.7 copy-done.1
  12.0 0.0 copy-done.2
  12.0 43.5 %advect_solve_pick.1 = f32[32,120,128]{2,1,0:T(8,128)} custom-call(f32[3,10,64,128]{3,2,1,0:T(8,128)} %tracers.3, s32[10,64,128]{2,1,0:T(8,128)} %offsets.1, f32[10,64,128]{2,1,0:T(8,128)} %weights.1, f32[9,64,128]{2,1,0:T(8,128)} %diffusion.1, f32[30,8,128]{2,1,0:T(8,128)} %bitcast.6, f32[30,8,128]{2,1,0:T(8,128)} %bitcast.7, s32[1,32,512]{2,1,0:T(8,128)} %index.1, ...), custom_call_target="tpu_custom_call" | custom-call | tf_op jit(solution)/shard_map/advect_solve_pick/pallas_call | solution.py:191
  55.5 0.0 copy-start.3
  55.5 6.1 %all-to-all-start = ((f32[32,120,128]{2,1,0:T(8,128)}), f32[32,120,128]{2,1,0:T(8,128)S(1)}, u32[]{:S(2)}, u32[]{:S(2)}) async-start(f32[32,120,128]{2,1,0:T(8,128)} %advect_solve_pick.1), calls=%async_computation | async-start | bytes 3932160 | tf_op jit(solution)/shard_map/all_to_all | solution.py:277
  61.6 0.0 copy-done.3
  61.6 96.2 %all-gather = s32[32,1,32]{2,1,0:T(1,128)} all-gather(s32[1,1,32]{2,1,0:T(1,128)S(1)} %bitcast.9), channel_id=1, replica_groups=mesh['lon'=16,'lat'=2] {'lon','lat'}, dimensions={0}, use_global_device_ids=true | all-gather | bytes 4224 | tf_op jit(solution)/shard_map/all_gather | solution.py:272
  157.9 0.0 all-to-all-done.arrived
  157.9 0.0 copy-start
  157.9 1.3 copy-done
  159.2 6.3 %place_owned.1 = f32[10,3,8192]{2,1,0:T(4,128)} custom-call(f32[32,120,128]{2,1,0:T(8,128)} %copy-done, s32[32,32]{1,0:T(8,128)} %bitcast.8, s32[1]{0:T(128)} %bitcast.4.own), custom_call_target="tpu_custom_call" | custom-call | tf_op jit(solution)/shard_map/place_owned/pallas_call | solution.py:247
Async XLA Ops:
  3.0 8.3 %collective-permute-start = (f32[10,3,8,128]{3,2,1,0:T(8,128)}, f32[10,3,8,128]{3,2,1,0:T(8,128)S(1)}, u32[]{:S(2)}, u32[]{:S(2)}) collective-permute-start(f32[10,3,8,128]{3,2,1,0:T(8,128)} %get-tuple-element.7), channel_id=1, source_target_pairs={{0,2},{2,4},{4,6},{6,8},{8,10},{10,12},{12,14},{14,16},{16,18},{18... | collective-permute-start | bytes 368648 | tf_op jit(solution)/shard_map/ppermute | solution.py:270
  3.5 7.8 %collective-permute-start.1 = (f32[10,3,8,128]{3,2,1,0:T(8,128)}, f32[10,3,8,128]{3,2,1,0:T(8,128)S(1)}, u32[]{:S(2)}, u32[]{:S(2)}) collective-permute-start(f32[10,3,8,128]{3,2,1,0:T(8,128)} %get-tuple-element.8), channel_id=1, source_target_pairs={{0,30},{2,0},{4,2},{6,4},{8,6},{10,8},{12,10},{14,12},{16,14},{18,... | collective-permute-start | bytes 368648 | tf_op jit(solution)/shard_map/ppermute | solution.py:271
  11.3 0.7 copy-start.1
  11.3 0.7 copy-start.2
  55.5 6.1 %copy-start.3 = (s32[1,32]{1,0:T(1,128)S(1)}, s32[1,32]{1,0:T(1,128)}, u32[]{:S(2)}) copy-start(s32[1,32]{1,0:T(1,128)} %count.1) | copy-start | bytes 388
  55.5 102.4 %all-to-all-start = ((f32[32,120,128]{2,1,0:T(8,128)}), f32[32,120,128]{2,1,0:T(8,128)S(1)}, u32[]{:S(2)}, u32[]{:S(2)}) async-start(f32[32,120,128]{2,1,0:T(8,128)} %advect_solve_pick.1), calls=%async_computation | async-start | bytes 3932160 | tf_op jit(solution)/shard_map/all_to_all | solution.py:277
  157.9 1.3 copy-start

commit v2 on v1

--- a/solution.py
+++ b/solution.py
@@ -10,7 +10,8 @@
 HALO = 16
 LANES = 128
 SUB = 8
-VMEM_LIMIT = 56 * 1024 * 1024
+SLOT = 32
+MIB = 1024 * 1024
 
 
 def take_lanes(block, index):
@@ -54,7 +55,7 @@
         out_shape=(shape, shape),
         in_specs=[pl.BlockSpec(memory_space=pltpu.VMEM)],
         out_specs=[pl.BlockSpec(memory_space=pltpu.VMEM)] * 2,
-        compiler_params=pltpu.CompilerParams(vmem_limit_bytes=VMEM_LIMIT),
+        compiler_params=pltpu.CompilerParams(vmem_limit_bytes=16 * MIB),
         name="pack_halo",
     )(tracers)
 
@@ -115,32 +116,27 @@
                 reduced[tracer].append(value * inverse)
         for tracer in range(ntr):
             x = reduced[tracer][levels - 1]
-            solved[(levels - 1) * ntr + tracer, rows, :] = x
-            for level in range(levels - 2, -1, -1):
-                x = reduced[tracer][level] + upper[level] * x
-                solved[level * ntr + tracer, rows, :] = x
+            for level in range(levels - 1, -1, -1):
+                if level < levels - 1:
+                    x = reduced[tracer][level] + upper[level] * x
+                solved[pl.ds(part * SUB * SLOT + level * ntr + tracer, SUB, stride=SLOT), :] = x
         return carry
 
     lax.fori_loop(0, lats // SUB, one_part, 0)
 
 
 def build_table(solved, table):
-    values, lats, _ = solved.shape
-    upper_half = lax.broadcasted_iota(jnp.int32, (SUB, LANES), 0) < 4
-
-    def one_row(row, carry):
-        tiles = []
-        for pair in range(values // 2):
-            first = jnp.broadcast_to(solved[2 * pair, pl.ds(row, 1), :], (SUB, LANES))
-            second = jnp.broadcast_to(solved[2 * pair + 1, pl.ds(row, 1), :], (SUB, LANES))
-            tiles.append(jnp.where(upper_half, first, second))
-        while len(tiles) < LANES // SUB:
-            tiles.append(jnp.zeros((SUB, LANES), jnp.float32))
-        block = jnp.concatenate(tiles, axis=0)
-        table[pl.ds(pl.multiple_of(row * LANES, LANES), LANES), :] = block.T
-        return carry
-
-    lax.fori_loop(0, lats, one_row, 0)
+    rows_per = LANES // SLOT
+    spread = lane_ids(LANES) // 4
+
+    def four_rows(step, carry):
+        block = solved[pl.ds(pl.multiple_of(step * LANES, LANES), LANES), :].T
+        for item in range(rows_per):
+            start = pl.multiple_of((step * rows_per + item) * LANES, LANES)
+            table[pl.ds(start, LANES), :] = take_lanes(block, spread + item * SLOT)
+        return carry
+
+    lax.fori_loop(0, solved.shape[0] // LANES, four_rows, 0)
 
 
 def pick_rows(table, index, count, packed, sent):
@@ -159,7 +155,7 @@
             start = pl.multiple_of(step * SUB, SUB)
             for line in range(SUB):
                 picked = [
-                    table[pl.ds(index[0, owner, place + start + line], 1), :] for owner, place in places
+                    table[index[0, owner, place + start + line]] for owner, place in places
                 ]
                 low = jnp.where(stream == 0, picked[0], picked[1])
                 high = jnp.where(stream == 2, picked[2], picked[3])
@@ -173,34 +169,30 @@
     lax.fori_loop(0, blocks, one_block, 0)
 
 
-def send_kernel(tracers, offsets, weights, diffusion, west, east, index, count, sent, halo, solved, table, packed):
-    merge_halo(west, east, halo, solved.shape[0])
+def solve_kernel(tracers, offsets, weights, diffusion, west, east, table, halo, solved):
+    values = west.shape[0]
+    merge_halo(west, east, halo, values)
+    for value in range(values, SLOT):
+        solved[pl.ds(value, tracers.shape[2], stride=SLOT), :] = jnp.zeros((tracers.shape[2], LANES), jnp.float32)
     advect_and_solve(tracers, offsets, weights, diffusion, halo, solved)
     build_table(solved, table)
-    packed[...] = jnp.zeros_like(packed)
-    pick_rows(table, index, count, packed, sent)
-
-
-def make_sent(tracers, offsets, weights, diffusion, west, east, index, count):
+
+
+def make_table(tracers, offsets, weights, diffusion, west, east):
     ntr, levels, lats, lons = tracers.shape
     values = ntr * levels
-    lists, cap = index.shape[1:]
-    blocks = lists * (cap // LANES) // 4
     vmem = pl.BlockSpec(memory_space=pltpu.VMEM)
-    smem = pl.BlockSpec(memory_space=pltpu.SMEM)
     return pl.pallas_call(
-        send_kernel,
-        out_shape=jax.ShapeDtypeStruct((blocks, 4 * values, LANES), jnp.float32),
-        in_specs=[vmem] * 6 + [smem] * 2,
+        solve_kernel,
+        out_shape=jax.ShapeDtypeStruct((lats * lons, LANES), jnp.float32),
+        in_specs=[vmem] * 6,
         out_specs=vmem,
         scratch_shapes=[
             pltpu.VMEM((values, 2, SUB, LANES), jnp.float32),
-            pltpu.VMEM((values, lats, LANES), jnp.float32),
-            pltpu.VMEM((lats * lons, LANES), jnp.float32),
-            pltpu.VMEM((LANES, LANES), jnp.float32),
+            pltpu.VMEM((lats * SLOT, LANES), jnp.float32),
         ],
-        compiler_params=pltpu.CompilerParams(vmem_limit_bytes=VMEM_LIMIT),
-        name="advect_solve_pick",
+        compiler_params=pltpu.CompilerParams(vmem_limit_bytes=16 * MIB),
+        name="advect_solve",
     )(
         tracers,
         offsets,
@@ -208,27 +200,54 @@
         diffusion,
         west.reshape(values, SUB, LANES),
         east.reshape(values, SUB, LANES),
-        index,
-        count,
     )
 
 
-def place_kernel(arrived, counts, own, owned, row):
+def pick_kernel(table, index, count, sent, packed):
+    packed[...] = jnp.zeros_like(packed)
+    pick_rows(table, index, count, packed, sent)
+
+
+def pick_columns(table, index, count, values):
+    lists, cap = index.shape[1:]
+    blocks = lists * (cap // LANES) // 4
+    vmem = pl.BlockSpec(memory_space=pltpu.VMEM)
+    smem = pl.BlockSpec(memory_space=pltpu.SMEM)
+    return pl.pallas_call(
+        pick_kernel,
+        out_shape=jax.ShapeDtypeStruct((blocks, 4 * values, LANES), jnp.float32),
+        in_specs=[vmem, smem, smem],
+        out_specs=vmem,
+        scratch_shapes=[pltpu.VMEM((LANES, LANES), jnp.float32)],
+        compiler_params=pltpu.CompilerParams(vmem_limit_bytes=16 * MIB),
+        name="pick_columns",
+    )(table.reshape(-1, 1, LANES), index, count)
+
+
+def place_kernel(arrived, counts, own, owned, held, row, ready):
     sources, height, _ = arrived.shape
     levels, ntr, columns = owned.shape
     values = levels * ntr
     parts = height // values
     lane = lane_ids(1)
 
+    def fetch(turn):
+        source = lax.rem(own[0] - turn + sources, sources)
+        return pltpu.make_async_copy(arrived.at[source], held.at[turn], ready.at[turn])
+
+    def start_fetch(turn, carry):
+        fetch(turn).start()
+        return carry
+
     def one_source(turn, start):
-        source = lax.rem(own[0] - turn + sources, sources)
-        total = counts[source, own[0]]
+        fetch(turn).wait()
+        total = counts[0, lax.rem(own[0] - turn + sources, sources)]
         rows = (total + (parts - 1)) // parts
         for part in range(parts):
             place = start + jnp.minimum(part * rows, total)
             tile = place // LANES
             shift = place % LANES
-            piece = arrived[source, pl.ds(part, values, stride=parts), :]
+            piece = held[turn, pl.ds(part, values, stride=parts), :]
             rolled = pltpu.roll(piece, shift, 1)
             here = pl.ds(pl.multiple_of(tile * LANES, LANES), LANES)
             after = pl.ds(pl.multiple_of(tile * LANES + LANES, LANES), LANES)
@@ -236,21 +255,27 @@
             row[:, after] = rolled
         return start + total
 
+    lax.fori_loop(0, sources, start_fetch, 0)
     lax.fori_loop(0, sources, one_source, 0)
     for level in range(levels):
         owned[level] = row[level * ntr : (level + 1) * ntr, :columns]
 
 
 def place_owned(arrived, counts, own, levels, ntr, columns):
+    sources = arrived.shape[0]
     vmem = pl.BlockSpec(memory_space=pltpu.VMEM)
     smem = pl.BlockSpec(memory_space=pltpu.SMEM)
     return pl.pallas_call(
         place_kernel,
         out_shape=jax.ShapeDtypeStruct((levels, ntr, columns), jnp.float32),
-        in_specs=[vmem, smem, smem],
+        in_specs=[pl.BlockSpec(memory_space=pl.ANY), smem, smem],
         out_specs=vmem,
-        scratch_shapes=[pltpu.VMEM((levels * ntr, columns + 2 * LANES), jnp.float32)],
-        compiler_params=pltpu.CompilerParams(vmem_limit_bytes=VMEM_LIMIT),
+        scratch_shapes=[
+            pltpu.VMEM(arrived.shape, jnp.float32),
+            pltpu.VMEM((levels * ntr, columns + 2 * LANES), jnp.float32),
+            pltpu.SemaphoreType.DMA((sources,)),
+        ],
+        compiler_params=pltpu.CompilerParams(vmem_limit_bytes=16 * MIB),
         name="place_owned",
     )(arrived, counts, own)
 
@@ -269,8 +294,9 @@
     west_cells, east_cells = pack_halo(tracers)
     from_west = lax.ppermute(east_cells, "lon", ring("lon", 1))
     from_east = lax.ppermute(west_cells, "lon", ring("lon", -1))
-    counts = lax.all_gather(send_count, ("lon", "lat"), axis=0, tiled=True)
-    sent = make_sent(tracers, offsets, weights, diffusion, from_west, from_east, send_index, send_count)
+    counts = lax.all_to_all(send_count, ("lon", "lat"), split_axis=1, concat_axis=1, tiled=True)
+    table = make_table(tracers, offsets, weights, diffusion, from_west, from_east)
+    sent = pick_columns(table, send_index, send_count, values)
     if parts < 4:
         sent = sent.reshape(-1, values, 4 // parts, parts, LANES)
         sent = jnp.transpose(sent, (0, 2, 1, 3, 4)).reshape(lists, values * parts, LANES)

time: 166 us -> 120 us (0.72)
  blocking collectives: 96.2 us -> 0 us
  waiting for transfers between devices: 2.88 us -> 45.2 us
  local copies, waits for them, and re-layouts: 2 us -> 6.65 us
  starting transfers between devices: 11.5 us -> 14.9 us
    all_gather x1 -> x0, blocking collectives: 96.2 us -> none  [body(): counts = lax.all_gather(send_count, ('lon', 'lat'), axis=0, tiled=True)]
    all_to_all x1, waiting for transfers between devices: 0.01 us -> 45.2 us  [body(): lax.all_to_all(sent, ('lon', 'lat'), split_axis=0, concat_axis=0, tiled=T...]
    all_to_all x0 -> x1, starting transfers between devices: none -> 3.56 us  [body(): lax.all_to_all(send_count, ('lon', 'lat'), split_axis=1, concat_axis=1, t...]
    unnamed x8 -> x14, local copies, waits for them, and re-layouts: 2 us -> 5.31 us
    ppermute x1, waiting for transfers between devices: 2.88 us -> 0.01 us  [body(): from_west = lax.ppermute(east_cells, 'lon', ring('lon', 1))]
    pallas_call x1, Pallas kernels: 6.34 us -> 8.61 us  [place_owned(): pl.pallas_call(place_kernel, out_shape=jax.ShapeDtypeStruct((levels, ntr,...]
    pallas_call x1, Pallas kernels: 3.02 us -> 1.12 us  [pack_halo(): pl.pallas_call(pack_halo_kernel, out_shape=(shape, shape), in_specs=[pl.B...]
    pallas_call x1 -> x2, Pallas kernels: 43.5 us -> 42.7 us  [the longest x1 29.4 us: pick_columns(): pl.pallas_call(pick_kernel, out_shape=jax.ShapeDtypeStruct((blocks, 4 * v...]
  transfers between devices with their start and end apart: 3 -> 4, of which waited for: 1 -> 1; matrix products, arithmetic and copies ran while one was open for 0% -> 2% of each run, Pallas kernels for 0% -> 36%
where the time goes in v2:
time: 120 us
  Pallas kernels  52.5 us (44%)
  waiting for transfers between devices  45.2 us (38%)
  starting transfers between devices  14.9 us (12%)
  local copies, waits for them, and re-layouts  6.65 us (6%)
    all_to_all x1, waiting for transfers between devices, body(): lax.all_to_all(sent, ('lon', 'lat'), split_axis=0, concat_axis=0, tiled=T...  45.2 us
    pallas_call x1, Pallas kernels, pick_columns(): pl.pallas_call(pick_kernel, out_shape=jax.ShapeDtypeStruct((blocks, 4 * v...  29.4 us
    pallas_call x1, Pallas kernels, make_table(): pl.pallas_call(solve_kernel, out_shape=jax.ShapeDtypeStruct((lats * lons,...  13.3 us
    pallas_call x1, Pallas kernels, place_owned(): pl.pallas_call(place_kernel, out_shape=jax.ShapeDtypeStruct((levels, ntr,...  8.61 us
    all_to_all x1, starting transfers between devices, body(): lax.all_to_all(sent, ('lon', 'lat'), split_axis=0, concat_axis=0, tiled=T...  5.83 us
    unnamed x14, local copies, waits for them, and re-layouts  5.31 us
    ppermute x1, starting transfers between devices, body(): from_east = lax.ppermute(west_cells, 'lon', ring('lon', -1))  5.03 us
    all_to_all x1, starting transfers between devices, body(): lax.all_to_all(send_count, ('lon', 'lat'), split_axis=1, concat_axis=1, t...  3.56 us
  transfers between devices with their start and end apart: 4, of which 1 were waited for; matrix products, arithmetic and copies ran while one was open for 2% of the time, Pallas kernels for 36%

profile of v2, /device:TPU:0, one launch (start us, length us, event | category | flops | bytes accessed | tf_op | source)
XLA Modules:
  0.0 120.0 jit_solution(5353736131259183728)
XLA Ops:
  0.0 0.0 copy-start
  0.0 1.2 copy-done
  1.2 1.1 pack_halo.1
  2.3 0.5 collective-permute-start
  2.8 5.0 %collective-permute-start.1 = (f32[10,3,8,128]{3,2,1,0:T(8,128)S(1)}, f32[10,3,8,128]{3,2,1,0:T(8,128)S(1)}, u32[]{:S(2)}, u32[]{:S(2)}) collective-permute-start(f32[10,3,8,128]{3,2,1,0:T(8,128)S(1)} %get-tuple-element.8), channel_id=1, source_target_pairs={{0,30},{2,0},{4,2},{6,4},{8,6},{10,8},{12,10},{14,12},{16,14},{18,... | collective-permute-start | bytes 368648 | tf_op jit(solution)/shard_map/ppermute | solution.py:296
  7.9 1.3 %copy.8 = s32[1,32,1]{2,0,1:T(1,128)} copy(s32[1,32,1]{1,2,0:T(1,128)} %bitcast.10) | data formatting | bytes 256 | tf_op jit(solution)/shard_map/all_to_all | solution.py:297
  9.2 3.6 %all-to-all-start.1 = ((s32[1,32,1]{2,0,1:T(1,128)}), s32[1,32,1]{2,0,1:T(1,128)S(1)}, u32[]{:S(2)}, u32[]{:S(2)}) async-start(s32[1,32,1]{2,0,1:T(1,128)} %copy.8), calls=%async_computation.1 | async-start | bytes 32768 | tf_op jit(solution)/shard_map/all_to_all | solution.py:297
  12.8 0.0 collective-permute-done
  12.8 0.0 collective-permute-done.1
  12.8 0.0 copy-start.1
  12.8 1.2 copy-done.1
  14.0 0.0 copy-start.2
  14.0 1.0 copy-done.2
  15.0 0.0 copy-start.3
  15.0 1.0 copy-done.3
  15.9 0.0 copy-start.4
  15.9 1.0 copy-done.4
  16.9 0.0 copy-start.5
  16.9 0.0 copy-start.6
  16.9 13.3 %advect_solve.1 = f32[8192,128]{1,0:T(8,128)S(1)} custom-call(f32[3,10,64,128]{3,2,1,0:T(8,128)S(1)} %copy-done.1, s32[10,64,128]{2,1,0:T(8,128)S(1)} %copy-done.2, f32[10,64,128]{2,1,0:T(8,128)S(1)} %copy-done.3, f32[9,64,128]{2,1,0:T(8,128)S(1)} %copy-done.4, f32[30,8,128]{2,1,0:T(8,128)S(1)} %bitcast.8, f32[30,8,128]{2,1,0:T(8,128)S(1)} %bitcast.9), custom_call_target="tpu_custom_call" | custom-call | tf_op jit(solution)/shard_map/advect_solve/pallas_call | solution.py:185
  30.2 0.0 copy-done.5
  30.2 0.0 copy-done.6
  30.2 29.4 %pick_columns.1 = f32[32,120,128]{2,1,0:T(8,128)} custom-call(f32[8192,1,128]{2,1,0:T(1,128)S(1)} %bitcast.7, s32[1,32,512]{2,1,0:T(8,128)S(1)} %copy-done.5, s32[1,32]{1,0:T(1,128)S(1)} %copy-done.6), custom_call_target="tpu_custom_call" | custom-call | tf_op jit(solution)/shard_map/pick_columns/pallas_call | solution.py:216
  59.7 0.0 all-to-all-done.1
  59.7 5.8 %all-to-all-start = ((f32[32,120,128]{2,1,0:T(8,128)}), f32[32,120,128]{2,1,0:T(8,128)S(1)}, u32[]{:S(2)}, u32[]{:S(2)}) async-start(f32[32,120,128]{2,1,0:T(8,128)} %pick_columns.1), calls=%async_computation | async-start | bytes 3932160 | tf_op jit(solution)/shard_map/all_to_all | solution.py:303
  65.5 0.7 reduce
  66.2 45.2 %all-to-all-done.arrived = f32[32,120,128]{2,1,0:T(8,128)S(1)} async-done(((f32[32,120,128]{2,1,0:T(8,128)}), f32[32,120,128]{2,1,0:T(8,128)S(1)}, u32[]{:S(2)}, u32[]{:S(2)}) %all-to-all-start) | async-done | bytes 1966112 | tf_op jit(solution)/shard_map/all_to_all | solution.py:303
  111.4 8.6 %place_owned.1 = f32[10,3,8192]{2,1,0:T(4,128)} custom-call(f32[32,120,128]{2,1,0:T(8,128)S(1)} %all-to-all-done.arrived, s32[1,32]{1,0:T(1,128)S(1)} %bitcast.11, s32[1]{0:T(128)} %bitcast.4.own), custom_call_target="tpu_custom_call" | custom-call | tf_op jit(solution)/shard_map/place_owned/pallas_call | solution.py:268
Async XLA Ops:
  0.0 1.2 %copy-start = (f32[3,10,64,128]{3,2,1,0:T(8,128)S(1)}, f32[3,10,64,128]{3,2,1,0:T(8,128)}, u32[]{:S(2)}) copy-start(f32[3,10,64,128]{3,2,1,0:T(8,128)} %tracers.3) | copy-start | bytes 2949124
  2.3 10.4 %collective-permute-start = (f32[10,3,8,128]{3,2,1,0:T(8,128)S(1)}, f32[10,3,8,128]{3,2,1,0:T(8,128)S(1)}, u32[]{:S(2)}, u32[]{:S(2)}) collective-permute-start(f32[10,3,8,128]{3,2,1,0:T(8,128)S(1)} %get-tuple-element.7), channel_id=1, source_target_pairs={{0,2},{2,4},{4,6},{6,8},{8,10},{10,12},{12,14},{14,16},{16,18},{18... | collective-permute-start | bytes 368648 | tf_op jit(solution)/shard_map/ppermute | solution.py:295
  2.8 10.0 %collective-permute-start.1 = (f32[10,3,8,128]{3,2,1,0:T(8,128)S(1)}, f32[10,3,8,128]{3,2,1,0:T(8,128)S(1)}, u32[]{:S(2)}, u32[]{:S(2)}) collective-permute-start(f32[10,3,8,128]{3,2,1,0:T(8,128)S(1)} %get-tuple-element.8), channel_id=1, source_target_pairs={{0,30},{2,0},{4,2},{6,4},{8,6},{10,8},{12,10},{14,12},{16,14},{18,... | collective-permute-start | bytes 368648 | tf_op jit(solution)/shard_map/ppermute | solution.py:296
  9.2 50.5 %all-to-all-start.1 = ((s32[1,32,1]{2,0,1:T(1,128)}), s32[1,32,1]{2,0,1:T(1,128)S(1)}, u32[]{:S(2)}, u32[]{:S(2)}) async-start(s32[1,32,1]{2,0,1:T(1,128)} %copy.8), calls=%async_computation.1 | async-start | bytes 32768 | tf_op jit(solution)/shard_map/all_to_all | solution.py:297
  12.8 1.2 %copy-start.1 = (f32[3,10,64,128]{3,2,1,0:T(8,128)S(1)}, f32[3,10,64,128]{3,2,1,0:T(8,128)}, u32[]{:S(2)}) copy-start(f32[3,10,64,128]{3,2,1,0:T(8,128)} %tracers.3) | copy-start | bytes 2949124
  14.0 1.0 copy-start.2
  15.0 1.0 copy-start.3
  15.9 1.0 copy-start.4
  16.9 13.3 %copy-start.5 = (s32[1,32,512]{2,1,0:T(8,128)S(1)}, s32[1,32,512]{2,1,0:T(8,128)}, u32[]{:S(2)}) copy-start(s32[1,32,512]{2,1,0:T(8,128)} %index.1) | copy-start | bytes 196612
  16.9 13.3 %copy-start.6 = (s32[1,32]{1,0:T(1,128)S(1)}, s32[1,32]{1,0:T(1,128)}, u32[]{:S(2)}) copy-start(s32[1,32]{1,0:T(1,128)} %count.1) | copy-start | bytes 388
  59.7 51.7 %all-to-all-start = ((f32[32,120,128]{2,1,0:T(8,128)}), f32[32,120,128]{2,1,0:T(8,128)S(1)}, u32[]{:S(2)}, u32[]{:S(2)}) async-start(f32[32,120,128]{2,1,0:T(8,128)} %pick_columns.1), calls=%async_computation | async-start | bytes 3932160 | tf_op jit(solution)/shard_map/all_to_all | solution.py:303

commit v3 on v2

--- a/solution.py
+++ b/solution.py
@@ -11,6 +11,7 @@
 LANES = 128
 SUB = 8
 SLOT = 32
+LINES = 16
 MIB = 1024 * 1024
 
 
@@ -63,15 +64,21 @@
 def merge_halo(west, east, halo, count):
     lane = lane_ids(SUB)
     cell = lane % (2 * HALO)
-    for half in range(2):
-        source = (half * 4 + lane // (2 * HALO)) * HALO + cell % HALO
-
-        def one_value(value, carry, half=half, source=source):
-            merged = jnp.where(cell < HALO, take_lanes(west[value], source), take_lanes(east[value], source))
-            halo[value, half] = merged
-            return carry
-
-        lax.fori_loop(0, count, one_value, 0)
+    sources = [(half * 4 + lane // (2 * HALO)) * HALO + cell % HALO for half in range(2)]
+    chunk = 5 if count % 5 == 0 else 1
+
+    def some_values(step, carry):
+        merged = []
+        for item in range(chunk):
+            value = step * chunk + item
+            for half in range(2):
+                both = take_lanes(west[value], sources[half]), take_lanes(east[value], sources[half])
+                merged.append((value, half, jnp.where(cell < HALO, *both)))
+        for value, half, cells in merged:
+            halo[value, half] = cells
+        return carry
+
+    lax.fori_loop(0, count // chunk, some_values, 0)
 
 
 def advect_and_solve(tracers, offsets, weights, diffusion, halo, solved):
@@ -128,15 +135,20 @@
 def build_table(solved, table):
     rows_per = LANES // SLOT
     spread = lane_ids(LANES) // 4
-
-    def four_rows(step, carry):
-        block = solved[pl.ds(pl.multiple_of(step * LANES, LANES), LANES), :].T
-        for item in range(rows_per):
-            start = pl.multiple_of((step * rows_per + item) * LANES, LANES)
-            table[pl.ds(start, LANES), :] = take_lanes(block, spread + item * SLOT)
-        return carry
-
-    lax.fori_loop(0, solved.shape[0] // LANES, four_rows, 0)
+    together = 2
+
+    def some_rows(step, carry):
+        blocks = []
+        for item in range(together):
+            start = pl.multiple_of((step * together + item) * LANES, LANES)
+            blocks.append(solved[pl.ds(start, LANES), :].T)
+        for item, block in enumerate(blocks):
+            for row in range(rows_per):
+                start = pl.multiple_of(((step * together + item) * rows_per + row) * LANES, LANES)
+                table[pl.ds(start, LANES), :] = take_lanes(block, spread + row * SLOT)
+        return carry
+
+    lax.fori_loop(0, solved.shape[0] // (LANES * together), some_rows, 0)
 
 
 def pick_rows(table, index, count, packed, sent):
@@ -144,29 +156,41 @@
     parts = index.shape[2] // LANES
     lists = 4 // parts
     stream = lax.broadcasted_iota(jnp.int32, (1, LANES), 1) % 4
+    together = 2 if blocks % 2 == 0 else 1
 
     def one_block(block, carry):
         owners = [block * lists + item for item in range(lists)]
-        rows = [(count[0, owner] + (parts - 1)) // parts for owner in owners]
+        rows = [lax.div(count[0, owner] + (parts - 1), parts) for owner in owners]
         longest = functools.reduce(jnp.maximum, rows)
         places = [(owners[g // parts], (g % parts) * rows[g // parts]) for g in range(4)]
 
-        def eight_rows(step, inner):
-            start = pl.multiple_of(step * SUB, SUB)
-            for line in range(SUB):
-                picked = [
-                    table[index[0, owner, place + start + line]] for owner, place in places
-                ]
+        def some_lines(step, inner):
+            start = pl.multiple_of(step * LINES, LINES)
+            lines = []
+            for line in range(LINES):
+                picked = [table[index[0, owner, place + start + line]] for owner, place in places]
                 low = jnp.where(stream == 0, picked[0], picked[1])
                 high = jnp.where(stream == 2, picked[2], picked[3])
-                packed[pl.ds(start + line, 1), :] = jnp.where(stream < 2, low, high)
+                lines.append(jnp.where(stream < 2, low, high))
+            first = pl.multiple_of(block * LANES + start, LINES)
+            for line in range(LINES):
+                packed[pl.ds(first + line, 1), :] = lines[line]
             return inner
 
-        lax.fori_loop(0, (longest + (SUB - 1)) // SUB, eight_rows, 0)
-        sent[block] = packed[...].T[:height, :]
+        lax.fori_loop(0, lax.div(longest + (LINES - 1), LINES), some_lines, 0)
+        return carry
+
+    def turn_blocks(step, carry):
+        turned = []
+        for item in range(together):
+            start = pl.multiple_of((step * together + item) * LANES, LANES)
+            turned.append(packed[pl.ds(start, LANES), :].T)
+        for item in range(together):
+            sent[step * together + item] = turned[item][:height, :]
         return carry
 
     lax.fori_loop(0, blocks, one_block, 0)
+    lax.fori_loop(0, blocks // together, turn_blocks, 0)
 
 
 def solve_kernel(tracers, offsets, weights, diffusion, west, east, table, halo, solved):
@@ -204,7 +228,6 @@
 
 
 def pick_kernel(table, index, count, sent, packed):
-    packed[...] = jnp.zeros_like(packed)
     pick_rows(table, index, count, packed, sent)
 
 
@@ -218,63 +241,53 @@
         out_shape=jax.ShapeDtypeStruct((blocks, 4 * values, LANES), jnp.float32),
         in_specs=[vmem, smem, smem],
         out_specs=vmem,
-        scratch_shapes=[pltpu.VMEM((LANES, LANES), jnp.float32)],
+        scratch_shapes=[pltpu.VMEM((blocks * LANES, LANES), jnp.float32)],
         compiler_params=pltpu.CompilerParams(vmem_limit_bytes=16 * MIB),
         name="pick_columns",
     )(table.reshape(-1, 1, LANES), index, count)
 
 
-def place_kernel(arrived, counts, own, owned, held, row, ready):
+def place_kernel(arrived, counts, own, owned, row):
     sources, height, _ = arrived.shape
     levels, ntr, columns = owned.shape
     values = levels * ntr
     parts = height // values
-    lane = lane_ids(1)
-
-    def fetch(turn):
-        source = lax.rem(own[0] - turn + sources, sources)
-        return pltpu.make_async_copy(arrived.at[source], held.at[turn], ready.at[turn])
-
-    def start_fetch(turn, carry):
-        fetch(turn).start()
-        return carry
-
-    def one_source(turn, start):
-        fetch(turn).wait()
-        total = counts[0, lax.rem(own[0] - turn + sources, sources)]
-        rows = (total + (parts - 1)) // parts
-        for part in range(parts):
-            place = start + jnp.minimum(part * rows, total)
-            tile = place // LANES
-            shift = place % LANES
-            piece = held[turn, pl.ds(part, values, stride=parts), :]
-            rolled = pltpu.roll(piece, shift, 1)
-            here = pl.ds(pl.multiple_of(tile * LANES, LANES), LANES)
-            after = pl.ds(pl.multiple_of(tile * LANES + LANES, LANES), LANES)
-            row[:, here] = jnp.where(lane >= shift, rolled, row[:, here])
+    lane = lax.broadcasted_iota(jnp.int32, (values, LANES), 1)
+    together = 2 if sources % 2 == 0 else 1
+
+    def some_sources(step, start):
+        pieces = []
+        for item in range(together):
+            source = lax.rem(own[0] - (step * together + item) + sources, sources)
+            total = counts[0, source]
+            rows = lax.div(total + (parts - 1), parts)
+            for part in range(parts):
+                place = start + jnp.minimum(part * rows, total)
+                shift = lax.rem(place, LANES)
+                piece = arrived[source, pl.ds(part, values, stride=parts), :]
+                pieces.append((place - shift, shift, pltpu.roll(piece, shift, 1)))
+            start = start + total
+        for tile, shift, rolled in pieces:
+            here = pl.ds(pl.multiple_of(tile, LANES), LANES)
+            after = pl.ds(pl.multiple_of(tile + LANES, LANES), LANES)
+            pltpu.store(row.at[:, here], rolled, mask=lane >= shift)
             row[:, after] = rolled
-        return start + total
-
-    lax.fori_loop(0, sources, start_fetch, 0)
-    lax.fori_loop(0, sources, one_source, 0)
+        return start
+
+    lax.fori_loop(0, sources // together, some_sources, 0)
     for level in range(levels):
         owned[level] = row[level * ntr : (level + 1) * ntr, :columns]
 
 
 def place_owned(arrived, counts, own, levels, ntr, columns):
-    sources = arrived.shape[0]
     vmem = pl.BlockSpec(memory_space=pltpu.VMEM)
     smem = pl.BlockSpec(memory_space=pltpu.SMEM)
     return pl.pallas_call(
         place_kernel,
         out_shape=jax.ShapeDtypeStruct((levels, ntr, columns), jnp.float32),
-        in_specs=[pl.BlockSpec(memory_space=pl.ANY), smem, smem],
+        in_specs=[vmem, smem, smem],
         out_specs=vmem,
-        scratch_shapes=[
-            pltpu.VMEM(arrived.shape, jnp.float32),
-            pltpu.VMEM((levels * ntr, columns + 2 * LANES), jnp.float32),
-            pltpu.SemaphoreType.DMA((sources,)),
-        ],
+        scratch_shapes=[pltpu.VMEM((levels * ntr, columns + 2 * LANES), jnp.float32)],
         compiler_params=pltpu.CompilerParams(vmem_limit_bytes=16 * MIB),
         name="place_owned",
     )(arrived, counts, own)

time: 120 us -> 109 us (0.908)
  Pallas kernels: 52.5 us -> 40.5 us
    pallas_call x1, Pallas kernels: 13.3 us -> 7.07 us  [make_table(): pl.pallas_call(solve_kernel, out_shape=jax.ShapeDtypeStruct((lats * lons,...]
    pallas_call x1, Pallas kernels: 8.61 us -> 3.68 us  [place_owned(): pl.pallas_call(place_kernel, out_shape=jax.ShapeDtypeStruct((levels, ntr,...]
  transfers between devices with their start and end apart: 4 -> 4, of which waited for: 1 -> 1; matrix products, arithmetic and copies ran while one was open for 2% -> 2% of each run, Pallas kernels for 36% -> 33%
where the time goes in v3:
time: 109 us; the launch traced here: 108 us
  waiting for transfers between devices  45.2 us (41%)
  Pallas kernels  40.5 us (37%)
  starting transfers between devices  14.9 us (14%)
  local copies, waits for them, and re-layouts  6.65 us (6%)
    all_to_all x1, waiting for transfers between devices, body(): lax.all_to_all(sent, ('lon', 'lat'), split_axis=0, concat_axis=0, tiled=T...  45.2 us
    pallas_call x1, Pallas kernels, pick_columns(): pl.pallas_call(pick_kernel, out_shape=jax.ShapeDtypeStruct((blocks, 4 * v...  28.6 us
    pallas_call x1, Pallas kernels, make_table(): pl.pallas_call(solve_kernel, out_shape=jax.ShapeDtypeStruct((lats * lons,...  7.07 us
    all_to_all x1, starting transfers between devices, body(): lax.all_to_all(sent, ('lon', 'lat'), split_axis=0, concat_axis=0, tiled=T...  5.83 us
    unnamed x14, local copies, waits for them, and re-layouts  5.31 us
    ppermute x1, starting transfers between devices, body(): from_east = lax.ppermute(west_cells, 'lon', ring('lon', -1))  5.03 us
    pallas_call x1, Pallas kernels, place_owned(): pl.pallas_call(place_kernel, out_shape=jax.ShapeDtypeStruct((levels, ntr,...  3.68 us
    all_to_all x1, starting transfers between devices, body(): lax.all_to_all(send_count, ('lon', 'lat'), split_axis=1, concat_axis=1, t...  3.56 us
  transfers between devices with their start and end apart: 4, of which 1 were waited for; matrix products, arithmetic and copies ran while one was open for 2% of the time, Pallas kernels for 33%

profile of v3, /device:TPU:0, one launch (start us, length us, event | category | flops | bytes accessed | tf_op | source)
XLA Modules:
  0.0 108.0 jit_solution(8362415082154424372)
XLA Ops:
  0.0 0.0 copy-start
  0.0 1.2 %copy-done = f32[3,10,64,128]{3,2,1,0:T(8,128)S(1)} copy-done((f32[3,10,64,128]{3,2,1,0:T(8,128)S(1)}, f32[3,10,64,128]{3,2,1,0:T(8,128)}, u32[]{:S(2)}) %copy-start) | copy-done | bytes 983064
  1.2 1.1 %pack_halo.1 = (f32[10,3,8,128]{3,2,1,0:T(8,128)S(1)}, f32[10,3,8,128]{3,2,1,0:T(8,128)S(1)}) custom-call(f32[3,10,64,128]{3,2,1,0:T(8,128)S(1)} %copy-done), custom_call_target="tpu_custom_call" | custom-call | tf_op jit(solution)/shard_map/pack_halo/pallas_call | solution.py:54
  2.3 0.5 collective-permute-start
  2.8 5.0 %collective-permute-start.1 = (f32[10,3,8,128]{3,2,1,0:T(8,128)S(1)}, f32[10,3,8,128]{3,2,1,0:T(8,128)S(1)}, u32[]{:S(2)}, u32[]{:S(2)}) collective-permute-start(f32[10,3,8,128]{3,2,1,0:T(8,128)S(1)} %get-tuple-element.8), channel_id=1, source_target_pairs={{0,30},{2,0},{4,2},{6,4},{8,6},{10,8},{12,10},{14,12},{16,14},{18,... | collective-permute-start | bytes 368648 | tf_op jit(solution)/shard_map/ppermute | solution.py:309
  7.9 1.3 %copy.8 = s32[1,32,1]{2,0,1:T(1,128)} copy(s32[1,32,1]{1,2,0:T(1,128)} %bitcast.10) | data formatting | bytes 256 | tf_op jit(solution)/shard_map/all_to_all | solution.py:310
  9.2 3.6 %all-to-all-start.1 = ((s32[1,32,1]{2,0,1:T(1,128)}), s32[1,32,1]{2,0,1:T(1,128)S(1)}, u32[]{:S(2)}, u32[]{:S(2)}) async-start(s32[1,32,1]{2,0,1:T(1,128)} %copy.8), calls=%async_computation.1 | async-start | bytes 32768 | tf_op jit(solution)/shard_map/all_to_all | solution.py:310
  12.8 0.0 collective-permute-done
  12.8 0.0 collective-permute-done.1
  12.8 0.0 copy-start.1
  12.8 1.2 %copy-done.1 = f32[3,10,64,128]{3,2,1,0:T(8,128)S(1)} copy-done((f32[3,10,64,128]{3,2,1,0:T(8,128)S(1)}, f32[3,10,64,128]{3,2,1,0:T(8,128)}, u32[]{:S(2)}) %copy-start.1) | copy-done | bytes 983064
  14.0 0.0 copy-start.2
  14.0 1.0 copy-done.2
  15.0 0.0 copy-start.3
  15.0 1.0 copy-done.3
  15.9 0.0 copy-start.4
  15.9 1.0 copy-done.4
  16.9 0.0 copy-start.5
  16.9 0.0 copy-start.6
  16.9 7.1 %advect_solve.1 = f32[8192,128]{1,0:T(8,128)S(1)} custom-call(f32[3,10,64,128]{3,2,1,0:T(8,128)S(1)} %copy-done.1, s32[10,64,128]{2,1,0:T(8,128)S(1)} %copy-done.2, f32[10,64,128]{2,1,0:T(8,128)S(1)} %copy-done.3, f32[9,64,128]{2,1,0:T(8,128)S(1)} %copy-done.4, f32[30,8,128]{2,1,0:T(8,128)S(1)} %bitcast.8, f32[30,8,128]{2,1,0:T(8,128)S(1)} %bitcast.9), custom_call_target="tpu_custom_call" | custom-call | tf_op jit(solution)/shard_map/advect_solve/pallas_call | solution.py:209
  24.0 0.0 copy-done.5
  24.0 0.0 copy-done.6
  24.0 28.6 %pick_columns.1 = f32[32,120,128]{2,1,0:T(8,128)} custom-call(f32[8192,1,128]{2,1,0:T(1,128)S(1)} %bitcast.7, s32[1,32,512]{2,1,0:T(8,128)S(1)} %copy-done.5, s32[1,32]{1,0:T(1,128)S(1)} %copy-done.6), custom_call_target="tpu_custom_call" | custom-call | tf_op jit(solution)/shard_map/pick_columns/pallas_call | solution.py:239
  52.6 0.0 all-to-all-done.1
  52.6 5.8 %all-to-all-start = ((f32[32,120,128]{2,1,0:T(8,128)}), f32[32,120,128]{2,1,0:T(8,128)S(1)}, u32[]{:S(2)}, u32[]{:S(2)}) async-start(f32[32,120,128]{2,1,0:T(8,128)} %pick_columns.1), calls=%async_computation | async-start | bytes 3932160 | tf_op jit(solution)/shard_map/all_to_all | solution.py:316
  58.5 0.7 reduce
  59.1 45.2 %all-to-all-done.arrived = f32[32,120,128]{2,1,0:T(8,128)S(1)} async-done(((f32[32,120,128]{2,1,0:T(8,128)}), f32[32,120,128]{2,1,0:T(8,128)S(1)}, u32[]{:S(2)}, u32[]{:S(2)}) %all-to-all-start) | async-done | bytes 1966112 | tf_op jit(solution)/shard_map/all_to_all | solution.py:316
  104.3 3.7 %place_owned.1 = f32[10,3,8192]{2,1,0:T(4,128)} custom-call(f32[32,120,128]{2,1,0:T(8,128)S(1)} %all-to-all-done.arrived, s32[1,32]{1,0:T(1,128)S(1)} %bitcast.11, s32[1]{0:T(128)} %bitcast.4.own), custom_call_target="tpu_custom_call" | custom-call | tf_op jit(solution)/shard_map/place_owned/pallas_call | solution.py:285
Async XLA Ops:
  0.0 1.2 %copy-start = (f32[3,10,64,128]{3,2,1,0:T(8,128)S(1)}, f32[3,10,64,128]{3,2,1,0:T(8,128)}, u32[]{:S(2)}) copy-start(f32[3,10,64,128]{3,2,1,0:T(8,128)} %tracers.3) | copy-start | bytes 2949124
  2.3 10.4 %collective-permute-start = (f32[10,3,8,128]{3,2,1,0:T(8,128)S(1)}, f32[10,3,8,128]{3,2,1,0:T(8,128)S(1)}, u32[]{:S(2)}, u32[]{:S(2)}) collective-permute-start(f32[10,3,8,128]{3,2,1,0:T(8,128)S(1)} %get-tuple-element.7), channel_id=1, source_target_pairs={{0,2},{2,4},{4,6},{6,8},{8,10},{10,12},{12,14},{14,16},{16,18},{18... | collective-permute-start | bytes 368648 | tf_op jit(solution)/shard_map/ppermute | solution.py:308
  2.8 10.0 %collective-permute-start.1 = (f32[10,3,8,128]{3,2,1,0:T(8,128)S(1)}, f32[10,3,8,128]{3,2,1,0:T(8,128)S(1)}, u32[]{:S(2)}, u32[]{:S(2)}) collective-permute-start(f32[10,3,8,128]{3,2,1,0:T(8,128)S(1)} %get-tuple-element.8), channel_id=1, source_target_pairs={{0,30},{2,0},{4,2},{6,4},{8,6},{10,8},{12,10},{14,12},{16,14},{18,... | collective-permute-start | bytes 368648 | tf_op jit(solution)/shard_map/ppermute | solution.py:309
  9.2 43.4 %all-to-all-start.1 = ((s32[1,32,1]{2,0,1:T(1,128)}), s32[1,32,1]{2,0,1:T(1,128)S(1)}, u32[]{:S(2)}, u32[]{:S(2)}) async-start(s32[1,32,1]{2,0,1:T(1,128)} %copy.8), calls=%async_computation.1 | async-start | bytes 32768 | tf_op jit(solution)/shard_map/all_to_all | solution.py:310
  12.8 1.2 %copy-start.1 = (f32[3,10,64,128]{3,2,1,0:T(8,128)S(1)}, f32[3,10,64,128]{3,2,1,0:T(8,128)}, u32[]{:S(2)}) copy-start(f32[3,10,64,128]{3,2,1,0:T(8,128)} %tracers.3) | copy-start | bytes 2949124
  14.0 1.0 copy-start.2
  15.0 1.0 copy-start.3
  15.9 1.0 copy-start.4
  16.9 7.1 %copy-start.5 = (s32[1,32,512]{2,1,0:T(8,128)S(1)}, s32[1,32,512]{2,1,0:T(8,128)}, u32[]{:S(2)}) copy-start(s32[1,32,512]{2,1,0:T(8,128)} %index.1) | copy-start | bytes 196612
  16.9 7.1 %copy-start.6 = (s32[1,32]{1,0:T(1,128)S(1)}, s32[1,32]{1,0:T(1,128)}, u32[]{:S(2)}) copy-start(s32[1,32]{1,0:T(1,128)} %count.1) | copy-start | bytes 388
  52.6 51.7 %all-to-all-start = ((f32[32,120,128]{2,1,0:T(8,128)}), f32[32,120,128]{2,1,0:T(8,128)S(1)}, u32[]{:S(2)}, u32[]{:S(2)}) async-start(f32[32,120,128]{2,1,0:T(8,128)} %pick_columns.1), calls=%async_computation | async-start | bytes 3932160 | tf_op jit(solution)/shard_map/all_to_all | solution.py:316

commit v4 on v3

--- a/solution.py
+++ b/solution.py
@@ -151,9 +151,9 @@
     lax.fori_loop(0, solved.shape[0] // (LANES * together), some_rows, 0)
 
 
-def pick_rows(table, index, count, packed, sent):
+def pick_rows(table, index, count, packed, sent, wait_list):
     blocks, height, _ = sent.shape
-    parts = index.shape[2] // LANES
+    parts = index.shape[1] // LANES
     lists = 4 // parts
     stream = lax.broadcasted_iota(jnp.int32, (1, LANES), 1) % 4
     together = 2 if blocks % 2 == 0 else 1
@@ -161,6 +161,8 @@
     def one_block(block, carry):
         owners = [block * lists + item for item in range(lists)]
         rows = [lax.div(count[0, owner] + (parts - 1), parts) for owner in owners]
+        for owner in owners:
+            wait_list(owner)
         longest = functools.reduce(jnp.maximum, rows)
         places = [(owners[g // parts], (g % parts) * rows[g // parts]) for g in range(4)]
 
@@ -168,7 +170,7 @@
             start = pl.multiple_of(step * LINES, LINES)
             lines = []
             for line in range(LINES):
-                picked = [table[index[0, owner, place + start + line]] for owner, place in places]
+                picked = [table[index[owner, place + start + line]] for owner, place in places]
                 low = jnp.where(stream == 0, picked[0], picked[1])
                 high = jnp.where(stream == 2, picked[2], picked[3])
                 lines.append(jnp.where(stream < 2, low, high))
@@ -193,58 +195,68 @@
     lax.fori_loop(0, blocks // together, turn_blocks, 0)
 
 
-def solve_kernel(tracers, offsets, weights, diffusion, west, east, table, halo, solved):
-    values = west.shape[0]
-    merge_halo(west, east, halo, values)
-    for value in range(values, SLOT):
+def send_kernel(
+    tracers_in, offsets_in, weights_in, diffusion_in, west_in, east_in, index_in, count, sent,
+    tracers, offsets, weights, diffusion, west, east, halo, solved, table, packed, index, ready, listed,
+):
+    lists = index_in.shape[1]
+
+    def list_copy(item):
+        return pltpu.make_async_copy(index_in.at[0, item], index.at[item], listed.at[item])
+
+    def start_list(item, carry):
+        list_copy(item).start()
+        return carry
+
+    sources = (west_in, east_in, offsets_in, weights_in, diffusion_in, tracers_in)
+    targets = (west, east, offsets, weights, diffusion, tracers)
+    copies = [
+        pltpu.make_async_copy(source, target, ready.at[item])
+        for item, (source, target) in enumerate(zip(sources, targets))
+    ]
+    for copy in copies:
+        copy.start()
+    lax.fori_loop(0, lists, start_list, 0)
+    copies[0].wait()
+    copies[1].wait()
+    merge_halo(west, east, halo, west.shape[0])
+    for value in range(west.shape[0], SLOT):
         solved[pl.ds(value, tracers.shape[2], stride=SLOT), :] = jnp.zeros((tracers.shape[2], LANES), jnp.float32)
+    for copy in copies[2:]:
+        copy.wait()
     advect_and_solve(tracers, offsets, weights, diffusion, halo, solved)
-    build_table(solved, table)
-
-
-def make_table(tracers, offsets, weights, diffusion, west, east):
+    build_table(solved, table.reshape(table.shape[0], LANES))
+    pick_rows(table, index, count, packed, sent, lambda item: list_copy(item).wait())
+
+
+def make_sent(tracers, offsets, weights, diffusion, west, east, index, count):
     ntr, levels, lats, lons = tracers.shape
     values = ntr * levels
-    vmem = pl.BlockSpec(memory_space=pltpu.VMEM)
+    lists, cap = index.shape[1:]
+    blocks = lists * (cap // LANES) // 4
+    hbm = pl.BlockSpec(memory_space=pl.ANY)
+    smem = pl.BlockSpec(memory_space=pltpu.SMEM)
+    west = west.reshape(values, SUB, LANES)
+    east = east.reshape(values, SUB, LANES)
+    inputs = (tracers, offsets, weights, diffusion, west, east)
     return pl.pallas_call(
-        solve_kernel,
-        out_shape=jax.ShapeDtypeStruct((lats * lons, LANES), jnp.float32),
-        in_specs=[vmem] * 6,
-        out_specs=vmem,
-        scratch_shapes=[
+        send_kernel,
+        out_shape=jax.ShapeDtypeStruct((blocks, 4 * values, LANES), jnp.float32),
+        in_specs=[hbm] * 7 + [smem],
+        out_specs=pl.BlockSpec(memory_space=pltpu.VMEM),
+        scratch_shapes=[pltpu.VMEM(array.shape, array.dtype) for array in inputs]
+        + [
             pltpu.VMEM((values, 2, SUB, LANES), jnp.float32),
             pltpu.VMEM((lats * SLOT, LANES), jnp.float32),
+            pltpu.VMEM((lats * lons, 1, LANES), jnp.float32),
+            pltpu.VMEM((blocks * LANES, LANES), jnp.float32),
+            pltpu.SMEM((lists, cap), jnp.int32),
+            pltpu.SemaphoreType.DMA((len(inputs),)),
+            pltpu.SemaphoreType.DMA((lists,)),
         ],
-        compiler_params=pltpu.CompilerParams(vmem_limit_bytes=16 * MIB),
-        name="advect_solve",
-    )(
-        tracers,
-        offsets,
-        weights,
-        diffusion,
-        west.reshape(values, SUB, LANES),
-        east.reshape(values, SUB, LANES),
-    )
-
-
-def pick_kernel(table, index, count, sent, packed):
-    pick_rows(table, index, count, packed, sent)
-
-
-def pick_columns(table, index, count, values):
-    lists, cap = index.shape[1:]
-    blocks = lists * (cap // LANES) // 4
-    vmem = pl.BlockSpec(memory_space=pltpu.VMEM)
-    smem = pl.BlockSpec(memory_space=pltpu.SMEM)
-    return pl.pallas_call(
-        pick_kernel,
-        out_shape=jax.ShapeDtypeStruct((blocks, 4 * values, LANES), jnp.float32),
-        in_specs=[vmem, smem, smem],
-        out_specs=vmem,
-        scratch_shapes=[pltpu.VMEM((blocks * LANES, LANES), jnp.float32)],
-        compiler_params=pltpu.CompilerParams(vmem_limit_bytes=16 * MIB),
-        name="pick_columns",
-    )(table.reshape(-1, 1, LANES), index, count)
+        compiler_params=pltpu.CompilerParams(vmem_limit_bytes=56 * MIB),
+        name="advect_solve_pick",
+    )(*inputs, index, count)
 
 
 def place_kernel(arrived, counts, own, owned, row):
@@ -308,8 +320,7 @@
     from_west = lax.ppermute(east_cells, "lon", ring("lon", 1))
     from_east = lax.ppermute(west_cells, "lon", ring("lon", -1))
     counts = lax.all_to_all(send_count, ("lon", "lat"), split_axis=1, concat_axis=1, tiled=True)
-    table = make_table(tracers, offsets, weights, diffusion, from_west, from_east)
-    sent = pick_columns(table, send_index, send_count, values)
+    sent = make_sent(tracers, offsets, weights, diffusion, from_west, from_east, send_index, send_count)
     if parts < 4:
         sent = sent.reshape(-1, values, 4 // parts, parts, LANES)
         sent = jnp.transpose(sent, (0, 2, 1, 3, 4)).reshape(lists, values * parts, LANES)

time: 109 us -> 105 us (0.963)
  local copies, waits for them, and re-layouts: 6.65 us -> 3.21 us
    unnamed x14 -> x6, local copies, waits for them, and re-layouts: 5.31 us -> 1.88 us
    pallas_call x2 -> x1, Pallas kernels: 35.7 us -> 36 us  [make_sent(): pl.pallas_call(send_kernel, out_shape=jax.ShapeDtypeStruct((blocks, 4 * v...]
  transfers between devices with their start and end apart: 4 -> 4, of which waited for: 1 -> 1; matrix products, arithmetic and copies ran while one was open for 2% -> 2% of each run, Pallas kernels for 33% -> 34%
where the time goes in v4:
time: 105 us
  waiting for transfers between devices  45.2 us (43%)
  Pallas kernels  40.8 us (39%)
  starting transfers between devices  15.1 us (14%)
  local copies, waits for them, and re-layouts  3.21 us (3%)
    all_to_all x1, waiting for transfers between devices, body(): lax.all_to_all(sent, ('lon', 'lat'), split_axis=0, concat_axis=0, tiled=T...  45.2 us
    pallas_call x1, Pallas kernels, make_sent(): pl.pallas_call(send_kernel, out_shape=jax.ShapeDtypeStruct((blocks, 4 * v...  36 us
    all_to_all x1, starting transfers between devices, body(): lax.all_to_all(sent, ('lon', 'lat'), split_axis=0, concat_axis=0, tiled=T...  6 us
    ppermute x1, starting transfers between devices, body(): from_east = lax.ppermute(west_cells, 'lon', ring('lon', -1))  5.03 us
    pallas_call x1, Pallas kernels, place_owned(): pl.pallas_call(place_kernel, out_shape=jax.ShapeDtypeStruct((levels, ntr,...  3.68 us
    all_to_all x1, starting transfers between devices, body(): lax.all_to_all(send_count, ('lon', 'lat'), split_axis=1, concat_axis=1, t...  3.56 us
  transfers between devices with their start and end apart: 4, of which 1 were waited for; matrix products, arithmetic and copies ran while one was open for 2% of the time, Pallas kernels for 34%

profile of v4, /device:TPU:0, one launch (start us, length us, event | category | flops | bytes accessed | tf_op | source)
XLA Modules:
  0.0 105.1 jit_solution(17170010822564788694)
XLA Ops:
  0.0 0.0 copy-start
  0.0 1.2 %copy-done = f32[3,10,64,128]{3,2,1,0:T(8,128)S(1)} copy-done((f32[3,10,64,128]{3,2,1,0:T(8,128)S(1)}, f32[3,10,64,128]{3,2,1,0:T(8,128)}, u32[]{:S(2)}) %copy-start) | copy-done | bytes 983064
  1.2 1.1 %pack_halo.1 = (f32[10,3,8,128]{3,2,1,0:T(8,128)S(1)}, f32[10,3,8,128]{3,2,1,0:T(8,128)S(1)}) custom-call(f32[3,10,64,128]{3,2,1,0:T(8,128)S(1)} %copy-done), custom_call_target="tpu_custom_call" | custom-call | tf_op jit(solution)/shard_map/pack_halo/pallas_call | solution.py:54
  2.3 0.5 collective-permute-start
  2.8 5.0 %collective-permute-start.1 = (f32[10,3,8,128]{3,2,1,0:T(8,128)S(1)}, f32[10,3,8,128]{3,2,1,0:T(8,128)S(1)}, u32[]{:S(2)}, u32[]{:S(2)}) collective-permute-start(f32[10,3,8,128]{3,2,1,0:T(8,128)S(1)} %get-tuple-element.8), channel_id=1, source_target_pairs={{0,30},{2,0},{4,2},{6,4},{8,6},{10,8},{12,10},{14,12},{16,14},{18,... | collective-permute-start | bytes 368648 | tf_op jit(solution)/shard_map/ppermute | solution.py:321
  7.9 1.3 %copy.8 = s32[1,32,1]{2,0,1:T(1,128)} copy(s32[1,32,1]{1,2,0:T(1,128)} %bitcast.9) | data formatting | bytes 256 | tf_op jit(solution)/shard_map/all_to_all | solution.py:322
  9.2 3.6 %all-to-all-start.1 = ((s32[1,32,1]{2,0,1:T(1,128)}), s32[1,32,1]{2,0,1:T(1,128)S(1)}, u32[]{:S(2)}, u32[]{:S(2)}) async-start(s32[1,32,1]{2,0,1:T(1,128)} %copy.8), calls=%async_computation.1 | async-start | bytes 32768 | tf_op jit(solution)/shard_map/all_to_all | solution.py:322
  12.8 0.0 collective-permute-done
  12.8 0.0 copy-start.1
  12.8 0.0 collective-permute-done.1
  12.8 0.0 copy-start.2
  12.8 0.6 copy-done.1
  13.4 0.1 copy-done.2
  13.5 36.0 %advect_solve_pick.1 = f32[32,120,128]{2,1,0:T(8,128)} custom-call(f32[3,10,64,128]{3,2,1,0:T(8,128)} %tracers_in.1, s32[10,64,128]{2,1,0:T(8,128)} %offsets_in.1, f32[10,64,128]{2,1,0:T(8,128)} %weights_in.1, f32[9,64,128]{2,1,0:T(8,128)} %diffusion_in.1, f32[30,8,128]{2,1,0:T(8,128)} %bitcast.7, f32[30,8,128]{2,1,0:T(8,128)} %bitcast.8, ...), custom_call_target="tpu_custom_call" | custom-call | tf_op jit(solution)/shard_map/advect_solve_pick/pallas_call | solution.py:242
  49.5 0.0 all-to-all-done.1
  49.5 6.0 %all-to-all-start = ((f32[32,120,128]{2,1,0:T(8,128)}), f32[32,120,128]{2,1,0:T(8,128)S(1)}, u32[]{:S(2)}, u32[]{:S(2)}) async-start(f32[32,120,128]{2,1,0:T(8,128)} %advect_solve_pick.1), calls=%async_computation | async-start | bytes 3932160 | tf_op jit(solution)/shard_map/all_to_all | solution.py:327
  55.5 0.7 reduce
  56.2 45.2 %all-to-all-done.arrived = f32[32,120,128]{2,1,0:T(8,128)S(1)} async-done(((f32[32,120,128]{2,1,0:T(8,128)}), f32[32,120,128]{2,1,0:T(8,128)S(1)}, u32[]{:S(2)}, u32[]{:S(2)}) %all-to-all-start) | async-done | bytes 1966112 | tf_op jit(solution)/shard_map/all_to_all | solution.py:327
  101.4 3.7 %place_owned.1 = f32[10,3,8192]{2,1,0:T(4,128)} custom-call(f32[32,120,128]{2,1,0:T(8,128)S(1)} %all-to-all-done.arrived, s32[1,32]{1,0:T(1,128)S(1)} %bitcast.6, s32[1]{0:T(128)} %bitcast.3.own), custom_call_target="tpu_custom_call" | custom-call | tf_op jit(solution)/shard_map/place_owned/pallas_call | solution.py:297
Async XLA Ops:
  0.0 1.2 %copy-start = (f32[3,10,64,128]{3,2,1,0:T(8,128)S(1)}, f32[3,10,64,128]{3,2,1,0:T(8,128)}, u32[]{:S(2)}) copy-start(f32[3,10,64,128]{3,2,1,0:T(8,128)} %tracers_in.1) | copy-start | bytes 2949124
  2.3 10.4 %collective-permute-start = (f32[10,3,8,128]{3,2,1,0:T(8,128)S(1)}, f32[10,3,8,128]{3,2,1,0:T(8,128)S(1)}, u32[]{:S(2)}, u32[]{:S(2)}) collective-permute-start(f32[10,3,8,128]{3,2,1,0:T(8,128)S(1)} %get-tuple-element.7), channel_id=1, source_target_pairs={{0,2},{2,4},{4,6},{6,8},{8,10},{10,12},{12,14},{14,16},{16,18},{18... | collective-permute-start | bytes 368648 | tf_op jit(solution)/shard_map/ppermute | solution.py:320
  2.8 10.0 %collective-permute-start.1 = (f32[10,3,8,128]{3,2,1,0:T(8,128)S(1)}, f32[10,3,8,128]{3,2,1,0:T(8,128)S(1)}, u32[]{:S(2)}, u32[]{:S(2)}) collective-permute-start(f32[10,3,8,128]{3,2,1,0:T(8,128)S(1)} %get-tuple-element.8), channel_id=1, source_target_pairs={{0,30},{2,0},{4,2},{6,4},{8,6},{10,8},{12,10},{14,12},{16,14},{18,... | collective-permute-start | bytes 368648 | tf_op jit(solution)/shard_map/ppermute | solution.py:321
  9.2 40.3 %all-to-all-start.1 = ((s32[1,32,1]{2,0,1:T(1,128)}), s32[1,32,1]{2,0,1:T(1,128)S(1)}, u32[]{:S(2)}, u32[]{:S(2)}) async-start(s32[1,32,1]{2,0,1:T(1,128)} %copy.8), calls=%async_computation.1 | async-start | bytes 32768 | tf_op jit(solution)/shard_map/all_to_all | solution.py:322
  12.8 0.7 copy-start.1
  12.8 0.7 copy-start.2
  49.5 51.9 %all-to-all-start = ((f32[32,120,128]{2,1,0:T(8,128)}), f32[32,120,128]{2,1,0:T(8,128)S(1)}, u32[]{:S(2)}, u32[]{:S(2)}) async-start(f32[32,120,128]{2,1,0:T(8,128)} %advect_solve_pick.1), calls=%async_computation | async-start | bytes 3932160 | tf_op jit(solution)/shard_map/all_to_all | solution.py:327

commit v5 on v4

--- a/solution.py
+++ b/solution.py
@@ -1,5 +1,3 @@
-import functools
-
 import jax
 import jax.numpy as jnp
 from jax import lax
@@ -11,7 +9,6 @@
 LANES = 128
 SUB = 8
 SLOT = 32
-LINES = 16
 MIB = 1024 * 1024
 
 
@@ -132,108 +129,64 @@
     lax.fori_loop(0, lats // SUB, one_part, 0)
 
 
-def build_table(solved, table):
-    rows_per = LANES // SLOT
-    spread = lane_ids(LANES) // 4
-    together = 2
-
-    def some_rows(step, carry):
-        blocks = []
-        for item in range(together):
-            start = pl.multiple_of((step * together + item) * LANES, LANES)
-            blocks.append(solved[pl.ds(start, LANES), :].T)
-        for item, block in enumerate(blocks):
-            for row in range(rows_per):
-                start = pl.multiple_of(((step * together + item) * rows_per + row) * LANES, LANES)
-                table[pl.ds(start, LANES), :] = take_lanes(block, spread + row * SLOT)
-        return carry
-
-    lax.fori_loop(0, solved.shape[0] // (LANES * together), some_rows, 0)
-
-
-def pick_rows(table, index, count, packed, sent, wait_list):
-    blocks, height, _ = sent.shape
-    parts = index.shape[1] // LANES
-    lists = 4 // parts
-    stream = lax.broadcasted_iota(jnp.int32, (1, LANES), 1) % 4
-    together = 2 if blocks % 2 == 0 else 1
-
-    def one_block(block, carry):
-        owners = [block * lists + item for item in range(lists)]
-        rows = [lax.div(count[0, owner] + (parts - 1), parts) for owner in owners]
-        for owner in owners:
-            wait_list(owner)
-        longest = functools.reduce(jnp.maximum, rows)
-        places = [(owners[g // parts], (g % parts) * rows[g // parts]) for g in range(4)]
-
-        def some_lines(step, inner):
-            start = pl.multiple_of(step * LINES, LINES)
-            lines = []
-            for line in range(LINES):
-                picked = [table[index[owner, place + start + line]] for owner, place in places]
-                low = jnp.where(stream == 0, picked[0], picked[1])
-                high = jnp.where(stream == 2, picked[2], picked[3])
-                lines.append(jnp.where(stream < 2, low, high))
-            first = pl.multiple_of(block * LANES + start, LINES)
-            for line in range(LINES):
-                packed[pl.ds(first + line, 1), :] = lines[line]
+def pick_tiles(solved, index, count, sent, values):
+    parts, lists, _ = index.shape
+    rows = solved.shape[0] // SLOT
+    groups = [(first, min(SUB, values - first)) for first in range(0, values, SUB)]
+
+    def one_list(item, carry):
+        def one_tile(part, inner):
+            columns = jnp.broadcast_to(index[part, pl.ds(item, 1), :], (SUB, LANES))
+            row_of = lax.shift_right_logical(columns, 7)
+            lane_of = columns & (LANES - 1)
+            picked = [jnp.zeros((SUB, LANES), jnp.float32) for _ in groups]
+            for row in range(rows):
+                here = row_of == row
+                for place, (first, _) in enumerate(groups):
+                    cells = solved[row * SLOT + first : row * SLOT + first + SUB, :]
+                    picked[place] = jnp.where(here, take_lanes(cells, lane_of), picked[place])
+            for place, (first, size) in enumerate(groups):
+                sent[item, pl.ds(part + first * parts, size, stride=parts), :] = picked[place][:size]
             return inner
 
-        lax.fori_loop(0, lax.div(longest + (LINES - 1), LINES), some_lines, 0)
-        return carry
-
-    def turn_blocks(step, carry):
-        turned = []
-        for item in range(together):
-            start = pl.multiple_of((step * together + item) * LANES, LANES)
-            turned.append(packed[pl.ds(start, LANES), :].T)
-        for item in range(together):
-            sent[step * together + item] = turned[item][:height, :]
-        return carry
-
-    lax.fori_loop(0, blocks, one_block, 0)
-    lax.fori_loop(0, blocks // together, turn_blocks, 0)
+        lax.fori_loop(0, lax.div(count[0, item] + (LANES - 1), LANES), one_tile, 0)
+        return carry
+
+    lax.fori_loop(0, lists, one_list, 0)
 
 
 def send_kernel(
     tracers_in, offsets_in, weights_in, diffusion_in, west_in, east_in, index_in, count, sent,
-    tracers, offsets, weights, diffusion, west, east, halo, solved, table, packed, index, ready, listed,
+    tracers, offsets, weights, diffusion, west, east, index, halo, solved, ready,
 ):
-    lists = index_in.shape[1]
-
-    def list_copy(item):
-        return pltpu.make_async_copy(index_in.at[0, item], index.at[item], listed.at[item])
-
-    def start_list(item, carry):
-        list_copy(item).start()
-        return carry
-
-    sources = (west_in, east_in, offsets_in, weights_in, diffusion_in, tracers_in)
-    targets = (west, east, offsets, weights, diffusion, tracers)
+    values = west.shape[0]
+    parts = index.shape[0]
+    sources = [west_in, east_in, offsets_in, weights_in, diffusion_in, tracers_in]
+    targets = [west, east, offsets, weights, diffusion, tracers]
+    sources += [index_in.at[0, :, part * LANES : (part + 1) * LANES] for part in range(parts)]
+    targets += [index.at[part] for part in range(parts)]
     copies = [
         pltpu.make_async_copy(source, target, ready.at[item])
         for item, (source, target) in enumerate(zip(sources, targets))
     ]
     for copy in copies:
         copy.start()
-    lax.fori_loop(0, lists, start_list, 0)
     copies[0].wait()
     copies[1].wait()
-    merge_halo(west, east, halo, west.shape[0])
-    for value in range(west.shape[0], SLOT):
+    merge_halo(west, east, halo, values)
+    for value in range(values, SLOT):
         solved[pl.ds(value, tracers.shape[2], stride=SLOT), :] = jnp.zeros((tracers.shape[2], LANES), jnp.float32)
     for copy in copies[2:]:
         copy.wait()
     advect_and_solve(tracers, offsets, weights, diffusion, halo, solved)
-    build_table(solved, table.reshape(table.shape[0], LANES))
-    pick_rows(table, index, count, packed, sent, lambda item: list_copy(item).wait())
+    pick_tiles(solved, index, count, sent, values)
 
 
 def make_sent(tracers, offsets, weights, diffusion, west, east, index, count):
-    ntr, levels, lats, lons = tracers.shape
+    ntr, levels, lats, _ = tracers.shape
     values = ntr * levels
     lists, cap = index.shape[1:]
-    blocks = lists * (cap // LANES) // 4
+    parts = cap // LANES
     hbm = pl.BlockSpec(memory_space=pl.ANY)
     smem = pl.BlockSpec(memory_space=pltpu.SMEM)
     west = west.reshape(values, SUB, LANES)
@@ -241,18 +194,15 @@
     inputs = (tracers, offsets, weights, diffusion, west, east)
     return pl.pallas_call(
         send_kernel,
-        out_shape=jax.ShapeDtypeStruct((blocks, 4 * values, LANES), jnp.float32),
+        out_shape=jax.ShapeDtypeStruct((lists, values * parts, LANES), jnp.float32),
         in_specs=[hbm] * 7 + [smem],
         out_specs=pl.BlockSpec(memory_space=pltpu.VMEM),
         scratch_shapes=[pltpu.VMEM(array.shape, array.dtype) for array in inputs]
         + [
+            pltpu.VMEM((parts, lists, LANES), jnp.int32),
             pltpu.VMEM((values, 2, SUB, LANES), jnp.float32),
             pltpu.VMEM((lats * SLOT, LANES), jnp.float32),
-            pltpu.VMEM((lats * lons, 1, LANES), jnp.float32),
-            pltpu.VMEM((blocks * LANES, LANES), jnp.float32),
-            pltpu.SMEM((lists, cap), jnp.int32),
-            pltpu.SemaphoreType.DMA((len(inputs),)),
-            pltpu.SemaphoreType.DMA((lists,)),
+            pltpu.SemaphoreType.DMA((len(inputs) + parts,)),
         ],
         compiler_params=pltpu.CompilerParams(vmem_limit_bytes=56 * MIB),
         name="advect_solve_pick",
@@ -272,9 +222,8 @@
         for item in range(together):
             source = lax.rem(own[0] - (step * together + item) + sources, sources)
             total = counts[0, source]
-            rows = lax.div(total + (parts - 1), parts)
             for part in range(parts):
-                place = start + jnp.minimum(part * rows, total)
+                place = start + jnp.minimum(part * LANES, total)
                 shift = lax.rem(place, LANES)
                 piece = arrived[source, pl.ds(part, values, stride=parts), :]
                 pieces.append((place - shift, shift, pltpu.roll(piece, shift, 1)))
@@ -313,17 +262,11 @@
 def body(tracers, offsets, weights, diffusion, send_index, send_count):
     ntr, levels, lats, lons = tracers.shape
     columns = lats * lons
-    lists, cap = send_index.shape[1:]
-    parts = cap // LANES
-    values = ntr * levels
     west_cells, east_cells = pack_halo(tracers)
     from_west = lax.ppermute(east_cells, "lon", ring("lon", 1))
     from_east = lax.ppermute(west_cells, "lon", ring("lon", -1))
     counts = lax.all_to_all(send_count, ("lon", "lat"), split_axis=1, concat_axis=1, tiled=True)
     sent = make_sent(tracers, offsets, weights, diffusion, from_west, from_east, send_index, send_count)
-    if parts < 4:
-        sent = sent.reshape(-1, values, 4 // parts, parts, LANES)
-        sent = jnp.transpose(sent, (0, 2, 1, 3, 4)).reshape(lists, values * parts, LANES)
     arrived = lax.all_to_all(sent, ("lon", "lat"), split_axis=0, concat_axis=0, tiled=True)
     own = lax.axis_index(("lon", "lat")).astype(jnp.int32).reshape(1)
     owned = place_owned(arrived, counts, own, levels, ntr, columns)

time: 105 us -> 104 us (level)
  Pallas kernels: 40.8 us -> 39.6 us
    pallas_call x1, Pallas kernels: 36 us -> 34.9 us  [make_sent(): pl.pallas_call(send_kernel, out_shape=jax.ShapeDtypeStruct((lists, values...]
where the time goes in v5:
time: 104 us
  waiting for transfers between devices  45.2 us (43%)
  Pallas kernels  39.6 us (38%)
  starting transfers between devices  14.9 us (14%)
  local copies, waits for them, and re-layouts  3.21 us (3%)
    all_to_all x1, waiting for transfers between devices, body(): lax.all_to_all(sent, ('lon', 'lat'), split_axis=0, concat_axis=0, tiled=T...  45.2 us
    pallas_call x1, Pallas kernels, make_sent(): pl.pallas_call(send_kernel, out_shape=jax.ShapeDtypeStruct((lists, values...  34.9 us
    all_to_all x1, starting transfers between devices, body(): lax.all_to_all(sent, ('lon', 'lat'), split_axis=0, concat_axis=0, tiled=T...  5.84 us
    ppermute x1, starting transfers between devices, body(): from_east = lax.ppermute(west_cells, 'lon', ring('lon', -1))  5.03 us
    pallas_call x1, Pallas kernels, place_owned(): pl.pallas_call(place_kernel, out_shape=jax.ShapeDtypeStruct((levels, ntr,...  3.63 us
    all_to_all x1, starting transfers between devices, body(): lax.all_to_all(send_count, ('lon', 'lat'), split_axis=1, concat_axis=1, t...  3.56 us
  transfers between devices with their start and end apart: 4, of which 1 were waited for; matrix products, arithmetic and copies ran while one was open for 2% of the time, Pallas kernels for 34%

profile of v5, /device:TPU:0, one launch (start us, length us, event | category | flops | bytes accessed | tf_op | source)
XLA Modules:
  0.0 103.8 jit_solution(10543998831647421421)
XLA Ops:
  0.0 0.0 copy-start
  0.0 1.2 %copy-done = f32[3,10,64,128]{3,2,1,0:T(8,128)S(1)} copy-done((f32[3,10,64,128]{3,2,1,0:T(8,128)S(1)}, f32[3,10,64,128]{3,2,1,0:T(8,128)}, u32[]{:S(2)}) %copy-start) | copy-done | bytes 983064
  1.2 1.1 %pack_halo.1 = (f32[10,3,8,128]{3,2,1,0:T(8,128)S(1)}, f32[10,3,8,128]{3,2,1,0:T(8,128)S(1)}) custom-call(f32[3,10,64,128]{3,2,1,0:T(8,128)S(1)} %copy-done), custom_call_target="tpu_custom_call" | custom-call | tf_op jit(solution)/shard_map/pack_halo/pallas_call | solution.py:51
  2.3 0.5 collective-permute-start
  2.8 5.0 %collective-permute-start.1 = (f32[10,3,8,128]{3,2,1,0:T(8,128)S(1)}, f32[10,3,8,128]{3,2,1,0:T(8,128)S(1)}, u32[]{:S(2)}, u32[]{:S(2)}) collective-permute-start(f32[10,3,8,128]{3,2,1,0:T(8,128)S(1)} %get-tuple-element.8), channel_id=1, source_target_pairs={{0,30},{2,0},{4,2},{6,4},{8,6},{10,8},{12,10},{14,12},{16,14},{18,... | collective-permute-start | bytes 368648 | tf_op jit(solution)/shard_map/ppermute | solution.py:267
  7.9 1.3 %copy.8 = s32[1,32,1]{2,0,1:T(1,128)} copy(s32[1,32,1]{1,2,0:T(1,128)} %bitcast.9) | data formatting | bytes 256 | tf_op jit(solution)/shard_map/all_to_all | solution.py:268
  9.2 3.6 %all-to-all-start.1 = ((s32[1,32,1]{2,0,1:T(1,128)}), s32[1,32,1]{2,0,1:T(1,128)S(1)}, u32[]{:S(2)}, u32[]{:S(2)}) async-start(s32[1,32,1]{2,0,1:T(1,128)} %copy.8), calls=%async_computation.1 | async-start | bytes 32768 | tf_op jit(solution)/shard_map/all_to_all | solution.py:268
  12.8 0.0 collective-permute-done
  12.8 0.0 copy-start.1
  12.8 0.0 collective-permute-done.1
  12.8 0.0 copy-start.2
  12.8 0.6 copy-done.1
  13.4 0.1 copy-done.2
  13.5 34.9 %advect_solve_pick.1 = f32[32,120,128]{2,1,0:T(8,128)} custom-call(f32[3,10,64,128]{3,2,1,0:T(8,128)} %tracers_in.1, s32[10,64,128]{2,1,0:T(8,128)} %offsets_in.1, f32[10,64,128]{2,1,0:T(8,128)} %weights_in.1, f32[9,64,128]{2,1,0:T(8,128)} %diffusion_in.1, f32[30,8,128]{2,1,0:T(8,128)} %bitcast.7, f32[30,8,128]{2,1,0:T(8,128)} %bitcast.8, ...), custom_call_target="tpu_custom_call" | custom-call | tf_op jit(solution)/shard_map/advect_solve_pick/pallas_call | solution.py:195
  48.4 0.0 all-to-all-done.1
  48.4 5.8 %all-to-all-start = ((f32[32,120,128]{2,1,0:T(8,128)}), f32[32,120,128]{2,1,0:T(8,128)S(1)}, u32[]{:S(2)}, u32[]{:S(2)}) async-start(f32[32,120,128]{2,1,0:T(8,128)} %advect_solve_pick.1), calls=%async_computation | async-start | bytes 3932160 | tf_op jit(solution)/shard_map/all_to_all | solution.py:270
  54.2 0.7 reduce
  54.9 45.2 %all-to-all-done.arrived = f32[32,120,128]{2,1,0:T(8,128)S(1)} async-done(((f32[32,120,128]{2,1,0:T(8,128)}), f32[32,120,128]{2,1,0:T(8,128)S(1)}, u32[]{:S(2)}, u32[]{:S(2)}) %all-to-all-start) | async-done | bytes 1966112 | tf_op jit(solution)/shard_map/all_to_all | solution.py:270
  100.1 3.6 %place_owned.1 = f32[10,3,8192]{2,1,0:T(4,128)} custom-call(f32[32,120,128]{2,1,0:T(8,128)S(1)} %all-to-all-done.arrived, s32[1,32]{1,0:T(1,128)S(1)} %bitcast.6, s32[1]{0:T(128)} %bitcast.3.own), custom_call_target="tpu_custom_call" | custom-call | tf_op jit(solution)/shard_map/place_owned/pallas_call | solution.py:246
Async XLA Ops:
  0.0 1.2 %copy-start = (f32[3,10,64,128]{3,2,1,0:T(8,128)S(1)}, f32[3,10,64,128]{3,2,1,0:T(8,128)}, u32[]{:S(2)}) copy-start(f32[3,10,64,128]{3,2,1,0:T(8,128)} %tracers_in.1) | copy-start | bytes 2949124
  2.3 10.4 %collective-permute-start = (f32[10,3,8,128]{3,2,1,0:T(8,128)S(1)}, f32[10,3,8,128]{3,2,1,0:T(8,128)S(1)}, u32[]{:S(2)}, u32[]{:S(2)}) collective-permute-start(f32[10,3,8,128]{3,2,1,0:T(8,128)S(1)} %get-tuple-element.7), channel_id=1, source_target_pairs={{0,2},{2,4},{4,6},{6,8},{8,10},{10,12},{12,14},{14,16},{16,18},{18... | collective-permute-start | bytes 368648 | tf_op jit(solution)/shard_map/ppermute | solution.py:266
  2.8 10.0 %collective-permute-start.1 = (f32[10,3,8,128]{3,2,1,0:T(8,128)S(1)}, f32[10,3,8,128]{3,2,1,0:T(8,128)S(1)}, u32[]{:S(2)}, u32[]{:S(2)}) collective-permute-start(f32[10,3,8,128]{3,2,1,0:T(8,128)S(1)} %get-tuple-element.8), channel_id=1, source_target_pairs={{0,30},{2,0},{4,2},{6,4},{8,6},{10,8},{12,10},{14,12},{16,14},{18,... | collective-permute-start | bytes 368648 | tf_op jit(solution)/shard_map/ppermute | solution.py:267
  9.2 39.2 %all-to-all-start.1 = ((s32[1,32,1]{2,0,1:T(1,128)}), s32[1,32,1]{2,0,1:T(1,128)S(1)}, u32[]{:S(2)}, u32[]{:S(2)}) async-start(s32[1,32,1]{2,0,1:T(1,128)} %copy.8), calls=%async_computation.1 | async-start | bytes 32768 | tf_op jit(solution)/shard_map/all_to_all | solution.py:268
  12.8 0.7 copy-start.1
  12.8 0.7 copy-start.2
  48.4 51.7 %all-to-all-start = ((f32[32,120,128]{2,1,0:T(8,128)}), f32[32,120,128]{2,1,0:T(8,128)S(1)}, u32[]{:S(2)}, u32[]{:S(2)}) async-start(f32[32,120,128]{2,1,0:T(8,128)} %advect_solve_pick.1), calls=%async_computation | async-start | bytes 3932160 | tf_op jit(solution)/shard_map/all_to_all | solution.py:270

commit v6 on v4

--- a/solution.py
+++ b/solution.py
@@ -151,9 +151,9 @@
     lax.fori_loop(0, solved.shape[0] // (LANES * together), some_rows, 0)
 
 
-def pick_rows(table, index, count, packed, sent, wait_list):
+def pick_rows(table, index, count, cap, packed, sent, wait_list):
     blocks, height, _ = sent.shape
-    parts = index.shape[1] // LANES
+    parts = cap // LANES
     lists = 4 // parts
     stream = lax.broadcasted_iota(jnp.int32, (1, LANES), 1) % 4
     together = 2 if blocks % 2 == 0 else 1
@@ -164,13 +164,14 @@
         for owner in owners:
             wait_list(owner)
         longest = functools.reduce(jnp.maximum, rows)
-        places = [(owners[g // parts], (g % parts) * rows[g // parts]) for g in range(4)]
+        places = [owners[g // parts] * cap + (g % parts) * rows[g // parts] for g in range(4)]
 
         def some_lines(step, inner):
             start = pl.multiple_of(step * LINES, LINES)
+            bases = [place + start for place in places]
             lines = []
             for line in range(LINES):
-                picked = [table[index[owner, place + start + line]] for owner, place in places]
+                picked = [table[index[base + line]] for base in bases]
                 low = jnp.where(stream == 0, picked[0], picked[1])
                 high = jnp.where(stream == 2, picked[2], picked[3])
                 lines.append(jnp.where(stream < 2, low, high))
@@ -199,10 +200,11 @@
     tracers_in, offsets_in, weights_in, diffusion_in, west_in, east_in, index_in, count, sent,
     tracers, offsets, weights, diffusion, west, east, halo, solved, table, packed, index, ready, listed,
 ):
-    lists = index_in.shape[1]
+    lists, cap = index_in.shape[1:]
 
     def list_copy(item):
-        return pltpu.make_async_copy(index_in.at[0, item], index.at[item], listed.at[item])
+        place = pl.ds(pl.multiple_of(item * cap, LANES), cap)
+        return pltpu.make_async_copy(index_in.at[0, item], index.at[place], listed.at[item])
 
     def start_list(item, carry):
         list_copy(item).start()
@@ -226,7 +228,7 @@
         copy.wait()
     advect_and_solve(tracers, offsets, weights, diffusion, halo, solved)
     build_table(solved, table.reshape(table.shape[0], LANES))
-    pick_rows(table, index, count, packed, sent, lambda item: list_copy(item).wait())
+    pick_rows(table, index, count, cap, packed, sent, lambda item: list_copy(item).wait())
 
 
 def make_sent(tracers, offsets, weights, diffusion, west, east, index, count):
@@ -250,7 +252,7 @@
             pltpu.VMEM((lats * SLOT, LANES), jnp.float32),
             pltpu.VMEM((lats * lons, 1, LANES), jnp.float32),
             pltpu.VMEM((blocks * LANES, LANES), jnp.float32),
-            pltpu.SMEM((lists, cap), jnp.int32),
+            pltpu.SMEM((lists * cap,), jnp.int32),
             pltpu.SemaphoreType.DMA((len(inputs),)),
             pltpu.SemaphoreType.DMA((lists,)),
         ],

time: 105 us -> 90.1 us (0.86)
  Pallas kernels: 40.8 us -> 25.6 us
    pallas_call x1, Pallas kernels: 36 us -> 20.8 us  [make_sent(): pl.pallas_call(send_kernel, out_shape=jax.ShapeDtypeStruct((blocks, 4 * v...]
  transfers between devices with their start and end apart: 4 -> 4, of which waited for: 1 -> 1; matrix products, arithmetic and copies ran while one was open for 2% -> 2% of each run, Pallas kernels for 34% -> 23%
where the time goes in v6:
time: 90.1 us; the launch traced here: 89.7 us
  waiting for transfers between devices  45.2 us (50%)
  Pallas kernels  25.6 us (28%)
  starting transfers between devices  14.9 us (17%)
  local copies, waits for them, and re-layouts  3.21 us (4%)
    all_to_all x1, waiting for transfers between devices, body(): lax.all_to_all(sent, ('lon', 'lat'), split_axis=0, concat_axis=0, tiled=T...  45.2 us
    pallas_call x1, Pallas kernels, make_sent(): pl.pallas_call(send_kernel, out_shape=jax.ShapeDtypeStruct((blocks, 4 * v...  20.8 us
    all_to_all x1, starting transfers between devices, body(): lax.all_to_all(sent, ('lon', 'lat'), split_axis=0, concat_axis=0, tiled=T...  5.78 us
    ppermute x1, starting transfers between devices, body(): from_east = lax.ppermute(west_cells, 'lon', ring('lon', -1))  5.03 us
    pallas_call x1, Pallas kernels, place_owned(): pl.pallas_call(place_kernel, out_shape=jax.ShapeDtypeStruct((levels, ntr,...  3.68 us
    all_to_all x1, starting transfers between devices, body(): lax.all_to_all(send_count, ('lon', 'lat'), split_axis=1, concat_axis=1, t...  3.56 us
    unnamed x6, local copies, waits for them, and re-layouts  1.88 us
  transfers between devices with their start and end apart: 4, of which 1 were waited for; matrix products, arithmetic and copies ran while one was open for 2% of the time, Pallas kernels for 23%

profile of v6, /device:TPU:0, one launch (start us, length us, event | category | flops | bytes accessed | tf_op | source)
XLA Modules:
  0.0 89.7 jit_solution(13179826929769538331)
XLA Ops:
  0.0 0.0 copy-start
  0.0 1.2 %copy-done = f32[3,10,64,128]{3,2,1,0:T(8,128)S(1)} copy-done((f32[3,10,64,128]{3,2,1,0:T(8,128)S(1)}, f32[3,10,64,128]{3,2,1,0:T(8,128)}, u32[]{:S(2)}) %copy-start) | copy-done | bytes 983064
  1.2 1.1 %pack_halo.1 = (f32[10,3,8,128]{3,2,1,0:T(8,128)S(1)}, f32[10,3,8,128]{3,2,1,0:T(8,128)S(1)}) custom-call(f32[3,10,64,128]{3,2,1,0:T(8,128)S(1)} %copy-done), custom_call_target="tpu_custom_call" | custom-call | tf_op jit(solution)/shard_map/pack_halo/pallas_call | solution.py:54
  2.3 0.5 collective-permute-start
  2.8 5.0 %collective-permute-start.1 = (f32[10,3,8,128]{3,2,1,0:T(8,128)S(1)}, f32[10,3,8,128]{3,2,1,0:T(8,128)S(1)}, u32[]{:S(2)}, u32[]{:S(2)}) collective-permute-start(f32[10,3,8,128]{3,2,1,0:T(8,128)S(1)} %get-tuple-element.8), channel_id=1, source_target_pairs={{0,30},{2,0},{4,2},{6,4},{8,6},{10,8},{12,10},{14,12},{16,14},{18,... | collective-permute-start | bytes 368648 | tf_op jit(solution)/shard_map/ppermute | solution.py:323
  7.9 1.3 %copy.8 = s32[1,32,1]{2,0,1:T(1,128)} copy(s32[1,32,1]{1,2,0:T(1,128)} %bitcast.9) | data formatting | bytes 256 | tf_op jit(solution)/shard_map/all_to_all | solution.py:324
  9.2 3.6 %all-to-all-start.1 = ((s32[1,32,1]{2,0,1:T(1,128)}), s32[1,32,1]{2,0,1:T(1,128)S(1)}, u32[]{:S(2)}, u32[]{:S(2)}) async-start(s32[1,32,1]{2,0,1:T(1,128)} %copy.8), calls=%async_computation.1 | async-start | bytes 32768 | tf_op jit(solution)/shard_map/all_to_all | solution.py:324
  12.8 0.0 collective-permute-done
  12.8 0.0 copy-start.1
  12.8 0.0 collective-permute-done.1
  12.8 0.0 copy-start.2
  12.8 0.6 copy-done.1
  13.4 0.1 copy-done.2
  13.5 20.8 %advect_solve_pick.1 = f32[32,120,128]{2,1,0:T(8,128)} custom-call(f32[3,10,64,128]{3,2,1,0:T(8,128)} %tracers_in.1, s32[10,64,128]{2,1,0:T(8,128)} %offsets_in.1, f32[10,64,128]{2,1,0:T(8,128)} %weights_in.1, f32[9,64,128]{2,1,0:T(8,128)} %diffusion_in.1, f32[30,8,128]{2,1,0:T(8,128)} %bitcast.7, f32[30,8,128]{2,1,0:T(8,128)} %bitcast.8, ...), custom_call_target="tpu_custom_call" | custom-call | tf_op jit(solution)/shard_map/advect_solve_pick/pallas_call | solution.py:244
  34.3 0.0 all-to-all-done.1
  34.4 5.8 %all-to-all-start = ((f32[32,120,128]{2,1,0:T(8,128)}), f32[32,120,128]{2,1,0:T(8,128)S(1)}, u32[]{:S(2)}, u32[]{:S(2)}) async-start(f32[32,120,128]{2,1,0:T(8,128)} %advect_solve_pick.1), calls=%async_computation | async-start | bytes 3932160 | tf_op jit(solution)/shard_map/all_to_all | solution.py:329
  40.2 0.7 reduce
  40.8 45.2 %all-to-all-done.arrived = f32[32,120,128]{2,1,0:T(8,128)S(1)} async-done(((f32[32,120,128]{2,1,0:T(8,128)}), f32[32,120,128]{2,1,0:T(8,128)S(1)}, u32[]{:S(2)}, u32[]{:S(2)}) %all-to-all-start) | async-done | bytes 1966112 | tf_op jit(solution)/shard_map/all_to_all | solution.py:329
  86.0 3.7 %place_owned.1 = f32[10,3,8192]{2,1,0:T(4,128)} custom-call(f32[32,120,128]{2,1,0:T(8,128)S(1)} %all-to-all-done.arrived, s32[1,32]{1,0:T(1,128)S(1)} %bitcast.6, s32[1]{0:T(128)} %bitcast.3.own), custom_call_target="tpu_custom_call" | custom-call | tf_op jit(solution)/shard_map/place_owned/pallas_call | solution.py:299
Async XLA Ops:
  0.0 1.2 %copy-start = (f32[3,10,64,128]{3,2,1,0:T(8,128)S(1)}, f32[3,10,64,128]{3,2,1,0:T(8,128)}, u32[]{:S(2)}) copy-start(f32[3,10,64,128]{3,2,1,0:T(8,128)} %tracers_in.1) | copy-start | bytes 2949124
  2.3 10.4 %collective-permute-start = (f32[10,3,8,128]{3,2,1,0:T(8,128)S(1)}, f32[10,3,8,128]{3,2,1,0:T(8,128)S(1)}, u32[]{:S(2)}, u32[]{:S(2)}) collective-permute-start(f32[10,3,8,128]{3,2,1,0:T(8,128)S(1)} %get-tuple-element.7), channel_id=1, source_target_pairs={{0,2},{2,4},{4,6},{6,8},{8,10},{10,12},{12,14},{14,16},{16,18},{18... | collective-permute-start | bytes 368648 | tf_op jit(solution)/shard_map/ppermute | solution.py:322
  2.8 10.0 %collective-permute-start.1 = (f32[10,3,8,128]{3,2,1,0:T(8,128)S(1)}, f32[10,3,8,128]{3,2,1,0:T(8,128)S(1)}, u32[]{:S(2)}, u32[]{:S(2)}) collective-permute-start(f32[10,3,8,128]{3,2,1,0:T(8,128)S(1)} %get-tuple-element.8), channel_id=1, source_target_pairs={{0,30},{2,0},{4,2},{6,4},{8,6},{10,8},{12,10},{14,12},{16,14},{18,... | collective-permute-start | bytes 368648 | tf_op jit(solution)/shard_map/ppermute | solution.py:323
  9.2 25.1 %all-to-all-start.1 = ((s32[1,32,1]{2,0,1:T(1,128)}), s32[1,32,1]{2,0,1:T(1,128)S(1)}, u32[]{:S(2)}, u32[]{:S(2)}) async-start(s32[1,32,1]{2,0,1:T(1,128)} %copy.8), calls=%async_computation.1 | async-start | bytes 32768 | tf_op jit(solution)/shard_map/all_to_all | solution.py:324
  12.8 0.7 copy-start.1
  12.8 0.7 copy-start.2
  34.4 51.7 %all-to-all-start = ((f32[32,120,128]{2,1,0:T(8,128)}), f32[32,120,128]{2,1,0:T(8,128)S(1)}, u32[]{:S(2)}, u32[]{:S(2)}) async-start(f32[32,120,128]{2,1,0:T(8,128)} %advect_solve_pick.1), calls=%async_computation | async-start | bytes 3932160 | tf_op jit(solution)/shard_map/all_to_all | solution.py:329

commit v7 on v6

--- a/solution.py
+++ b/solution.py
@@ -132,9 +132,18 @@
     lax.fori_loop(0, lats // SUB, one_part, 0)
 
 
-def build_table(solved, table):
+def streams_of(rows, values, parts):
+    lane = lane_ids(rows)
+    width = values * parts
+    item = sum((lane >= width * step).astype(jnp.int32) for step in range(1, 4 // parts))
+    held = lane - item * width
+    part = held & (parts - 1)
+    return jnp.minimum(lax.shift_right_logical(held, parts.bit_length() - 1), values - 1), item * parts + part
+
+
+def build_table(solved, table, values, parts):
     rows_per = LANES // SLOT
-    spread = lane_ids(LANES) // 4
+    spread = streams_of(LANES, values, parts)[0]
     together = 2
 
     def some_rows(step, carry):
@@ -151,20 +160,20 @@
     lax.fori_loop(0, solved.shape[0] // (LANES * together), some_rows, 0)
 
 
-def pick_rows(table, index, count, cap, packed, sent, wait_list):
+def pick_rows(table, index, count, cap, chunk, parts, values, packed, sent, wait_list):
     blocks, height, _ = sent.shape
-    parts = cap // LANES
+    all_parts = cap // LANES
     lists = 4 // parts
-    stream = lax.broadcasted_iota(jnp.int32, (1, LANES), 1) % 4
+    stream = streams_of(1, values, parts)[1]
     together = 2 if blocks % 2 == 0 else 1
 
     def one_block(block, carry):
         owners = [block * lists + item for item in range(lists)]
-        rows = [lax.div(count[0, owner] + (parts - 1), parts) for owner in owners]
+        rows = [lax.div(count[0, owner] + (all_parts - 1), all_parts) for owner in owners]
         for owner in owners:
             wait_list(owner)
         longest = functools.reduce(jnp.maximum, rows)
-        places = [owners[g // parts] * cap + (g % parts) * rows[g // parts] for g in range(4)]
+        places = [owners[g // parts] * cap + (chunk * parts + g % parts) * rows[g // parts] for g in range(4)]
 
         def some_lines(step, inner):
             start = pl.multiple_of(step * LINES, LINES)
@@ -196,10 +205,7 @@
     lax.fori_loop(0, blocks // together, turn_blocks, 0)
 
 
-def send_kernel(
-    tracers_in, offsets_in, weights_in, diffusion_in, west_in, east_in, index_in, count, sent,
-    tracers, offsets, weights, diffusion, west, east, halo, solved, table, packed, index, ready, listed,
-):
+def list_copies(index_in, index, listed):
     lists, cap = index_in.shape[1:]
 
     def list_copy(item):
@@ -210,6 +216,15 @@
         list_copy(item).start()
         return carry
 
+    lax.fori_loop(0, lists, start_list, 0)
+    return lambda item: list_copy(item).wait()
+
+
+def solve_kernel(
+    parts, tracers_in, offsets_in, weights_in, diffusion_in, west_in, east_in, index_in, count, table, sent,
+    tracers, offsets, weights, diffusion, west, east, halo, solved, packed, index, ready, listed,
+):
+    values = west.shape[0]
     sources = (west_in, east_in, offsets_in, weights_in, diffusion_in, tracers_in)
     targets = (west, east, offsets, weights, diffusion, tracers)
     copies = [
@@ -218,77 +233,114 @@
     ]
     for copy in copies:
         copy.start()
-    lax.fori_loop(0, lists, start_list, 0)
+    wait_list = list_copies(index_in, index, listed)
     copies[0].wait()
     copies[1].wait()
-    merge_halo(west, east, halo, west.shape[0])
-    for value in range(west.shape[0], SLOT):
+    merge_halo(west, east, halo, values)
+    for value in range(values, SLOT):
         solved[pl.ds(value, tracers.shape[2], stride=SLOT), :] = jnp.zeros((tracers.shape[2], LANES), jnp.float32)
     for copy in copies[2:]:
         copy.wait()
     advect_and_solve(tracers, offsets, weights, diffusion, halo, solved)
-    build_table(solved, table.reshape(table.shape[0], LANES))
-    pick_rows(table, index, count, cap, packed, sent, lambda item: list_copy(item).wait())
+    build_table(solved, table.reshape(table.shape[0], LANES), values, parts)
+    pick_rows(table, index, count, index_in.shape[2], 0, parts, values, packed, sent, wait_list)
+
+
+def more_kernel(chunk, parts, values, table, index_in, count, sent, packed, index, listed):
+    wait_list = list_copies(index_in, index, listed)
+    pick_rows(table, index, count, index_in.shape[2], chunk, parts, values, packed, sent, wait_list)
 
 
 def make_sent(tracers, offsets, weights, diffusion, west, east, index, count):
     ntr, levels, lats, lons = tracers.shape
     values = ntr * levels
     lists, cap = index.shape[1:]
-    blocks = lists * (cap // LANES) // 4
+    chunks = 2 if cap // LANES % 2 == 0 else 1
+    parts = cap // LANES // chunks
+    blocks = lists * parts // 4
     hbm = pl.BlockSpec(memory_space=pl.ANY)
+    vmem = pl.BlockSpec(memory_space=pltpu.VMEM)
     smem = pl.BlockSpec(memory_space=pltpu.SMEM)
     west = west.reshape(values, SUB, LANES)
     east = east.reshape(values, SUB, LANES)
     inputs = (tracers, offsets, weights, diffusion, west, east)
-    return pl.pallas_call(
-        send_kernel,
-        out_shape=jax.ShapeDtypeStruct((blocks, 4 * values, LANES), jnp.float32),
+    sent_shape = jax.ShapeDtypeStruct((blocks, 4 * values, LANES), jnp.float32)
+    pick_scratch = [
+        pltpu.VMEM((blocks * LANES, LANES), jnp.float32),
+        pltpu.SMEM((lists * cap,), jnp.int32),
+    ]
+    table, first = pl.pallas_call(
+        functools.partial(solve_kernel, parts),
+        out_shape=(jax.ShapeDtypeStruct((lats * lons, 1, LANES), jnp.float32), sent_shape),
         in_specs=[hbm] * 7 + [smem],
-        out_specs=pl.BlockSpec(memory_space=pltpu.VMEM),
+        out_specs=(vmem, vmem),
         scratch_shapes=[pltpu.VMEM(array.shape, array.dtype) for array in inputs]
         + [
             pltpu.VMEM((values, 2, SUB, LANES), jnp.float32),
             pltpu.VMEM((lats * SLOT, LANES), jnp.float32),
-            pltpu.VMEM((lats * lons, 1, LANES), jnp.float32),
-            pltpu.VMEM((blocks * LANES, LANES), jnp.float32),
-            pltpu.SMEM((lists * cap,), jnp.int32),
+            *pick_scratch,
             pltpu.SemaphoreType.DMA((len(inputs),)),
             pltpu.SemaphoreType.DMA((lists,)),
         ],
-        compiler_params=pltpu.CompilerParams(vmem_limit_bytes=56 * MIB),
+        compiler_params=pltpu.CompilerParams(vmem_limit_bytes=20 * MIB),
         name="advect_solve_pick",
     )(*inputs, index, count)
-
-
-def place_kernel(arrived, counts, own, owned, row):
-    sources, height, _ = arrived.shape
+    sent = [first]
+    for chunk in range(1, chunks):
+        sent.append(
+            pl.pallas_call(
+                functools.partial(more_kernel, chunk, parts, values),
+                out_shape=sent_shape,
+                in_specs=[vmem, hbm, smem],
+                out_specs=vmem,
+                scratch_shapes=[*pick_scratch, pltpu.SemaphoreType.DMA((lists,))],
+                compiler_params=pltpu.CompilerParams(vmem_limit_bytes=16 * MIB),
+                name="pick_more",
+            )(table, index, count)
+        )
+    rows = values * parts
+    tile = max(size for size in (1, 2, 4, 8) if rows % size == 0)
+    return [array.reshape(lists, rows // tile, tile, LANES) for array in sent]
+
+
+def place_kernel(counts, own, *refs):
+    *arrived, owned, row, starts = refs
     levels, ntr, columns = owned.shape
     values = levels * ntr
-    parts = height // values
+    sources = counts.shape[1]
+    blocks, height, _ = arrived[0].shape
+    lists = sources // blocks
+    parts = height // values // lists
+    all_parts = parts * len(arrived)
     lane = lax.broadcasted_iota(jnp.int32, (values, LANES), 1)
-    together = 2 if sources % 2 == 0 else 1
-
-    def some_sources(step, start):
+
+    def one_start(turn, start):
+        source = lax.rem(own[0] - turn + sources, sources)
+        starts[source] = start
+        return start + counts[0, source]
+
+    def one_block(block, carry):
         pieces = []
-        for item in range(together):
-            source = lax.rem(own[0] - (step * together + item) + sources, sources)
+        for item in range(lists):
+            source = block * lists + item
             total = counts[0, source]
-            rows = lax.div(total + (parts - 1), parts)
-            for part in range(parts):
-                place = start + jnp.minimum(part * rows, total)
+            rows = lax.div(total + (all_parts - 1), all_parts)
+            for part in range(all_parts):
+                place = starts[source] + jnp.minimum(part * rows, total)
                 shift = lax.rem(place, LANES)
-                piece = arrived[source, pl.ds(part, values, stride=parts), :]
-                pieces.append((place - shift, shift, pltpu.roll(piece, shift, 1)))
-            start = start + total
-        for tile, shift, rolled in pieces:
+                end = shift + jnp.clip(total - part * rows, 0, rows)
+                first = item * values * parts + part % parts
+                piece = arrived[part // parts][block, pl.ds(first, values, stride=parts), :]
+                pieces.append((place - shift, shift, end, pltpu.roll(piece, shift, 1)))
+        for tile, shift, end, rolled in pieces:
             here = pl.ds(pl.multiple_of(tile, LANES), LANES)
             after = pl.ds(pl.multiple_of(tile + LANES, LANES), LANES)
-            pltpu.store(row.at[:, here], rolled, mask=lane >= shift)
-            row[:, after] = rolled
-        return start
-
-    lax.fori_loop(0, sources // together, some_sources, 0)
+            pltpu.store(row.at[:, here], rolled, mask=(lane >= shift) & (lane < end))
+            pltpu.store(row.at[:, after], rolled, mask=lane < end - LANES)
+        return carry
+
+    lax.fori_loop(0, sources, one_start, 0)
+    lax.fori_loop(0, blocks, one_block, 0)
     for level in range(levels):
         owned[level] = row[level * ntr : (level + 1) * ntr, :columns]
 
@@ -296,15 +348,20 @@
 def place_owned(arrived, counts, own, levels, ntr, columns):
     vmem = pl.BlockSpec(memory_space=pltpu.VMEM)
     smem = pl.BlockSpec(memory_space=pltpu.SMEM)
+    values = levels * ntr
+    arrived = [array.reshape(-1, 4 * values, LANES) for array in arrived]
     return pl.pallas_call(
         place_kernel,
         out_shape=jax.ShapeDtypeStruct((levels, ntr, columns), jnp.float32),
-        in_specs=[vmem, smem, smem],
+        in_specs=[smem, smem] + [vmem] * len(arrived),
         out_specs=vmem,
-        scratch_shapes=[pltpu.VMEM((levels * ntr, columns + 2 * LANES), jnp.float32)],
+        scratch_shapes=[
+            pltpu.VMEM((values, columns + 2 * LANES), jnp.float32),
+            pltpu.SMEM((counts.shape[1],), jnp.int32),
+        ],
         compiler_params=pltpu.CompilerParams(vmem_limit_bytes=16 * MIB),
         name="place_owned",
-    )(arrived, counts, own)
+    )(counts, own, *arrived)
 
 
 def ring(axis, distance):
@@ -315,18 +372,14 @@
 def body(tracers, offsets, weights, diffusion, send_index, send_count):
     ntr, levels, lats, lons = tracers.shape
     columns = lats * lons
-    lists, cap = send_index.shape[1:]
-    parts = cap // LANES
-    values = ntr * levels
     west_cells, east_cells = pack_halo(tracers)
     from_west = lax.ppermute(east_cells, "lon", ring("lon", 1))
     from_east = lax.ppermute(west_cells, "lon", ring("lon", -1))
     counts = lax.all_to_all(send_count, ("lon", "lat"), split_axis=1, concat_axis=1, tiled=True)
     sent = make_sent(tracers, offsets, weights, diffusion, from_west, from_east, send_index, send_count)
-    if parts < 4:
-        sent = sent.reshape(-1, values, 4 // parts, parts, LANES)
-        sent = jnp.transpose(sent, (0, 2, 1, 3, 4)).reshape(lists, values * parts, LANES)
-    arrived = lax.all_to_all(sent, ("lon", "lat"), split_axis=0, concat_axis=0, tiled=True)
+    arrived = [
+        lax.all_to_all(array, ("lon", "lat"), split_axis=0, concat_axis=0, tiled=True) for array in sent
+    ]
     own = lax.axis_index(("lon", "lat")).astype(jnp.int32).reshape(1)
     owned = place_owned(arrived, counts, own, levels, ntr, columns)
     return jnp.transpose(owned, (1, 0, 2))

time: 90.1 us -> 107 us (1.19)
  blocking collectives: 0 us -> 30.8 us
  waiting for transfers between devices: 45.2 us -> 24.2 us
  local copies, waits for them, and re-layouts: 3.21 us -> 8.13 us
  Pallas kernels: 25.6 us -> 30.5 us
  starting transfers between devices: 14.9 us -> 12.7 us
    all_to_all x0 -> x1, blocking collectives: none -> 30.8 us  [body(): lax.all_to_all(array, ('lon', 'lat'), split_axis=0, concat_axis=0, tiled=...]
    all_to_all x1, waiting for transfers between devices: 45.2 us -> 24.2 us  [body(): lax.all_to_all(array, ('lon', 'lat'), split_axis=0, concat_axis=0, tiled=...]
    unnamed x6 -> x14, local copies, waits for them, and re-layouts: 1.88 us -> 6.8 us
    pallas_call x1 -> x2, Pallas kernels: 20.8 us -> 25.4 us  [the longest x1 17.1 us: make_sent(): pl.pallas_call(functools.partial(solve_kernel, parts), out_shape=(jax.Sha...]
    all_to_all x1, starting transfers between devices: 5.78 us -> 3.62 us  [body(): lax.all_to_all(array, ('lon', 'lat'), split_axis=0, concat_axis=0, tiled=...]
  transfers between devices with their start and end apart: 4 -> 4, of which waited for: 1 -> 1; matrix products, arithmetic and copies ran while one was open for 2% -> 2% of each run, Pallas kernels for 23% -> 24%
where the time goes in v7:
time: 107 us
  blocking collectives  30.8 us (29%)
  Pallas kernels  30.5 us (29%)
  waiting for transfers between devices  24.2 us (23%)
  starting transfers between devices  12.7 us (12%)
  local copies, waits for them, and re-layouts  8.13 us (8%)
    all_to_all x1, blocking collectives, body(): lax.all_to_all(array, ('lon', 'lat'), split_axis=0, concat_axis=0, tiled=...  30.8 us
    all_to_all x1, waiting for transfers between devices, body(): lax.all_to_all(array, ('lon', 'lat'), split_axis=0, concat_axis=0, tiled=...  24.2 us
    pallas_call x1, Pallas kernels, make_sent(): pl.pallas_call(functools.partial(solve_kernel, parts), out_shape=(jax.Sha...  17.1 us
    pallas_call x1, Pallas kernels, make_sent(): pl.pallas_call(functools.partial(more_kernel, chunk, parts, values), out_...  8.34 us
    unnamed x14, local copies, waits for them, and re-layouts  6.8 us
    ppermute x1, starting transfers between devices, body(): from_east = lax.ppermute(west_cells, 'lon', ring('lon', -1))  5.03 us
    pallas_call x1, Pallas kernels, place_owned(): pl.pallas_call(place_kernel, out_shape=jax.ShapeDtypeStruct((levels, ntr,...  3.95 us
    all_to_all x1, starting transfers between devices, body(): lax.all_to_all(array, ('lon', 'lat'), split_axis=0, concat_axis=0, tiled=...  3.62 us
  transfers between devices with their start and end apart: 4, of which 1 were waited for; matrix products, arithmetic and copies ran while one was open for 2% of the time, Pallas kernels for 24%

profile of v7, /device:TPU:0, one launch (start us, length us, event | category | flops | bytes accessed | tf_op | source)
XLA Modules:
  0.0 107.1 jit_solution(4784903372112405645)
XLA Ops:
  0.0 0.0 copy-start
  0.0 1.2 %copy-done = f32[3,10,64,128]{3,2,1,0:T(8,128)S(1)} copy-done((f32[3,10,64,128]{3,2,1,0:T(8,128)S(1)}, f32[3,10,64,128]{3,2,1,0:T(8,128)}, u32[]{:S(2)}) %copy-start) | copy-done | bytes 983064
  1.2 1.1 %pack_halo.1 = (f32[10,3,8,128]{3,2,1,0:T(8,128)S(1)}, f32[10,3,8,128]{3,2,1,0:T(8,128)S(1)}) custom-call(f32[3,10,64,128]{3,2,1,0:T(8,128)S(1)} %copy-done), custom_call_target="tpu_custom_call" | custom-call | tf_op jit(solution)/shard_map/pack_halo/pallas_call | solution.py:54
  2.3 0.5 collective-permute-start
  2.8 5.0 %collective-permute-start.1 = (f32[10,3,8,128]{3,2,1,0:T(8,128)S(1)}, f32[10,3,8,128]{3,2,1,0:T(8,128)S(1)}, u32[]{:S(2)}, u32[]{:S(2)}) collective-permute-start(f32[10,3,8,128]{3,2,1,0:T(8,128)S(1)} %get-tuple-element.10), channel_id=1, source_target_pairs={{0,30},{2,0},{4,2},{6,4},{8,6},{10,8},{12,10},{14,12},{16,14},{18,... | collective-permute-start | bytes 368648 | tf_op jit(solution)/shard_map/ppermute | solution.py:377
  7.9 1.3 %copy.8 = s32[1,32,1]{2,0,1:T(1,128)} copy(s32[1,32,1]{1,2,0:T(1,128)} %bitcast.15) | data formatting | bytes 256 | tf_op jit(solution)/shard_map/all_to_all | solution.py:378
  9.2 3.6 %all-to-all-start = ((s32[1,32,1]{2,0,1:T(1,128)}), s32[1,32,1]{2,0,1:T(1,128)S(1)}, u32[]{:S(2)}, u32[]{:S(2)}) async-start(s32[1,32,1]{2,0,1:T(1,128)} %copy.8), calls=%async_computation | async-start | bytes 32768 | tf_op jit(solution)/shard_map/all_to_all | solution.py:378
  12.8 0.0 collective-permute-done
  12.8 0.0 collective-permute-done.1
  12.8 0.0 copy-start.1
  12.8 1.2 %copy-done.1 = f32[3,10,64,128]{3,2,1,0:T(8,128)S(1)} copy-done((f32[3,10,64,128]{3,2,1,0:T(8,128)S(1)}, f32[3,10,64,128]{3,2,1,0:T(8,128)}, u32[]{:S(2)}) %copy-start.1) | copy-done | bytes 983064
  14.0 0.0 copy-start.2
  14.0 1.0 copy-done.2
  15.0 0.0 copy-start.3
  15.0 1.0 copy-done.3
  15.9 0.0 copy-start.4
  15.9 1.0 copy-done.4
  16.9 0.0 copy-start.5
  16.9 0.8 copy-done.5
  17.7 0.0 copy-start.6
  17.7 0.7 copy-done.6
  18.4 17.1 %advect_solve_pick.1 = (f32[8192,1,128]{2,1,0:T(1,128)S(1)}, f32[16,120,128]{2,1,0:T(8,128)}) custom-call(f32[3,10,64,128]{3,2,1,0:T(8,128)S(1)} %copy-done.1, s32[10,64,128]{2,1,0:T(8,128)S(1)} %copy-done.2, f32[10,64,128]{2,1,0:T(8,128)S(1)} %copy-done.3, f32[9,64,128]{2,1,0:T(8,128)S(1)} %copy-done.4, f32[30,8,128]{2,1,0:T(8,128)S(1)} %bitcast.13, ...), custom_call_target="tpu_custom_call" | custom-call | tf_op jit(solution)/shard_map/advect_solve_pick/pallas_call | solution.py:272
  35.5 8.3 %pick_more.1 = f32[16,120,128]{2,1,0:T(8,128)S(1)} custom-call(f32[8192,1,128]{2,1,0:T(1,128)S(1)} %get-tuple-element.12.table, s32[1,32,512]{2,1,0:T(8,128)S(1)} %copy-done.5, s32[1,32]{1,0:T(1,128)S(1)} %copy-done.6), custom_call_target="tpu_custom_call" | custom-call | tf_op jit(solution)/shard_map/pick_more/pallas_call | solution.py:291
  43.8 0.0 all-to-all-done
  43.8 30.8 %all_to_all.21 = f32[32,15,4,128]{3,2,1,0:T(4,128)S(1)} all-to-all(f32[32,15,4,128]{3,2,1,0:T(4,128)S(1)} %bitcast.12), channel_id=1, replica_groups=mesh['lon'=16,'lat'=2] {'lon','lat'}, dimensions={0} | all-to-all | bytes 1966080 | tf_op jit(solution)/shard_map/all_to_all | solution.py:381
  74.6 3.6 %all-to-all-start.1 = ((f32[32,15,4,128]{3,2,1,0:T(4,128)}), f32[32,15,4,128]{3,2,1,0:T(4,128)S(1)}, u32[]{:S(2)}, u32[]{:S(2)}) async-start(f32[32,15,4,128]{3,2,1,0:T(4,128)} %bitcast.4), calls=%async_computation.1 | async-start | bytes 1966080 | tf_op jit(solution)/shard_map/all_to_all | solution.py:381
  78.3 0.7 reduce
  78.9 24.2 %all-to-all-done.1 = f32[32,15,4,128]{3,2,1,0:T(4,128)S(1)} async-done(((f32[32,15,4,128]{3,2,1,0:T(4,128)}), f32[32,15,4,128]{3,2,1,0:T(4,128)S(1)}, u32[]{:S(2)}, u32[]{:S(2)}) %all-to-all-start.1) | async-done | bytes 983072 | tf_op jit(solution)/shard_map/all_to_all | solution.py:381
  103.1 4.0 %place_owned.1 = f32[10,3,8192]{2,1,0:T(4,128)} custom-call(s32[1,32]{1,0:T(1,128)S(1)} %bitcast.16, s32[1]{0:T(128)} %bitcast.1.own, f32[16,120,128]{2,1,0:T(8,128)S(1)} %bitcast.11, f32[16,120,128]{2,1,0:T(8,128)S(1)} %bitcast.10), custom_call_target="tpu_custom_call" | custom-call | tf_op jit(solution)/shard_map/place_owned/pallas_call | solution.py:353
Async XLA Ops:
  0.0 1.2 %copy-start = (f32[3,10,64,128]{3,2,1,0:T(8,128)S(1)}, f32[3,10,64,128]{3,2,1,0:T(8,128)}, u32[]{:S(2)}) copy-start(f32[3,10,64,128]{3,2,1,0:T(8,128)} %tracers_in.1) | copy-start | bytes 2949124
  2.3 10.4 %collective-permute-start = (f32[10,3,8,128]{3,2,1,0:T(8,128)S(1)}, f32[10,3,8,128]{3,2,1,0:T(8,128)S(1)}, u32[]{:S(2)}, u32[]{:S(2)}) collective-permute-start(f32[10,3,8,128]{3,2,1,0:T(8,128)S(1)} %get-tuple-element.9), channel_id=1, source_target_pairs={{0,2},{2,4},{4,6},{6,8},{8,10},{10,12},{12,14},{14,16},{16,18},{18... | collective-permute-start | bytes 368648 | tf_op jit(solution)/shard_map/ppermute | solution.py:376
  2.8 9.9 %collective-permute-start.1 = (f32[10,3,8,128]{3,2,1,0:T(8,128)S(1)}, f32[10,3,8,128]{3,2,1,0:T(8,128)S(1)}, u32[]{:S(2)}, u32[]{:S(2)}) collective-permute-start(f32[10,3,8,128]{3,2,1,0:T(8,128)S(1)} %get-tuple-element.10), channel_id=1, source_target_pairs={{0,30},{2,0},{4,2},{6,4},{8,6},{10,8},{12,10},{14,12},{16,14},{18,... | collective-permute-start | bytes 368648 | tf_op jit(solution)/shard_map/ppermute | solution.py:377
  9.2 34.6 %all-to-all-start = ((s32[1,32,1]{2,0,1:T(1,128)}), s32[1,32,1]{2,0,1:T(1,128)S(1)}, u32[]{:S(2)}, u32[]{:S(2)}) async-start(s32[1,32,1]{2,0,1:T(1,128)} %copy.8), calls=%async_computation | async-start | bytes 32768 | tf_op jit(solution)/shard_map/all_to_all | solution.py:378
  12.8 1.2 %copy-start.1 = (f32[3,10,64,128]{3,2,1,0:T(8,128)S(1)}, f32[3,10,64,128]{3,2,1,0:T(8,128)}, u32[]{:S(2)}) copy-start(f32[3,10,64,128]{3,2,1,0:T(8,128)} %tracers_in.1) | copy-start | bytes 2949124
  14.0 1.0 copy-start.2
  15.0 1.0 copy-start.3
  15.9 1.0 copy-start.4
  16.9 0.8 copy-start.5
  17.7 0.7 copy-start.6
  74.6 28.5 %all-to-all-start.1 = ((f32[32,15,4,128]{3,2,1,0:T(4,128)}), f32[32,15,4,128]{3,2,1,0:T(4,128)S(1)}, u32[]{:S(2)}, u32[]{:S(2)}) async-start(f32[32,15,4,128]{3,2,1,0:T(4,128)} %bitcast.4), calls=%async_computation.1 | async-start | bytes 1966080 | tf_op jit(solution)/shard_map/all_to_all | solution.py:381

commit v8 on v7

v8 whole, which is shorter than its diff:
```python
import functools

import jax
import jax.numpy as jnp
from jax import lax
from jax.experimental import pallas as pl
from jax.experimental.pallas import tpu as pltpu
from jax.sharding import PartitionSpec as P

HALO = 16
LANES = 128
SUB = 8
SLOT = 32
LINES = 16
MIB = 1024 * 1024
LENGTH_BASE = 1000.0
BIG = 60 * MIB


def take_lanes(block, index):
    return jnp.take_along_axis(block, index, axis=1, mode="promise_in_bounds")


def lane_ids(rows):
    return lax.broadcasted_iota(jnp.int32, (rows, LANES), 1)


def pack_halo_kernel(tracers, west_cells, east_cells):
    ntr, levels, lats, _ = tracers.shape
    per_row = LANES // HALO
    group = lane_ids(SUB) // HALO

    def one_level(level, carry):
        for tracer in range(ntr):
            west = jnp.zeros((SUB, LANES), jnp.float32)
            east = jnp.zeros((SUB, LANES), jnp.float32)
            for part in range(lats // SUB):
                cells = tracers[tracer, level, part * SUB : (part + 1) * SUB, :]
                shift = part * HALO
                rolled_west = pltpu.roll(cells, shift, 1) if shift else cells
                shift = (part * HALO + HALO) % LANES
                rolled_east = pltpu.roll(cells, shift, 1) if shift else cells
                west = jnp.where(group == part, rolled_west, west)
                east = jnp.where(group == part, rolled_east, east)
            west_cells[level, tracer] = west
            east_cells[level, tracer] = east
        return carry

    assert lats == SUB * per_row
    lax.fori_loop(0, levels, one_level, 0)


def pack_halo(tracers):
    ntr, levels, _, _ = tracers.shape
    shape = jax.ShapeDtypeStruct((levels, ntr, SUB, LANES), jnp.float32)
    return pl.pallas_call(
        pack_halo_kernel,
        out_shape=(shape, shape),
        in_specs=[pl.BlockSpec(memory_space=pltpu.VMEM)],
        out_specs=[pl.BlockSpec(memory_space=pltpu.VMEM)] * 2,
        compiler_params=pltpu.CompilerParams(vmem_limit_bytes=16 * MIB),
        name="pack_halo",
    )(tracers)


def merge_halo(west, east, halo, count):
    lane = lane_ids(SUB)
    cell = lane % (2 * HALO)
    sources = [(half * 4 + lane // (2 * HALO)) * HALO + cell % HALO for half in range(2)]
    chunk = 5 if count % 5 == 0 else 1

    def some_values(step, carry):
        merged = []
        for item in range(chunk):
            value = step * chunk + item
            for half in range(2):
                both = take_lanes(west[value], sources[half]), take_lanes(east[value], sources[half])
                merged.append((value, half, jnp.where(cell < HALO, *both)))
        for value, half, cells in merged:
            halo[value, half] = cells
        return carry

    lax.fori_loop(0, count // chunk, some_values, 0)


def fetch(sources, targets, ready):
    copies = [
        pltpu.make_async_copy(source, target, ready.at[item])
        for item, (source, target) in enumerate(zip(sources, targets))
    ]
    for copy in copies:
        copy.start()
    return copies


def inside_kernel(
    tracers_in, offsets_in, weights_in, diffusion_in, index_in, count,
    inside, left_cell, west_edge, east_edge, lower, upper, lists,
    tracers, offsets, weights, diffusion, ready,
):
    ntr, levels, lats, _ = tracers.shape
    lane = lane_ids(SUB)
    owners = count.shape[1]
    copies = fetch(
        (diffusion_in, offsets_in, weights_in, tracers_in, index_in.at[0]),
        (diffusion, offsets, weights, tracers, lists.at[pl.ds(0, owners)]),
        ready,
    )
    lists[owners : owners + 1, :owners] = count[...]
    for copy in copies:
        copy.wait()

    def one_part(part, carry):
        rows = pl.ds(pl.multiple_of(part * SUB, SUB), SUB)
        coefs = [diffusion[level, rows, :] for level in range(levels - 1)]
        lowers, uppers, edges, results = [], [], [], []
        for level in range(levels):
            denom = 1.0
            if level > 0:
                denom = denom + coefs[level - 1]
            if level < levels - 1:
                denom = denom + coefs[level]
            if level > 0:
                denom = denom - coefs[level - 1] * uppers[level - 1]
            inverse = 1.0 / denom
            if level > 0:
                lowers.append(coefs[level - 1] * inverse)
            if level < levels - 1:
                uppers.append(coefs[level] * inverse)
            left = lane + offsets[level, rows, :]
            right = left + 1
            weight = weights[level, rows, :]
            west_weight = (1.0 - weight) * inverse
            east_weight = weight * inverse
            left_in = (left >= 0) & (left < LANES)
            right_in = (right >= 0) & (right < LANES)
            edges.append((left, jnp.where(left_in, 0.0, west_weight), jnp.where(right_in, 0.0, east_weight)))
            west_weight = jnp.where(left_in, west_weight, 0.0)
            east_weight = jnp.where(right_in, east_weight, 0.0)
            left = left & (LANES - 1)
            right = right & (LANES - 1)
            for tracer in range(ntr):
                cells = tracers[tracer, level, rows, :]
                results.append(west_weight * take_lanes(cells, left) + east_weight * take_lanes(cells, right))
        for value, result in enumerate(results):
            inside[value, rows, :] = result
        for level, (left, west_weight, east_weight) in enumerate(edges):
            left_cell[level, rows, :] = left
            west_edge[level, rows, :] = west_weight
            east_edge[level, rows, :] = east_weight
        for level in range(levels - 1):
            lower[level, rows, :] = lowers[level]
            upper[level, rows, :] = uppers[level]
        return carry

    lax.fori_loop(0, lats // SUB, one_part, 0)


def advect_inside(tracers, offsets, weights, diffusion, index, count):
    ntr, levels, lats, lons = tracers.shape
    lists, cap = index.shape[1:]
    vmem = pl.BlockSpec(memory_space=pltpu.VMEM)
    field = lambda count, kind=jnp.float32: jax.ShapeDtypeStruct((count, lats, lons), kind)
    outputs = (
        field(ntr * levels),
        field(levels, jnp.int32),
        field(levels),
        field(levels),
        field(levels - 1),
        field(levels - 1),
        jax.ShapeDtypeStruct((lists + SUB, cap), jnp.int32),
    )
    return pl.pallas_call(
        inside_kernel,
        out_shape=outputs,
        in_specs=[pl.BlockSpec(memory_space=pl.ANY)] * 5 + [vmem],
        out_specs=(vmem,) * len(outputs),
        scratch_shapes=[pltpu.VMEM(array.shape, array.dtype) for array in (tracers, offsets, weights, diffusion)]
        + [pltpu.SemaphoreType.DMA((5,))],
        compiler_params=pltpu.CompilerParams(vmem_limit_bytes=BIG),
        cost_estimate=pl.CostEstimate(flops=0, bytes_accessed=20 * MIB, transcendentals=0),
        name="advect_inside",
    )(tracers, offsets, weights, diffusion, index, count)


def add_edges_and_solve(inside, left_cell, west_edge, east_edge, lower, upper, halo, solved):
    levels, lats, _ = left_cell.shape
    ntr = inside.shape[0] // levels

    def one_part(part, carry):
        rows = pl.ds(pl.multiple_of(part * SUB, SUB), SUB)
        half = part // 4
        base = (part % 4) * (2 * HALO)
        reduced = [[] for _ in range(ntr)]
        for level in range(levels):
            left = left_cell[level, rows, :]
            right = base + ((left + (HALO + 1)) & (2 * HALO - 1))
            left = base + ((left + HALO) & (2 * HALO - 1))
            west_weight = west_edge[level, rows, :]
            east_weight = east_edge[level, rows, :]
            for tracer in range(ntr):
                value = level * ntr + tracer
                cells = halo[value, half]
                edges = west_weight * take_lanes(cells, left) + east_weight * take_lanes(cells, right)
                total = inside[value, rows, :] + edges
                if level > 0:
                    total = total + lower[level - 1, rows, :] * reduced[tracer][level - 1]
                reduced[tracer].append(total)
        results = []
        for tracer in range(ntr):
            x = reduced[tracer][levels - 1]
            for level in range(levels - 1, -1, -1):
                if level < levels - 1:
                    x = reduced[tracer][level] + upper[level, rows, :] * x
                results.append((level * ntr + tracer, x))
        for value, x in results:
            solved[pl.ds(part * SUB * SLOT + value, SUB, stride=SLOT), :] = x
        return carry

    lax.fori_loop(0, lats // SUB, one_part, 0)


def streams_of(rows, values, parts):
    lane = lane_ids(rows)
    width = values * parts
    item = sum((lane >= width * step).astype(jnp.int32) for step in range(1, 4 // parts))
    held = lane - item * width
    part = held & (parts - 1)
    return jnp.minimum(lax.shift_right_logical(held, parts.bit_length() - 1), values - 1), item * parts + part


def build_table(solved, table, values, parts):
    rows_per = LANES // SLOT
    spread = streams_of(LANES, values, parts)[0]
    together = 2

    def some_rows(step, carry):
        blocks = []
        for item in range(together):
            start = pl.multiple_of((step * together + item) * LANES, LANES)
            blocks.append(solved[pl.ds(start, LANES), :].T)
        for item, block in enumerate(blocks):
            for row in range(rows_per):
                start = pl.multiple_of(((step * together + item) * rows_per + row) * LANES, LANES)
                table[pl.ds(start, LANES), :] = take_lanes(block, spread + row * SLOT)
        return carry

    lax.fori_loop(0, solved.shape[0] // (LANES * together), some_rows, 0)


def pick_rows(table, index, count, cap, chunk, parts, values, packed, sent, wait_list):
    blocks, height, _ = sent.shape
    all_parts = cap // LANES
    lists = 4 // parts
    stream = streams_of(1, values, parts)[1]
    together = 2 if blocks % 2 == 0 else 1

    def one_block(block, carry):
        owners = [block * lists + item for item in range(lists)]
        rows = [lax.div(count[owner] + (all_parts - 1), all_parts) for owner in owners]
        for owner in owners:
            wait_list(owner)
        longest = functools.reduce(jnp.maximum, rows)
        places = [owners[g // parts] * cap + (chunk * parts + g % parts) * rows[g // parts] for g in range(4)]

        def some_lines(step, inner):
            start = pl.multiple_of(step * LINES, LINES)
            bases = [place + start for place in places]
            lines = []
            for line in range(LINES):
                picked = [table[index[base + line]] for base in bases]
                low = jnp.where(stream == 0, picked[0], picked[1])
                high = jnp.where(stream == 2, picked[2], picked[3])
                lines.append(jnp.where(stream < 2, low, high))
            first = pl.multiple_of(block * LANES + start, LINES)
            for line in range(LINES):
                packed[pl.ds(first + line, 1), :] = lines[line]
            return inner

        lax.fori_loop(0, lax.div(longest + (LINES - 1), LINES), some_lines, 0)
        return carry

    def turn_blocks(step, carry):
        turned = []
        for item in range(together):
            start = pl.multiple_of((step * together + item) * LANES, LANES)
            turned.append(packed[pl.ds(start, LANES), :].T)
        for item in range(together):
            block = step * together + item
            sent[block] = turned[item][:height, :]
            for owner in range(lists if last else 0):
                total = count[block * lists + owner]
                row = sent.at[block, pl.ds((owner * values + 1) * parts - 1, 1), :]
                note = jnp.full((1, LANES), LENGTH_BASE + total.astype(jnp.float32))
                pltpu.store(row, note, mask=(lane_ids(1) == LANES - 1) & (total < cap))
        return carry

    last = (chunk + 1) * parts == all_parts
    lax.fori_loop(0, blocks, one_block, 0)
    lax.fori_loop(0, blocks // together, turn_blocks, 0)


def list_copies(lists_in, index, count, listed):
    owners = lists_in.shape[0] - SUB
    cap = lists_in.shape[1]
    lengths = pltpu.make_async_copy(lists_in.at[owners], count, listed.at[owners])

    def list_copy(item):
        place = pl.ds(pl.multiple_of(item * cap, LANES), cap)
        return pltpu.make_async_copy(lists_in.at[item], index.at[place], listed.at[item])

    def start_list(item, carry):
        list_copy(item).start()
        return carry

    lengths.start()
    lax.fori_loop(0, owners, start_list, 0)
    return lengths.wait, lambda item: list_copy(item).wait()


def solve_kernel(
    chunk, parts, west_in, east_in, inside_in, left_cell_in, west_edge_in, east_edge_in, lower_in, upper_in, lists_in,
    sent, west, east, inside, left_cell, west_edge, east_edge, lower, upper, ready,
    halo, solved, table, packed, index, count, listed,
):
    values, lats, _ = inside.shape
    sources = (west_in, east_in, left_cell_in, west_edge_in, east_edge_in, lower_in, upper_in, inside_in)
    copies = fetch(sources, (west, east, left_cell, west_edge, east_edge, lower, upper, inside), ready)
    wait_lengths, wait_list = list_copies(lists_in, index, count, listed)
    for value in range(values, SLOT):
        solved[pl.ds(value, lats, stride=SLOT), :] = jnp.zeros((lats, LANES), jnp.float32)
    for copy in copies[:2]:
        copy.wait()
    merge_halo(west, east, halo, values)
    for copy in copies[2:]:
        copy.wait()
    add_edges_and_solve(inside, left_cell, west_edge, east_edge, lower, upper, halo, solved)
    build_table(solved, table.reshape(table.shape[0], LANES), values, parts)
    wait_lengths()
    pick_rows(table, index, count, lists_in.shape[1], chunk, parts, values, packed, sent, wait_list)


def make_sent(west, east, fields, lists_in):
    values, lats, lons = fields[0].shape
    lists, cap = lists_in.shape[0] - SUB, lists_in.shape[1]
    parts = cap // LANES
    blocks = lists * parts // 4
    inputs = (west.reshape(values, SUB, LANES), east.reshape(values, SUB, LANES), *fields)
    sent = pl.pallas_call(
        functools.partial(solve_kernel, 0, parts),
        out_shape=jax.ShapeDtypeStruct((blocks, 4 * values, LANES), jnp.float32),
        in_specs=[pl.BlockSpec(memory_space=pl.ANY)] * (len(inputs) + 1),
        out_specs=pl.BlockSpec(memory_space=pltpu.VMEM),
        scratch_shapes=[pltpu.VMEM(array.shape, array.dtype) for array in inputs]
        + [
            pltpu.SemaphoreType.DMA((len(inputs),)),
            pltpu.VMEM((values, 2, SUB, LANES), jnp.float32),
            pltpu.VMEM((lats * SLOT, LANES), jnp.float32),
            pltpu.VMEM((lats * lons, 1, LANES), jnp.float32),
            pltpu.VMEM((blocks * LANES, LANES), jnp.float32),
            pltpu.SMEM((lists * cap,), jnp.int32),
            pltpu.SMEM((cap,), jnp.int32),
            pltpu.SemaphoreType.DMA((lists + 1,)),
        ],
        compiler_params=pltpu.CompilerParams(vmem_limit_bytes=BIG),
        cost_estimate=pl.CostEstimate(flops=0, bytes_accessed=40 * MIB, transcendentals=0),
        name="solve_pick",
    )(*inputs, lists_in)
    rows = values * parts
    tile = max(size for size in (1, 2, 4, 8) if rows % size == 0)
    return sent.reshape(lists, rows // tile, tile, LANES)


def place_kernel(own, *refs):
    *arrived, owned, row, totals, starts = refs
    levels, ntr, columns = owned.shape
    values = levels * ntr
    sources = totals.shape[0]
    blocks, height, _ = arrived[0].shape
    lists = sources // blocks
    parts = height // values // lists
    all_parts = parts * len(arrived)
    lane = lax.broadcasted_iota(jnp.int32, (values, LANES), 1)

    for source in range(sources):
        note_row = (source % lists * values + 1) * parts - 1
        note = arrived[0][source // lists, note_row : note_row + 1, :]
        total = jnp.where(note > 0.5 * LENGTH_BASE, note - LENGTH_BASE, 1.0 * all_parts * LANES)
        totals[source] = total.astype(jnp.int32)[0, LANES - 1]

    def one_start(turn, start):
        source = lax.rem(own[0] - turn + sources, sources)
        starts[source] = start
        return start + totals[source]

    def one_block(block, carry):
        pieces = []
        for item in range(lists):
            source = block * lists + item
            total = totals[source]
            rows = lax.div(total + (all_parts - 1), all_parts)
            for part in range(all_parts):
                place = starts[source] + jnp.minimum(part * rows, total)
                shift = lax.rem(place, LANES)
                end = shift + jnp.clip(total - part * rows, 0, rows)
                first = item * values * parts + part % parts
                piece = arrived[-1 - part // parts][block, pl.ds(first, values, stride=parts), :]
                pieces.append((place - shift, shift, end, pltpu.roll(piece, shift, 1)))
        for tile, shift, end, rolled in pieces:
            here = pl.ds(pl.multiple_of(tile, LANES), LANES)
            after = pl.ds(pl.multiple_of(tile + LANES, LANES), LANES)
            pltpu.store(row.at[:, here], rolled, mask=(lane >= shift) & (lane < end))
            pltpu.store(row.at[:, after], rolled, mask=lane < end - LANES)
        return carry

    lax.fori_loop(0, sources, one_start, 0)
    lax.fori_loop(0, blocks, one_block, 0)
    for level in range(levels):
        owned[level] = row[level * ntr : (level + 1) * ntr, :columns]


def place_owned(arrived, own, levels, ntr, columns):
    vmem = pl.BlockSpec(memory_space=pltpu.VMEM)
    smem = pl.BlockSpec(memory_space=pltpu.SMEM)
    values = levels * ntr
    sources = arrived[0].shape[0]
    arrived = [array.reshape(-1, 4 * values, LANES) for array in arrived]
    return pl.pallas_call(
        place_kernel,
        out_shape=jax.ShapeDtypeStruct((levels, ntr, columns), jnp.float32),
        in_specs=[smem] + [vmem] * len(arrived),
        out_specs=vmem,
        scratch_shapes=[
            pltpu.VMEM((values, columns + 2 * LANES), jnp.float32),
            pltpu.SMEM((sources,), jnp.int32),
            pltpu.SMEM((sources,), jnp.int32),
        ],
        compiler_params=pltpu.CompilerParams(vmem_limit_bytes=16 * MIB),
        name="place_owned",
    )(own, *arrived)


def ring(axis, distance):
    size = lax.axis_size(axis)
    return [(i, (i + distance) % size) for i in range(size)]


def body(tracers, offsets, weights, diffusion, send_index, send_count):
    ntr, levels, lats, lons = tracers.shape
    columns = lats * lons
    west_cells, east_cells = pack_halo(tracers)
    from_west = lax.ppermute(east_cells, "lon", ring("lon", 1))
    from_east = lax.ppermute(west_cells, "lon", ring("lon", -1))
    *fields, lists = advect_inside(tracers, offsets, weights, diffusion, send_index, send_count)
    sent = make_sent(from_west, from_east, fields, lists)
    arrived = lax.all_to_all(sent, ("lon", "lat"), split_axis=0, concat_axis=0, tiled=True)
    own = lax.axis_index(("lon", "lat")).astype(jnp.int32).reshape(1)
    owned = place_owned([arrived], own, levels, ntr, columns)
    return jnp.transpose(owned, (1, 0, 2))


def solution(mesh):
    return jax.shard_map(
        body,
        mesh=mesh,
        in_specs=(
            P(None, None, "lat", "lon"),
            P(None, "lat", "lon"),
            P(None, "lat", "lon"),
            P(None, "lat", "lon"),
            P(("lon", "lat"), None, None),
            P(("lon", "lat"), None),
        ),
        out_specs=P(None, None, ("lon", "lat")),
        check_vma=False,
    )
```

time: 107 us -> 87 us (0.81)
  blocking collectives: 30.8 us -> 0 us
  waiting for transfers between devices: 24.2 us -> 45.9 us
  local copies, waits for them, and re-layouts: 8.13 us -> 1.86 us
  starting transfers between devices: 12.7 us -> 9.12 us
    all_to_all x1 -> x0, blocking collectives: 30.8 us -> none  [body(): lax.all_to_all(array, ('lon', 'lat'), split_axis=0, concat_axis=0, tiled=...]
    all_to_all x2 -> x1, waiting for transfers between devices: 24.2 us -> 45.9 us  [body(): lax.all_to_all(sent, ('lon', 'lat'), split_axis=0, concat_axis=0, tiled=T...]
    unnamed x14 -> x6, local copies, waits for them, and re-layouts: 6.8 us -> 1.86 us
    all_to_all x2 -> x1, starting transfers between devices: 7.18 us -> 3.59 us  [body(): lax.all_to_all(sent, ('lon', 'lat'), split_axis=0, concat_axis=0, tiled=T...]
    pallas_call x2, Pallas kernels: 25.4 us -> 24 us  [the longest x1 18.9 us: make_sent(): pl.pallas_call(functools.partial(solve_kernel, 0, parts), out_shape=jax.S...]
    all_to_all x1 -> x0, local copies, waits for them, and re-layouts: 1.33 us -> none  [body(): lax.all_to_all(send_count, ('lon', 'lat'), split_axis=1, concat_axis=1, t...]
  transfers between devices with their start and end apart: 4 -> 3, of which waited for: 1 -> 1; matrix products, arithmetic and copies ran while one was open for 2% -> 0% of each run, Pallas kernels for 24% -> 6%
where the time goes in v8:
time: 87 us; the launch traced here: 86.7 us
  waiting for transfers between devices  45.9 us (53%)
  Pallas kernels  29.8 us (34%)
  starting transfers between devices  9.12 us (10%)
  local copies, waits for them, and re-layouts  1.86 us (2%)
    all_to_all x1, waiting for transfers between devices, body(): lax.all_to_all(sent, ('lon', 'lat'), split_axis=0, concat_axis=0, tiled=T...  45.9 us
    pallas_call x1, Pallas kernels, make_sent(): pl.pallas_call(functools.partial(solve_kernel, 0, parts), out_shape=jax.S...  18.9 us
    pallas_call x1, Pallas kernels, advect_inside(): pl.pallas_call(inside_kernel, out_shape=outputs, in_specs=[pl.BlockSpec(m...  5.12 us
    ppermute x1, starting transfers between devices, body(): from_east = lax.ppermute(west_cells, 'lon', ring('lon', -1))  5.03 us
    pallas_call x1, Pallas kernels, place_owned(): pl.pallas_call(place_kernel, out_shape=jax.ShapeDtypeStruct((levels, ntr,...  4.67 us
    all_to_all x1, starting transfers between devices, body(): lax.all_to_all(sent, ('lon', 'lat'), split_axis=0, concat_axis=0, tiled=T...  3.59 us
    unnamed x6, local copies, waits for them, and re-layouts  1.86 us
  transfers between devices with their start and end apart: 3, of which 1 were waited for; matrix products, arithmetic and copies ran while one was open for 0% of the time, Pallas kernels for 6%

profile of v8, /device:TPU:0, one launch (start us, length us, event | category | flops | bytes accessed | tf_op | source)
XLA Modules:
  0.0 86.7 jit_solution(9399431627353287020)
XLA Ops:
  0.0 0.0 copy-start
  0.0 1.2 %copy-done = f32[3,10,64,128]{3,2,1,0:T(8,128)S(1)} copy-done((f32[3,10,64,128]{3,2,1,0:T(8,128)S(1)}, f32[3,10,64,128]{3,2,1,0:T(8,128)}, u32[]{:S(2)}) %copy-start) | copy-done | bytes 983064
  1.2 1.1 %pack_halo.1 = (f32[10,3,8,128]{3,2,1,0:T(8,128)S(1)}, f32[10,3,8,128]{3,2,1,0:T(8,128)S(1)}) custom-call(f32[3,10,64,128]{3,2,1,0:T(8,128)S(1)} %copy-done), custom_call_target="tpu_custom_call" | custom-call | tf_op jit(solution)/shard_map/pack_halo/pallas_call | solution.py:56
  2.3 0.5 collective-permute-start
  2.8 5.0 %collective-permute-start.1 = (f32[10,3,8,128]{3,2,1,0:T(8,128)S(1)}, f32[10,3,8,128]{3,2,1,0:T(8,128)S(1)}, u32[]{:S(2)}, u32[]{:S(2)}) collective-permute-start(f32[10,3,8,128]{3,2,1,0:T(8,128)S(1)} %get-tuple-element.15), channel_id=1, source_target_pairs={{0,30},{2,0},{4,2},{6,4},{8,6},{10,8},{12,10},{14,12},{16,14},{18,... | collective-permute-start | bytes 368648 | tf_op jit(solution)/shard_map/ppermute | solution.py:453
  7.9 5.1 %advect_inside.1 = (f32[30,64,128]{2,1,0:T(8,128)}, s32[10,64,128]{2,1,0:T(8,128)}, f32[10,64,128]{2,1,0:T(8,128)}, f32[10,64,128]{2,1,0:T(8,128)}, f32[9,64,128...) custom-call(f32[3,10,64,128]{3,2,1,0:T(8,128)} %tracers_in.1, s32[10,64,128]{2,1,0:T(8,128)} %offsets_in.1, ...), custom_call_target="tpu_custom_call" | custom-call | bytes 20971520 | tf_op jit(solution)/shard_map/advect_inside/pallas_call | solution.py:173
  13.0 0.0 collective-permute-done
  13.0 0.0 copy-start.1
  13.0 0.0 collective-permute-done.1
  13.0 0.0 copy-start.2
  13.0 0.6 copy-done.1
  13.6 0.0 copy-done.2
  13.7 18.9 %solve_pick.1 = f32[32,120,128]{2,1,0:T(8,128)} custom-call(f32[30,8,128]{2,1,0:T(8,128)} %bitcast.8, f32[30,8,128]{2,1,0:T(8,128)} %bitcast.9, f32[30,64,128]{2,1,0:T(8,128)} %get-tuple-element.16.inside_in, s32[10,64,128]{2,1,0:T(8,128)} %get-tuple-element.17.left_cell_in, f32[10,64,128]{2,1,0:T(8,128)} %get-tuple-element.18.west_edge_in, ...), custom_call_target="tpu_custom_call" | custom-call | bytes 41943040 | tf_op jit(solution)/shard_map/solve_pick/pallas_call | solution.py:349
  32.6 3.6 %all-to-all-start = ((f32[32,15,8,128]{3,2,1,0:T(8,128)}), f32[32,15,8,128]{3,2,1,0:T(8,128)S(1)}, u32[]{:S(2)}, u32[]{:S(2)}) async-start(f32[32,15,8,128]{3,2,1,0:T(8,128)} %bitcast.7), calls=%async_computation | async-start | bytes 3932160 | tf_op jit(solution)/shard_map/all_to_all | solution.py:456
  36.2 45.9 %all-to-all-done = f32[32,15,8,128]{3,2,1,0:T(8,128)S(1)} async-done(((f32[32,15,8,128]{3,2,1,0:T(8,128)}), f32[32,15,8,128]{3,2,1,0:T(8,128)S(1)}, u32[]{:S(2)}, u32[]{:S(2)}) %all-to-all-start) | async-done | bytes 1966112 | tf_op jit(solution)/shard_map/all_to_all | solution.py:456
  82.1 4.7 %place_owned.1 = f32[10,3,8192]{2,1,0:T(4,128)} custom-call(s32[1]{0:T(128)} %bitcast.own, f32[32,120,128]{2,1,0:T(8,128)S(1)} %bitcast.6), custom_call_target="tpu_custom_call" | custom-call | tf_op jit(solution)/shard_map/place_owned/pallas_call | solution.py:428
Async XLA Ops:
  0.0 1.2 %copy-start = (f32[3,10,64,128]{3,2,1,0:T(8,128)S(1)}, f32[3,10,64,128]{3,2,1,0:T(8,128)}, u32[]{:S(2)}) copy-start(f32[3,10,64,128]{3,2,1,0:T(8,128)} %tracers_in.1) | copy-start | bytes 2949124
  2.3 10.7 %collective-permute-start = (f32[10,3,8,128]{3,2,1,0:T(8,128)S(1)}, f32[10,3,8,128]{3,2,1,0:T(8,128)S(1)}, u32[]{:S(2)}, u32[]{:S(2)}) collective-permute-start(f32[10,3,8,128]{3,2,1,0:T(8,128)S(1)} %get-tuple-element.14), channel_id=1, source_target_pairs={{0,2},{2,4},{4,6},{6,8},{8,10},{10,12},{12,14},{14,16},{16,18},{18... | collective-permute-start | bytes 368648 | tf_op jit(solution)/shard_map/ppermute | solution.py:452
  2.8 10.2 %collective-permute-start.1 = (f32[10,3,8,128]{3,2,1,0:T(8,128)S(1)}, f32[10,3,8,128]{3,2,1,0:T(8,128)S(1)}, u32[]{:S(2)}, u32[]{:S(2)}) collective-permute-start(f32[10,3,8,128]{3,2,1,0:T(8,128)S(1)} %get-tuple-element.15), channel_id=1, source_target_pairs={{0,30},{2,0},{4,2},{6,4},{8,6},{10,8},{12,10},{14,12},{16,14},{18,... | collective-permute-start | bytes 368648 | tf_op jit(solution)/shard_map/ppermute | solution.py:453
  13.0 0.6 copy-start.1
  13.0 0.7 copy-start.2
  32.6 49.5 %all-to-all-start = ((f32[32,15,8,128]{3,2,1,0:T(8,128)}), f32[32,15,8,128]{3,2,1,0:T(8,128)S(1)}, u32[]{:S(2)}, u32[]{:S(2)}) async-start(f32[32,15,8,128]{3,2,1,0:T(8,128)} %bitcast.7), calls=%async_computation | async-start | bytes 3932160 | tf_op jit(solution)/shard_map/all_to_all | solution.py:456

commit v9 on v8

--- a/solution.py
+++ b/solution.py
@@ -248,20 +248,21 @@
     lax.fori_loop(0, solved.shape[0] // (LANES * together), some_rows, 0)
 
 
-def pick_rows(table, index, count, cap, chunk, parts, values, packed, sent, wait_list):
-    blocks, height, _ = sent.shape
-    all_parts = cap // LANES
-    lists = 4 // parts
-    stream = streams_of(1, values, parts)[1]
-    together = 2 if blocks % 2 == 0 else 1
-
-    def one_block(block, carry):
-        owners = [block * lists + item for item in range(lists)]
-        rows = [lax.div(count[owner] + (all_parts - 1), all_parts) for owner in owners]
-        for owner in owners:
-            wait_list(owner)
-        longest = functools.reduce(jnp.maximum, rows)
-        places = [owners[g // parts] * cap + (chunk * parts + g % parts) * rows[g // parts] for g in range(4)]
+def device_index():
+    return lax.axis_index("lon") * lax.axis_size("lat") + lax.axis_index("lat")
+
+
+def pick_rows(table, index, count, cap, values, packed, sent, wait_list):
+    parts = cap // LANES
+    turns = len(sent)
+    stream = streams_of(1, values, parts)[1] & (parts - 1)
+    own = device_index()
+
+    def one_turn(turn, carry):
+        owner = lax.rem(own + turn, turns)
+        rows = lax.div(count[owner] + (parts - 1), parts)
+        wait_list(owner)
+        places = [owner * cap + part * rows for part in range(parts)]
 
         def some_lines(step, inner):
             start = pl.multiple_of(step * LINES, LINES)
@@ -269,35 +270,27 @@
             lines = []
             for line in range(LINES):
                 picked = [table[index[base + line]] for base in bases]
-                low = jnp.where(stream == 0, picked[0], picked[1])
-                high = jnp.where(stream == 2, picked[2], picked[3])
-                lines.append(jnp.where(stream < 2, low, high))
-            first = pl.multiple_of(block * LANES + start, LINES)
+                merged = picked[0]
+                for part in range(1, parts):
+                    merged = jnp.where(stream == part, picked[part], merged)
+                lines.append(merged)
+            first = pl.multiple_of(turn * LANES + start, LINES)
             for line in range(LINES):
                 packed[pl.ds(first + line, 1), :] = lines[line]
             return inner
 
-        lax.fori_loop(0, lax.div(longest + (LINES - 1), LINES), some_lines, 0)
-        return carry
-
-    def turn_blocks(step, carry):
-        turned = []
-        for item in range(together):
-            start = pl.multiple_of((step * together + item) * LANES, LANES)
-            turned.append(packed[pl.ds(start, LANES), :].T)
-        for item in range(together):
-            block = step * together + item
-            sent[block] = turned[item][:height, :]
-            for owner in range(lists if last else 0):
-                total = count[block * lists + owner]
-                row = sent.at[block, pl.ds((owner * values + 1) * parts - 1, 1), :]
-                note = jnp.full((1, LANES), LENGTH_BASE + total.astype(jnp.float32))
-                pltpu.store(row, note, mask=(lane_ids(1) == LANES - 1) & (total < cap))
-        return carry
-
-    last = (chunk + 1) * parts == all_parts
-    lax.fori_loop(0, blocks, one_block, 0)
-    lax.fori_loop(0, blocks // together, turn_blocks, 0)
+        lax.fori_loop(0, lax.div(rows + (LINES - 1), LINES), some_lines, 0)
+        return carry
+
+    lax.fori_loop(0, turns, one_turn, 0)
+    for first in range(0, turns, 2):
+        turned = [packed[turn * LANES : (turn + 1) * LANES, :].T for turn in range(first, min(first + 2, turns))]
+        for turn, block in enumerate(turned, first):
+            sent[turn][...] = block[: values * parts, :]
+            total = count[lax.rem(own + turn, turns)]
+            note = jnp.full((1, LANES), LENGTH_BASE + total.astype(jnp.float32))
+            mask = (lane_ids(1) == LANES - 1) & (total < cap)
+            pltpu.store(sent[turn].at[pl.ds(parts - 1, 1), :], note, mask=mask)
 
 
 def list_copies(lists_in, index, count, listed):
@@ -319,10 +312,14 @@
 
 
 def solve_kernel(
-    chunk, parts, west_in, east_in, inside_in, left_cell_in, west_edge_in, east_edge_in, lower_in, upper_in, lists_in,
-    sent, west, east, inside, left_cell, west_edge, east_edge, lower, upper, ready,
-    halo, solved, table, packed, index, count, listed,
+    parts, west_in, east_in, inside_in, left_cell_in, west_edge_in, east_edge_in, lower_in, upper_in, lists_in, *refs
 ):
+    turns = lists_in.shape[0] - SUB
+    sent = refs[:turns]
+    (
+        west, east, inside, left_cell, west_edge, east_edge, lower, upper, ready,
+        halo, solved, table, packed, index, count, listed,
+    ) = refs[turns:]
     values, lats, _ = inside.shape
     sources = (west_in, east_in, left_cell_in, west_edge_in, east_edge_in, lower_in, upper_in, inside_in)
     copies = fetch(sources, (west, east, left_cell, west_edge, east_edge, lower, upper, inside), ready)
@@ -337,27 +334,26 @@
     add_edges_and_solve(inside, left_cell, west_edge, east_edge, lower, upper, halo, solved)
     build_table(solved, table.reshape(table.shape[0], LANES), values, parts)
     wait_lengths()
-    pick_rows(table, index, count, lists_in.shape[1], chunk, parts, values, packed, sent, wait_list)
+    pick_rows(table, index, count, lists_in.shape[1], values, packed, sent, wait_list)
 
 
 def make_sent(west, east, fields, lists_in):
     values, lats, lons = fields[0].shape
     lists, cap = lists_in.shape[0] - SUB, lists_in.shape[1]
     parts = cap // LANES
-    blocks = lists * parts // 4
     inputs = (west.reshape(values, SUB, LANES), east.reshape(values, SUB, LANES), *fields)
-    sent = pl.pallas_call(
-        functools.partial(solve_kernel, 0, parts),
-        out_shape=jax.ShapeDtypeStruct((blocks, 4 * values, LANES), jnp.float32),
+    return pl.pallas_call(
+        functools.partial(solve_kernel, parts),
+        out_shape=(jax.ShapeDtypeStruct((parts * values, LANES), jnp.float32),) * lists,
         in_specs=[pl.BlockSpec(memory_space=pl.ANY)] * (len(inputs) + 1),
-        out_specs=pl.BlockSpec(memory_space=pltpu.VMEM),
+        out_specs=(pl.BlockSpec(memory_space=pltpu.VMEM),) * lists,
         scratch_shapes=[pltpu.VMEM(array.shape, array.dtype) for array in inputs]
         + [
             pltpu.SemaphoreType.DMA((len(inputs),)),
             pltpu.VMEM((values, 2, SUB, LANES), jnp.float32),
             pltpu.VMEM((lats * SLOT, LANES), jnp.float32),
             pltpu.VMEM((lats * lons, 1, LANES), jnp.float32),
-            pltpu.VMEM((blocks * LANES, LANES), jnp.float32),
+            pltpu.VMEM((lists * LANES, LANES), jnp.float32),
             pltpu.SMEM((lists * cap,), jnp.int32),
             pltpu.SMEM((cap,), jnp.int32),
             pltpu.SemaphoreType.DMA((lists + 1,)),
@@ -366,78 +362,59 @@
         cost_estimate=pl.CostEstimate(flops=0, bytes_accessed=40 * MIB, transcendentals=0),
         name="solve_pick",
     )(*inputs, lists_in)
-    rows = values * parts
-    tile = max(size for size in (1, 2, 4, 8) if rows % size == 0)
-    return sent.reshape(lists, rows // tile, tile, LANES)
-
-
-def place_kernel(own, *refs):
-    *arrived, owned, row, totals, starts = refs
+
+
+def place_kernel(parts, *refs):
+    *arrived, owned, row = refs
     levels, ntr, columns = owned.shape
     values = levels * ntr
-    sources = totals.shape[0]
-    blocks, height, _ = arrived[0].shape
-    lists = sources // blocks
-    parts = height // values // lists
-    all_parts = parts * len(arrived)
     lane = lax.broadcasted_iota(jnp.int32, (values, LANES), 1)
-
-    for source in range(sources):
-        note_row = (source % lists * values + 1) * parts - 1
-        note = arrived[0][source // lists, note_row : note_row + 1, :]
-        total = jnp.where(note > 0.5 * LENGTH_BASE, note - LENGTH_BASE, 1.0 * all_parts * LANES)
-        totals[source] = total.astype(jnp.int32)[0, LANES - 1]
-
-    def one_start(turn, start):
-        source = lax.rem(own[0] - turn + sources, sources)
-        starts[source] = start
-        return start + totals[source]
-
-    def one_block(block, carry):
+    totals = []
+    for held in arrived:
+        note = held[parts - 1 : parts, :]
+        total = jnp.where(note > 0.5 * LENGTH_BASE, note - LENGTH_BASE, 1.0 * parts * LANES)
+        totals.append(total.astype(jnp.int32)[0, LANES - 1])
+    start = 0
+    for held, total in zip(arrived, totals):
+        rows = lax.div(total + (parts - 1), parts)
         pieces = []
-        for item in range(lists):
-            source = block * lists + item
-            total = totals[source]
-            rows = lax.div(total + (all_parts - 1), all_parts)
-            for part in range(all_parts):
-                place = starts[source] + jnp.minimum(part * rows, total)
-                shift = lax.rem(place, LANES)
-                end = shift + jnp.clip(total - part * rows, 0, rows)
-                first = item * values * parts + part % parts
-                piece = arrived[-1 - part // parts][block, pl.ds(first, values, stride=parts), :]
-                pieces.append((place - shift, shift, end, pltpu.roll(piece, shift, 1)))
-        for tile, shift, end, rolled in pieces:
+        for part in range(parts):
+            place = start + jnp.minimum(part * rows, total)
+            shift = lax.rem(place, LANES)
+            piece = held[pl.ds(part, values, stride=parts), :]
+            pieces.append((place - shift, shift, pltpu.roll(piece, shift, 1)))
+        for tile, shift, rolled in pieces:
             here = pl.ds(pl.multiple_of(tile, LANES), LANES)
             after = pl.ds(pl.multiple_of(tile + LANES, LANES), LANES)
-            pltpu.store(row.at[:, here], rolled, mask=(lane >= shift) & (lane < end))
-            pltpu.store(row.at[:, after], rolled, mask=lane < end - LANES)
-        return carry
-
-    lax.fori_loop(0, sources, one_start, 0)
-    lax.fori_loop(0, blocks, one_block, 0)
+            pltpu.store(row.at[:, here], rolled, mask=lane >= shift)
+            row[:, after] = rolled
+        start = start + total
     for level in range(levels):
         owned[level] = row[level * ntr : (level + 1) * ntr, :columns]
 
 
-def place_owned(arrived, own, levels, ntr, columns):
+def place_owned(arrived, levels, ntr, columns):
     vmem = pl.BlockSpec(memory_space=pltpu.VMEM)
-    smem = pl.BlockSpec(memory_space=pltpu.SMEM)
     values = levels * ntr
-    sources = arrived[0].shape[0]
-    arrived = [array.reshape(-1, 4 * values, LANES) for array in arrived]
     return pl.pallas_call(
-        place_kernel,
+        functools.partial(place_kernel, arrived[0].shape[0] // values),
         out_shape=jax.ShapeDtypeStruct((levels, ntr, columns), jnp.float32),
-        in_specs=[smem] + [vmem] * len(arrived),
+        in_specs=[vmem] * len(arrived),
         out_specs=vmem,
-        scratch_shapes=[
-            pltpu.VMEM((values, columns + 2 * LANES), jnp.float32),
-            pltpu.SMEM((sources,), jnp.int32),
-            pltpu.SMEM((sources,), jnp.int32),
-        ],
+        scratch_shapes=[pltpu.VMEM((values, columns + 2 * LANES), jnp.float32)],
         compiler_params=pltpu.CompilerParams(vmem_limit_bytes=16 * MIB),
         name="place_owned",
-    )(own, *arrived)
+    )(*arrived)
+
+
+def exchange_order(devices):
+    half = devices // 2
+    order = [half]
+    for step in range(1, half):
+        distance = half - step if step % 2 else step
+        order += [distance, devices - distance]
+    seen = list(dict.fromkeys(order))
+    return seen + [d for d in range(1, devices) if d not in seen]
 
 
 def ring(axis, distance):
@@ -453,9 +430,11 @@
     from_east = lax.ppermute(west_cells, "lon", ring("lon", -1))
     *fields, lists = advect_inside(tracers, offsets, weights, diffusion, send_index, send_count)
     sent = make_sent(from_west, from_east, fields, lists)
-    arrived = lax.all_to_all(sent, ("lon", "lat"), split_axis=0, concat_axis=0, tiled=True)
-    own = lax.axis_index(("lon", "lat")).astype(jnp.int32).reshape(1)
-    owned = place_owned([arrived], own, levels, ntr, columns)
+    axes = ("lon", "lat")
+    arrived = {0: sent[0]}
+    for turn in exchange_order(len(sent)):
+        arrived[turn] = lax.ppermute(sent[turn], axes, ring(axes, turn))
+    owned = place_owned([arrived[turn] for turn in range(len(sent))], levels, ntr, columns)
     return jnp.transpose(owned, (1, 0, 2))
 
 

time: 87 us -> 97.7 us (1.12)
  starting transfers between devices: 9.12 us -> 51.9 us
  waiting for transfers between devices: 45.9 us -> 16 us
  Pallas kernels: 29.8 us -> 26.7 us
    ppermute x0 -> x31, starting transfers between devices: none -> 46.3 us  [body(): arrived[turn] = lax.ppermute(sent[turn], axes, ring(axes, turn))]
    all_to_all x1 -> x0, waiting for transfers between devices: 45.9 us -> none  [body(): lax.all_to_all(sent, ('lon', 'lat'), split_axis=0, concat_axis=0, tiled=T...]
    ppermute x0 -> x31, waiting for transfers between devices: none -> 16 us  [body(): arrived[turn] = lax.ppermute(sent[turn], axes, ring(axes, turn))]
    all_to_all x1 -> x0, starting transfers between devices: 3.59 us -> none  [body(): lax.all_to_all(sent, ('lon', 'lat'), split_axis=0, concat_axis=0, tiled=T...]
    pallas_call x2, Pallas kernels: 23.6 us -> 20.5 us  [the longest x1 18.2 us: make_sent(): pl.pallas_call(functools.partial(solve_kernel, parts), out_shape=(jax.Sha...]
    unnamed x6 -> x8, local copies, waits for them, and re-layouts: 1.86 us -> 2.7 us
  transfers between devices with their start and end apart: 3 -> 33, of which waited for: 1 -> 12; matrix products, arithmetic and copies ran while one was open for 0% -> 0% of each run, Pallas kernels for 6% -> 5%
where the time goes in v9:
time: 97.7 us; the launch traced here: 97.3 us
  starting transfers between devices  51.9 us (53%)
  Pallas kernels  26.7 us (27%)
  waiting for transfers between devices  16 us (16%)
  local copies, waits for them, and re-layouts  2.7 us (3%)
    ppermute x31, starting transfers between devices, body(): arrived[turn] = lax.ppermute(sent[turn], axes, ring(axes, turn))  46.3 us
    pallas_call x1, Pallas kernels, make_sent(): pl.pallas_call(functools.partial(solve_kernel, parts), out_shape=(jax.Sha...  18.2 us
    ppermute x31, waiting for transfers between devices, body(): arrived[turn] = lax.ppermute(sent[turn], axes, ring(axes, turn))  16 us
    pallas_call x1, Pallas kernels, advect_inside(): pl.pallas_call(inside_kernel, out_shape=outputs, in_specs=[pl.BlockSpec(m...  5.12 us
    ppermute x1, starting transfers between devices, body(): from_east = lax.ppermute(west_cells, 'lon', ring('lon', -1))  5.03 us
    unnamed x8, local copies, waits for them, and re-layouts  2.7 us
    pallas_call x1, Pallas kernels, place_owned(): pl.pallas_call(functools.partial(place_kernel, arrived[0].shape[0] // val...  2.27 us
  transfers between devices with their start and end apart: 33, of which 12 were waited for; matrix products, arithmetic and copies ran while one was open for 0% of the time, Pallas kernels for 5%

profile of v9, /device:TPU:0, one launch (start us, length us, event | category | flops | bytes accessed | tf_op | source)
XLA Modules:
  0.0 97.3 jit_solution(1552870370909176968)
XLA Ops:
  0.0 1.2 %copy-done = f32[3,10,64,128]{3,2,1,0:T(8,128)S(1)} copy-done((f32[3,10,64,128]{3,2,1,0:T(8,128)S(1)}, f32[3,10,64,128]{3,2,1,0:T(8,128)}, u32[]{:S(2)}) %copy-start) | copy-done | bytes 983064
  1.2 1.1 %pack_halo.1 = (f32[10,3,8,128]{3,2,1,0:T(8,128)S(1)}, f32[10,3,8,128]{3,2,1,0:T(8,128)S(1)}) custom-call(f32[3,10,64,128]{3,2,1,0:T(8,128)S(1)} %copy-done), custom_call_target="tpu_custom_call" | custom-call | tf_op jit(solution)/shard_map/pack_halo/pallas_call | solution.py:56
  2.8 5.0 %collective-permute-start.1 = (f32[10,3,8,128]{3,2,1,0:T(8,128)S(1)}, f32[10,3,8,128]{3,2,1,0:T(8,128)S(1)}, u32[]{:S(2)}, u32[]{:S(2)}) collective-permute-start(f32[10,3,8,128]{3,2,1,0:T(8,128)S(1)} %get-tuple-element.47), channel_id=1, source_target_pairs={{0,30},{2,0},{4,2},{6,4},{8,6},{10,8},{12,10},{14,12},{16,14},{18,... | collective-permute-start | bytes 368648 | tf_op jit(solution)/shard_map/ppermute | solution.py:430
  7.9 5.1 %advect_inside.1 = (f32[30,64,128]{2,1,0:T(8,128)}, s32[10,64,128]{2,1,0:T(8,128)}, f32[10,64,128]{2,1,0:T(8,128)}, f32[10,64,128]{2,1,0:T(8,128)}, f32[9,64,128...) custom-call(f32[3,10,64,128]{3,2,1,0:T(8,128)} %tracers_in.1, s32[10,64,128]{2,1,0:T(8,128)} %offsets_in.1, ...), custom_call_target="tpu_custom_call" | custom-call | bytes 20971520 | tf_op jit(solution)/shard_map/advect_inside/pallas_call | solution.py:173
  13.7 18.2 %solve_pick.1 = (f32[120,128]{1,0:T(8,128)}, f32[120,128]{1,0:T(8,128)}, f32[120,128]{1,0:T(8,128)}, f32[120,128]{1,0:T(8,128)}, f32[120,128]{1,0:T(8,128)}, /*i...) custom-call(f32[30,8,128]{2,1,0:T(8,128)} %bitcast.3, ...), custom_call_target="tpu_custom_call" | custom-call | bytes 41943040 | tf_op jit(solution)/shard_map/solve_pick/pallas_call | solution.py:345
  31.9 2.0 %collective-permute-start.2 = (f32[120,128]{1,0:T(8,128)}, f32[120,128]{1,0:T(8,128)S(1)}, u32[]{:S(2)}, u32[]{:S(2)}) collective-permute-start(f32[120,128]{1,0:T(8,128)} %get-tuple-element.56), channel_id=1, source_target_pairs={{0,1},{1,2},{2,3},{3,4},{4,5},{5,6},{6,7},{7,8},{8,9},{9,10},{10,1... | collective-permute-start | bytes 184328 | tf_op jit(solution)/shard_map/ppermute | solution.py:436
  34.9 1.7 %collective-permute-start.6 = (f32[120,128]{1,0:T(8,128)}, f32[120,128]{1,0:T(8,128)S(1)}, u32[]{:S(2)}, u32[]{:S(2)}) collective-permute-start(f32[120,128]{1,0:T(8,128)} %get-tuple-element.60), channel_id=1, source_target_pairs={{0,5},{1,6},{2,7},{3,8},{4,9},{5,10},{6,11},{7,12},{8,13},{9,14},{... | collective-permute-start | bytes 184328 | tf_op jit(solution)/shard_map/ppermute | solution.py:436
  36.6 2.8 %collective-permute-done.2.refs_1_ = f32[120,128]{1,0:T(8,128)S(1)} collective-permute-done((f32[120,128]{1,0:T(8,128)}, f32[120,128]{1,0:T(8,128)S(1)}, u32[]{:S(2)}, u32[]{:S(2)}) %collective-permute-start.2) | collective-permute-done | bytes 61472 | tf_op jit(solution)/shard_map/ppermute | solution.py:436
  39.4 1.1 %collective-permute-done.3.refs_2_ = f32[120,128]{1,0:T(8,128)S(1)} collective-permute-done((f32[120,128]{1,0:T(8,128)}, f32[120,128]{1,0:T(8,128)S(1)}, u32[]{:S(2)}, u32[]{:S(2)}) %collective-permute-start.3) | collective-permute-done | bytes 61472 | tf_op jit(solution)/shard_map/ppermute | solution.py:436
  40.5 1.9 %collective-permute-done.4.refs_3_ = f32[120,128]{1,0:T(8,128)S(1)} collective-permute-done((f32[120,128]{1,0:T(8,128)}, f32[120,128]{1,0:T(8,128)S(1)}, u32[]{:S(2)}, u32[]{:S(2)}) %collective-permute-start.4) | collective-permute-done | bytes 61472 | tf_op jit(solution)/shard_map/ppermute | solution.py:436
  42.8 1.7 %collective-permute-start.11 = (f32[120,128]{1,0:T(8,128)}, f32[120,128]{1,0:T(8,128)S(1)}, u32[]{:S(2)}, u32[]{:S(2)}) collective-permute-start(f32[120,128]{1,0:T(8,128)} %get-tuple-element.65), channel_id=1, source_target_pairs={{0,10},{1,11},{2,12},{3,13},{4,14},{5,15},{6,16},{7,17},{8,18},{9,... | collective-permute-start | bytes 184328 | tf_op jit(solution)/shard_map/ppermute | solution.py:436
  45.1 1.6 %collective-permute-start.12 = (f32[120,128]{1,0:T(8,128)}, f32[120,128]{1,0:T(8,128)S(1)}, u32[]{:S(2)}, u32[]{:S(2)}) collective-permute-start(f32[120,128]{1,0:T(8,128)} %get-tuple-element.66), channel_id=1, source_target_pairs={{0,11},{1,12},{2,13},{3,14},{4,15},{5,16},{6,17},{7,18},{8,19},{9,... | collective-permute-start | bytes 184328 | tf_op jit(solution)/shard_map/ppermute | solution.py:436
  46.6 1.0 %collective-permute-done.8.refs_7_ = f32[120,128]{1,0:T(8,128)S(1)} collective-permute-done((f32[120,128]{1,0:T(8,128)}, f32[120,128]{1,0:T(8,128)S(1)}, u32[]{:S(2)}, u32[]{:S(2)}) %collective-permute-start.8) | collective-permute-done | bytes 61472 | tf_op jit(solution)/shard_map/ppermute | solution.py:436
  47.7 1.2 %collective-permute-start.13 = (f32[120,128]{1,0:T(8,128)}, f32[120,128]{1,0:T(8,128)S(1)}, u32[]{:S(2)}, u32[]{:S(2)}) collective-permute-start(f32[120,128]{1,0:T(8,128)} %get-tuple-element.67), channel_id=1, source_target_pairs={{0,12},{1,13},{2,14},{3,15},{4,16},{5,17},{6,18},{7,19},{8,20},{9,... | collective-permute-start | bytes 184328 | tf_op jit(solution)/shard_map/ppermute | solution.py:436
  48.9 2.1 %collective-permute-start.14 = (f32[120,128]{1,0:T(8,128)}, f32[120,128]{1,0:T(8,128)S(1)}, u32[]{:S(2)}, u32[]{:S(2)}) collective-permute-start(f32[120,128]{1,0:T(8,128)} %get-tuple-element.68), channel_id=1, source_target_pairs={{0,13},{1,14},{2,15},{3,16},{4,17},{5,18},{6,19},{7,20},{8,21},{9,... | collective-permute-start | bytes 184328 | tf_op jit(solution)/shard_map/ppermute | solution.py:436
  51.0 2.4 %collective-permute-done.10.refs_9_ = f32[120,128]{1,0:T(8,128)S(1)} collective-permute-done((f32[120,128]{1,0:T(8,128)}, f32[120,128]{1,0:T(8,128)S(1)}, u32[]{:S(2)}, u32[]{:S(2)}) %collective-permute-start.10) | collective-permute-done | bytes 61472 | tf_op jit(solution)/shard_map/ppermute | solution.py:436
  54.1 2.8 %collective-permute-done.12.refs_11_ = f32[120,128]{1,0:T(8,128)S(1)} collective-permute-done((f32[120,128]{1,0:T(8,128)}, f32[120,128]{1,0:T(8,128)S(1)}, u32[]{:S(2)}, u32[]{:S(2)}) %collective-permute-start.12) | collective-permute-done | bytes 61472 | tf_op jit(solution)/shard_map/ppermute | solution.py:436
  57.2 3.8 %collective-permute-start.18 = (f32[120,128]{1,0:T(8,128)}, f32[120,128]{1,0:T(8,128)S(1)}, u32[]{:S(2)}, u32[]{:S(2)}) collective-permute-start(f32[120,128]{1,0:T(8,128)} %get-tuple-element.72), channel_id=1, source_target_pairs={{0,17},{1,18},{2,19},{3,20},{4,21},{5,22},{6,23},{7,24},{8,25},{9,... | collective-permute-start | bytes 184328 | tf_op jit(solution)/shard_map/ppermute | solution.py:436
  61.6 5.2 %collective-permute-start.19 = (f32[120,128]{1,0:T(8,128)}, f32[120,128]{1,0:T(8,128)S(1)}, u32[]{:S(2)}, u32[]{:S(2)}) collective-permute-start(f32[120,128]{1,0:T(8,128)} %get-tuple-element.73), channel_id=1, source_target_pairs={{0,18},{1,19},{2,20},{3,21},{4,22},{5,23},{6,24},{7,25},{8,26},{9,... | collective-permute-start | bytes 184328 | tf_op jit(solution)/shard_map/ppermute | solution.py:436
  66.8 2.4 %collective-permute-start.21 = (f32[120,128]{1,0:T(8,128)}, f32[120,128]{1,0:T(8,128)S(1)}, u32[]{:S(2)}, u32[]{:S(2)}) collective-permute-start(f32[120,128]{1,0:T(8,128)} %get-tuple-element.75), channel_id=1, source_target_pairs={{0,20},{1,21},{2,22},{3,23},{4,24},{5,25},{6,26},{7,27},{8,28},{9,... | collective-permute-start | bytes 184328 | tf_op jit(solution)/shard_map/ppermute | solution.py:436
  69.2 2.1 %collective-permute-start.22 = (f32[120,128]{1,0:T(8,128)}, f32[120,128]{1,0:T(8,128)S(1)}, u32[]{:S(2)}, u32[]{:S(2)}) collective-permute-start(f32[120,128]{1,0:T(8,128)} %get-tuple-element.76), channel_id=1, source_target_pairs={{0,21},{1,22},{2,23},{3,24},{4,25},{5,26},{6,27},{7,28},{8,29},{9,... | collective-permute-start | bytes 184328 | tf_op jit(solution)/shard_map/ppermute | solution.py:436
  71.3 4.1 %collective-permute-start.23 = (f32[120,128]{1,0:T(8,128)}, f32[120,128]{1,0:T(8,128)S(1)}, u32[]{:S(2)}, u32[]{:S(2)}) collective-permute-start(f32[120,128]{1,0:T(8,128)} %get-tuple-element.77), channel_id=1, source_target_pairs={{0,22},{1,23},{2,24},{3,25},{4,26},{5,27},{6,28},{7,29},{8,30},{9,... | collective-permute-start | bytes 184328 | tf_op jit(solution)/shard_map/ppermute | solution.py:436
  75.5 1.1 %collective-permute-start.25 = (f32[120,128]{1,0:T(8,128)}, f32[120,128]{1,0:T(8,128)S(1)}, u32[]{:S(2)}, u32[]{:S(2)}) collective-permute-start(f32[120,128]{1,0:T(8,128)} %get-tuple-element.79), channel_id=1, source_target_pairs={{0,24},{1,25},{2,26},{3,27},{4,28},{5,29},{6,30},{7,31},{8,0},{9,1... | collective-permute-start | bytes 184328 | tf_op jit(solution)/shard_map/ppermute | solution.py:436
  76.6 1.5 %collective-permute-start.26 = (f32[120,128]{1,0:T(8,128)}, f32[120,128]{1,0:T(8,128)S(1)}, u32[]{:S(2)}, u32[]{:S(2)}) collective-permute-start(f32[120,128]{1,0:T(8,128)} %get-tuple-element.80), channel_id=1, source_target_pairs={{0,25},{1,26},{2,27},{3,28},{4,29},{5,30},{6,31},{7,0},{8,1},{9,2}... | collective-permute-start | bytes 184328 | tf_op jit(solution)/shard_map/ppermute | solution.py:436
  78.1 1.5 %collective-permute-start.27 = (f32[120,128]{1,0:T(8,128)}, f32[120,128]{1,0:T(8,128)S(1)}, u32[]{:S(2)}, u32[]{:S(2)}) collective-permute-start(f32[120,128]{1,0:T(8,128)} %get-tuple-element.81), channel_id=1, source_target_pairs={{0,26},{1,27},{2,28},{3,29},{4,30},{5,31},{6,0},{7,1},{8,2},{9,3},... | collective-permute-start | bytes 184328 | tf_op jit(solution)/shard_map/ppermute | solution.py:436
  79.6 1.3 %collective-permute-start.28 = (f32[120,128]{1,0:T(8,128)}, f32[120,128]{1,0:T(8,128)S(1)}, u32[]{:S(2)}, u32[]{:S(2)}) collective-permute-start(f32[120,128]{1,0:T(8,128)} %get-tuple-element.82), channel_id=1, source_target_pairs={{0,27},{1,28},{2,29},{3,30},{4,31},{5,0},{6,1},{7,2},{8,3},{9,4},{... | collective-permute-start | bytes 184328 | tf_op jit(solution)/shard_map/ppermute | solution.py:436
  81.4 4.1 %collective-permute-start.29 = (f32[120,128]{1,0:T(8,128)}, f32[120,128]{1,0:T(8,128)S(1)}, u32[]{:S(2)}, u32[]{:S(2)}) collective-permute-start(f32[120,128]{1,0:T(8,128)} %get-tuple-element.83), channel_id=1, source_target_pairs={{0,28},{1,29},{2,30},{3,31},{4,0},{5,1},{6,2},{7,3},{8,4},{9,5},{1... | collective-permute-start | bytes 184328 | tf_op jit(solution)/shard_map/ppermute | solution.py:436
  85.5 1.9 %collective-permute-start.30 = (f32[120,128]{1,0:T(8,128)}, f32[120,128]{1,0:T(8,128)S(1)}, u32[]{:S(2)}, u32[]{:S(2)}) collective-permute-start(f32[120,128]{1,0:T(8,128)} %get-tuple-element.84), channel_id=1, source_target_pairs={{0,29},{1,30},{2,31},{3,0},{4,1},{5,2},{6,3},{7,4},{8,5},{9,6},{10... | collective-permute-start | bytes 184328 | tf_op jit(solution)/shard_map/ppermute | solution.py:436
  87.4 1.0 %collective-permute-start.31 = (f32[120,128]{1,0:T(8,128)}, f32[120,128]{1,0:T(8,128)S(1)}, u32[]{:S(2)}, u32[]{:S(2)}) collective-permute-start(f32[120,128]{1,0:T(8,128)} %get-tuple-element.85), channel_id=1, source_target_pairs={{0,30},{1,31},{2,0},{3,1},{4,2},{5,3},{6,4},{7,5},{8,6},{9,7},{10,... | collective-permute-start | bytes 184328 | tf_op jit(solution)/shard_map/ppermute | solution.py:436
  88.4 3.6 %collective-permute-start.32 = (f32[120,128]{1,0:T(8,128)}, f32[120,128]{1,0:T(8,128)S(1)}, u32[]{:S(2)}, u32[]{:S(2)}) collective-permute-start(f32[120,128]{1,0:T(8,128)} %get-tuple-element.86), channel_id=1, source_target_pairs={{0,31},{1,0},{2,1},{3,2},{4,3},{5,4},{6,5},{7,6},{8,7},{9,8},{10,9... | collective-permute-start | bytes 184328 | tf_op jit(solution)/shard_map/ppermute | solution.py:436
  92.2 2.0 %collective-permute-done.32.refs_31_ = f32[120,128]{1,0:T(8,128)S(1)} collective-permute-done((f32[120,128]{1,0:T(8,128)}, f32[120,128]{1,0:T(8,128)S(1)}, u32[]{:S(2)}, u32[]{:S(2)}) %collective-permute-start.32) | collective-permute-done | bytes 61472 | tf_op jit(solution)/shard_map/ppermute | solution.py:436
  95.1 2.3 %place_owned.1 = f32[10,3,8192]{2,1,0:T(4,128)} custom-call(f32[120,128]{1,0:T(8,128)S(1)} %copy-done.1, f32[120,128]{1,0:T(8,128)S(1)} %collective-permute-done.2.refs_1_, f32[120,128]{1,0:T(8,128)S(1)} %collective-permute-done.3.refs_2_, f32[120,128]{1,0:T(8,128)S(1)} %collective-permute-done.4.refs_3_, f32[120,128]{1,0:T(8,128)S(1)} %collective-permute-done.5.refs_4_, ...), custom_call_target="tpu_custom_call" | custom-call | tf_op jit(solution)/shard_map/place_owned/pallas_call | solution.py:399
  (46 shorter events, 6.2 us)
Async XLA Ops:
  2.3 10.7 %collective-permute-start = (f32[10,3,8,128]{3,2,1,0:T(8,128)S(1)}, f32[10,3,8,128]{3,2,1,0:T(8,128)S(1)}, u32[]{:S(2)}, u32[]{:S(2)}) collective-permute-start(f32[10,3,8,128]{3,2,1,0:T(8,128)S(1)} %get-tuple-element.46), channel_id=1, source_target_pairs={{0,2},{2,4},{4,6},{6,8},{8,10},{10,12},{12,14},{14,16},{16,18},{18... | collective-permute-start | bytes 368648 | tf_op jit(solution)/shard_map/ppermute | solution.py:429
  2.8 10.2 %collective-permute-start.1 = (f32[10,3,8,128]{3,2,1,0:T(8,128)S(1)}, f32[10,3,8,128]{3,2,1,0:T(8,128)S(1)}, u32[]{:S(2)}, u32[]{:S(2)}) collective-permute-start(f32[10,3,8,128]{3,2,1,0:T(8,128)S(1)} %get-tuple-element.47), channel_id=1, source_target_pairs={{0,30},{2,0},{4,2},{6,4},{8,6},{10,8},{12,10},{14,12},{16,14},{18,... | collective-permute-start | bytes 368648 | tf_op jit(solution)/shard_map/ppermute | solution.py:430
  31.9 7.5 %collective-permute-start.2 = (f32[120,128]{1,0:T(8,128)}, f32[120,128]{1,0:T(8,128)S(1)}, u32[]{:S(2)}, u32[]{:S(2)}) collective-permute-start(f32[120,128]{1,0:T(8,128)} %get-tuple-element.56), channel_id=1, source_target_pairs={{0,1},{1,2},{2,3},{3,4},{4,5},{5,6},{6,7},{7,8},{8,9},{9,10},{10,1... | collective-permute-start | bytes 184328 | tf_op jit(solution)/shard_map/ppermute | solution.py:436
  33.9 6.7 %collective-permute-start.3 = (f32[120,128]{1,0:T(8,128)}, f32[120,128]{1,0:T(8,128)S(1)}, u32[]{:S(2)}, u32[]{:S(2)}) collective-permute-start(f32[120,128]{1,0:T(8,128)} %get-tuple-element.57), channel_id=1, source_target_pairs={{0,2},{1,3},{2,4},{3,5},{4,6},{5,7},{6,8},{7,9},{8,10},{9,11},{10,... | collective-permute-start | bytes 184328 | tf_op jit(solution)/shard_map/ppermute | solution.py:436
  33.9 8.6 %collective-permute-start.4 = (f32[120,128]{1,0:T(8,128)}, f32[120,128]{1,0:T(8,128)S(1)}, u32[]{:S(2)}, u32[]{:S(2)}) collective-permute-start(f32[120,128]{1,0:T(8,128)} %get-tuple-element.58), channel_id=1, source_target_pairs={{0,3},{1,4},{2,5},{3,6},{4,7},{5,8},{6,9},{7,10},{8,11},{9,12},{10... | collective-permute-start | bytes 184328 | tf_op jit(solution)/shard_map/ppermute | solution.py:436
  33.9 8.6 %collective-permute-start.5 = (f32[120,128]{1,0:T(8,128)}, f32[120,128]{1,0:T(8,128)S(1)}, u32[]{:S(2)}, u32[]{:S(2)}) collective-permute-start(f32[120,128]{1,0:T(8,128)} %get-tuple-element.59), channel_id=1, source_target_pairs={{0,4},{1,5},{2,6},{3,7},{4,8},{5,9},{6,10},{7,11},{8,12},{9,13},{1... | collective-permute-start | bytes 184328 | tf_op jit(solution)/shard_map/ppermute | solution.py:436
  34.9 7.9 %collective-permute-start.6 = (f32[120,128]{1,0:T(8,128)}, f32[120,128]{1,0:T(8,128)S(1)}, u32[]{:S(2)}, u32[]{:S(2)}) collective-permute-start(f32[120,128]{1,0:T(8,128)} %get-tuple-element.60), channel_id=1, source_target_pairs={{0,5},{1,6},{2,7},{3,8},{4,9},{5,10},{6,11},{7,12},{8,13},{9,14},{... | collective-permute-start | bytes 184328 | tf_op jit(solution)/shard_map/ppermute | solution.py:436
  39.4 5.7 %collective-permute-start.7 = (f32[120,128]{1,0:T(8,128)}, f32[120,128]{1,0:T(8,128)S(1)}, u32[]{:S(2)}, u32[]{:S(2)}) collective-permute-start(f32[120,128]{1,0:T(8,128)} %get-tuple-element.61), channel_id=1, source_target_pairs={{0,6},{1,7},{2,8},{3,9},{4,10},{5,11},{6,12},{7,13},{8,14},{9,15},... | collective-permute-start | bytes 184328 | tf_op jit(solution)/shard_map/ppermute | solution.py:436
  40.5 7.1 %collective-permute-start.8 = (f32[120,128]{1,0:T(8,128)}, f32[120,128]{1,0:T(8,128)S(1)}, u32[]{:S(2)}, u32[]{:S(2)}) collective-permute-start(f32[120,128]{1,0:T(8,128)} %get-tuple-element.62), channel_id=1, source_target_pairs={{0,7},{1,8},{2,9},{3,10},{4,11},{5,12},{6,13},{7,14},{8,15},{9,16}... | collective-permute-start | bytes 184328 | tf_op jit(solution)/shard_map/ppermute | solution.py:436
  42.5 6.4 %collective-permute-start.9 = (f32[120,128]{1,0:T(8,128)}, f32[120,128]{1,0:T(8,128)S(1)}, u32[]{:S(2)}, u32[]{:S(2)}) collective-permute-start(f32[120,128]{1,0:T(8,128)} %get-tuple-element.63), channel_id=1, source_target_pairs={{0,8},{1,9},{2,10},{3,11},{4,12},{5,13},{6,14},{7,15},{8,16},{9,17... | collective-permute-start | bytes 184328 | tf_op jit(solution)/shard_map/ppermute | solution.py:436
  42.5 10.9 %collective-permute-start.10 = (f32[120,128]{1,0:T(8,128)}, f32[120,128]{1,0:T(8,128)S(1)}, u32[]{:S(2)}, u32[]{:S(2)}) collective-permute-start(f32[120,128]{1,0:T(8,128)} %get-tuple-element.64), channel_id=1, source_target_pairs={{0,9},{1,10},{2,11},{3,12},{4,13},{5,14},{6,15},{7,16},{8,17},{9,1... | collective-permute-start | bytes 184328 | tf_op jit(solution)/shard_map/ppermute | solution.py:436
  42.8 11.0 %collective-permute-start.11 = (f32[120,128]{1,0:T(8,128)}, f32[120,128]{1,0:T(8,128)S(1)}, u32[]{:S(2)}, u32[]{:S(2)}) collective-permute-start(f32[120,128]{1,0:T(8,128)} %get-tuple-element.65), channel_id=1, source_target_pairs={{0,10},{1,11},{2,12},{3,13},{4,14},{5,15},{6,16},{7,17},{8,18},{9,... | collective-permute-start | bytes 184328 | tf_op jit(solution)/shard_map/ppermute | solution.py:436
  45.1 11.8 %collective-permute-start.12 = (f32[120,128]{1,0:T(8,128)}, f32[120,128]{1,0:T(8,128)S(1)}, u32[]{:S(2)}, u32[]{:S(2)}) collective-permute-start(f32[120,128]{1,0:T(8,128)} %get-tuple-element.66), channel_id=1, source_target_pairs={{0,11},{1,12},{2,13},{3,14},{4,15},{5,16},{6,17},{7,18},{8,19},{9,... | collective-permute-start | bytes 184328 | tf_op jit(solution)/shard_map/ppermute | solution.py:436
  47.7 9.5 %collective-permute-start.13 = (f32[120,128]{1,0:T(8,128)}, f32[120,128]{1,0:T(8,128)S(1)}, u32[]{:S(2)}, u32[]{:S(2)}) collective-permute-start(f32[120,128]{1,0:T(8,128)} %get-tuple-element.67), channel_id=1, source_target_pairs={{0,12},{1,13},{2,14},{3,15},{4,16},{5,17},{6,18},{7,19},{8,20},{9,... | collective-permute-start | bytes 184328 | tf_op jit(solution)/shard_map/ppermute | solution.py:436
  48.9 12.7 %collective-permute-start.14 = (f32[120,128]{1,0:T(8,128)}, f32[120,128]{1,0:T(8,128)S(1)}, u32[]{:S(2)}, u32[]{:S(2)}) collective-permute-start(f32[120,128]{1,0:T(8,128)} %get-tuple-element.68), channel_id=1, source_target_pairs={{0,13},{1,14},{2,15},{3,16},{4,17},{5,18},{6,19},{7,20},{8,21},{9,... | collective-permute-start | bytes 184328 | tf_op jit(solution)/shard_map/ppermute | solution.py:436
  53.4 13.4 %collective-permute-start.15 = (f32[120,128]{1,0:T(8,128)}, f32[120,128]{1,0:T(8,128)S(1)}, u32[]{:S(2)}, u32[]{:S(2)}) collective-permute-start(f32[120,128]{1,0:T(8,128)} %get-tuple-element.69), channel_id=1, source_target_pairs={{0,14},{1,15},{2,16},{3,17},{4,18},{5,19},{6,20},{7,21},{8,22},{9,... | collective-permute-start | bytes 184328 | tf_op jit(solution)/shard_map/ppermute | solution.py:436
  53.8 13.0 %collective-permute-start.16 = (f32[120,128]{1,0:T(8,128)}, f32[120,128]{1,0:T(8,128)S(1)}, u32[]{:S(2)}, u32[]{:S(2)}) collective-permute-start(f32[120,128]{1,0:T(8,128)} %get-tuple-element.70), channel_id=1, source_target_pairs={{0,15},{1,16},{2,17},{3,18},{4,19},{5,20},{6,21},{7,22},{8,23},{9,... | collective-permute-start | bytes 184328 | tf_op jit(solution)/shard_map/ppermute | solution.py:436
  56.9 12.3 %collective-permute-start.17 = (f32[120,128]{1,0:T(8,128)}, f32[120,128]{1,0:T(8,128)S(1)}, u32[]{:S(2)}, u32[]{:S(2)}) collective-permute-start(f32[120,128]{1,0:T(8,128)} %get-tuple-element.71), channel_id=1, source_target_pairs={{0,16},{1,17},{2,18},{3,19},{4,20},{5,21},{6,22},{7,23},{8,24},{9,... | collective-permute-start | bytes 184328 | tf_op jit(solution)/shard_map/ppermute | solution.py:436
  57.2 14.1 %collective-permute-start.18 = (f32[120,128]{1,0:T(8,128)}, f32[120,128]{1,0:T(8,128)S(1)}, u32[]{:S(2)}, u32[]{:S(2)}) collective-permute-start(f32[120,128]{1,0:T(8,128)} %get-tuple-element.72), channel_id=1, source_target_pairs={{0,17},{1,18},{2,19},{3,20},{4,21},{5,22},{6,23},{7,24},{8,25},{9,... | collective-permute-start | bytes 184328 | tf_op jit(solution)/shard_map/ppermute | solution.py:436
  61.6 13.9 %collective-permute-start.19 = (f32[120,128]{1,0:T(8,128)}, f32[120,128]{1,0:T(8,128)S(1)}, u32[]{:S(2)}, u32[]{:S(2)}) collective-permute-start(f32[120,128]{1,0:T(8,128)} %get-tuple-element.73), channel_id=1, source_target_pairs={{0,18},{1,19},{2,20},{3,21},{4,22},{5,23},{6,24},{7,25},{8,26},{9,... | collective-permute-start | bytes 184328 | tf_op jit(solution)/shard_map/ppermute | solution.py:436
  66.8 8.7 %collective-permute-start.20 = (f32[120,128]{1,0:T(8,128)}, f32[120,128]{1,0:T(8,128)S(1)}, u32[]{:S(2)}, u32[]{:S(2)}) collective-permute-start(f32[120,128]{1,0:T(8,128)} %get-tuple-element.74), channel_id=1, source_target_pairs={{0,19},{1,20},{2,21},{3,22},{4,23},{5,24},{6,25},{7,26},{8,27},{9,... | collective-permute-start | bytes 184328 | tf_op jit(solution)/shard_map/ppermute | solution.py:436
  66.8 9.8 %collective-permute-start.21 = (f32[120,128]{1,0:T(8,128)}, f32[120,128]{1,0:T(8,128)S(1)}, u32[]{:S(2)}, u32[]{:S(2)}) collective-permute-start(f32[120,128]{1,0:T(8,128)} %get-tuple-element.75), channel_id=1, source_target_pairs={{0,20},{1,21},{2,22},{3,23},{4,24},{5,25},{6,26},{7,27},{8,28},{9,... | collective-permute-start | bytes 184328 | tf_op jit(solution)/shard_map/ppermute | solution.py:436
  69.2 8.9 %collective-permute-start.22 = (f32[120,128]{1,0:T(8,128)}, f32[120,128]{1,0:T(8,128)S(1)}, u32[]{:S(2)}, u32[]{:S(2)}) collective-permute-start(f32[120,128]{1,0:T(8,128)} %get-tuple-element.76), channel_id=1, source_target_pairs={{0,21},{1,22},{2,23},{3,24},{4,25},{5,26},{6,27},{7,28},{8,29},{9,... | collective-permute-start | bytes 184328 | tf_op jit(solution)/shard_map/ppermute | solution.py:436
  71.3 8.3 %collective-permute-start.23 = (f32[120,128]{1,0:T(8,128)}, f32[120,128]{1,0:T(8,128)S(1)}, u32[]{:S(2)}, u32[]{:S(2)}) collective-permute-start(f32[120,128]{1,0:T(8,128)} %get-tuple-element.77), channel_id=1, source_target_pairs={{0,22},{1,23},{2,24},{3,25},{4,26},{5,27},{6,28},{7,29},{8,30},{9,... | collective-permute-start | bytes 184328 | tf_op jit(solution)/shard_map/ppermute | solution.py:436
  75.5 5.9 %collective-permute-start.24 = (f32[120,128]{1,0:T(8,128)}, f32[120,128]{1,0:T(8,128)S(1)}, u32[]{:S(2)}, u32[]{:S(2)}) collective-permute-start(f32[120,128]{1,0:T(8,128)} %get-tuple-element.78), channel_id=1, source_target_pairs={{0,23},{1,24},{2,25},{3,26},{4,27},{5,28},{6,29},{7,30},{8,31},{9,... | collective-permute-start | bytes 184328 | tf_op jit(solution)/shard_map/ppermute | solution.py:436
  75.5 10.0 %collective-permute-start.25 = (f32[120,128]{1,0:T(8,128)}, f32[120,128]{1,0:T(8,128)S(1)}, u32[]{:S(2)}, u32[]{:S(2)}) collective-permute-start(f32[120,128]{1,0:T(8,128)} %get-tuple-element.79), channel_id=1, source_target_pairs={{0,24},{1,25},{2,26},{3,27},{4,28},{5,29},{6,30},{7,31},{8,0},{9,1... | collective-permute-start | bytes 184328 | tf_op jit(solution)/shard_map/ppermute | solution.py:436
  76.6 10.8 %collective-permute-start.26 = (f32[120,128]{1,0:T(8,128)}, f32[120,128]{1,0:T(8,128)S(1)}, u32[]{:S(2)}, u32[]{:S(2)}) collective-permute-start(f32[120,128]{1,0:T(8,128)} %get-tuple-element.80), channel_id=1, source_target_pairs={{0,25},{1,26},{2,27},{3,28},{4,29},{5,30},{6,31},{7,0},{8,1},{9,2}... | collective-permute-start | bytes 184328 | tf_op jit(solution)/shard_map/ppermute | solution.py:436
  78.1 10.3 %collective-permute-start.27 = (f32[120,128]{1,0:T(8,128)}, f32[120,128]{1,0:T(8,128)S(1)}, u32[]{:S(2)}, u32[]{:S(2)}) collective-permute-start(f32[120,128]{1,0:T(8,128)} %get-tuple-element.81), channel_id=1, source_target_pairs={{0,26},{1,27},{2,28},{3,29},{4,30},{5,31},{6,0},{7,1},{8,2},{9,3},... | collective-permute-start | bytes 184328 | tf_op jit(solution)/shard_map/ppermute | solution.py:436
  79.6 12.4 %collective-permute-start.28 = (f32[120,128]{1,0:T(8,128)}, f32[120,128]{1,0:T(8,128)S(1)}, u32[]{:S(2)}, u32[]{:S(2)}) collective-permute-start(f32[120,128]{1,0:T(8,128)} %get-tuple-element.82), channel_id=1, source_target_pairs={{0,27},{1,28},{2,29},{3,30},{4,31},{5,0},{6,1},{7,2},{8,3},{9,4},{... | collective-permute-start | bytes 184328 | tf_op jit(solution)/shard_map/ppermute | solution.py:436
  81.4 10.7 %collective-permute-start.29 = (f32[120,128]{1,0:T(8,128)}, f32[120,128]{1,0:T(8,128)S(1)}, u32[]{:S(2)}, u32[]{:S(2)}) collective-permute-start(f32[120,128]{1,0:T(8,128)} %get-tuple-element.83), channel_id=1, source_target_pairs={{0,28},{1,29},{2,30},{3,31},{4,0},{5,1},{6,2},{7,3},{8,4},{9,5},{1... | collective-permute-start | bytes 184328 | tf_op jit(solution)/shard_map/ppermute | solution.py:436
  85.5 6.8 %collective-permute-start.30 = (f32[120,128]{1,0:T(8,128)}, f32[120,128]{1,0:T(8,128)S(1)}, u32[]{:S(2)}, u32[]{:S(2)}) collective-permute-start(f32[120,128]{1,0:T(8,128)} %get-tuple-element.84), channel_id=1, source_target_pairs={{0,29},{1,30},{2,31},{3,0},{4,1},{5,2},{6,3},{7,4},{8,5},{9,6},{10... | collective-permute-start | bytes 184328 | tf_op jit(solution)/shard_map/ppermute | solution.py:436
  88.4 5.8 %collective-permute-start.32 = (f32[120,128]{1,0:T(8,128)}, f32[120,128]{1,0:T(8,128)S(1)}, u32[]{:S(2)}, u32[]{:S(2)}) collective-permute-start(f32[120,128]{1,0:T(8,128)} %get-tuple-element.86), channel_id=1, source_target_pairs={{0,31},{1,0},{2,1},{3,2},{4,3},{5,4},{6,5},{7,6},{8,7},{9,8},{10,9... | collective-permute-start | bytes 184328 | tf_op jit(solution)/shard_map/ppermute | solution.py:436
  (5 other events, 8.2 us)

commit v10 on v9

--- a/solution.py
+++ b/solution.py
@@ -11,7 +11,6 @@
 LANES = 128
 SUB = 8
 SLOT = 32
-LINES = 16
 MIB = 1024 * 1024
 LENGTH_BASE = 1000.0
 BIG = 60 * MIB
@@ -248,49 +247,70 @@
     lax.fori_loop(0, solved.shape[0] // (LANES * together), some_rows, 0)
 
 
-def device_index():
-    return lax.axis_index("lon") * lax.axis_size("lat") + lax.axis_index("lat")
-
-
-def pick_rows(table, index, count, cap, values, packed, sent, wait_list):
+def pick_rows(table, index, count, cap, values, packed, turned, sent, copied, wait_list):
+    blocks, height, _ = sent.shape
     parts = cap // LANES
-    turns = len(sent)
-    stream = streams_of(1, values, parts)[1] & (parts - 1)
-    own = device_index()
-
-    def one_turn(turn, carry):
-        owner = lax.rem(own + turn, turns)
-        rows = lax.div(count[owner] + (parts - 1), parts)
-        wait_list(owner)
-        places = [owner * cap + part * rows for part in range(parts)]
-
-        def some_lines(step, inner):
-            start = pl.multiple_of(step * LINES, LINES)
+    lists = 4 // parts
+    stream = streams_of(1, values, parts)[1]
+    together = 2 if blocks % 2 == 0 else 1
+
+    def copy_out(block):
+        return pltpu.make_async_copy(turned.at[block], sent.at[block], copied.at[block])
+
+    def pick_block(block, item):
+        owners = [block * lists + member for member in range(lists)]
+        rows = [lax.div(count[owner] + (parts - 1), parts) for owner in owners]
+        for owner in owners:
+            wait_list(owner)
+        longest = functools.reduce(jnp.maximum, rows)
+        places = [owners[g // parts] * cap + (g % parts) * rows[g // parts] for g in range(4)]
+
+        def pick_lines(start, lines):
             bases = [place + start for place in places]
-            lines = []
-            for line in range(LINES):
+            merged = []
+            for line in range(lines):
                 picked = [table[index[base + line]] for base in bases]
-                merged = picked[0]
-                for part in range(1, parts):
-                    merged = jnp.where(stream == part, picked[part], merged)
-                lines.append(merged)
-            first = pl.multiple_of(turn * LANES + start, LINES)
-            for line in range(LINES):
-                packed[pl.ds(first + line, 1), :] = lines[line]
-            return inner
-
-        lax.fori_loop(0, lax.div(rows + (LINES - 1), LINES), some_lines, 0)
-        return carry
-
-    lax.fori_loop(0, turns, one_turn, 0)
-    for first in range(0, turns, 2):
-        turned = [packed[turn * LANES : (turn + 1) * LANES, :].T for turn in range(first, min(first + 2, turns))]
-        for turn, block in enumerate(turned, first):
-            sent[turn][...] = block[: values * parts, :]
-            total = count[lax.rem(own + turn, turns)]
-            note = jnp.full((1, LANES), LENGTH_BASE + total.astype(jnp.float32))
-            mask = (lane_ids(1) == LANES - 1) & (total < cap)
-            pltpu.store(sent[turn].at[pl.ds(parts - 1, 1), :], note, mask=mask)
+                low = jnp.where(stream == 0, picked[0], picked[1])
+                high = jnp.where(stream == 2, picked[2], picked[3])
+                merged.append(jnp.where(stream < 2, low, high))
+            first = pl.multiple_of(item * LANES + start, SUB)
+            for line in range(lines):
+                packed[pl.ds(first + line, 1), :] = merged[line]
+
+        def steps(begin, trips, lines):
+            def one_step(step, carry):
+                pick_lines(pl.multiple_of(begin + step * lines, SUB), lines)
+                return carry
+
+            lax.fori_loop(0, trips, one_step, 0)
+            return begin + trips * lines
+
+        eights = lax.div(longest + (SUB - 1), SUB)
+        done = steps(0, lax.div(eights, 4), 4 * SUB)
+        done = steps(done, lax.div(lax.rem(eights, 4), 2), 2 * SUB)
+        steps(done, lax.rem(eights, 2), SUB)
+
+    def some_blocks(step, carry):
+        for item in range(together):
+            pick_block(step * together + item, item)
+        results = [packed[item * LANES : (item + 1) * LANES, :].T for item in range(together)]
+        for item in range(together):
+            block = step * together + item
+            turned[block] = results[item][:height, :]
+            for member in range(lists):
+                total = count[block * lists + member]
+                row = turned.at[block, pl.ds((member * values + 1) * parts - 1, 1), :]
+                note = jnp.full((1, LANES), LENGTH_BASE + total.astype(jnp.float32))
+                pltpu.store(row, note, mask=(lane_ids(1) == LANES - 1) & (total < cap))
+            copy_out(block).start()
+        return carry
+
+    def finish(block, carry):
+        copy_out(block).wait()
+        return carry
+
+    lax.fori_loop(0, blocks // together, some_blocks, 0)
+    lax.fori_loop(0, blocks, finish, 0)
 
 
 def list_copies(lists_in, index, count, listed):
@@ -312,14 +332,10 @@
 
 
 def solve_kernel(
-    parts, west_in, east_in, inside_in, left_cell_in, west_edge_in, east_edge_in, lower_in, upper_in, lists_in, *refs
+    parts, west_in, east_in, inside_in, left_cell_in, west_edge_in, east_edge_in, lower_in, upper_in, lists_in,
+    sent, west, east, inside, left_cell, west_edge, east_edge, lower, upper, ready,
+    halo, solved, table, packed, turned, index, count, listed, copied,
 ):
-    turns = lists_in.shape[0] - SUB
-    sent = refs[:turns]
-    (
-        west, east, inside, left_cell, west_edge, east_edge, lower, upper, ready,
-        halo, solved, table, packed, index, count, listed,
-    ) = refs[turns:]
     values, lats, _ = inside.shape
     sources = (west_in, east_in, left_cell_in, west_edge_in, east_edge_in, lower_in, upper_in, inside_in)
     copies = fetch(sources, (west, east, left_cell, west_edge, east_edge, lower, upper, inside), ready)
@@ -334,54 +350,62 @@
     add_edges_and_solve(inside, left_cell, west_edge, east_edge, lower, upper, halo, solved)
     build_table(solved, table.reshape(table.shape[0], LANES), values, parts)
     wait_lengths()
-    pick_rows(table, index, count, lists_in.shape[1], values, packed, sent, wait_list)
+    pick_rows(table, index, count, lists_in.shape[1], values, packed, turned, sent, copied, wait_list)
 
 
 def make_sent(west, east, fields, lists_in):
     values, lats, lons = fields[0].shape
     lists, cap = lists_in.shape[0] - SUB, lists_in.shape[1]
     parts = cap // LANES
+    blocks = lists * parts // 4
     inputs = (west.reshape(values, SUB, LANES), east.reshape(values, SUB, LANES), *fields)
-    return pl.pallas_call(
+    sent = pl.pallas_call(
         functools.partial(solve_kernel, parts),
-        out_shape=(jax.ShapeDtypeStruct((parts * values, LANES), jnp.float32),) * lists,
+        out_shape=jax.ShapeDtypeStruct((blocks, 4 * values, LANES), jnp.float32),
         in_specs=[pl.BlockSpec(memory_space=pl.ANY)] * (len(inputs) + 1),
-        out_specs=(pl.BlockSpec(memory_space=pltpu.VMEM),) * lists,
+        out_specs=pl.BlockSpec(memory_space=pl.ANY),
         scratch_shapes=[pltpu.VMEM(array.shape, array.dtype) for array in inputs]
         + [
             pltpu.SemaphoreType.DMA((len(inputs),)),
             pltpu.VMEM((values, 2, SUB, LANES), jnp.float32),
             pltpu.VMEM((lats * SLOT, LANES), jnp.float32),
             pltpu.VMEM((lats * lons, 1, LANES), jnp.float32),
-            pltpu.VMEM((lists * LANES, LANES), jnp.float32),
+            pltpu.VMEM((2 * LANES, LANES), jnp.float32),
+            pltpu.VMEM((blocks, 4 * values, LANES), jnp.float32),
             pltpu.SMEM((lists * cap,), jnp.int32),
             pltpu.SMEM((cap,), jnp.int32),
             pltpu.SemaphoreType.DMA((lists + 1,)),
+            pltpu.SemaphoreType.DMA((blocks,)),
         ],
         compiler_params=pltpu.CompilerParams(vmem_limit_bytes=BIG),
         cost_estimate=pl.CostEstimate(flops=0, bytes_accessed=40 * MIB, transcendentals=0),
         name="solve_pick",
     )(*inputs, lists_in)
-
-
-def place_kernel(parts, *refs):
-    *arrived, owned, row = refs
+    rows = values * parts
+    tile = max(size for size in (1, 2, 4, 8) if rows % size == 0)
+    return sent.reshape(lists, rows // tile, tile, LANES)
+
+
+def place_kernel(own, arrived, owned, row):
+    sources, height, _ = arrived.shape
     levels, ntr, columns = owned.shape
     values = levels * ntr
+    parts = height // values
     lane = lax.broadcasted_iota(jnp.int32, (values, LANES), 1)
+    order = [lax.rem(own[0] - turn + sources, sources) for turn in range(sources)]
     totals = []
-    for held in arrived:
-        note = held[parts - 1 : parts, :]
+    for source in order:
+        note = arrived[source, parts - 1 : parts, :]
         total = jnp.where(note > 0.5 * LENGTH_BASE, note - LENGTH_BASE, 1.0 * parts * LANES)
         totals.append(total.astype(jnp.int32)[0, LANES - 1])
     start = 0
-    for held, total in zip(arrived, totals):
+    for source, total in zip(order, totals):
         rows = lax.div(total + (parts - 1), parts)
         pieces = []
         for part in range(parts):
             place = start + jnp.minimum(part * rows, total)
             shift = lax.rem(place, LANES)
-            piece = held[pl.ds(part, values, stride=parts), :]
+            piece = arrived[source, pl.ds(part, values, stride=parts), :]
             pieces.append((place - shift, shift, pltpu.roll(piece, shift, 1)))
         for tile, shift, rolled in pieces:
             here = pl.ds(pl.multiple_of(tile, LANES), LANES)
@@ -393,28 +417,19 @@
         owned[level] = row[level * ntr : (level + 1) * ntr, :columns]
 
 
-def place_owned(arrived, levels, ntr, columns):
+def place_owned(arrived, own, levels, ntr, columns):
     vmem = pl.BlockSpec(memory_space=pltpu.VMEM)
+    smem = pl.BlockSpec(memory_space=pltpu.SMEM)
     values = levels * ntr
     return pl.pallas_call(
-        functools.partial(place_kernel, arrived[0].shape[0] // values),
+        place_kernel,
         out_shape=jax.ShapeDtypeStruct((levels, ntr, columns), jnp.float32),
-        in_specs=[vmem] * len(arrived),
+        in_specs=[smem, vmem],
         out_specs=vmem,
         scratch_shapes=[pltpu.VMEM((values, columns + 2 * LANES), jnp.float32)],
         compiler_params=pltpu.CompilerParams(vmem_limit_bytes=16 * MIB),
         name="place_owned",
-    )(*arrived)
-
-
-def exchange_order(devices):
-    half = devices // 2
-    order = [half]
-    for step in range(1, half):
-        distance = half - step if step % 2 else step
-        order += [distance, devices - distance]
-    seen = list(dict.fromkeys(order))
-    return seen + [d for d in range(1, devices) if d not in seen]
+    )(own, arrived.reshape(arrived.shape[0], -1, LANES))
 
 
 def ring(axis, distance):
@@ -430,11 +445,9 @@
     from_east = lax.ppermute(west_cells, "lon", ring("lon", -1))
     *fields, lists = advect_inside(tracers, offsets, weights, diffusion, send_index, send_count)
     sent = make_sent(from_west, from_east, fields, lists)
-    axes = ("lon", "lat")
-    arrived = {0: sent[0]}
-    for turn in exchange_order(len(sent)):
-        arrived[turn] = lax.ppermute(sent[turn], axes, ring(axes, turn))
-    owned = place_owned([arrived[turn] for turn in range(len(sent))], levels, ntr, columns)
+    arrived = lax.all_to_all(sent, ("lon", "lat"), split_axis=0, concat_axis=0, tiled=True)
+    own = lax.axis_index(("lon", "lat")).astype(jnp.int32).reshape(1)
+    owned = place_owned(arrived, own, levels, ntr, columns)
     return jnp.transpose(owned, (1, 0, 2))
 
 

time: 97.7 us -> 84 us (0.86)
  starting transfers between devices: 51.9 us -> 9.13 us
  waiting for transfers between devices: 16 us -> 45.9 us
    ppermute x31 -> x0, starting transfers between devices: 46.3 us -> none  [body(): arrived[turn] = lax.ppermute(sent[turn], axes, ring(axes, turn))]
    all_to_all x0 -> x1, waiting for transfers between devices: none -> 45.9 us  [body(): lax.all_to_all(sent, ('lon', 'lat'), split_axis=0, concat_axis=0, tiled=T...]
    ppermute x31 -> x0, waiting for transfers between devices: 16 us -> none  [body(): arrived[turn] = lax.ppermute(sent[turn], axes, ring(axes, turn))]
    all_to_all x0 -> x1, starting transfers between devices: none -> 3.59 us  [body(): lax.all_to_all(sent, ('lon', 'lat'), split_axis=0, concat_axis=0, tiled=T...]
    unnamed x8 -> x6, local copies, waits for them, and re-layouts: 2.7 us -> 1.86 us
  transfers between devices with their start and end apart: 33 -> 3, of which waited for: 12 -> 1; matrix products, arithmetic and copies ran while one was open for 0% -> 0% of each run, Pallas kernels for 5% -> 6%
where the time goes in v10:
time: 84 us; the launch traced here: 83.7 us
  waiting for transfers between devices  45.9 us (55%)
  Pallas kernels  26.7 us (32%)
  starting transfers between devices  9.13 us (11%)
  local copies, waits for them, and re-layouts  1.86 us (2%)
    all_to_all x1, waiting for transfers between devices, body(): lax.all_to_all(sent, ('lon', 'lat'), split_axis=0, concat_axis=0, tiled=T...  45.9 us
    pallas_call x1, Pallas kernels, make_sent(): pl.pallas_call(functools.partial(solve_kernel, parts), out_shape=jax.Shap...  18.2 us
    pallas_call x1, Pallas kernels, advect_inside(): pl.pallas_call(inside_kernel, out_shape=outputs, in_specs=[pl.BlockSpec(m...  5.12 us
    ppermute x1, starting transfers between devices, body(): from_east = lax.ppermute(west_cells, 'lon', ring('lon', -1))  5.03 us
    all_to_all x1, starting transfers between devices, body(): lax.all_to_all(sent, ('lon', 'lat'), split_axis=0, concat_axis=0, tiled=T...  3.59 us
    pallas_call x1, Pallas kernels, place_owned(): pl.pallas_call(place_kernel, out_shape=jax.ShapeDtypeStruct((levels, ntr,...  2.28 us
    unnamed x6, local copies, waits for them, and re-layouts  1.86 us
  transfers between devices with their start and end apart: 3, of which 1 were waited for; matrix products, arithmetic and copies ran while one was open for 0% of the time, Pallas kernels for 6%

profile of v10, /device:TPU:0, one launch (start us, length us, event | category | flops | bytes accessed | tf_op | source)
XLA Modules:
  0.0 83.7 jit_solution(15233924811423072891)
XLA Ops:
  0.0 0.0 copy-start
  0.0 1.2 %copy-done = f32[3,10,64,128]{3,2,1,0:T(8,128)S(1)} copy-done((f32[3,10,64,128]{3,2,1,0:T(8,128)S(1)}, f32[3,10,64,128]{3,2,1,0:T(8,128)}, u32[]{:S(2)}) %copy-start) | copy-done | bytes 983064
  1.2 1.1 %pack_halo.1 = (f32[10,3,8,128]{3,2,1,0:T(8,128)S(1)}, f32[10,3,8,128]{3,2,1,0:T(8,128)S(1)}) custom-call(f32[3,10,64,128]{3,2,1,0:T(8,128)S(1)} %copy-done), custom_call_target="tpu_custom_call" | custom-call | tf_op jit(solution)/shard_map/pack_halo/pallas_call | solution.py:55
  2.3 0.5 collective-permute-start
  2.8 5.0 %collective-permute-start.1 = (f32[10,3,8,128]{3,2,1,0:T(8,128)S(1)}, f32[10,3,8,128]{3,2,1,0:T(8,128)S(1)}, u32[]{:S(2)}, u32[]{:S(2)}) collective-permute-start(f32[10,3,8,128]{3,2,1,0:T(8,128)S(1)} %get-tuple-element.15), channel_id=1, source_target_pairs={{0,30},{2,0},{4,2},{6,4},{8,6},{10,8},{12,10},{14,12},{16,14},{18,... | collective-permute-start | bytes 368648 | tf_op jit(solution)/shard_map/ppermute | solution.py:445
  7.9 5.1 %advect_inside.1 = (f32[30,64,128]{2,1,0:T(8,128)}, s32[10,64,128]{2,1,0:T(8,128)}, f32[10,64,128]{2,1,0:T(8,128)}, f32[10,64,128]{2,1,0:T(8,128)}, f32[9,64,128...) custom-call(f32[3,10,64,128]{3,2,1,0:T(8,128)} %tracers_in.1, s32[10,64,128]{2,1,0:T(8,128)} %offsets_in.1, ...), custom_call_target="tpu_custom_call" | custom-call | bytes 20971520 | tf_op jit(solution)/shard_map/advect_inside/pallas_call | solution.py:172
  13.0 0.0 collective-permute-done
  13.0 0.0 copy-start.1
  13.0 0.0 collective-permute-done.1
  13.0 0.0 copy-start.2
  13.0 0.6 copy-done.1
  13.6 0.0 copy-done.2
  13.7 18.2 %solve_pick.1 = f32[32,120,128]{2,1,0:T(8,128)} custom-call(f32[30,8,128]{2,1,0:T(8,128)} %bitcast.8, f32[30,8,128]{2,1,0:T(8,128)} %bitcast.9, f32[30,64,128]{2,1,0:T(8,128)} %get-tuple-element.16.inside_in, s32[10,64,128]{2,1,0:T(8,128)} %get-tuple-element.17.left_cell_in, f32[10,64,128]{2,1,0:T(8,128)} %get-tuple-element.18.west_edge_in, ...), custom_call_target="tpu_custom_call" | custom-call | bytes 41943040 | tf_op jit(solution)/shard_map/solve_pick/pallas_call | solution.py:362
  31.9 3.6 %all-to-all-start = ((f32[32,15,8,128]{3,2,1,0:T(8,128)}), f32[32,15,8,128]{3,2,1,0:T(8,128)S(1)}, u32[]{:S(2)}, u32[]{:S(2)}) async-start(f32[32,15,8,128]{3,2,1,0:T(8,128)} %bitcast.7), calls=%async_computation | async-start | bytes 3932160 | tf_op jit(solution)/shard_map/all_to_all | solution.py:448
  35.5 45.9 %all-to-all-done = f32[32,15,8,128]{3,2,1,0:T(8,128)S(1)} async-done(((f32[32,15,8,128]{3,2,1,0:T(8,128)}), f32[32,15,8,128]{3,2,1,0:T(8,128)S(1)}, u32[]{:S(2)}, u32[]{:S(2)}) %all-to-all-start) | async-done | bytes 1966112 | tf_op jit(solution)/shard_map/all_to_all | solution.py:448
  81.4 2.3 %place_owned.1 = f32[10,3,8192]{2,1,0:T(4,128)} custom-call(s32[1]{0:T(128)} %bitcast.own, f32[32,120,128]{2,1,0:T(8,128)S(1)} %bitcast.6), custom_call_target="tpu_custom_call" | custom-call | tf_op jit(solution)/shard_map/place_owned/pallas_call | solution.py:424
Async XLA Ops:
  0.0 1.2 %copy-start = (f32[3,10,64,128]{3,2,1,0:T(8,128)S(1)}, f32[3,10,64,128]{3,2,1,0:T(8,128)}, u32[]{:S(2)}) copy-start(f32[3,10,64,128]{3,2,1,0:T(8,128)} %tracers_in.1) | copy-start | bytes 2949124
  2.3 10.7 %collective-permute-start = (f32[10,3,8,128]{3,2,1,0:T(8,128)S(1)}, f32[10,3,8,128]{3,2,1,0:T(8,128)S(1)}, u32[]{:S(2)}, u32[]{:S(2)}) collective-permute-start(f32[10,3,8,128]{3,2,1,0:T(8,128)S(1)} %get-tuple-element.14), channel_id=1, source_target_pairs={{0,2},{2,4},{4,6},{6,8},{8,10},{10,12},{12,14},{14,16},{16,18},{18... | collective-permute-start | bytes 368648 | tf_op jit(solution)/shard_map/ppermute | solution.py:444
  2.8 10.2 %collective-permute-start.1 = (f32[10,3,8,128]{3,2,1,0:T(8,128)S(1)}, f32[10,3,8,128]{3,2,1,0:T(8,128)S(1)}, u32[]{:S(2)}, u32[]{:S(2)}) collective-permute-start(f32[10,3,8,128]{3,2,1,0:T(8,128)S(1)} %get-tuple-element.15), channel_id=1, source_target_pairs={{0,30},{2,0},{4,2},{6,4},{8,6},{10,8},{12,10},{14,12},{16,14},{18,... | collective-permute-start | bytes 368648 | tf_op jit(solution)/shard_map/ppermute | solution.py:445
  13.0 0.6 copy-start.1
  13.0 0.7 copy-start.2
  31.9 49.5 %all-to-all-start = ((f32[32,15,8,128]{3,2,1,0:T(8,128)}), f32[32,15,8,128]{3,2,1,0:T(8,128)S(1)}, u32[]{:S(2)}, u32[]{:S(2)}) async-start(f32[32,15,8,128]{3,2,1,0:T(8,128)} %bitcast.7), calls=%async_computation | async-start | bytes 3932160 | tf_op jit(solution)/shard_map/all_to_all | solution.py:448

commit v11 on v10

--- a/solution.py
+++ b/solution.py
@@ -266,10 +266,10 @@
         places = [owners[g // parts] * cap + (g % parts) * rows[g // parts] for g in range(4)]
 
         def pick_lines(start, lines):
-            bases = [place + start for place in places]
+            views = [index.at[pl.ds(place + start, lines)] for place in places]
             merged = []
             for line in range(lines):
-                picked = [table[index[base + line]] for base in bases]
+                picked = [table[view[line]] for view in views]
                 low = jnp.where(stream == 0, picked[0], picked[1])
                 high = jnp.where(stream == 2, picked[2], picked[3])
                 merged.append(jnp.where(stream < 2, low, high))

time: 84 us -> 82.5 us (0.982)
  Pallas kernels: 26.7 us -> 25.2 us
    pallas_call x1, Pallas kernels: 18.2 us -> 16.7 us  [make_sent(): pl.pallas_call(functools.partial(solve_kernel, parts), out_shape=jax.Shap...]
where the time goes in v11:
time: 82.5 us; the launch traced here: 82.2 us
  waiting for transfers between devices  45.9 us (56%)
  Pallas kernels  25.2 us (31%)
  starting transfers between devices  9.13 us (11%)
  local copies, waits for them, and re-layouts  1.86 us (2%)
    all_to_all x1, waiting for transfers between devices, body(): lax.all_to_all(sent, ('lon', 'lat'), split_axis=0, concat_axis=0, tiled=T...  45.9 us
    pallas_call x1, Pallas kernels, make_sent(): pl.pallas_call(functools.partial(solve_kernel, parts), out_shape=jax.Shap...  16.7 us
    pallas_call x1, Pallas kernels, advect_inside(): pl.pallas_call(inside_kernel, out_shape=outputs, in_specs=[pl.BlockSpec(m...  5.12 us
    ppermute x1, starting transfers between devices, body(): from_east = lax.ppermute(west_cells, 'lon', ring('lon', -1))  5.03 us
    all_to_all x1, starting transfers between devices, body(): lax.all_to_all(sent, ('lon', 'lat'), split_axis=0, concat_axis=0, tiled=T...  3.6 us
    pallas_call x1, Pallas kernels, place_owned(): pl.pallas_call(place_kernel, out_shape=jax.ShapeDtypeStruct((levels, ntr,...  2.28 us
    unnamed x6, local copies, waits for them, and re-layouts  1.86 us
  transfers between devices with their start and end apart: 3, of which 1 were waited for; matrix products, arithmetic and copies ran while one was open for 0% of the time, Pallas kernels for 6%

profile of v11, /device:TPU:0, one launch (start us, length us, event | category | flops | bytes accessed | tf_op | source)
XLA Modules:
  0.0 82.2 jit_solution(718885482865615042)
XLA Ops:
  0.0 0.0 copy-start
  0.0 1.2 %copy-done = f32[3,10,64,128]{3,2,1,0:T(8,128)S(1)} copy-done((f32[3,10,64,128]{3,2,1,0:T(8,128)S(1)}, f32[3,10,64,128]{3,2,1,0:T(8,128)}, u32[]{:S(2)}) %copy-start) | copy-done | bytes 983064
  1.2 1.1 %pack_halo.1 = (f32[10,3,8,128]{3,2,1,0:T(8,128)S(1)}, f32[10,3,8,128]{3,2,1,0:T(8,128)S(1)}) custom-call(f32[3,10,64,128]{3,2,1,0:T(8,128)S(1)} %copy-done), custom_call_target="tpu_custom_call" | custom-call | tf_op jit(solution)/shard_map/pack_halo/pallas_call | solution.py:55
  2.3 0.5 collective-permute-start
  2.8 5.0 %collective-permute-start.1 = (f32[10,3,8,128]{3,2,1,0:T(8,128)S(1)}, f32[10,3,8,128]{3,2,1,0:T(8,128)S(1)}, u32[]{:S(2)}, u32[]{:S(2)}) collective-permute-start(f32[10,3,8,128]{3,2,1,0:T(8,128)S(1)} %get-tuple-element.15), channel_id=1, source_target_pairs={{0,30},{2,0},{4,2},{6,4},{8,6},{10,8},{12,10},{14,12},{16,14},{18,... | collective-permute-start | bytes 368648 | tf_op jit(solution)/shard_map/ppermute | solution.py:445
  7.9 5.1 %advect_inside.1 = (f32[30,64,128]{2,1,0:T(8,128)}, s32[10,64,128]{2,1,0:T(8,128)}, f32[10,64,128]{2,1,0:T(8,128)}, f32[10,64,128]{2,1,0:T(8,128)}, f32[9,64,128...) custom-call(f32[3,10,64,128]{3,2,1,0:T(8,128)} %tracers_in.1, s32[10,64,128]{2,1,0:T(8,128)} %offsets_in.1, ...), custom_call_target="tpu_custom_call" | custom-call | bytes 20971520 | tf_op jit(solution)/shard_map/advect_inside/pallas_call | solution.py:172
  13.0 0.0 collective-permute-done
  13.0 0.0 copy-start.1
  13.0 0.0 collective-permute-done.1
  13.0 0.0 copy-start.2
  13.0 0.6 copy-done.1
  13.6 0.0 copy-done.2
  13.7 16.7 %solve_pick.1 = f32[32,120,128]{2,1,0:T(8,128)} custom-call(f32[30,8,128]{2,1,0:T(8,128)} %bitcast.8, f32[30,8,128]{2,1,0:T(8,128)} %bitcast.9, f32[30,64,128]{2,1,0:T(8,128)} %get-tuple-element.16.inside_in, s32[10,64,128]{2,1,0:T(8,128)} %get-tuple-element.17.left_cell_in, f32[10,64,128]{2,1,0:T(8,128)} %get-tuple-element.18.west_edge_in, ...), custom_call_target="tpu_custom_call" | custom-call | bytes 41943040 | tf_op jit(solution)/shard_map/solve_pick/pallas_call | solution.py:362
  30.4 3.6 %all-to-all-start = ((f32[32,15,8,128]{3,2,1,0:T(8,128)}), f32[32,15,8,128]{3,2,1,0:T(8,128)S(1)}, u32[]{:S(2)}, u32[]{:S(2)}) async-start(f32[32,15,8,128]{3,2,1,0:T(8,128)} %bitcast.7), calls=%async_computation | async-start | bytes 3932160 | tf_op jit(solution)/shard_map/all_to_all | solution.py:448
  34.0 45.9 %all-to-all-done = f32[32,15,8,128]{3,2,1,0:T(8,128)S(1)} async-done(((f32[32,15,8,128]{3,2,1,0:T(8,128)}), f32[32,15,8,128]{3,2,1,0:T(8,128)S(1)}, u32[]{:S(2)}, u32[]{:S(2)}) %all-to-all-start) | async-done | bytes 1966112 | tf_op jit(solution)/shard_map/all_to_all | solution.py:448
  79.9 2.3 %place_owned.1 = f32[10,3,8192]{2,1,0:T(4,128)} custom-call(s32[1]{0:T(128)} %bitcast.own, f32[32,120,128]{2,1,0:T(8,128)S(1)} %bitcast.6), custom_call_target="tpu_custom_call" | custom-call | tf_op jit(solution)/shard_map/place_owned/pallas_call | solution.py:424
Async XLA Ops:
  0.0 1.2 %copy-start = (f32[3,10,64,128]{3,2,1,0:T(8,128)S(1)}, f32[3,10,64,128]{3,2,1,0:T(8,128)}, u32[]{:S(2)}) copy-start(f32[3,10,64,128]{3,2,1,0:T(8,128)} %tracers_in.1) | copy-start | bytes 2949124
  2.3 10.7 %collective-permute-start = (f32[10,3,8,128]{3,2,1,0:T(8,128)S(1)}, f32[10,3,8,128]{3,2,1,0:T(8,128)S(1)}, u32[]{:S(2)}, u32[]{:S(2)}) collective-permute-start(f32[10,3,8,128]{3,2,1,0:T(8,128)S(1)} %get-tuple-element.14), channel_id=1, source_target_pairs={{0,2},{2,4},{4,6},{6,8},{8,10},{10,12},{12,14},{14,16},{16,18},{18... | collective-permute-start | bytes 368648 | tf_op jit(solution)/shard_map/ppermute | solution.py:444
  2.8 10.2 %collective-permute-start.1 = (f32[10,3,8,128]{3,2,1,0:T(8,128)S(1)}, f32[10,3,8,128]{3,2,1,0:T(8,128)S(1)}, u32[]{:S(2)}, u32[]{:S(2)}) collective-permute-start(f32[10,3,8,128]{3,2,1,0:T(8,128)S(1)} %get-tuple-element.15), channel_id=1, source_target_pairs={{0,30},{2,0},{4,2},{6,4},{8,6},{10,8},{12,10},{14,12},{16,14},{18,... | collective-permute-start | bytes 368648 | tf_op jit(solution)/shard_map/ppermute | solution.py:445
  13.0 0.6 copy-start.1
  13.0 0.7 copy-start.2
  30.4 49.5 %all-to-all-start = ((f32[32,15,8,128]{3,2,1,0:T(8,128)}), f32[32,15,8,128]{3,2,1,0:T(8,128)S(1)}, u32[]{:S(2)}, u32[]{:S(2)}) async-start(f32[32,15,8,128]{3,2,1,0:T(8,128)} %bitcast.7), calls=%async_computation | async-start | bytes 3932160 | tf_op jit(solution)/shard_map/all_to_all | solution.py:448

commit v12 on v11

--- a/solution.py
+++ b/solution.py
@@ -212,8 +212,9 @@
                 if level < levels - 1:
                     x = reduced[tracer][level] + upper[level, rows, :] * x
                 results.append((level * ntr + tracer, x))
+        target = solved.at[pl.ds(pl.multiple_of(part * (SUB * SLOT), SUB * SLOT), SUB * SLOT), :]
         for value, x in results:
-            solved[pl.ds(part * SUB * SLOT + value, SUB, stride=SLOT), :] = x
+            target[pl.ds(value, SUB, stride=SLOT), :] = x
         return carry
 
     lax.fori_loop(0, lats // SUB, one_part, 0)
@@ -273,9 +274,9 @@
                 low = jnp.where(stream == 0, picked[0], picked[1])
                 high = jnp.where(stream == 2, picked[2], picked[3])
                 merged.append(jnp.where(stream < 2, low, high))
-            first = pl.multiple_of(item * LANES + start, SUB)
+            target = packed.at[pl.ds(pl.multiple_of(item * LANES + start, SUB), lines), :]
             for line in range(lines):
-                packed[pl.ds(first + line, 1), :] = merged[line]
+                target[line : line + 1, :] = merged[line]
 
         def steps(begin, trips, lines):
             def one_step(step, carry):

time: 82.5 us -> 82.4 us (level)
  no operation moved by 1% of the time
where the time goes in v12:
time: 82.4 us; the launch traced here: 82.1 us
  waiting for transfers between devices  45.9 us (56%)
  Pallas kernels  25.2 us (31%)
  starting transfers between devices  9.14 us (11%)
  local copies, waits for them, and re-layouts  1.86 us (2%)
    all_to_all x1, waiting for transfers between devices, body(): lax.all_to_all(sent, ('lon', 'lat'), split_axis=0, concat_axis=0, tiled=T...  45.9 us
    pallas_call x1, Pallas kernels, make_sent(): pl.pallas_call(functools.partial(solve_kernel, parts), out_shape=jax.Shap...  16.7 us
    pallas_call x1, Pallas kernels, advect_inside(): pl.pallas_call(inside_kernel, out_shape=outputs, in_specs=[pl.BlockSpec(m...  5.12 us
    ppermute x1, starting transfers between devices, body(): from_east = lax.ppermute(west_cells, 'lon', ring('lon', -1))  5.03 us
    all_to_all x1, starting transfers between devices, body(): lax.all_to_all(sent, ('lon', 'lat'), split_axis=0, concat_axis=0, tiled=T...  3.6 us
    pallas_call x1, Pallas kernels, place_owned(): pl.pallas_call(place_kernel, out_shape=jax.ShapeDtypeStruct((levels, ntr,...  2.28 us
    unnamed x6, local copies, waits for them, and re-layouts  1.86 us
  transfers between devices with their start and end apart: 3, of which 1 were waited for; matrix products, arithmetic and copies ran while one was open for 0% of the time, Pallas kernels for 6%

profile of v12, /device:TPU:0, one launch (start us, length us, event | category | flops | bytes accessed | tf_op | source)
XLA Modules:
  0.0 82.1 jit_solution(718885482865615042)
XLA Ops:
  0.0 0.0 copy-start
  0.0 1.2 %copy-done = f32[3,10,64,128]{3,2,1,0:T(8,128)S(1)} copy-done((f32[3,10,64,128]{3,2,1,0:T(8,128)S(1)}, f32[3,10,64,128]{3,2,1,0:T(8,128)}, u32[]{:S(2)}) %copy-start) | copy-done | bytes 983064
  1.2 1.1 %pack_halo.1 = (f32[10,3,8,128]{3,2,1,0:T(8,128)S(1)}, f32[10,3,8,128]{3,2,1,0:T(8,128)S(1)}) custom-call(f32[3,10,64,128]{3,2,1,0:T(8,128)S(1)} %copy-done), custom_call_target="tpu_custom_call" | custom-call | tf_op jit(solution)/shard_map/pack_halo/pallas_call | solution.py:55
  2.3 0.5 collective-permute-start
  2.8 5.0 %collective-permute-start.1 = (f32[10,3,8,128]{3,2,1,0:T(8,128)S(1)}, f32[10,3,8,128]{3,2,1,0:T(8,128)S(1)}, u32[]{:S(2)}, u32[]{:S(2)}) collective-permute-start(f32[10,3,8,128]{3,2,1,0:T(8,128)S(1)} %get-tuple-element.15), channel_id=1, source_target_pairs={{0,30},{2,0},{4,2},{6,4},{8,6},{10,8},{12,10},{14,12},{16,14},{18,... | collective-permute-start | bytes 368648 | tf_op jit(solution)/shard_map/ppermute | solution.py:446
  7.9 5.1 %advect_inside.1 = (f32[30,64,128]{2,1,0:T(8,128)}, s32[10,64,128]{2,1,0:T(8,128)}, f32[10,64,128]{2,1,0:T(8,128)}, f32[10,64,128]{2,1,0:T(8,128)}, f32[9,64,128...) custom-call(f32[3,10,64,128]{3,2,1,0:T(8,128)} %tracers_in.1, s32[10,64,128]{2,1,0:T(8,128)} %offsets_in.1, ...), custom_call_target="tpu_custom_call" | custom-call | bytes 20971520 | tf_op jit(solution)/shard_map/advect_inside/pallas_call | solution.py:172
  13.0 0.0 collective-permute-done
  13.0 0.0 copy-start.1
  13.0 0.0 collective-permute-done.1
  13.0 0.0 copy-start.2
  13.0 0.6 copy-done.1
  13.6 0.0 copy-done.2
  13.7 16.7 %solve_pick.1 = f32[32,120,128]{2,1,0:T(8,128)} custom-call(f32[30,8,128]{2,1,0:T(8,128)} %bitcast.8, f32[30,8,128]{2,1,0:T(8,128)} %bitcast.9, f32[30,64,128]{2,1,0:T(8,128)} %get-tuple-element.16.inside_in, s32[10,64,128]{2,1,0:T(8,128)} %get-tuple-element.17.left_cell_in, f32[10,64,128]{2,1,0:T(8,128)} %get-tuple-element.18.west_edge_in, ...), custom_call_target="tpu_custom_call" | custom-call | bytes 41943040 | tf_op jit(solution)/shard_map/solve_pick/pallas_call | solution.py:363
  30.4 3.6 %all-to-all-start = ((f32[32,15,8,128]{3,2,1,0:T(8,128)}), f32[32,15,8,128]{3,2,1,0:T(8,128)S(1)}, u32[]{:S(2)}, u32[]{:S(2)}) async-start(f32[32,15,8,128]{3,2,1,0:T(8,128)} %bitcast.7), calls=%async_computation | async-start | bytes 3932160 | tf_op jit(solution)/shard_map/all_to_all | solution.py:449
  34.0 45.9 %all-to-all-done = f32[32,15,8,128]{3,2,1,0:T(8,128)S(1)} async-done(((f32[32,15,8,128]{3,2,1,0:T(8,128)}), f32[32,15,8,128]{3,2,1,0:T(8,128)S(1)}, u32[]{:S(2)}, u32[]{:S(2)}) %all-to-all-start) | async-done | bytes 1966112 | tf_op jit(solution)/shard_map/all_to_all | solution.py:449
  79.9 2.3 %place_owned.1 = f32[10,3,8192]{2,1,0:T(4,128)} custom-call(s32[1]{0:T(128)} %bitcast.own, f32[32,120,128]{2,1,0:T(8,128)S(1)} %bitcast.6), custom_call_target="tpu_custom_call" | custom-call | tf_op jit(solution)/shard_map/place_owned/pallas_call | solution.py:425
Async XLA Ops:
  0.0 1.2 %copy-start = (f32[3,10,64,128]{3,2,1,0:T(8,128)S(1)}, f32[3,10,64,128]{3,2,1,0:T(8,128)}, u32[]{:S(2)}) copy-start(f32[3,10,64,128]{3,2,1,0:T(8,128)} %tracers_in.1) | copy-start | bytes 2949124
  2.3 10.7 %collective-permute-start = (f32[10,3,8,128]{3,2,1,0:T(8,128)S(1)}, f32[10,3,8,128]{3,2,1,0:T(8,128)S(1)}, u32[]{:S(2)}, u32[]{:S(2)}) collective-permute-start(f32[10,3,8,128]{3,2,1,0:T(8,128)S(1)} %get-tuple-element.14), channel_id=1, source_target_pairs={{0,2},{2,4},{4,6},{6,8},{8,10},{10,12},{12,14},{14,16},{16,18},{18... | collective-permute-start | bytes 368648 | tf_op jit(solution)/shard_map/ppermute | solution.py:445
  2.8 10.2 %collective-permute-start.1 = (f32[10,3,8,128]{3,2,1,0:T(8,128)S(1)}, f32[10,3,8,128]{3,2,1,0:T(8,128)S(1)}, u32[]{:S(2)}, u32[]{:S(2)}) collective-permute-start(f32[10,3,8,128]{3,2,1,0:T(8,128)S(1)} %get-tuple-element.15), channel_id=1, source_target_pairs={{0,30},{2,0},{4,2},{6,4},{8,6},{10,8},{12,10},{14,12},{16,14},{18,... | collective-permute-start | bytes 368648 | tf_op jit(solution)/shard_map/ppermute | solution.py:446
  13.0 0.6 copy-start.1
  13.0 0.7 copy-start.2
  30.4 49.5 %all-to-all-start = ((f32[32,15,8,128]{3,2,1,0:T(8,128)}), f32[32,15,8,128]{3,2,1,0:T(8,128)S(1)}, u32[]{:S(2)}, u32[]{:S(2)}) async-start(f32[32,15,8,128]{3,2,1,0:T(8,128)} %bitcast.7), calls=%async_computation | async-start | bytes 3932160 | tf_op jit(solution)/shard_map/all_to_all | solution.py:449

commit v13 on v12

--- a/solution.py
+++ b/solution.py
@@ -5,9 +5,10 @@
 from jax import lax
 from jax.experimental import pallas as pl
 from jax.experimental.pallas import tpu as pltpu
-from jax.sharding import PartitionSpec as P
+from jax.sharding import Mesh, PartitionSpec as P
 
 HALO = 16
+LON = ("half", "rest")
 LANES = 128
 SUB = 8
 SLOT = 32
@@ -248,6 +249,10 @@
     lax.fori_loop(0, solved.shape[0] // (LANES * together), some_rows, 0)
 
 
+def owner_at(place, devices):
+    return lax.rem(place, 2) * (devices // 2) + lax.div(place, 2)
+
+
 def pick_rows(table, index, count, cap, values, packed, turned, sent, copied, wait_list):
     blocks, height, _ = sent.shape
     parts = cap // LANES
@@ -259,7 +264,7 @@
         return pltpu.make_async_copy(turned.at[block], sent.at[block], copied.at[block])
 
     def pick_block(block, item):
-        owners = [block * lists + member for member in range(lists)]
+        owners = [owner_at(block * lists + member, index.shape[0] // cap) for member in range(lists)]
         rows = [lax.div(count[owner] + (parts - 1), parts) for owner in owners]
         for owner in owners:
             wait_list(owner)
@@ -299,7 +304,7 @@
             block = step * together + item
             turned[block] = results[item][:height, :]
             for member in range(lists):
-                total = count[block * lists + member]
+                total = count[owner_at(block * lists + member, index.shape[0] // cap)]
                 row = turned.at[block, pl.ds((member * values + 1) * parts - 1, 1), :]
                 note = jnp.full((1, LANES), LENGTH_BASE + total.astype(jnp.float32))
                 pltpu.store(row, note, mask=(lane_ids(1) == LANES - 1) & (total < cap))
@@ -394,6 +399,7 @@
     parts = height // values
     lane = lax.broadcasted_iota(jnp.int32, (values, LANES), 1)
     order = [lax.rem(own[0] - turn + sources, sources) for turn in range(sources)]
+    order = [2 * lax.rem(source, sources // 2) + lax.div(source, sources // 2) for source in order]
     totals = []
     for source in order:
         note = arrived[source, parts - 1 : parts, :]
@@ -442,28 +448,29 @@
     ntr, levels, lats, lons = tracers.shape
     columns = lats * lons
     west_cells, east_cells = pack_halo(tracers)
-    from_west = lax.ppermute(east_cells, "lon", ring("lon", 1))
-    from_east = lax.ppermute(west_cells, "lon", ring("lon", -1))
+    from_west = lax.ppermute(east_cells, LON, ring(LON, 1))
+    from_east = lax.ppermute(west_cells, LON, ring(LON, -1))
     *fields, lists = advect_inside(tracers, offsets, weights, diffusion, send_index, send_count)
     sent = make_sent(from_west, from_east, fields, lists)
-    arrived = lax.all_to_all(sent, ("lon", "lat"), split_axis=0, concat_axis=0, tiled=True)
-    own = lax.axis_index(("lon", "lat")).astype(jnp.int32).reshape(1)
+    arrived = lax.all_to_all(sent, ("rest", "lat", "half"), split_axis=0, concat_axis=0, tiled=True)
+    own = lax.axis_index((*LON, "lat")).astype(jnp.int32).reshape(1)
     owned = place_owned(arrived, own, levels, ntr, columns)
     return jnp.transpose(owned, (1, 0, 2))
 
 
 def solution(mesh):
+    devices = mesh.devices.reshape(2, mesh.shape["lon"] // 2, mesh.shape["lat"])
     return jax.shard_map(
         body,
-        mesh=mesh,
+        mesh=Mesh(devices, (*LON, "lat")),
         in_specs=(
-            P(None, None, "lat", "lon"),
-            P(None, "lat", "lon"),
-            P(None, "lat", "lon"),
-            P(None, "lat", "lon"),
-            P(("lon", "lat"), None, None),
-            P(("lon", "lat"), None),
+            P(None, None, "lat", LON),
+            P(None, "lat", LON),
+            P(None, "lat", LON),
+            P(None, "lat", LON),
+            P((*LON, "lat"), None, None),
+            P((*LON, "lat"), None),
         ),
-        out_specs=P(None, None, ("lon", "lat")),
+        out_specs=P(None, None, (*LON, "lat")),
         check_vma=False,
     )

time: 82.4 us -> 83.7 us (1.016)
  waiting for transfers between devices: 45.9 us -> 46.9 us
    all_to_all x1, waiting for transfers between devices: 45.9 us -> 46.9 us  [body(): lax.all_to_all(sent, ('rest', 'lat', 'half'), split_axis=0, concat_axis=0...]
where the time goes in v13:
time: 83.7 us; the launch traced here: 83.5 us
  waiting for transfers between devices  46.9 us (56%)
  Pallas kernels  25.5 us (30%)
  starting transfers between devices  9.11 us (11%)
  local copies, waits for them, and re-layouts  1.86 us (2%)
    all_to_all x1, waiting for transfers between devices, body(): lax.all_to_all(sent, ('rest', 'lat', 'half'), split_axis=0, concat_axis=0...  46.9 us
    pallas_call x1, Pallas kernels, make_sent(): pl.pallas_call(functools.partial(solve_kernel, parts), out_shape=jax.Shap...  16.9 us
    pallas_call x1, Pallas kernels, advect_inside(): pl.pallas_call(inside_kernel, out_shape=outputs, in_specs=[pl.BlockSpec(m...  5.12 us
    ppermute x1, starting transfers between devices, body(): from_east = lax.ppermute(west_cells, LON, ring(LON, -1))  5.03 us
    all_to_all x1, starting transfers between devices, body(): lax.all_to_all(sent, ('rest', 'lat', 'half'), split_axis=0, concat_axis=0...  3.57 us
    pallas_call x1, Pallas kernels, place_owned(): pl.pallas_call(place_kernel, out_shape=jax.ShapeDtypeStruct((levels, ntr,...  2.34 us
    unnamed x6, local copies, waits for them, and re-layouts  1.86 us
  transfers between devices with their start and end apart: 3, of which 1 were waited for; matrix products, arithmetic and copies ran while one was open for 0% of the time, Pallas kernels for 6%

profile of v13, /device:TPU:0, one launch (start us, length us, event | category | flops | bytes accessed | tf_op | source)
XLA Modules:
  0.0 83.5 jit_solution(14479571083189986792)
XLA Ops:
  0.0 0.0 copy-start
  0.0 1.2 %copy-done = f32[3,10,64,128]{3,2,1,0:T(8,128)S(1)} copy-done((f32[3,10,64,128]{3,2,1,0:T(8,128)S(1)}, f32[3,10,64,128]{3,2,1,0:T(8,128)}, u32[]{:S(2)}) %copy-start) | copy-done | bytes 983064
  1.2 1.1 %pack_halo.1 = (f32[10,3,8,128]{3,2,1,0:T(8,128)S(1)}, f32[10,3,8,128]{3,2,1,0:T(8,128)S(1)}) custom-call(f32[3,10,64,128]{3,2,1,0:T(8,128)S(1)} %copy-done), custom_call_target="tpu_custom_call" | custom-call | tf_op jit(solution)/shard_map/pack_halo/pallas_call | solution.py:56
  2.3 0.5 collective-permute-start
  2.8 5.0 %collective-permute-start.1 = (f32[10,3,8,128]{3,2,1,0:T(8,128)S(1)}, f32[10,3,8,128]{3,2,1,0:T(8,128)S(1)}, u32[]{:S(2)}, u32[]{:S(2)}) collective-permute-start(f32[10,3,8,128]{3,2,1,0:T(8,128)S(1)} %get-tuple-element.15), channel_id=1, source_target_pairs={{0,30},{2,0},{4,2},{6,4},{8,6},{10,8},{12,10},{14,12},{16,14},{18,... | collective-permute-start | bytes 368648 | tf_op jit(solution)/shard_map/ppermute | solution.py:452
  7.9 5.1 %advect_inside.1 = (f32[30,64,128]{2,1,0:T(8,128)}, s32[10,64,128]{2,1,0:T(8,128)}, f32[10,64,128]{2,1,0:T(8,128)}, f32[10,64,128]{2,1,0:T(8,128)}, f32[9,64,128...) custom-call(f32[3,10,64,128]{3,2,1,0:T(8,128)} %tracers_in.1, s32[10,64,128]{2,1,0:T(8,128)} %offsets_in.1, ...), custom_call_target="tpu_custom_call" | custom-call | bytes 20971520 | tf_op jit(solution)/shard_map/advect_inside/pallas_call | solution.py:173
  13.0 0.0 collective-permute-done
  13.0 0.0 copy-start.1
  13.0 0.0 collective-permute-done.1
  13.0 0.0 copy-start.2
  13.0 0.6 copy-done.1
  13.6 0.0 copy-done.2
  13.7 16.9 %solve_pick.1 = f32[32,120,128]{2,1,0:T(8,128)} custom-call(f32[30,8,128]{2,1,0:T(8,128)} %bitcast.8, f32[30,8,128]{2,1,0:T(8,128)} %bitcast.9, f32[30,64,128]{2,1,0:T(8,128)} %get-tuple-element.16.inside_in, s32[10,64,128]{2,1,0:T(8,128)} %get-tuple-element.17.left_cell_in, f32[10,64,128]{2,1,0:T(8,128)} %get-tuple-element.18.west_edge_in, ...), custom_call_target="tpu_custom_call" | custom-call | bytes 41943040 | tf_op jit(solution)/shard_map/solve_pick/pallas_call | solution.py:368
  30.6 3.6 %all-to-all-start = ((f32[32,15,8,128]{3,2,1,0:T(8,128)}), f32[32,15,8,128]{3,2,1,0:T(8,128)S(1)}, u32[]{:S(2)}, u32[]{:S(2)}) async-start(f32[32,15,8,128]{3,2,1,0:T(8,128)} %bitcast.7), calls=%async_computation | async-start | bytes 3932160 | tf_op jit(solution)/shard_map/all_to_all | solution.py:455
  34.2 46.9 %all-to-all-done = f32[32,15,8,128]{3,2,1,0:T(8,128)S(1)} async-done(((f32[32,15,8,128]{3,2,1,0:T(8,128)}), f32[32,15,8,128]{3,2,1,0:T(8,128)S(1)}, u32[]{:S(2)}, u32[]{:S(2)}) %all-to-all-start) | async-done | bytes 1966112 | tf_op jit(solution)/shard_map/all_to_all | solution.py:455
  81.1 2.3 %place_owned.1 = f32[10,3,8192]{2,1,0:T(4,128)} custom-call(s32[1]{0:T(128)} %bitcast.own, f32[32,120,128]{2,1,0:T(8,128)S(1)} %bitcast.6), custom_call_target="tpu_custom_call" | custom-call | tf_op jit(solution)/shard_map/place_owned/pallas_call | solution.py:431
Async XLA Ops:
  0.0 1.2 %copy-start = (f32[3,10,64,128]{3,2,1,0:T(8,128)S(1)}, f32[3,10,64,128]{3,2,1,0:T(8,128)}, u32[]{:S(2)}) copy-start(f32[3,10,64,128]{3,2,1,0:T(8,128)} %tracers_in.1) | copy-start | bytes 2949124
  2.3 10.7 %collective-permute-start = (f32[10,3,8,128]{3,2,1,0:T(8,128)S(1)}, f32[10,3,8,128]{3,2,1,0:T(8,128)S(1)}, u32[]{:S(2)}, u32[]{:S(2)}) collective-permute-start(f32[10,3,8,128]{3,2,1,0:T(8,128)S(1)} %get-tuple-element.14), channel_id=1, source_target_pairs={{0,2},{2,4},{4,6},{6,8},{8,10},{10,12},{12,14},{14,16},{16,18},{18... | collective-permute-start | bytes 368648 | tf_op jit(solution)/shard_map/ppermute | solution.py:451
  2.8 10.2 %collective-permute-start.1 = (f32[10,3,8,128]{3,2,1,0:T(8,128)S(1)}, f32[10,3,8,128]{3,2,1,0:T(8,128)S(1)}, u32[]{:S(2)}, u32[]{:S(2)}) collective-permute-start(f32[10,3,8,128]{3,2,1,0:T(8,128)S(1)} %get-tuple-element.15), channel_id=1, source_target_pairs={{0,30},{2,0},{4,2},{6,4},{8,6},{10,8},{12,10},{14,12},{16,14},{18,... | collective-permute-start | bytes 368648 | tf_op jit(solution)/shard_map/ppermute | solution.py:452
  13.0 0.6 copy-start.1
  13.0 0.7 copy-start.2
  30.6 50.5 %all-to-all-start = ((f32[32,15,8,128]{3,2,1,0:T(8,128)}), f32[32,15,8,128]{3,2,1,0:T(8,128)S(1)}, u32[]{:S(2)}, u32[]{:S(2)}) async-start(f32[32,15,8,128]{3,2,1,0:T(8,128)} %bitcast.7), calls=%async_computation | async-start | bytes 3932160 | tf_op jit(solution)/shard_map/all_to_all | solution.py:455

commit v14 on v11

--- a/solution.py
+++ b/solution.py
@@ -11,6 +11,7 @@
 LANES = 128
 SUB = 8
 SLOT = 32
+FIRST = 32
 MIB = 1024 * 1024
 LENGTH_BASE = 1000.0
 BIG = 60 * MIB
@@ -24,12 +25,28 @@
     return lax.broadcasted_iota(jnp.int32, (rows, LANES), 1)
 
 
-def pack_halo_kernel(tracers, west_cells, east_cells):
+def fetch(sources, targets, ready):
+    copies = [
+        pltpu.make_async_copy(source, target, ready.at[item])
+        for item, (source, target) in enumerate(zip(sources, targets))
+    ]
+    for copy in copies:
+        copy.start()
+    return copies
+
+
+def pack_halo_kernel(tracers_in, west_cells, east_cells, tracers, ready):
     ntr, levels, lats, _ = tracers.shape
     per_row = LANES // HALO
     group = lane_ids(SUB) // HALO
-
-    def one_level(level, carry):
+    assert lats == SUB * per_row
+    copies = fetch(
+        [tracers_in.at[:, level] for level in range(levels)],
+        [tracers.at[:, level] for level in range(levels)],
+        ready,
+    )
+    for level in range(levels):
+        copies[level].wait()
         for tracer in range(ntr):
             west = jnp.zeros((SUB, LANES), jnp.float32)
             east = jnp.zeros((SUB, LANES), jnp.float32)
@@ -43,10 +60,6 @@
                 east = jnp.where(group == part, rolled_east, east)
             west_cells[level, tracer] = west
             east_cells[level, tracer] = east
-        return carry
-
-    assert lats == SUB * per_row
-    lax.fori_loop(0, levels, one_level, 0)
 
 
 def pack_halo(tracers):
@@ -55,9 +68,10 @@
     return pl.pallas_call(
         pack_halo_kernel,
         out_shape=(shape, shape),
-        in_specs=[pl.BlockSpec(memory_space=pltpu.VMEM)],
+        in_specs=[pl.BlockSpec(memory_space=pl.ANY)],
         out_specs=[pl.BlockSpec(memory_space=pltpu.VMEM)] * 2,
-        compiler_params=pltpu.CompilerParams(vmem_limit_bytes=16 * MIB),
+        scratch_shapes=[pltpu.VMEM(tracers.shape, jnp.float32), pltpu.SemaphoreType.DMA((levels,))],
+        compiler_params=pltpu.CompilerParams(vmem_limit_bytes=BIG),
         name="pack_halo",
     )(tracers)
 
@@ -80,16 +94,6 @@
         return carry
 
     lax.fori_loop(0, count // chunk, some_values, 0)
-
-
-def fetch(sources, targets, ready):
-    copies = [
-        pltpu.make_async_copy(source, target, ready.at[item])
-        for item, (source, target) in enumerate(zip(sources, targets))
-    ]
-    for copy in copies:
-        copy.start()
-    return copies
 
 
 def inside_kernel(
@@ -185,8 +189,9 @@
 def add_edges_and_solve(inside, left_cell, west_edge, east_edge, lower, upper, halo, solved):
     levels, lats, _ = left_cell.shape
     ntr = inside.shape[0] // levels
-
-    def one_part(part, carry):
+    together = 2
+
+    def solve_part(part):
         rows = pl.ds(pl.multiple_of(part * SUB, SUB), SUB)
         half = part // 4
         base = (part % 4) * (2 * HALO)
@@ -205,18 +210,25 @@
                 if level > 0:
                     total = total + lower[level - 1, rows, :] * reduced[tracer][level - 1]
                 reduced[tracer].append(total)
-        results = []
-        for tracer in range(ntr):
-            x = reduced[tracer][levels - 1]
-            for level in range(levels - 1, -1, -1):
+        results = {}
+        for level in range(levels - 1, -1, -1):
+            for tracer in range(ntr):
+                x = reduced[tracer][level]
                 if level < levels - 1:
-                    x = reduced[tracer][level] + upper[level, rows, :] * x
-                results.append((level * ntr + tracer, x))
-        for value, x in results:
-            solved[pl.ds(part * SUB * SLOT + value, SUB, stride=SLOT), :] = x
-        return carry
-
-    lax.fori_loop(0, lats // SUB, one_part, 0)
+                    x = x + upper[level, rows, :] * results[(level + 1) * ntr + tracer]
+                results[level * ntr + tracer] = x
+        return results
+
+    def some_parts(step, carry):
+        solutions = [solve_part(step * together + item) for item in range(together)]
+        for item, results in enumerate(solutions):
+            first = pl.multiple_of((step * together + item) * (SUB * SLOT), SUB * SLOT)
+            target = solved.at[pl.ds(first, SUB * SLOT), :]
+            for value, x in results.items():
+                target[pl.ds(value, SUB, stride=SLOT), :] = x
+        return carry
+
+    lax.fori_loop(0, lats // (SUB * together), some_parts, 0)
 
 
 def streams_of(rows, values, parts):
@@ -231,7 +243,7 @@
 def build_table(solved, table, values, parts):
     rows_per = LANES // SLOT
     spread = streams_of(LANES, values, parts)[0]
-    together = 2
+    together = 4
 
     def some_rows(step, carry):
         blocks = []
@@ -252,20 +264,32 @@
     parts = cap // LANES
     lists = 4 // parts
     stream = streams_of(1, values, parts)[1]
-    together = 2 if blocks % 2 == 0 else 1
 
     def copy_out(block):
-        return pltpu.make_async_copy(turned.at[block], sent.at[block], copied.at[block])
-
-    def pick_block(block, item):
+        return pltpu.make_async_copy(turned.at[block + 1], sent.at[block], copied.at[block])
+
+    def turn(block):
+        half = pl.multiple_of(lax.rem(block + 2, 2) * LANES, LANES)
+        return packed[pl.ds(half, LANES), :].T
+
+    def send(block, result):
+        turned[block + 1] = result[:height, :]
+        for member in range(lists):
+            total = count[jnp.maximum(block, 0) * lists + member]
+            row = turned.at[block + 1, pl.ds((member * values + 1) * parts - 1, 1), :]
+            note = jnp.full((1, LANES), LENGTH_BASE + total.astype(jnp.float32))
+            pltpu.store(row, note, mask=(lane_ids(1) == LANES - 1) & (total < cap))
+
+    def one_block(block, carry):
         owners = [block * lists + member for member in range(lists)]
         rows = [lax.div(count[owner] + (parts - 1), parts) for owner in owners]
         for owner in owners:
             wait_list(owner)
         longest = functools.reduce(jnp.maximum, rows)
         places = [owners[g // parts] * cap + (g % parts) * rows[g // parts] for g in range(4)]
-
-        def pick_lines(start, lines):
+        half = lax.rem(block, 2) * LANES
+
+        def load_lines(start, lines):
             views = [index.at[pl.ds(place + start, lines)] for place in places]
             merged = []
             for line in range(lines):
@@ -273,43 +297,44 @@
                 low = jnp.where(stream == 0, picked[0], picked[1])
                 high = jnp.where(stream == 2, picked[2], picked[3])
                 merged.append(jnp.where(stream < 2, low, high))
-            first = pl.multiple_of(item * LANES + start, SUB)
-            for line in range(lines):
-                packed[pl.ds(first + line, 1), :] = merged[line]
+            return merged
+
+        def store_lines(start, merged):
+            target = packed.at[pl.ds(pl.multiple_of(half + start, SUB), len(merged)), :]
+            for line, value in enumerate(merged):
+                target[line : line + 1, :] = value
 
         def steps(begin, trips, lines):
-            def one_step(step, carry):
-                pick_lines(pl.multiple_of(begin + step * lines, SUB), lines)
-                return carry
+            def one_step(step, inner):
+                start = pl.multiple_of(begin + step * lines, SUB)
+                store_lines(start, load_lines(start, lines))
+                return inner
 
             lax.fori_loop(0, trips, one_step, 0)
             return begin + trips * lines
 
-        eights = lax.div(longest + (SUB - 1), SUB)
-        done = steps(0, lax.div(eights, 4), 4 * SUB)
+        before = turn(block - 1)
+        merged = load_lines(0, FIRST)
+        store_lines(0, merged)
+        send(block - 1, before)
+
+        @pl.when(block > 0)
+        def _():
+            copy_out(block - 1).start()
+
+        eights = jnp.maximum(lax.div(longest + (SUB - 1), SUB) - FIRST // SUB, 0)
+        done = steps(FIRST, lax.div(eights, 4), 4 * SUB)
         done = steps(done, lax.div(lax.rem(eights, 4), 2), 2 * SUB)
         steps(done, lax.rem(eights, 2), SUB)
-
-    def some_blocks(step, carry):
-        for item in range(together):
-            pick_block(step * together + item, item)
-        results = [packed[item * LANES : (item + 1) * LANES, :].T for item in range(together)]
-        for item in range(together):
-            block = step * together + item
-            turned[block] = results[item][:height, :]
-            for member in range(lists):
-                total = count[block * lists + member]
-                row = turned.at[block, pl.ds((member * values + 1) * parts - 1, 1), :]
-                note = jnp.full((1, LANES), LENGTH_BASE + total.astype(jnp.float32))
-                pltpu.store(row, note, mask=(lane_ids(1) == LANES - 1) & (total < cap))
-            copy_out(block).start()
         return carry
 
     def finish(block, carry):
         copy_out(block).wait()
         return carry
 
-    lax.fori_loop(0, blocks // together, some_blocks, 0)
+    lax.fori_loop(0, blocks, one_block, 0)
+    send(blocks - 1, turn(blocks - 1))
+    copy_out(blocks - 1).start()
     lax.fori_loop(0, blocks, finish, 0)
 
 
@@ -371,7 +396,7 @@
             pltpu.VMEM((lats * SLOT, LANES), jnp.float32),
             pltpu.VMEM((lats * lons, 1, LANES), jnp.float32),
             pltpu.VMEM((2 * LANES, LANES), jnp.float32),
-            pltpu.VMEM((blocks, 4 * values, LANES), jnp.float32),
+            pltpu.VMEM((blocks + 1, 4 * values, LANES), jnp.float32),
             pltpu.SMEM((lists * cap,), jnp.int32),
             pltpu.SMEM((cap,), jnp.int32),
             pltpu.SemaphoreType.DMA((lists + 1,)),

time: 82.5 us -> 81.4 us (0.987)
  local copies, waits for them, and re-layouts: 1.86 us -> 0.67 us
    pallas_call x1, Pallas kernels: 16.7 us -> 15 us  [make_sent(): pl.pallas_call(functools.partial(solve_kernel, parts), out_shape=jax.Shap...]
    pallas_call x1, Pallas kernels: 1.12 us -> 2.8 us  [pack_halo(): pl.pallas_call(pack_halo_kernel, out_shape=(shape, shape), in_specs=[pl.B...]
    unnamed x6 -> x4, local copies, waits for them, and re-layouts: 1.86 us -> 0.67 us
where the time goes in v14:
time: 81.4 us; the launch traced here: 81.1 us
  waiting for transfers between devices  45.9 us (56%)
  Pallas kernels  25.2 us (31%)
  starting transfers between devices  9.3 us (11%)
    all_to_all x1, waiting for transfers between devices, body(): lax.all_to_all(sent, ('lon', 'lat'), split_axis=0, concat_axis=0, tiled=T...  45.9 us
    pallas_call x1, Pallas kernels, make_sent(): pl.pallas_call(functools.partial(solve_kernel, parts), out_shape=jax.Shap...  15 us
    pallas_call x1, Pallas kernels, advect_inside(): pl.pallas_call(inside_kernel, out_shape=outputs, in_specs=[pl.BlockSpec(m...  5.12 us
    ppermute x1, starting transfers between devices, body(): from_east = lax.ppermute(west_cells, 'lon', ring('lon', -1))  5.03 us
    all_to_all x1, starting transfers between devices, body(): lax.all_to_all(sent, ('lon', 'lat'), split_axis=0, concat_axis=0, tiled=T...  3.76 us
    pallas_call x1, Pallas kernels, pack_halo(): pl.pallas_call(pack_halo_kernel, out_shape=(shape, shape), in_specs=[pl.B...  2.8 us
    pallas_call x1, Pallas kernels, place_owned(): pl.pallas_call(place_kernel, out_shape=jax.ShapeDtypeStruct((levels, ntr,...  2.28 us
  transfers between devices with their start and end apart: 3, of which 1 were waited for; matrix products, arithmetic and copies ran while one was open for 0% of the time, Pallas kernels for 6%

profile of v14, /device:TPU:0, one launch (start us, length us, event | category | flops | bytes accessed | tf_op | source)
XLA Modules:
  0.0 81.1 jit_solution(17646775214164326502)
XLA Ops:
  0.0 2.8 %pack_halo.1 = (f32[10,3,8,128]{3,2,1,0:T(8,128)}, f32[10,3,8,128]{3,2,1,0:T(8,128)}) custom-call(f32[3,10,64,128]{3,2,1,0:T(8,128)} %tracers_in.3), custom_call_target="tpu_custom_call" | custom-call | tf_op jit(solution)/shard_map/pack_halo/pallas_call | solution.py:68
  2.8 0.5 collective-permute-start
  3.3 5.0 %collective-permute-start.1 = (f32[10,3,8,128]{3,2,1,0:T(8,128)}, f32[10,3,8,128]{3,2,1,0:T(8,128)S(1)}, u32[]{:S(2)}, u32[]{:S(2)}) collective-permute-start(f32[10,3,8,128]{3,2,1,0:T(8,128)} %get-tuple-element.15), channel_id=1, source_target_pairs={{0,30},{2,0},{4,2},{6,4},{8,6},{10,8},{12,10},{14,12},{16,14},{18,... | collective-permute-start | bytes 368648 | tf_op jit(solution)/shard_map/ppermute | solution.py:470
  8.3 5.1 %advect_inside.1 = (f32[30,64,128]{2,1,0:T(8,128)}, s32[10,64,128]{2,1,0:T(8,128)}, f32[10,64,128]{2,1,0:T(8,128)}, f32[10,64,128]{2,1,0:T(8,128)}, f32[9,64,128...) custom-call(f32[3,10,64,128]{3,2,1,0:T(8,128)} %tracers_in.3, s32[10,64,128]{2,1,0:T(8,128)} %offsets_in.1, ...), custom_call_target="tpu_custom_call" | custom-call | bytes 20971520 | tf_op jit(solution)/shard_map/advect_inside/pallas_call | solution.py:176
  13.5 0.0 collective-permute-done
  13.5 0.0 copy-start
  13.5 0.0 collective-permute-done.1
  13.5 0.0 copy-start.1
  13.5 0.6 copy-done
  14.1 0.0 copy-done.1
  14.2 15.0 %solve_pick.1 = f32[32,120,128]{2,1,0:T(8,128)} custom-call(f32[30,8,128]{2,1,0:T(8,128)} %bitcast.8, f32[30,8,128]{2,1,0:T(8,128)} %bitcast.9, f32[30,64,128]{2,1,0:T(8,128)} %get-tuple-element.16.inside_in, s32[10,64,128]{2,1,0:T(8,128)} %get-tuple-element.17.left_cell_in, f32[10,64,128]{2,1,0:T(8,128)} %get-tuple-element.18.west_edge_in, ...), custom_call_target="tpu_custom_call" | custom-call | bytes 41943040 | tf_op jit(solution)/shard_map/solve_pick/pallas_call | solution.py:387
  29.2 3.8 %all-to-all-start = ((f32[32,15,8,128]{3,2,1,0:T(8,128)}), f32[32,15,8,128]{3,2,1,0:T(8,128)S(1)}, u32[]{:S(2)}, u32[]{:S(2)}) async-start(f32[32,15,8,128]{3,2,1,0:T(8,128)} %bitcast.7), calls=%async_computation | async-start | bytes 3932160 | tf_op jit(solution)/shard_map/all_to_all | solution.py:473
  32.9 45.9 %all-to-all-done = f32[32,15,8,128]{3,2,1,0:T(8,128)S(1)} async-done(((f32[32,15,8,128]{3,2,1,0:T(8,128)}), f32[32,15,8,128]{3,2,1,0:T(8,128)S(1)}, u32[]{:S(2)}, u32[]{:S(2)}) %all-to-all-start) | async-done | bytes 1966112 | tf_op jit(solution)/shard_map/all_to_all | solution.py:473
  78.8 2.3 %place_owned.1 = f32[10,3,8192]{2,1,0:T(4,128)} custom-call(s32[1]{0:T(128)} %bitcast.own, f32[32,120,128]{2,1,0:T(8,128)S(1)} %bitcast.6), custom_call_target="tpu_custom_call" | custom-call | tf_op jit(solution)/shard_map/place_owned/pallas_call | solution.py:449
Async XLA Ops:
  2.8 10.7 %collective-permute-start = (f32[10,3,8,128]{3,2,1,0:T(8,128)}, f32[10,3,8,128]{3,2,1,0:T(8,128)S(1)}, u32[]{:S(2)}, u32[]{:S(2)}) collective-permute-start(f32[10,3,8,128]{3,2,1,0:T(8,128)} %get-tuple-element.14), channel_id=1, source_target_pairs={{0,2},{2,4},{4,6},{6,8},{8,10},{10,12},{12,14},{14,16},{16,18},{18... | collective-permute-start | bytes 368648 | tf_op jit(solution)/shard_map/ppermute | solution.py:469
  3.3 10.2 %collective-permute-start.1 = (f32[10,3,8,128]{3,2,1,0:T(8,128)}, f32[10,3,8,128]{3,2,1,0:T(8,128)S(1)}, u32[]{:S(2)}, u32[]{:S(2)}) collective-permute-start(f32[10,3,8,128]{3,2,1,0:T(8,128)} %get-tuple-element.15), channel_id=1, source_target_pairs={{0,30},{2,0},{4,2},{6,4},{8,6},{10,8},{12,10},{14,12},{16,14},{18,... | collective-permute-start | bytes 368648 | tf_op jit(solution)/shard_map/ppermute | solution.py:470
  13.5 0.7 copy-start
  13.5 0.7 copy-start.1
  29.2 49.7 %all-to-all-start = ((f32[32,15,8,128]{3,2,1,0:T(8,128)}), f32[32,15,8,128]{3,2,1,0:T(8,128)S(1)}, u32[]{:S(2)}, u32[]{:S(2)}) async-start(f32[32,15,8,128]{3,2,1,0:T(8,128)} %bitcast.7), calls=%async_computation | async-start | bytes 3932160 | tf_op jit(solution)/shard_map/all_to_all | solution.py:473

commit v15 on v14

--- a/solution.py
+++ b/solution.py
@@ -15,6 +15,8 @@
 MIB = 1024 * 1024
 LENGTH_BASE = 1000.0
 BIG = 60 * MIB
+SOLVE = 107 * MIB // 2
+LIST_ROWS = 256
 
 
 def take_lanes(block, index):
@@ -35,18 +37,12 @@
     return copies
 
 
-def pack_halo_kernel(tracers_in, west_cells, east_cells, tracers, ready):
+def pack_halo_kernel(tracers, west_cells, east_cells):
     ntr, levels, lats, _ = tracers.shape
     per_row = LANES // HALO
     group = lane_ids(SUB) // HALO
-    assert lats == SUB * per_row
-    copies = fetch(
-        [tracers_in.at[:, level] for level in range(levels)],
-        [tracers.at[:, level] for level in range(levels)],
-        ready,
-    )
-    for level in range(levels):
-        copies[level].wait()
+
+    def one_level(level, carry):
         for tracer in range(ntr):
             west = jnp.zeros((SUB, LANES), jnp.float32)
             east = jnp.zeros((SUB, LANES), jnp.float32)
@@ -60,6 +56,10 @@
                 east = jnp.where(group == part, rolled_east, east)
             west_cells[level, tracer] = west
             east_cells[level, tracer] = east
+        return carry
+
+    assert lats == SUB * per_row
+    lax.fori_loop(0, levels, one_level, 0)
 
 
 def pack_halo(tracers):
@@ -68,10 +68,9 @@
     return pl.pallas_call(
         pack_halo_kernel,
         out_shape=(shape, shape),
-        in_specs=[pl.BlockSpec(memory_space=pl.ANY)],
+        in_specs=[pl.BlockSpec(memory_space=pltpu.VMEM)],
         out_specs=[pl.BlockSpec(memory_space=pltpu.VMEM)] * 2,
-        scratch_shapes=[pltpu.VMEM(tracers.shape, jnp.float32), pltpu.SemaphoreType.DMA((levels,))],
-        compiler_params=pltpu.CompilerParams(vmem_limit_bytes=BIG),
+        compiler_params=pltpu.CompilerParams(vmem_limit_bytes=16 * MIB),
         name="pack_halo",
     )(tracers)
 
@@ -171,7 +170,7 @@
         field(levels),
         field(levels - 1),
         field(levels - 1),
-        jax.ShapeDtypeStruct((lists + SUB, cap), jnp.int32),
+        jax.ShapeDtypeStruct((max(lists + SUB, LIST_ROWS), cap), jnp.int32),
     )
     return pl.pallas_call(
         inside_kernel,
@@ -339,8 +338,8 @@
 
 
 def list_copies(lists_in, index, count, listed):
-    owners = lists_in.shape[0] - SUB
     cap = lists_in.shape[1]
+    owners = index.shape[0] // cap
     lengths = pltpu.make_async_copy(lists_in.at[owners], count, listed.at[owners])
 
     def list_copy(item):
@@ -357,20 +356,18 @@
 
 
 def solve_kernel(
-    parts, west_in, east_in, inside_in, left_cell_in, west_edge_in, east_edge_in, lower_in, upper_in, lists_in,
-    sent, west, east, inside, left_cell, west_edge, east_edge, lower, upper, ready,
+    parts, west, east, inside_in, left_cell_in, west_edge_in, east_edge_in, lower_in, upper_in, lists_in,
+    sent, inside, left_cell, west_edge, east_edge, lower, upper, ready,
     halo, solved, table, packed, turned, index, count, listed, copied,
 ):
     values, lats, _ = inside.shape
-    sources = (west_in, east_in, left_cell_in, west_edge_in, east_edge_in, lower_in, upper_in, inside_in)
-    copies = fetch(sources, (west, east, left_cell, west_edge, east_edge, lower, upper, inside), ready)
+    sources = (left_cell_in, west_edge_in, east_edge_in, lower_in, upper_in, inside_in)
+    copies = fetch(sources, (left_cell, west_edge, east_edge, lower, upper, inside), ready)
     wait_lengths, wait_list = list_copies(lists_in, index, count, listed)
     for value in range(values, SLOT):
         solved[pl.ds(value, lats, stride=SLOT), :] = jnp.zeros((lats, LANES), jnp.float32)
-    for copy in copies[:2]:
-        copy.wait()
     merge_halo(west, east, halo, values)
-    for copy in copies[2:]:
+    for copy in copies:
         copy.wait()
     add_edges_and_solve(inside, left_cell, west_edge, east_edge, lower, upper, halo, solved)
     build_table(solved, table.reshape(table.shape[0], LANES), values, parts)
@@ -378,20 +375,20 @@
     pick_rows(table, index, count, lists_in.shape[1], values, packed, turned, sent, copied, wait_list)
 
 
-def make_sent(west, east, fields, lists_in):
+def make_sent(west, east, fields, lists_in, lists):
     values, lats, lons = fields[0].shape
-    lists, cap = lists_in.shape[0] - SUB, lists_in.shape[1]
+    cap = lists_in.shape[1]
     parts = cap // LANES
     blocks = lists * parts // 4
-    inputs = (west.reshape(values, SUB, LANES), east.reshape(values, SUB, LANES), *fields)
+    halos = (west.reshape(values, SUB, LANES), east.reshape(values, SUB, LANES))
     sent = pl.pallas_call(
         functools.partial(solve_kernel, parts),
         out_shape=jax.ShapeDtypeStruct((blocks, 4 * values, LANES), jnp.float32),
-        in_specs=[pl.BlockSpec(memory_space=pl.ANY)] * (len(inputs) + 1),
+        in_specs=[pl.BlockSpec(memory_space=pltpu.VMEM)] * 2 + [pl.BlockSpec(memory_space=pl.ANY)] * (len(fields) + 1),
         out_specs=pl.BlockSpec(memory_space=pl.ANY),
-        scratch_shapes=[pltpu.VMEM(array.shape, array.dtype) for array in inputs]
+        scratch_shapes=[pltpu.VMEM(array.shape, array.dtype) for array in fields]
         + [
-            pltpu.SemaphoreType.DMA((len(inputs),)),
+            pltpu.SemaphoreType.DMA((len(fields),)),
             pltpu.VMEM((values, 2, SUB, LANES), jnp.float32),
             pltpu.VMEM((lats * SLOT, LANES), jnp.float32),
             pltpu.VMEM((lats * lons, 1, LANES), jnp.float32),
@@ -402,10 +399,10 @@
             pltpu.SemaphoreType.DMA((lists + 1,)),
             pltpu.SemaphoreType.DMA((blocks,)),
         ],
-        compiler_params=pltpu.CompilerParams(vmem_limit_bytes=BIG),
+        compiler_params=pltpu.CompilerParams(vmem_limit_bytes=SOLVE),
         cost_estimate=pl.CostEstimate(flops=0, bytes_accessed=40 * MIB, transcendentals=0),
         name="solve_pick",
-    )(*inputs, lists_in)
+    )(*halos, *fields, lists_in)
     rows = values * parts
     tile = max(size for size in (1, 2, 4, 8) if rows % size == 0)
     return sent.reshape(lists, rows // tile, tile, LANES)
@@ -469,7 +466,7 @@
     from_west = lax.ppermute(east_cells, "lon", ring("lon", 1))
     from_east = lax.ppermute(west_cells, "lon", ring("lon", -1))
     *fields, lists = advect_inside(tracers, offsets, weights, diffusion, send_index, send_count)
-    sent = make_sent(from_west, from_east, fields, lists)
+    sent = make_sent(from_west, from_east, fields, lists, send_count.shape[1])
     arrived = lax.all_to_all(sent, ("lon", "lat"), split_axis=0, concat_axis=0, tiled=True)
     own = lax.axis_index(("lon", "lat")).astype(jnp.int32).reshape(1)
     owned = place_owned(arrived, own, levels, ntr, columns)

time: 81.4 us -> 80.1 us (0.984)
  Pallas kernels: 25.2 us -> 23.5 us
    pallas_call x1, Pallas kernels: 2.8 us -> 1.12 us  [pack_halo(): pl.pallas_call(pack_halo_kernel, out_shape=(shape, shape), in_specs=[pl.B...]
  transfers between devices with their start and end apart: 3 -> 3, of which waited for: 1 -> 1; matrix products, arithmetic and copies ran while one was open for 0% -> 0% of each run, Pallas kernels for 6% -> 7%
where the time goes in v15:
time: 80.1 us; the launch traced here: 79.8 us
  waiting for transfers between devices  45.9 us (57%)
  Pallas kernels  23.5 us (29%)
  starting transfers between devices  9.12 us (11%)
  local copies, waits for them, and re-layouts  1.2 us (1%)
    all_to_all x1, waiting for transfers between devices, body(): lax.all_to_all(sent, ('lon', 'lat'), split_axis=0, concat_axis=0, tiled=T...  45.9 us
    pallas_call x1, Pallas kernels, make_sent(): pl.pallas_call(functools.partial(solve_kernel, parts), out_shape=jax.Shap...  14.9 us
    pallas_call x1, Pallas kernels, advect_inside(): pl.pallas_call(inside_kernel, out_shape=outputs, in_specs=[pl.BlockSpec(m...  5.26 us
    ppermute x1, starting transfers between devices, body(): from_east = lax.ppermute(west_cells, 'lon', ring('lon', -1))  5.03 us
    all_to_all x1, starting transfers between devices, body(): lax.all_to_all(sent, ('lon', 'lat'), split_axis=0, concat_axis=0, tiled=T...  3.58 us
    pallas_call x1, Pallas kernels, place_owned(): pl.pallas_call(place_kernel, out_shape=jax.ShapeDtypeStruct((levels, ntr,...  2.28 us
  transfers between devices with their start and end apart: 3, of which 1 were waited for; matrix products, arithmetic and copies ran while one was open for 0% of the time, Pallas kernels for 7%

profile of v15, /device:TPU:0, one launch (start us, length us, event | category | flops | bytes accessed | tf_op | source)
XLA Modules:
  0.0 79.8 jit_solution(4736293762111200383)
XLA Ops:
  0.0 0.0 copy-start
  0.0 1.2 %copy-done = f32[3,10,64,128]{3,2,1,0:T(8,128)S(1)} copy-done((f32[3,10,64,128]{3,2,1,0:T(8,128)S(1)}, f32[3,10,64,128]{3,2,1,0:T(8,128)}, u32[]{:S(2)}) %copy-start) | copy-done | bytes 983064
  1.2 1.1 %pack_halo.1 = (f32[10,3,8,128]{3,2,1,0:T(8,128)S(1)}, f32[10,3,8,128]{3,2,1,0:T(8,128)S(1)}) custom-call(f32[3,10,64,128]{3,2,1,0:T(8,128)S(1)} %copy-done), custom_call_target="tpu_custom_call" | custom-call | tf_op jit(solution)/shard_map/pack_halo/pallas_call | solution.py:68
  2.3 0.5 collective-permute-start
  2.8 5.0 %collective-permute-start.1 = (f32[10,3,8,128]{3,2,1,0:T(8,128)S(1)}, f32[10,3,8,128]{3,2,1,0:T(8,128)S(1)}, u32[]{:S(2)}, u32[]{:S(2)}) collective-permute-start(f32[10,3,8,128]{3,2,1,0:T(8,128)S(1)} %get-tuple-element.15), channel_id=1, source_target_pairs={{0,30},{2,0},{4,2},{6,4},{8,6},{10,8},{12,10},{14,12},{16,14},{18,... | collective-permute-start | bytes 368648 | tf_op jit(solution)/shard_map/ppermute | solution.py:467
  7.9 5.3 %advect_inside.1 = (f32[30,64,128]{2,1,0:T(8,128)}, s32[10,64,128]{2,1,0:T(8,128)}, f32[10,64,128]{2,1,0:T(8,128)}, f32[10,64,128]{2,1,0:T(8,128)}, f32[9,64,128...) custom-call(f32[3,10,64,128]{3,2,1,0:T(8,128)} %tracers_in.1, s32[10,64,128]{2,1,0:T(8,128)} %offsets_in.1, ...), custom_call_target="tpu_custom_call" | custom-call | bytes 20971520 | tf_op jit(solution)/shard_map/advect_inside/pallas_call | solution.py:175
  13.1 0.0 collective-permute-done
  13.1 0.0 collective-permute-done.1
  13.2 14.9 %solve_pick.1 = f32[32,120,128]{2,1,0:T(8,128)} custom-call(f32[30,8,128]{2,1,0:T(8,128)S(1)} %bitcast.7, f32[30,8,128]{2,1,0:T(8,128)S(1)} %bitcast.8, f32[30,64,128]{2,1,0:T(8,128)} %get-tuple-element.16.inside_in, s32[10,64,128]{2,1,0:T(8,128)} %get-tuple-element.17.left_cell_in, f32[10,64,128]{2,1,0:T(8,128)} %get-tuple-element.18.west_edge_in, ...), custom_call_target="tpu_custom_call" | custom-call | bytes 41943040 | tf_op jit(solution)/shard_map/solve_pick/pallas_call | solution.py:384
  28.0 3.6 %all-to-all-start = ((f32[32,15,8,128]{3,2,1,0:T(8,128)}), f32[32,15,8,128]{3,2,1,0:T(8,128)S(1)}, u32[]{:S(2)}, u32[]{:S(2)}) async-start(f32[32,15,8,128]{3,2,1,0:T(8,128)} %bitcast.9), calls=%async_computation | async-start | bytes 3932160 | tf_op jit(solution)/shard_map/all_to_all | solution.py:470
  31.6 45.9 %all-to-all-done = f32[32,15,8,128]{3,2,1,0:T(8,128)S(1)} async-done(((f32[32,15,8,128]{3,2,1,0:T(8,128)}), f32[32,15,8,128]{3,2,1,0:T(8,128)S(1)}, u32[]{:S(2)}, u32[]{:S(2)}) %all-to-all-start) | async-done | bytes 1966112 | tf_op jit(solution)/shard_map/all_to_all | solution.py:470
  77.5 2.3 %place_owned.1 = f32[10,3,8192]{2,1,0:T(4,128)} custom-call(s32[1]{0:T(128)} %bitcast.own, f32[32,120,128]{2,1,0:T(8,128)S(1)} %bitcast.6), custom_call_target="tpu_custom_call" | custom-call | tf_op jit(solution)/shard_map/place_owned/pallas_call | solution.py:446
Async XLA Ops:
  0.0 1.2 %copy-start = (f32[3,10,64,128]{3,2,1,0:T(8,128)S(1)}, f32[3,10,64,128]{3,2,1,0:T(8,128)}, u32[]{:S(2)}) copy-start(f32[3,10,64,128]{3,2,1,0:T(8,128)} %tracers_in.1) | copy-start | bytes 2949124
  2.3 10.8 %collective-permute-start = (f32[10,3,8,128]{3,2,1,0:T(8,128)S(1)}, f32[10,3,8,128]{3,2,1,0:T(8,128)S(1)}, u32[]{:S(2)}, u32[]{:S(2)}) collective-permute-start(f32[10,3,8,128]{3,2,1,0:T(8,128)S(1)} %get-tuple-element.14), channel_id=1, source_target_pairs={{0,2},{2,4},{4,6},{6,8},{8,10},{10,12},{12,14},{14,16},{16,18},{18... | collective-permute-start | bytes 368648 | tf_op jit(solution)/shard_map/ppermute | solution.py:466
  2.8 10.3 %collective-permute-start.1 = (f32[10,3,8,128]{3,2,1,0:T(8,128)S(1)}, f32[10,3,8,128]{3,2,1,0:T(8,128)S(1)}, u32[]{:S(2)}, u32[]{:S(2)}) collective-permute-start(f32[10,3,8,128]{3,2,1,0:T(8,128)S(1)} %get-tuple-element.15), channel_id=1, source_target_pairs={{0,30},{2,0},{4,2},{6,4},{8,6},{10,8},{12,10},{14,12},{16,14},{18,... | collective-permute-start | bytes 368648 | tf_op jit(solution)/shard_map/ppermute | solution.py:467
  28.0 49.5 %all-to-all-start = ((f32[32,15,8,128]{3,2,1,0:T(8,128)}), f32[32,15,8,128]{3,2,1,0:T(8,128)S(1)}, u32[]{:S(2)}, u32[]{:S(2)}) async-start(f32[32,15,8,128]{3,2,1,0:T(8,128)} %bitcast.9), calls=%async_computation | async-start | bytes 3932160 | tf_op jit(solution)/shard_map/all_to_all | solution.py:470

commit v16 on v15

--- a/solution.py
+++ b/solution.py
@@ -37,12 +37,18 @@
     return copies
 
 
-def pack_halo_kernel(tracers, west_cells, east_cells):
+def pack_halo_kernel(tracers_in, west_cells, east_cells, tracers, ready):
     ntr, levels, lats, _ = tracers.shape
     per_row = LANES // HALO
     group = lane_ids(SUB) // HALO
-
-    def one_level(level, carry):
+    assert lats == SUB * per_row
+    copies = fetch(
+        [tracers_in.at[:, level] for level in range(levels)],
+        [tracers.at[:, level] for level in range(levels)],
+        ready,
+    )
+    for level in range(levels):
+        copies[level].wait()
         for tracer in range(ntr):
             west = jnp.zeros((SUB, LANES), jnp.float32)
             east = jnp.zeros((SUB, LANES), jnp.float32)
@@ -56,10 +62,6 @@
                 east = jnp.where(group == part, rolled_east, east)
             west_cells[level, tracer] = west
             east_cells[level, tracer] = east
-        return carry
-
-    assert lats == SUB * per_row
-    lax.fori_loop(0, levels, one_level, 0)
 
 
 def pack_halo(tracers):
@@ -68,9 +70,10 @@
     return pl.pallas_call(
         pack_halo_kernel,
         out_shape=(shape, shape),
-        in_specs=[pl.BlockSpec(memory_space=pltpu.VMEM)],
+        in_specs=[pl.BlockSpec(memory_space=pl.ANY)],
         out_specs=[pl.BlockSpec(memory_space=pltpu.VMEM)] * 2,
-        compiler_params=pltpu.CompilerParams(vmem_limit_bytes=16 * MIB),
+        scratch_shapes=[pltpu.VMEM(tracers.shape, jnp.float32), pltpu.SemaphoreType.DMA((levels,))],
+        compiler_params=pltpu.CompilerParams(vmem_limit_bytes=SOLVE),
         name="pack_halo",
     )(tracers)
 
@@ -79,7 +82,7 @@
     lane = lane_ids(SUB)
     cell = lane % (2 * HALO)
     sources = [(half * 4 + lane // (2 * HALO)) * HALO + cell % HALO for half in range(2)]
-    chunk = 5 if count % 5 == 0 else 1
+    chunk = 10 if count % 10 == 0 else 1
 
     def some_values(step, carry):
         merged = []
@@ -408,7 +411,7 @@
     return sent.reshape(lists, rows // tile, tile, LANES)
 
 
-def place_kernel(own, arrived, owned, row):
+def place_kernel(own, arrived, owned_out, row, owned, written):
     sources, height, _ = arrived.shape
     levels, ntr, columns = owned.shape
     values = levels * ntr
@@ -435,8 +438,13 @@
             pltpu.store(row.at[:, here], rolled, mask=lane >= shift)
             row[:, after] = rolled
         start = start + total
+    copies = []
     for level in range(levels):
         owned[level] = row[level * ntr : (level + 1) * ntr, :columns]
+        copies.append(pltpu.make_async_copy(owned.at[level], owned_out.at[level], written.at[level]))
+        copies[level].start()
+    for copy in copies:
+        copy.wait()
 
 
 def place_owned(arrived, own, levels, ntr, columns):
@@ -447,8 +455,12 @@
         place_kernel,
         out_shape=jax.ShapeDtypeStruct((levels, ntr, columns), jnp.float32),
         in_specs=[smem, vmem],
-        out_specs=vmem,
-        scratch_shapes=[pltpu.VMEM((values, columns + 2 * LANES), jnp.float32)],
+        out_specs=pl.BlockSpec(memory_space=pl.ANY),
+        scratch_shapes=[
+            pltpu.VMEM((values, columns + 2 * LANES), jnp.float32),
+            pltpu.VMEM((levels, ntr, columns), jnp.float32),
+            pltpu.SemaphoreType.DMA((levels,)),
+        ],
         compiler_params=pltpu.CompilerParams(vmem_limit_bytes=16 * MIB),
         name="place_owned",
     )(own, arrived.reshape(arrived.shape[0], -1, LANES))

time: 80.1 us -> 79.7 us (level)
  local copies, waits for them, and re-layouts: 1.2 us -> 0 us
  Pallas kernels: 23.5 us -> 24.4 us
    unnamed x2 -> x0, local copies, waits for them, and re-layouts: 1.2 us -> none
    pallas_call x1, Pallas kernels: 1.12 us -> 2.1 us  [pack_halo(): pl.pallas_call(pack_halo_kernel, out_shape=(shape, shape), in_specs=[pl.B...]
where the time goes in v16:
time: 79.7 us; the launch traced here: 79.4 us
  waiting for transfers between devices  45.9 us (58%)
  Pallas kernels  24.4 us (31%)
  starting transfers between devices  9.1 us (11%)
    all_to_all x1, waiting for transfers between devices, body(): lax.all_to_all(sent, ('lon', 'lat'), split_axis=0, concat_axis=0, tiled=T...  45.9 us
    pallas_call x1, Pallas kernels, make_sent(): pl.pallas_call(functools.partial(solve_kernel, parts), out_shape=jax.Shap...  14.9 us
    pallas_call x1, Pallas kernels, advect_inside(): pl.pallas_call(inside_kernel, out_shape=outputs, in_specs=[pl.BlockSpec(m...  5.26 us
    ppermute x1, starting transfers between devices, body(): from_east = lax.ppermute(west_cells, 'lon', ring('lon', -1))  5.03 us
    all_to_all x1, starting transfers between devices, body(): lax.all_to_all(sent, ('lon', 'lat'), split_axis=0, concat_axis=0, tiled=T...  3.57 us
    pallas_call x1, Pallas kernels, place_owned(): pl.pallas_call(place_kernel, out_shape=jax.ShapeDtypeStruct((levels, ntr,...  2.12 us
    pallas_call x1, Pallas kernels, pack_halo(): pl.pallas_call(pack_halo_kernel, out_shape=(shape, shape), in_specs=[pl.B...  2.1 us
  transfers between devices with their start and end apart: 3, of which 1 were waited for; matrix products, arithmetic and copies ran while one was open for 0% of the time, Pallas kernels for 7%

profile of v16, /device:TPU:0, one launch (start us, length us, event | category | flops | bytes accessed | tf_op | source)
XLA Modules:
  0.0 79.4 jit_solution(16286649841462097803)
XLA Ops:
  0.0 2.1 %pack_halo.1 = (f32[10,3,8,128]{3,2,1,0:T(8,128)S(1)}, f32[10,3,8,128]{3,2,1,0:T(8,128)S(1)}) custom-call(f32[3,10,64,128]{3,2,1,0:T(8,128)} %tracers_in.3), custom_call_target="tpu_custom_call" | custom-call | tf_op jit(solution)/shard_map/pack_halo/pallas_call | solution.py:70
  2.1 0.5 collective-permute-start
  2.6 5.0 %collective-permute-start.1 = (f32[10,3,8,128]{3,2,1,0:T(8,128)S(1)}, f32[10,3,8,128]{3,2,1,0:T(8,128)S(1)}, u32[]{:S(2)}, u32[]{:S(2)}) collective-permute-start(f32[10,3,8,128]{3,2,1,0:T(8,128)S(1)} %get-tuple-element.15), channel_id=1, source_target_pairs={{0,30},{2,0},{4,2},{6,4},{8,6},{10,8},{12,10},{14,12},{16,14},{18,... | collective-permute-start | bytes 368648 | tf_op jit(solution)/shard_map/ppermute | solution.py:479
  7.6 5.3 %advect_inside.1 = (f32[30,64,128]{2,1,0:T(8,128)}, s32[10,64,128]{2,1,0:T(8,128)}, f32[10,64,128]{2,1,0:T(8,128)}, f32[10,64,128]{2,1,0:T(8,128)}, f32[9,64,128...) custom-call(f32[3,10,64,128]{3,2,1,0:T(8,128)} %tracers_in.3, s32[10,64,128]{2,1,0:T(8,128)} %offsets_in.1, ...), custom_call_target="tpu_custom_call" | custom-call | bytes 20971520 | tf_op jit(solution)/shard_map/advect_inside/pallas_call | solution.py:178
  12.9 0.0 collective-permute-done
  12.9 0.0 collective-permute-done.1
  12.9 14.9 %solve_pick.1 = f32[32,120,128]{2,1,0:T(8,128)} custom-call(f32[30,8,128]{2,1,0:T(8,128)S(1)} %bitcast.7, f32[30,8,128]{2,1,0:T(8,128)S(1)} %bitcast.8, f32[30,64,128]{2,1,0:T(8,128)} %get-tuple-element.16.inside_in, s32[10,64,128]{2,1,0:T(8,128)} %get-tuple-element.17.left_cell_in, f32[10,64,128]{2,1,0:T(8,128)} %get-tuple-element.18.west_edge_in, ...), custom_call_target="tpu_custom_call" | custom-call | bytes 41943040 | tf_op jit(solution)/shard_map/solve_pick/pallas_call | solution.py:387
  27.8 3.6 %all-to-all-start = ((f32[32,15,8,128]{3,2,1,0:T(8,128)}), f32[32,15,8,128]{3,2,1,0:T(8,128)S(1)}, u32[]{:S(2)}, u32[]{:S(2)}) async-start(f32[32,15,8,128]{3,2,1,0:T(8,128)} %bitcast.9), calls=%async_computation | async-start | bytes 3932160 | tf_op jit(solution)/shard_map/all_to_all | solution.py:482
  31.4 45.9 %all-to-all-done = f32[32,15,8,128]{3,2,1,0:T(8,128)S(1)} async-done(((f32[32,15,8,128]{3,2,1,0:T(8,128)}), f32[32,15,8,128]{3,2,1,0:T(8,128)S(1)}, u32[]{:S(2)}, u32[]{:S(2)}) %all-to-all-start) | async-done | bytes 1966112 | tf_op jit(solution)/shard_map/all_to_all | solution.py:482
  77.3 2.1 %place_owned.1 = f32[10,3,8192]{2,1,0:T(4,128)} custom-call(s32[1]{0:T(128)} %bitcast.own, f32[32,120,128]{2,1,0:T(8,128)S(1)} %bitcast.6), custom_call_target="tpu_custom_call" | custom-call | tf_op jit(solution)/shard_map/place_owned/pallas_call | solution.py:454
Async XLA Ops:
  2.1 10.8 %collective-permute-start = (f32[10,3,8,128]{3,2,1,0:T(8,128)S(1)}, f32[10,3,8,128]{3,2,1,0:T(8,128)S(1)}, u32[]{:S(2)}, u32[]{:S(2)}) collective-permute-start(f32[10,3,8,128]{3,2,1,0:T(8,128)S(1)} %get-tuple-element.14), channel_id=1, source_target_pairs={{0,2},{2,4},{4,6},{6,8},{8,10},{10,12},{12,14},{14,16},{16,18},{18... | collective-permute-start | bytes 368648 | tf_op jit(solution)/shard_map/ppermute | solution.py:478
  2.6 10.3 %collective-permute-start.1 = (f32[10,3,8,128]{3,2,1,0:T(8,128)S(1)}, f32[10,3,8,128]{3,2,1,0:T(8,128)S(1)}, u32[]{:S(2)}, u32[]{:S(2)}) collective-permute-start(f32[10,3,8,128]{3,2,1,0:T(8,128)S(1)} %get-tuple-element.15), channel_id=1, source_target_pairs={{0,30},{2,0},{4,2},{6,4},{8,6},{10,8},{12,10},{14,12},{16,14},{18,... | collective-permute-start | bytes 368648 | tf_op jit(solution)/shard_map/ppermute | solution.py:479
  27.8 49.5 %all-to-all-start = ((f32[32,15,8,128]{3,2,1,0:T(8,128)}), f32[32,15,8,128]{3,2,1,0:T(8,128)S(1)}, u32[]{:S(2)}, u32[]{:S(2)}) async-start(f32[32,15,8,128]{3,2,1,0:T(8,128)} %bitcast.9), calls=%async_computation | async-start | bytes 3932160 | tf_op jit(solution)/shard_map/all_to_all | solution.py:482

commit v17 on v16

--- a/solution.py
+++ b/solution.py
@@ -12,6 +12,7 @@
 SUB = 8
 SLOT = 32
 FIRST = 32
+PAIR = 65536
 MIB = 1024 * 1024
 LENGTH_BASE = 1000.0
 BIG = 60 * MIB
@@ -101,19 +102,21 @@
 def inside_kernel(
     tracers_in, offsets_in, weights_in, diffusion_in, index_in, count,
     inside, left_cell, west_edge, east_edge, lower, upper, lists,
-    tracers, offsets, weights, diffusion, ready,
+    tracers, offsets, weights, diffusion, index, ready,
 ):
     ntr, levels, lats, _ = tracers.shape
     lane = lane_ids(SUB)
     owners = count.shape[1]
     copies = fetch(
         (diffusion_in, offsets_in, weights_in, tracers_in, index_in.at[0]),
-        (diffusion, offsets, weights, tracers, lists.at[pl.ds(0, owners)]),
+        (diffusion, offsets, weights, tracers, index),
         ready,
     )
     lists[owners : owners + 1, :owners] = count[...]
     for copy in copies:
         copy.wait()
+    following = pltpu.roll(index[...], index.shape[1] - 1, 1)
+    lists[:owners, :] = index[...] + following * PAIR
 
     def one_part(part, carry):
         rows = pl.ds(pl.multiple_of(part * SUB, SUB), SUB)
@@ -181,7 +184,7 @@
         in_specs=[pl.BlockSpec(memory_space=pl.ANY)] * 5 + [vmem],
         out_specs=(vmem,) * len(outputs),
         scratch_shapes=[pltpu.VMEM(array.shape, array.dtype) for array in (tracers, offsets, weights, diffusion)]
-        + [pltpu.SemaphoreType.DMA((5,))],
+        + [pltpu.VMEM((lists, cap), jnp.int32), pltpu.SemaphoreType.DMA((5,))],
         compiler_params=pltpu.CompilerParams(vmem_limit_bytes=BIG),
         cost_estimate=pl.CostEstimate(flops=0, bytes_accessed=20 * MIB, transcendentals=0),
         name="advect_inside",
@@ -294,11 +297,16 @@
         def load_lines(start, lines):
             views = [index.at[pl.ds(place + start, lines)] for place in places]
             merged = []
-            for line in range(lines):
-                picked = [table[view[line]] for view in views]
-                low = jnp.where(stream == 0, picked[0], picked[1])
-                high = jnp.where(stream == 2, picked[2], picked[3])
-                merged.append(jnp.where(stream < 2, low, high))
+            for line in range(0, lines, 2):
+                pairs = [view[line] for view in views]
+                for columns in (
+                    [pair & (PAIR - 1) for pair in pairs],
+                    [lax.shift_right_logical(pair, 16) for pair in pairs],
+                ):
+                    picked = [table[column] for column in columns]
+                    low = jnp.where(stream == 0, picked[0], picked[1])
+                    high = jnp.where(stream == 2, picked[2], picked[3])
+                    merged.append(jnp.where(stream < 2, low, high))
             return merged
 
         def store_lines(start, merged):

time: 79.7 us -> 80.7 us (1.013)
  Pallas kernels: 24.4 us -> 25.4 us
    pallas_call x1, Pallas kernels: 14.9 us -> 15.8 us  [make_sent(): pl.pallas_call(functools.partial(solve_kernel, parts), out_shape=jax.Shap...]
where the time goes in v17:
time: 80.7 us; the launch traced here: 80.4 us
  waiting for transfers between devices  45.9 us (57%)
  Pallas kernels  25.4 us (31%)
  starting transfers between devices  9.1 us (11%)
    all_to_all x1, waiting for transfers between devices, body(): lax.all_to_all(sent, ('lon', 'lat'), split_axis=0, concat_axis=0, tiled=T...  45.9 us
    pallas_call x1, Pallas kernels, make_sent(): pl.pallas_call(functools.partial(solve_kernel, parts), out_shape=jax.Shap...  15.8 us
    pallas_call x1, Pallas kernels, advect_inside(): pl.pallas_call(inside_kernel, out_shape=outputs, in_specs=[pl.BlockSpec(m...  5.35 us
    ppermute x1, starting transfers between devices, body(): from_east = lax.ppermute(west_cells, 'lon', ring('lon', -1))  5.03 us
    all_to_all x1, starting transfers between devices, body(): lax.all_to_all(sent, ('lon', 'lat'), split_axis=0, concat_axis=0, tiled=T...  3.57 us
    pallas_call x1, Pallas kernels, place_owned(): pl.pallas_call(place_kernel, out_shape=jax.ShapeDtypeStruct((levels, ntr,...  2.12 us
    pallas_call x1, Pallas kernels, pack_halo(): pl.pallas_call(pack_halo_kernel, out_shape=(shape, shape), in_specs=[pl.B...  2.1 us
  transfers between devices with their start and end apart: 3, of which 1 were waited for; matrix products, arithmetic and copies ran while one was open for 0% of the time, Pallas kernels for 7%

profile of v17, /device:TPU:0, one launch (start us, length us, event | category | flops | bytes accessed | tf_op | source)
XLA Modules:
  0.0 80.4 jit_solution(1431783556759612653)
XLA Ops:
  0.0 2.1 %pack_halo.1 = (f32[10,3,8,128]{3,2,1,0:T(8,128)S(1)}, f32[10,3,8,128]{3,2,1,0:T(8,128)S(1)}) custom-call(f32[3,10,64,128]{3,2,1,0:T(8,128)} %tracers_in.3), custom_call_target="tpu_custom_call" | custom-call | tf_op jit(solution)/shard_map/pack_halo/pallas_call | solution.py:71
  2.1 0.5 collective-permute-start
  2.6 5.0 %collective-permute-start.1 = (f32[10,3,8,128]{3,2,1,0:T(8,128)S(1)}, f32[10,3,8,128]{3,2,1,0:T(8,128)S(1)}, u32[]{:S(2)}, u32[]{:S(2)}) collective-permute-start(f32[10,3,8,128]{3,2,1,0:T(8,128)S(1)} %get-tuple-element.15), channel_id=1, source_target_pairs={{0,30},{2,0},{4,2},{6,4},{8,6},{10,8},{12,10},{14,12},{16,14},{18,... | collective-permute-start | bytes 368648 | tf_op jit(solution)/shard_map/ppermute | solution.py:487
  7.6 5.3 %advect_inside.1 = (f32[30,64,128]{2,1,0:T(8,128)}, s32[10,64,128]{2,1,0:T(8,128)}, f32[10,64,128]{2,1,0:T(8,128)}, f32[10,64,128]{2,1,0:T(8,128)}, f32[9,64,128...) custom-call(f32[3,10,64,128]{3,2,1,0:T(8,128)} %tracers_in.3, s32[10,64,128]{2,1,0:T(8,128)} %offsets_in.1, ...), custom_call_target="tpu_custom_call" | custom-call | bytes 20971520 | tf_op jit(solution)/shard_map/advect_inside/pallas_call | solution.py:181
  13.0 0.0 collective-permute-done
  13.0 0.0 collective-permute-done.1
  13.0 15.8 %solve_pick.1 = f32[32,120,128]{2,1,0:T(8,128)} custom-call(f32[30,8,128]{2,1,0:T(8,128)S(1)} %bitcast.7, f32[30,8,128]{2,1,0:T(8,128)S(1)} %bitcast.8, f32[30,64,128]{2,1,0:T(8,128)} %get-tuple-element.16.inside_in, s32[10,64,128]{2,1,0:T(8,128)} %get-tuple-element.17.left_cell_in, f32[10,64,128]{2,1,0:T(8,128)} %get-tuple-element.18.west_edge_in, ...), custom_call_target="tpu_custom_call" | custom-call | bytes 41943040 | tf_op jit(solution)/shard_map/solve_pick/pallas_call | solution.py:395
  28.8 3.6 %all-to-all-start = ((f32[32,15,8,128]{3,2,1,0:T(8,128)}), f32[32,15,8,128]{3,2,1,0:T(8,128)S(1)}, u32[]{:S(2)}, u32[]{:S(2)}) async-start(f32[32,15,8,128]{3,2,1,0:T(8,128)} %bitcast.9), calls=%async_computation | async-start | bytes 3932160 | tf_op jit(solution)/shard_map/all_to_all | solution.py:490
  32.4 45.9 %all-to-all-done = f32[32,15,8,128]{3,2,1,0:T(8,128)S(1)} async-done(((f32[32,15,8,128]{3,2,1,0:T(8,128)}), f32[32,15,8,128]{3,2,1,0:T(8,128)S(1)}, u32[]{:S(2)}, u32[]{:S(2)}) %all-to-all-start) | async-done | bytes 1966112 | tf_op jit(solution)/shard_map/all_to_all | solution.py:490
  78.3 2.1 %place_owned.1 = f32[10,3,8192]{2,1,0:T(4,128)} custom-call(s32[1]{0:T(128)} %bitcast.own, f32[32,120,128]{2,1,0:T(8,128)S(1)} %bitcast.6), custom_call_target="tpu_custom_call" | custom-call | tf_op jit(solution)/shard_map/place_owned/pallas_call | solution.py:462
Async XLA Ops:
  2.1 10.9 %collective-permute-start = (f32[10,3,8,128]{3,2,1,0:T(8,128)S(1)}, f32[10,3,8,128]{3,2,1,0:T(8,128)S(1)}, u32[]{:S(2)}, u32[]{:S(2)}) collective-permute-start(f32[10,3,8,128]{3,2,1,0:T(8,128)S(1)} %get-tuple-element.14), channel_id=1, source_target_pairs={{0,2},{2,4},{4,6},{6,8},{8,10},{10,12},{12,14},{14,16},{16,18},{18... | collective-permute-start | bytes 368648 | tf_op jit(solution)/shard_map/ppermute | solution.py:486
  2.6 10.4 %collective-permute-start.1 = (f32[10,3,8,128]{3,2,1,0:T(8,128)S(1)}, f32[10,3,8,128]{3,2,1,0:T(8,128)S(1)}, u32[]{:S(2)}, u32[]{:S(2)}) collective-permute-start(f32[10,3,8,128]{3,2,1,0:T(8,128)S(1)} %get-tuple-element.15), channel_id=1, source_target_pairs={{0,30},{2,0},{4,2},{6,4},{8,6},{10,8},{12,10},{14,12},{16,14},{18,... | collective-permute-start | bytes 368648 | tf_op jit(solution)/shard_map/ppermute | solution.py:487
  28.8 49.5 %all-to-all-start = ((f32[32,15,8,128]{3,2,1,0:T(8,128)}), f32[32,15,8,128]{3,2,1,0:T(8,128)S(1)}, u32[]{:S(2)}, u32[]{:S(2)}) async-start(f32[32,15,8,128]{3,2,1,0:T(8,128)} %bitcast.9), calls=%async_computation | async-start | bytes 3932160 | tf_op jit(solution)/shard_map/all_to_all | solution.py:490

commit v18 on v16

--- a/solution.py
+++ b/solution.py
@@ -195,8 +195,8 @@
 
     def solve_part(part):
         rows = pl.ds(pl.multiple_of(part * SUB, SUB), SUB)
-        half = part // 4
-        base = (part % 4) * (2 * HALO)
+        half = shift_down(part, 4)
+        base = (part & 3) * (2 * HALO)
         reduced = [[] for _ in range(ntr)]
         for level in range(levels):
             left = left_cell[level, rows, :]
@@ -261,6 +261,10 @@
     lax.fori_loop(0, solved.shape[0] // (LANES * together), some_rows, 0)
 
 
+def shift_down(number, power):
+    return lax.shift_right_logical(number, power.bit_length() - 1)
+
+
 def pick_rows(table, index, count, cap, values, packed, turned, sent, copied, wait_list):
     blocks, height, _ = sent.shape
     parts = cap // LANES
@@ -271,7 +275,7 @@
         return pltpu.make_async_copy(turned.at[block + 1], sent.at[block], copied.at[block])
 
     def turn(block):
-        half = pl.multiple_of(lax.rem(block + 2, 2) * LANES, LANES)
+        half = pl.multiple_of((block & 1) * LANES, LANES)
         return packed[pl.ds(half, LANES), :].T
 
     def send(block, result):
@@ -284,12 +288,12 @@
 
     def one_block(block, carry):
         owners = [block * lists + member for member in range(lists)]
-        rows = [lax.div(count[owner] + (parts - 1), parts) for owner in owners]
+        rows = [shift_down(count[owner] + (parts - 1), parts) for owner in owners]
         for owner in owners:
             wait_list(owner)
         longest = functools.reduce(jnp.maximum, rows)
         places = [owners[g // parts] * cap + (g % parts) * rows[g // parts] for g in range(4)]
-        half = lax.rem(block, 2) * LANES
+        half = (block & 1) * LANES
 
         def load_lines(start, lines):
             views = [index.at[pl.ds(place + start, lines)] for place in places]
@@ -324,10 +328,10 @@
         def _():
             copy_out(block - 1).start()
 
-        eights = jnp.maximum(lax.div(longest + (SUB - 1), SUB) - FIRST // SUB, 0)
-        done = steps(FIRST, lax.div(eights, 4), 4 * SUB)
-        done = steps(done, lax.div(lax.rem(eights, 4), 2), 2 * SUB)
-        steps(done, lax.rem(eights, 2), SUB)
+        eights = jnp.maximum(shift_down(longest + (SUB - 1), SUB) - FIRST // SUB, 0)
+        done = steps(FIRST, shift_down(eights, 4), 4 * SUB)
+        done = steps(done, shift_down(eights & 3, 2), 2 * SUB)
+        steps(done, eights & 1, SUB)
         return carry
 
     def finish(block, carry):
@@ -417,7 +421,8 @@
     values = levels * ntr
     parts = height // values
     lane = lax.broadcasted_iota(jnp.int32, (values, LANES), 1)
-    order = [lax.rem(own[0] - turn + sources, sources) for turn in range(sources)]
+    order = [own[0] - turn for turn in range(sources)]
+    order = [jnp.where(source < 0, source + sources, source) for source in order]
     totals = []
     for source in order:
         note = arrived[source, parts - 1 : parts, :]
@@ -425,11 +430,11 @@
         totals.append(total.astype(jnp.int32)[0, LANES - 1])
     start = 0
     for source, total in zip(order, totals):
-        rows = lax.div(total + (parts - 1), parts)
+        rows = shift_down(total + (parts - 1), parts)
         pieces = []
         for part in range(parts):
             place = start + jnp.minimum(part * rows, total)
-            shift = lax.rem(place, LANES)
+            shift = place & (LANES - 1)
             piece = arrived[source, pl.ds(part, values, stride=parts), :]
             pieces.append((place - shift, shift, pltpu.roll(piece, shift, 1)))
         for tile, shift, rolled in pieces:

time: 79.7 us -> 79.2 us (level)
  no operation moved by 1% of the time
where the time goes in v18:
time: 79.2 us; the launch traced here: 79 us
  waiting for transfers between devices  45.9 us (58%)
  Pallas kernels  23.9 us (30%)
  starting transfers between devices  9.1 us (11%)
    all_to_all x1, waiting for transfers between devices, body(): lax.all_to_all(sent, ('lon', 'lat'), split_axis=0, concat_axis=0, tiled=T...  45.9 us
    pallas_call x1, Pallas kernels, make_sent(): pl.pallas_call(functools.partial(solve_kernel, parts), out_shape=jax.Shap...  14.6 us
    pallas_call x1, Pallas kernels, advect_inside(): pl.pallas_call(inside_kernel, out_shape=outputs, in_specs=[pl.BlockSpec(m...  5.26 us
    ppermute x1, starting transfers between devices, body(): from_east = lax.ppermute(west_cells, 'lon', ring('lon', -1))  5.03 us
    all_to_all x1, starting transfers between devices, body(): lax.all_to_all(sent, ('lon', 'lat'), split_axis=0, concat_axis=0, tiled=T...  3.57 us
    pallas_call x1, Pallas kernels, pack_halo(): pl.pallas_call(pack_halo_kernel, out_shape=(shape, shape), in_specs=[pl.B...  2.1 us
    pallas_call x1, Pallas kernels, place_owned(): pl.pallas_call(place_kernel, out_shape=jax.ShapeDtypeStruct((levels, ntr,...  1.9 us
  transfers between devices with their start and end apart: 3, of which 1 were waited for; matrix products, arithmetic and copies ran while one was open for 0% of the time, Pallas kernels for 7%

profile of v18, /device:TPU:0, one launch (start us, length us, event | category | flops | bytes accessed | tf_op | source)
XLA Modules:
  0.0 79.0 jit_solution(1768579159860649356)
XLA Ops:
  0.0 2.1 %pack_halo.1 = (f32[10,3,8,128]{3,2,1,0:T(8,128)S(1)}, f32[10,3,8,128]{3,2,1,0:T(8,128)S(1)}) custom-call(f32[3,10,64,128]{3,2,1,0:T(8,128)} %tracers_in.3), custom_call_target="tpu_custom_call" | custom-call | tf_op jit(solution)/shard_map/pack_halo/pallas_call | solution.py:70
  2.1 0.5 collective-permute-start
  2.6 5.0 %collective-permute-start.1 = (f32[10,3,8,128]{3,2,1,0:T(8,128)S(1)}, f32[10,3,8,128]{3,2,1,0:T(8,128)S(1)}, u32[]{:S(2)}, u32[]{:S(2)}) collective-permute-start(f32[10,3,8,128]{3,2,1,0:T(8,128)S(1)} %get-tuple-element.15), channel_id=1, source_target_pairs={{0,30},{2,0},{4,2},{6,4},{8,6},{10,8},{12,10},{14,12},{16,14},{18,... | collective-permute-start | bytes 368648 | tf_op jit(solution)/shard_map/ppermute | solution.py:484
  7.6 5.3 %advect_inside.1 = (f32[30,64,128]{2,1,0:T(8,128)}, s32[10,64,128]{2,1,0:T(8,128)}, f32[10,64,128]{2,1,0:T(8,128)}, f32[10,64,128]{2,1,0:T(8,128)}, f32[9,64,128...) custom-call(f32[3,10,64,128]{3,2,1,0:T(8,128)} %tracers_in.3, s32[10,64,128]{2,1,0:T(8,128)} %offsets_in.1, ...), custom_call_target="tpu_custom_call" | custom-call | bytes 20971520 | tf_op jit(solution)/shard_map/advect_inside/pallas_call | solution.py:178
  12.9 0.0 collective-permute-done
  12.9 0.0 collective-permute-done.1
  12.9 14.6 %solve_pick.1 = f32[32,120,128]{2,1,0:T(8,128)} custom-call(f32[30,8,128]{2,1,0:T(8,128)S(1)} %bitcast.7, f32[30,8,128]{2,1,0:T(8,128)S(1)} %bitcast.8, f32[30,64,128]{2,1,0:T(8,128)} %get-tuple-element.16.inside_in, s32[10,64,128]{2,1,0:T(8,128)} %get-tuple-element.17.left_cell_in, f32[10,64,128]{2,1,0:T(8,128)} %get-tuple-element.18.west_edge_in, ...), custom_call_target="tpu_custom_call" | custom-call | bytes 41943040 | tf_op jit(solution)/shard_map/solve_pick/pallas_call | solution.py:391
  27.6 3.6 %all-to-all-start = ((f32[32,15,8,128]{3,2,1,0:T(8,128)}), f32[32,15,8,128]{3,2,1,0:T(8,128)S(1)}, u32[]{:S(2)}, u32[]{:S(2)}) async-start(f32[32,15,8,128]{3,2,1,0:T(8,128)} %bitcast.9), calls=%async_computation | async-start | bytes 3932160 | tf_op jit(solution)/shard_map/all_to_all | solution.py:487
  31.2 45.9 %all-to-all-done = f32[32,15,8,128]{3,2,1,0:T(8,128)S(1)} async-done(((f32[32,15,8,128]{3,2,1,0:T(8,128)}), f32[32,15,8,128]{3,2,1,0:T(8,128)S(1)}, u32[]{:S(2)}, u32[]{:S(2)}) %all-to-all-start) | async-done | bytes 1966112 | tf_op jit(solution)/shard_map/all_to_all | solution.py:487
  77.1 1.9 %place_owned.1 = f32[10,3,8192]{2,1,0:T(4,128)} custom-call(s32[1]{0:T(128)} %bitcast.own, f32[32,120,128]{2,1,0:T(8,128)S(1)} %bitcast.6), custom_call_target="tpu_custom_call" | custom-call | tf_op jit(solution)/shard_map/place_owned/pallas_call | solution.py:459
Async XLA Ops:
  2.1 10.8 %collective-permute-start = (f32[10,3,8,128]{3,2,1,0:T(8,128)S(1)}, f32[10,3,8,128]{3,2,1,0:T(8,128)S(1)}, u32[]{:S(2)}, u32[]{:S(2)}) collective-permute-start(f32[10,3,8,128]{3,2,1,0:T(8,128)S(1)} %get-tuple-element.14), channel_id=1, source_target_pairs={{0,2},{2,4},{4,6},{6,8},{8,10},{10,12},{12,14},{14,16},{16,18},{18... | collective-permute-start | bytes 368648 | tf_op jit(solution)/shard_map/ppermute | solution.py:483
  2.6 10.3 %collective-permute-start.1 = (f32[10,3,8,128]{3,2,1,0:T(8,128)S(1)}, f32[10,3,8,128]{3,2,1,0:T(8,128)S(1)}, u32[]{:S(2)}, u32[]{:S(2)}) collective-permute-start(f32[10,3,8,128]{3,2,1,0:T(8,128)S(1)} %get-tuple-element.15), channel_id=1, source_target_pairs={{0,30},{2,0},{4,2},{6,4},{8,6},{10,8},{12,10},{14,12},{16,14},{18,... | collective-permute-start | bytes 368648 | tf_op jit(solution)/shard_map/ppermute | solution.py:484
  27.6 49.5 %all-to-all-start = ((f32[32,15,8,128]{3,2,1,0:T(8,128)}), f32[32,15,8,128]{3,2,1,0:T(8,128)S(1)}, u32[]{:S(2)}, u32[]{:S(2)}) async-start(f32[32,15,8,128]{3,2,1,0:T(8,128)} %bitcast.9), calls=%async_computation | async-start | bytes 3932160 | tf_op jit(solution)/shard_map/all_to_all | solution.py:487

commit v19 on v18

--- a/solution.py
+++ b/solution.py
@@ -21,6 +21,10 @@
 
 def take_lanes(block, index):
     return jnp.take_along_axis(block, index, axis=1, mode="promise_in_bounds")
+
+
+def shift_down(number, power):
+    return lax.shift_right_logical(number, power.bit_length() - 1)
 
 
 def lane_ids(rows):
@@ -98,9 +102,22 @@
     lax.fori_loop(0, count // chunk, some_values, 0)
 
 
+def edge_place(part):
+    quarter = part & 3
+    group = shift_down(lane_ids(SUB), 2 * HALO) == quarter
+    return shift_down(part, 4), group, (quarter * (2 * HALO) + HALO) & (LANES - 1)
+
+
+def edge_tile(kind, level, half, levels, lats):
+    tile = (kind * levels + level) * 2 + half
+    per_plane = lats // SUB
+    row = pl.multiple_of((tile & (per_plane - 1)) * SUB, SUB)
+    return shift_down(tile, per_plane), pl.ds(row, SUB)
+
+
 def inside_kernel(
     tracers_in, offsets_in, weights_in, diffusion_in, index_in, count,
-    inside, left_cell, west_edge, east_edge, lower, upper, lists,
+    inside, lower, upper, lists,
     tracers, offsets, weights, diffusion, ready,
 ):
     ntr, levels, lats, _ = tracers.shape
@@ -139,7 +156,7 @@
             east_weight = weight * inverse
             left_in = (left >= 0) & (left < LANES)
             right_in = (right >= 0) & (right < LANES)
-            edges.append((left, jnp.where(left_in, 0.0, west_weight), jnp.where(right_in, 0.0, east_weight)))
+            edges.append((left.astype(jnp.float32), jnp.where(left_in, 0.0, west_weight), jnp.where(right_in, 0.0, east_weight)))
             west_weight = jnp.where(left_in, west_weight, 0.0)
             east_weight = jnp.where(right_in, east_weight, 0.0)
             left = left & (LANES - 1)
@@ -149,10 +166,12 @@
                 results.append(west_weight * take_lanes(cells, left) + east_weight * take_lanes(cells, right))
         for value, result in enumerate(results):
             inside[value, rows, :] = result
-        for level, (left, west_weight, east_weight) in enumerate(edges):
-            left_cell[level, rows, :] = left
-            west_edge[level, rows, :] = west_weight
-            east_edge[level, rows, :] = east_weight
+        half, group, shift = edge_place(part)
+        packed = [[pltpu.roll(field, shift, 1) for field in fields] for fields in edges]
+        for level, fields in enumerate(packed):
+            for kind, field in enumerate(fields):
+                plane, band = edge_tile(kind, level, half, levels, lats)
+                pltpu.store(inside.at[ntr * levels + plane, band, :], field, mask=group)
         for level in range(levels - 1):
             lower[level, rows, :] = lowers[level]
             upper[level, rows, :] = uppers[level]
@@ -165,12 +184,10 @@
     ntr, levels, lats, lons = tracers.shape
     lists, cap = index.shape[1:]
     vmem = pl.BlockSpec(memory_space=pltpu.VMEM)
-    field = lambda count, kind=jnp.float32: jax.ShapeDtypeStruct((count, lats, lons), kind)
+    field = lambda count: jax.ShapeDtypeStruct((count, lats, lons), jnp.float32)
+    edge_planes = -(-3 * levels * 2 * SUB // lats)
     outputs = (
-        field(ntr * levels),
-        field(levels, jnp.int32),
-        field(levels),
-        field(levels),
+        field(ntr * levels + edge_planes),
         field(levels - 1),
         field(levels - 1),
         jax.ShapeDtypeStruct((max(lists + SUB, LIST_ROWS), cap), jnp.int32),
@@ -188,27 +205,50 @@
     )(tracers, offsets, weights, diffusion, index, count)
 
 
-def add_edges_and_solve(inside, left_cell, west_edge, east_edge, lower, upper, halo, solved):
-    levels, lats, _ = left_cell.shape
-    ntr = inside.shape[0] // levels
-    together = 2
-
-    def solve_part(part):
-        rows = pl.ds(pl.multiple_of(part * SUB, SUB), SUB)
-        half = shift_down(part, 4)
-        base = (part & 3) * (2 * HALO)
-        reduced = [[] for _ in range(ntr)]
-        for level in range(levels):
-            left = left_cell[level, rows, :]
-            right = base + ((left + (HALO + 1)) & (2 * HALO - 1))
-            left = base + ((left + HALO) & (2 * HALO - 1))
-            west_weight = west_edge[level, rows, :]
-            east_weight = east_edge[level, rows, :]
+def make_edges(fields, halo, edges, levels):
+    ntr = edges.shape[0] // levels
+    lats = fields.shape[1]
+    group = lane_ids(SUB) & (LANES - 2 * HALO)
+
+    def one_level(level, carry):
+        results = []
+        for half in range(2):
+            left, west_weight, east_weight = [
+                fields[plane, band, :]
+                for plane, band in [edge_tile(kind, level, half, levels, lats) for kind in range(3)]
+            ]
+            left = left.astype(jnp.int32) + HALO
+            right = group + ((left + 1) & (2 * HALO - 1))
+            left = group + (left & (2 * HALO - 1))
             for tracer in range(ntr):
                 value = level * ntr + tracer
                 cells = halo[value, half]
-                edges = west_weight * take_lanes(cells, left) + east_weight * take_lanes(cells, right)
-                total = inside[value, rows, :] + edges
+                share = west_weight * take_lanes(cells, left)
+                results.append((value, half, share + east_weight * take_lanes(cells, right)))
+        for value, half, share in results:
+            edges[value, half] = share
+        return carry
+
+    lax.fori_loop(0, levels, one_level, 0)
+
+
+def add_edges_and_solve(inside, lower, upper, edges, solved, together, wait_rows):
+    values, lats, _ = inside.shape
+    levels = upper.shape[0] + 1
+    ntr = values // levels
+    lane = lane_ids(SUB)
+    at_edge = (lane < HALO) | (lane >= LANES - HALO)
+
+    def solve_part(part):
+        rows = pl.ds(pl.multiple_of(part * SUB, SUB), SUB)
+        half, _, shift = edge_place(part)
+        back = (LANES - shift) & (LANES - 1)
+        reduced = [[] for _ in range(ntr)]
+        for level in range(levels):
+            for tracer in range(ntr):
+                value = level * ntr + tracer
+                share = jnp.where(at_edge, pltpu.roll(edges[value, half], back, 1), 0.0)
+                total = inside[value, rows, :] + share
                 if level > 0:
                     total = total + lower[level - 1, rows, :] * reduced[tracer][level - 1]
                 reduced[tracer].append(total)
@@ -222,6 +262,7 @@
         return results
 
     def some_parts(step, carry):
+        wait_rows(step)
         solutions = [solve_part(step * together + item) for item in range(together)]
         for item, results in enumerate(solutions):
             first = pl.multiple_of((step * together + item) * (SUB * SLOT), SUB * SLOT)
@@ -261,10 +302,6 @@
     lax.fori_loop(0, solved.shape[0] // (LANES * together), some_rows, 0)
 
 
-def shift_down(number, power):
-    return lax.shift_right_logical(number, power.bit_length() - 1)
-
-
 def pick_rows(table, index, count, cap, values, packed, turned, sent, copied, wait_list):
     blocks, height, _ = sent.shape
     parts = cap // LANES
@@ -363,27 +400,47 @@
 
 
 def solve_kernel(
-    parts, west, east, inside_in, left_cell_in, west_edge_in, east_edge_in, lower_in, upper_in, lists_in,
-    sent, inside, left_cell, west_edge, east_edge, lower, upper, ready,
-    halo, solved, table, packed, turned, index, count, listed, copied,
+    parts, west, east, inside_in, lower_in, upper_in, lists_in, sent, inside, lower, upper, edge_fields, ready, arrived,
+    halo, edges, solved, table, packed, turned, index, count, listed, copied,
 ):
     values, lats, _ = inside.shape
-    sources = (left_cell_in, west_edge_in, east_edge_in, lower_in, upper_in, inside_in)
-    copies = fetch(sources, (left_cell, west_edge, east_edge, lower, upper, inside), ready)
+    together = 2
+    band = SUB * together
+
+    def row_copies(step):
+        rows = pl.ds(pl.multiple_of(step * band, band), band)
+        return [
+            pltpu.make_async_copy(source.at[: target.shape[0], rows], target.at[:, rows], arrived.at[step, item])
+            for item, (source, target) in enumerate(
+                ((inside_in, inside), (lower_in, lower), (upper_in, upper))
+            )
+        ]
+
+    def wait_rows(step):
+        for copy in row_copies(step):
+            copy.wait()
+
+    copies = fetch([inside_in.at[values:]], [edge_fields], ready)
+    for step in range(lats // band):
+        for copy in row_copies(step):
+            copy.start()
     wait_lengths, wait_list = list_copies(lists_in, index, count, listed)
     for value in range(values, SLOT):
         solved[pl.ds(value, lats, stride=SLOT), :] = jnp.zeros((lats, LANES), jnp.float32)
     merge_halo(west, east, halo, values)
     for copy in copies:
         copy.wait()
-    add_edges_and_solve(inside, left_cell, west_edge, east_edge, lower, upper, halo, solved)
+    make_edges(edge_fields, halo, edges, upper.shape[0] + 1)
+    add_edges_and_solve(inside, lower, upper, edges, solved, together, wait_rows)
     build_table(solved, table.reshape(table.shape[0], LANES), values, parts)
     wait_lengths()
     pick_rows(table, index, count, lists_in.shape[1], values, packed, turned, sent, copied, wait_list)
 
 
 def make_sent(west, east, fields, lists_in, lists):
-    values, lats, lons = fields[0].shape
+    _, lats, lons = fields[0].shape
+    values = west.shape[0] * west.shape[1]
+    edge_planes = fields[0].shape[0] - values
     cap = lists_in.shape[1]
     parts = cap // LANES
     blocks = lists * parts // 4
@@ -393,9 +450,14 @@
         out_shape=jax.ShapeDtypeStruct((blocks, 4 * values, LANES), jnp.float32),
         in_specs=[pl.BlockSpec(memory_space=pltpu.VMEM)] * 2 + [pl.BlockSpec(memory_space=pl.ANY)] * (len(fields) + 1),
         out_specs=pl.BlockSpec(memory_space=pl.ANY),
-        scratch_shapes=[pltpu.VMEM(array.shape, array.dtype) for array in fields]
-        + [
-            pltpu.SemaphoreType.DMA((len(fields),)),
+        scratch_shapes=[
+            pltpu.VMEM((values, lats, lons), jnp.float32),
+            pltpu.VMEM(fields[1].shape, jnp.float32),
+            pltpu.VMEM(fields[2].shape, jnp.float32),
+            pltpu.VMEM((edge_planes, lats, lons), jnp.float32),
+            pltpu.SemaphoreType.DMA((1,)),
+            pltpu.SemaphoreType.DMA((lats // (2 * SUB), 3)),
+            pltpu.VMEM((values, 2, SUB, LANES), jnp.float32),
             pltpu.VMEM((values, 2, SUB, LANES), jnp.float32),
             pltpu.VMEM((lats * SLOT, LANES), jnp.float32),
             pltpu.VMEM((lats * lons, 1, LANES), jnp.float32),

time: 79.2 us -> 79.7 us (level)
  no operation moved by 1% of the time
where the time goes in v19:
time: 79.7 us; the launch traced here: 79.3 us
  waiting for transfers between devices  45.9 us (58%)
  Pallas kernels  24.3 us (30%)
  starting transfers between devices  9.1 us (11%)
    all_to_all x1, waiting for transfers between devices, body(): lax.all_to_all(sent, ('lon', 'lat'), split_axis=0, concat_axis=0, tiled=T...  45.9 us
    pallas_call x1, Pallas kernels, make_sent(): pl.pallas_call(functools.partial(solve_kernel, parts), out_shape=jax.Shap...  14.8 us
    pallas_call x1, Pallas kernels, advect_inside(): pl.pallas_call(inside_kernel, out_shape=outputs, in_specs=[pl.BlockSpec(m...  5.45 us
    ppermute x1, starting transfers between devices, body(): from_east = lax.ppermute(west_cells, 'lon', ring('lon', -1))  5.03 us
    all_to_all x1, starting transfers between devices, body(): lax.all_to_all(sent, ('lon', 'lat'), split_axis=0, concat_axis=0, tiled=T...  3.57 us
    pallas_call x1, Pallas kernels, pack_halo(): pl.pallas_call(pack_halo_kernel, out_shape=(shape, shape), in_specs=[pl.B...  2.1 us
    pallas_call x1, Pallas kernels, place_owned(): pl.pallas_call(place_kernel, out_shape=jax.ShapeDtypeStruct((levels, ntr,...  1.9 us
  transfers between devices with their start and end apart: 3, of which 1 were waited for; matrix products, arithmetic and copies ran while one was open for 0% of the time, Pallas kernels for 7%

profile of v19, /device:TPU:0, one launch (start us, length us, event | category | flops | bytes accessed | tf_op | source)
XLA Modules:
  0.0 79.3 jit_solution(13982424186400245470)
XLA Ops:
  0.0 2.1 %pack_halo.1 = (f32[10,3,8,128]{3,2,1,0:T(8,128)S(1)}, f32[10,3,8,128]{3,2,1,0:T(8,128)S(1)}) custom-call(f32[3,10,64,128]{3,2,1,0:T(8,128)} %tracers_in.3), custom_call_target="tpu_custom_call" | custom-call | tf_op jit(solution)/shard_map/pack_halo/pallas_call | solution.py:74
  2.1 0.5 collective-permute-start
  2.6 5.0 %collective-permute-start.1 = (f32[10,3,8,128]{3,2,1,0:T(8,128)S(1)}, f32[10,3,8,128]{3,2,1,0:T(8,128)S(1)}, u32[]{:S(2)}, u32[]{:S(2)}) collective-permute-start(f32[10,3,8,128]{3,2,1,0:T(8,128)S(1)} %get-tuple-element.12), channel_id=1, source_target_pairs={{0,30},{2,0},{4,2},{6,4},{8,6},{10,8},{12,10},{14,12},{16,14},{18,... | collective-permute-start | bytes 368648 | tf_op jit(solution)/shard_map/ppermute | solution.py:546
  7.6 5.4 %advect_inside.1 = (f32[38,64,128]{2,1,0:T(8,128)}, f32[9,64,128]{2,1,0:T(8,128)}, f32[9,64,128]{2,1,0:T(8,128)}, s32[256,512]{1,0:T(8,128)}) custom-call(f32[3,10,64,128]{3,2,1,0:T(8,128)} %tracers_in.3, s32[10,64,128]{2,1,0:T(8,128)} %offsets_in.1, f32[10,64,128]{2,1,0:T(8,128)} %weights_in.1, f32[9,64,128]{2,1,0:T(8,128)} %diffusion_in.1, ...), custom_call_target="tpu_custom_call" | custom-call | bytes 20971520 | tf_op jit(solution)/shard_map/advect_inside/pallas_call | solution.py:195
  13.1 0.0 collective-permute-done
  13.1 0.0 collective-permute-done.1
  13.1 14.8 %solve_pick.1 = f32[32,120,128]{2,1,0:T(8,128)} custom-call(f32[30,8,128]{2,1,0:T(8,128)S(1)} %bitcast.7, f32[30,8,128]{2,1,0:T(8,128)S(1)} %bitcast.8, f32[38,64,128]{2,1,0:T(8,128)} %get-tuple-element.13.inside_in, f32[9,64,128]{2,1,0:T(8,128)} %get-tuple-element.14.lower_in, f32[9,64,128]{2,1,0:T(8,128)} %get-tuple-element.15.upper_in, ...), custom_call_target="tpu_custom_call" | custom-call | bytes 41943040 | tf_op jit(solution)/shard_map/solve_pick/pallas_call | solution.py:448
  28.0 3.6 %all-to-all-start = ((f32[32,15,8,128]{3,2,1,0:T(8,128)}), f32[32,15,8,128]{3,2,1,0:T(8,128)S(1)}, u32[]{:S(2)}, u32[]{:S(2)}) async-start(f32[32,15,8,128]{3,2,1,0:T(8,128)} %bitcast.9), calls=%async_computation | async-start | bytes 3932160 | tf_op jit(solution)/shard_map/all_to_all | solution.py:549
  31.5 45.9 %all-to-all-done = f32[32,15,8,128]{3,2,1,0:T(8,128)S(1)} async-done(((f32[32,15,8,128]{3,2,1,0:T(8,128)}), f32[32,15,8,128]{3,2,1,0:T(8,128)S(1)}, u32[]{:S(2)}, u32[]{:S(2)}) %all-to-all-start) | async-done | bytes 1966112 | tf_op jit(solution)/shard_map/all_to_all | solution.py:549
  77.4 1.9 %place_owned.1 = f32[10,3,8192]{2,1,0:T(4,128)} custom-call(s32[1]{0:T(128)} %bitcast.own, f32[32,120,128]{2,1,0:T(8,128)S(1)} %bitcast.6), custom_call_target="tpu_custom_call" | custom-call | tf_op jit(solution)/shard_map/place_owned/pallas_call | solution.py:521
Async XLA Ops:
  2.1 11.0 %collective-permute-start = (f32[10,3,8,128]{3,2,1,0:T(8,128)S(1)}, f32[10,3,8,128]{3,2,1,0:T(8,128)S(1)}, u32[]{:S(2)}, u32[]{:S(2)}) collective-permute-start(f32[10,3,8,128]{3,2,1,0:T(8,128)S(1)} %get-tuple-element.11), channel_id=1, source_target_pairs={{0,2},{2,4},{4,6},{6,8},{8,10},{10,12},{12,14},{14,16},{16,18},{18... | collective-permute-start | bytes 368648 | tf_op jit(solution)/shard_map/ppermute | solution.py:545
  2.6 10.5 %collective-permute-start.1 = (f32[10,3,8,128]{3,2,1,0:T(8,128)S(1)}, f32[10,3,8,128]{3,2,1,0:T(8,128)S(1)}, u32[]{:S(2)}, u32[]{:S(2)}) collective-permute-start(f32[10,3,8,128]{3,2,1,0:T(8,128)S(1)} %get-tuple-element.12), channel_id=1, source_target_pairs={{0,30},{2,0},{4,2},{6,4},{8,6},{10,8},{12,10},{14,12},{16,14},{18,... | collective-permute-start | bytes 368648 | tf_op jit(solution)/shard_map/ppermute | solution.py:546
  28.0 49.5 %all-to-all-start = ((f32[32,15,8,128]{3,2,1,0:T(8,128)}), f32[32,15,8,128]{3,2,1,0:T(8,128)S(1)}, u32[]{:S(2)}, u32[]{:S(2)}) async-start(f32[32,15,8,128]{3,2,1,0:T(8,128)} %bitcast.9), calls=%async_computation | async-start | bytes 3932160 | tf_op jit(solution)/shard_map/all_to_all | solution.py:549

commit v20 on v18

--- a/solution.py
+++ b/solution.py
@@ -245,7 +245,7 @@
 def build_table(solved, table, values, parts):
     rows_per = LANES // SLOT
     spread = streams_of(LANES, values, parts)[0]
-    together = 4
+    together = 8
 
     def some_rows(step, carry):
         blocks = []
@@ -317,7 +317,6 @@
                 return inner
 
             lax.fori_loop(0, trips, one_step, 0)
-            return begin + trips * lines
 
         before = turn(block - 1)
         merged = load_lines(0, FIRST)
@@ -329,9 +328,18 @@
             copy_out(block - 1).start()
 
         eights = jnp.maximum(shift_down(longest + (SUB - 1), SUB) - FIRST // SUB, 0)
-        done = steps(FIRST, shift_down(eights, 4), 4 * SUB)
-        done = steps(done, shift_down(eights & 3, 2), 2 * SUB)
-        steps(done, eights & 1, SUB)
+        steps(FIRST, shift_down(eights, 4), 4 * SUB)
+
+        @pl.when((eights & 2) != 0)
+        def _():
+            start = pl.multiple_of(FIRST + shift_down(eights, 4) * (4 * SUB), SUB)
+            store_lines(start, load_lines(start, 2 * SUB))
+
+        @pl.when((eights & 1) != 0)
+        def _():
+            start = pl.multiple_of(FIRST + (eights - 1) * SUB, SUB)
+            store_lines(start, load_lines(start, SUB))
+
         return carry
 
     def finish(block, carry):

time: 79.2 us -> 79 us (level)
  no operation moved by 1% of the time
where the time goes in v20:
time: 79 us; the launch traced here: 78.8 us
  waiting for transfers between devices  45.9 us (58%)
  Pallas kernels  23.7 us (30%)
  starting transfers between devices  9.1 us (12%)
    all_to_all x1, waiting for transfers between devices, body(): lax.all_to_all(sent, ('lon', 'lat'), split_axis=0, concat_axis=0, tiled=T...  45.9 us
    pallas_call x1, Pallas kernels, make_sent(): pl.pallas_call(functools.partial(solve_kernel, parts), out_shape=jax.Shap...  14.5 us
    pallas_call x1, Pallas kernels, advect_inside(): pl.pallas_call(inside_kernel, out_shape=outputs, in_specs=[pl.BlockSpec(m...  5.26 us
    ppermute x1, starting transfers between devices, body(): from_east = lax.ppermute(west_cells, 'lon', ring('lon', -1))  5.03 us
    all_to_all x1, starting transfers between devices, body(): lax.all_to_all(sent, ('lon', 'lat'), split_axis=0, concat_axis=0, tiled=T...  3.57 us
    pallas_call x1, Pallas kernels, pack_halo(): pl.pallas_call(pack_halo_kernel, out_shape=(shape, shape), in_specs=[pl.B...  2.1 us
    pallas_call x1, Pallas kernels, place_owned(): pl.pallas_call(place_kernel, out_shape=jax.ShapeDtypeStruct((levels, ntr,...  1.9 us
  transfers between devices with their start and end apart: 3, of which 1 were waited for; matrix products, arithmetic and copies ran while one was open for 0% of the time, Pallas kernels for 7%

profile of v20, /device:TPU:0, one launch (start us, length us, event | category | flops | bytes accessed | tf_op | source)
XLA Modules:
  0.0 78.8 jit_solution(6209773960365571453)
XLA Ops:
  0.0 2.1 %pack_halo.1 = (f32[10,3,8,128]{3,2,1,0:T(8,128)S(1)}, f32[10,3,8,128]{3,2,1,0:T(8,128)S(1)}) custom-call(f32[3,10,64,128]{3,2,1,0:T(8,128)} %tracers_in.3), custom_call_target="tpu_custom_call" | custom-call | tf_op jit(solution)/shard_map/pack_halo/pallas_call | solution.py:70
  2.1 0.5 collective-permute-start
  2.6 5.0 %collective-permute-start.1 = (f32[10,3,8,128]{3,2,1,0:T(8,128)S(1)}, f32[10,3,8,128]{3,2,1,0:T(8,128)S(1)}, u32[]{:S(2)}, u32[]{:S(2)}) collective-permute-start(f32[10,3,8,128]{3,2,1,0:T(8,128)S(1)} %get-tuple-element.15), channel_id=1, source_target_pairs={{0,30},{2,0},{4,2},{6,4},{8,6},{10,8},{12,10},{14,12},{16,14},{18,... | collective-permute-start | bytes 368648 | tf_op jit(solution)/shard_map/ppermute | solution.py:492
  7.6 5.3 %advect_inside.1 = (f32[30,64,128]{2,1,0:T(8,128)}, s32[10,64,128]{2,1,0:T(8,128)}, f32[10,64,128]{2,1,0:T(8,128)}, f32[10,64,128]{2,1,0:T(8,128)}, f32[9,64,128...) custom-call(f32[3,10,64,128]{3,2,1,0:T(8,128)} %tracers_in.3, s32[10,64,128]{2,1,0:T(8,128)} %offsets_in.1, ...), custom_call_target="tpu_custom_call" | custom-call | bytes 20971520 | tf_op jit(solution)/shard_map/advect_inside/pallas_call | solution.py:178
  12.9 0.0 collective-permute-done
  12.9 0.0 collective-permute-done.1
  12.9 14.5 %solve_pick.1 = f32[32,120,128]{2,1,0:T(8,128)} custom-call(f32[30,8,128]{2,1,0:T(8,128)S(1)} %bitcast.7, f32[30,8,128]{2,1,0:T(8,128)S(1)} %bitcast.8, f32[30,64,128]{2,1,0:T(8,128)} %get-tuple-element.16.inside_in, s32[10,64,128]{2,1,0:T(8,128)} %get-tuple-element.17.left_cell_in, f32[10,64,128]{2,1,0:T(8,128)} %get-tuple-element.18.west_edge_in, ...), custom_call_target="tpu_custom_call" | custom-call | bytes 41943040 | tf_op jit(solution)/shard_map/solve_pick/pallas_call | solution.py:399
  27.4 3.6 %all-to-all-start = ((f32[32,15,8,128]{3,2,1,0:T(8,128)}), f32[32,15,8,128]{3,2,1,0:T(8,128)S(1)}, u32[]{:S(2)}, u32[]{:S(2)}) async-start(f32[32,15,8,128]{3,2,1,0:T(8,128)} %bitcast.9), calls=%async_computation | async-start | bytes 3932160 | tf_op jit(solution)/shard_map/all_to_all | solution.py:495
  31.0 45.9 %all-to-all-done = f32[32,15,8,128]{3,2,1,0:T(8,128)S(1)} async-done(((f32[32,15,8,128]{3,2,1,0:T(8,128)}), f32[32,15,8,128]{3,2,1,0:T(8,128)S(1)}, u32[]{:S(2)}, u32[]{:S(2)}) %all-to-all-start) | async-done | bytes 1966112 | tf_op jit(solution)/shard_map/all_to_all | solution.py:495
  76.9 1.9 %place_owned.1 = f32[10,3,8192]{2,1,0:T(4,128)} custom-call(s32[1]{0:T(128)} %bitcast.own, f32[32,120,128]{2,1,0:T(8,128)S(1)} %bitcast.6), custom_call_target="tpu_custom_call" | custom-call | tf_op jit(solution)/shard_map/place_owned/pallas_call | solution.py:467
Async XLA Ops:
  2.1 10.8 %collective-permute-start = (f32[10,3,8,128]{3,2,1,0:T(8,128)S(1)}, f32[10,3,8,128]{3,2,1,0:T(8,128)S(1)}, u32[]{:S(2)}, u32[]{:S(2)}) collective-permute-start(f32[10,3,8,128]{3,2,1,0:T(8,128)S(1)} %get-tuple-element.14), channel_id=1, source_target_pairs={{0,2},{2,4},{4,6},{6,8},{8,10},{10,12},{12,14},{14,16},{16,18},{18... | collective-permute-start | bytes 368648 | tf_op jit(solution)/shard_map/ppermute | solution.py:491
  2.6 10.3 %collective-permute-start.1 = (f32[10,3,8,128]{3,2,1,0:T(8,128)S(1)}, f32[10,3,8,128]{3,2,1,0:T(8,128)S(1)}, u32[]{:S(2)}, u32[]{:S(2)}) collective-permute-start(f32[10,3,8,128]{3,2,1,0:T(8,128)S(1)} %get-tuple-element.15), channel_id=1, source_target_pairs={{0,30},{2,0},{4,2},{6,4},{8,6},{10,8},{12,10},{14,12},{16,14},{18,... | collective-permute-start | bytes 368648 | tf_op jit(solution)/shard_map/ppermute | solution.py:492
  27.4 49.5 %all-to-all-start = ((f32[32,15,8,128]{3,2,1,0:T(8,128)}), f32[32,15,8,128]{3,2,1,0:T(8,128)S(1)}, u32[]{:S(2)}, u32[]{:S(2)}) async-start(f32[32,15,8,128]{3,2,1,0:T(8,128)} %bitcast.9), calls=%async_computation | async-start | bytes 3932160 | tf_op jit(solution)/shard_map/all_to_all | solution.py:495

commit v21 on v20

--- a/solution.py
+++ b/solution.py
@@ -271,84 +271,95 @@
     lists = 4 // parts
     stream = streams_of(1, values, parts)[1]
 
+    together = 2 if blocks % 2 == 0 else 1
+
     def copy_out(block):
-        return pltpu.make_async_copy(turned.at[block + 1], sent.at[block], copied.at[block])
+        return pltpu.make_async_copy(turned.at[block + together], sent.at[block], copied.at[block])
+
+    def buffer_of(block):
+        return pl.multiple_of((block & (2 * together - 1)) * LANES, LANES)
 
     def turn(block):
-        half = pl.multiple_of((block & 1) * LANES, LANES)
-        return packed[pl.ds(half, LANES), :].T
+        return packed[pl.ds(buffer_of(block), LANES), :].T
 
     def send(block, result):
-        turned[block + 1] = result[:height, :]
+        turned[block + together] = result[:height, :]
         for member in range(lists):
             total = count[jnp.maximum(block, 0) * lists + member]
-            row = turned.at[block + 1, pl.ds((member * values + 1) * parts - 1, 1), :]
+            row = turned.at[block + together, pl.ds((member * values + 1) * parts - 1, 1), :]
             note = jnp.full((1, LANES), LENGTH_BASE + total.astype(jnp.float32))
             pltpu.store(row, note, mask=(lane_ids(1) == LANES - 1) & (total < cap))
 
-    def one_block(block, carry):
+    def plan(block):
         owners = [block * lists + member for member in range(lists)]
         rows = [shift_down(count[owner] + (parts - 1), parts) for owner in owners]
         for owner in owners:
             wait_list(owner)
         longest = functools.reduce(jnp.maximum, rows)
-        places = [owners[g // parts] * cap + (g % parts) * rows[g // parts] for g in range(4)]
-        half = (block & 1) * LANES
-
-        def load_lines(start, lines):
-            views = [index.at[pl.ds(place + start, lines)] for place in places]
-            merged = []
-            for line in range(lines):
-                picked = [table[view[line]] for view in views]
-                low = jnp.where(stream == 0, picked[0], picked[1])
-                high = jnp.where(stream == 2, picked[2], picked[3])
-                merged.append(jnp.where(stream < 2, low, high))
-            return merged
-
-        def store_lines(start, merged):
-            target = packed.at[pl.ds(pl.multiple_of(half + start, SUB), len(merged)), :]
-            for line, value in enumerate(merged):
-                target[line : line + 1, :] = value
-
-        def steps(begin, trips, lines):
-            def one_step(step, inner):
-                start = pl.multiple_of(begin + step * lines, SUB)
-                store_lines(start, load_lines(start, lines))
-                return inner
-
-            lax.fori_loop(0, trips, one_step, 0)
-
-        before = turn(block - 1)
-        merged = load_lines(0, FIRST)
-        store_lines(0, merged)
-        send(block - 1, before)
-
-        @pl.when(block > 0)
-        def _():
-            copy_out(block - 1).start()
-
         eights = jnp.maximum(shift_down(longest + (SUB - 1), SUB) - FIRST // SUB, 0)
-        steps(FIRST, shift_down(eights, 4), 4 * SUB)
+        return eights, [owners[g // parts] * cap + (g % parts) * rows[g // parts] for g in range(4)]
+
+    def load_lines(places, start, lines):
+        views = [index.at[pl.ds(place + start, lines)] for place in places]
+        merged = []
+        for line in range(lines):
+            picked = [table[view[line]] for view in views]
+            low = jnp.where(stream == 0, picked[0], picked[1])
+            high = jnp.where(stream == 2, picked[2], picked[3])
+            merged.append(jnp.where(stream < 2, low, high))
+        return merged
+
+    def store_lines(block, start, merged):
+        target = packed.at[pl.ds(pl.multiple_of(buffer_of(block) + start, SUB), len(merged)), :]
+        for line, value in enumerate(merged):
+            target[line : line + 1, :] = value
+
+    def finish_block(block, eights, places):
+        def one_step(step, inner):
+            start = pl.multiple_of(FIRST + step * (4 * SUB), SUB)
+            store_lines(block, start, load_lines(places, start, 4 * SUB))
+            return inner
+
+        lax.fori_loop(0, shift_down(eights, 4), one_step, 0)
 
         @pl.when((eights & 2) != 0)
         def _():
             start = pl.multiple_of(FIRST + shift_down(eights, 4) * (4 * SUB), SUB)
-            store_lines(start, load_lines(start, 2 * SUB))
+            store_lines(block, start, load_lines(places, start, 2 * SUB))
 
         @pl.when((eights & 1) != 0)
         def _():
             start = pl.multiple_of(FIRST + (eights - 1) * SUB, SUB)
-            store_lines(start, load_lines(start, SUB))
-
+            store_lines(block, start, load_lines(places, start, SUB))
+
+    def some_blocks(step, carry):
+        group = [step * together + item for item in range(together)]
+        plans = [plan(block) for block in group]
+        before = [turn(block - together) for block in group]
+        merged = [load_lines(places, 0, FIRST) for _, places in plans]
+        for block, lines in zip(group, merged):
+            store_lines(block, 0, lines)
+        for block, result in zip(group, before):
+            send(block - together, result)
+
+        @pl.when(step > 0)
+        def _():
+            for block in group:
+                copy_out(block - together).start()
+
+        for block, (eights, places) in zip(group, plans):
+            finish_block(block, eights, places)
         return carry
 
     def finish(block, carry):
         copy_out(block).wait()
         return carry
 
-    lax.fori_loop(0, blocks, one_block, 0)
-    send(blocks - 1, turn(blocks - 1))
-    copy_out(blocks - 1).start()
+    lax.fori_loop(0, blocks // together, some_blocks, 0)
+    last = range(blocks - together, blocks)
+    for block, result in zip(last, [turn(block) for block in last]):
+        send(block, result)
+        copy_out(block).start()
     lax.fori_loop(0, blocks, finish, 0)
 
 
@@ -407,8 +418,8 @@
             pltpu.VMEM((values, 2, SUB, LANES), jnp.float32),
             pltpu.VMEM((lats * SLOT, LANES), jnp.float32),
             pltpu.VMEM((lats * lons, 1, LANES), jnp.float32),
-            pltpu.VMEM((2 * LANES, LANES), jnp.float32),
-            pltpu.VMEM((blocks + 1, 4 * values, LANES), jnp.float32),
+            pltpu.VMEM((4 * LANES, LANES), jnp.float32),
+            pltpu.VMEM((blocks + 2, 4 * values, LANES), jnp.float32),
             pltpu.SMEM((lists * cap,), jnp.int32),
             pltpu.SMEM((cap,), jnp.int32),
             pltpu.SemaphoreType.DMA((lists + 1,)),

time: 79 us -> 79.2 us (level)
  no operation moved by 1% of the time
where the time goes in v21:
time: 79.2 us; the launch traced here: 78.9 us
  waiting for transfers between devices  45.9 us (58%)
  Pallas kernels  23.8 us (30%)
  starting transfers between devices  9.1 us (11%)
    all_to_all x1, waiting for transfers between devices, body(): lax.all_to_all(sent, ('lon', 'lat'), split_axis=0, concat_axis=0, tiled=T...  45.9 us
    pallas_call x1, Pallas kernels, make_sent(): pl.pallas_call(functools.partial(solve_kernel, parts), out_shape=jax.Shap...  14.6 us
    pallas_call x1, Pallas kernels, advect_inside(): pl.pallas_call(inside_kernel, out_shape=outputs, in_specs=[pl.BlockSpec(m...  5.26 us
    ppermute x1, starting transfers between devices, body(): from_east = lax.ppermute(west_cells, 'lon', ring('lon', -1))  5.03 us
    all_to_all x1, starting transfers between devices, body(): lax.all_to_all(sent, ('lon', 'lat'), split_axis=0, concat_axis=0, tiled=T...  3.56 us
    pallas_call x1, Pallas kernels, pack_halo(): pl.pallas_call(pack_halo_kernel, out_shape=(shape, shape), in_specs=[pl.B...  2.1 us
    pallas_call x1, Pallas kernels, place_owned(): pl.pallas_call(place_kernel, out_shape=jax.ShapeDtypeStruct((levels, ntr,...  1.9 us
  transfers between devices with their start and end apart: 3, of which 1 were waited for; matrix products, arithmetic and copies ran while one was open for 0% of the time, Pallas kernels for 7%

profile of v21, /device:TPU:0, one launch (start us, length us, event | category | flops | bytes accessed | tf_op | source)
XLA Modules:
  0.0 78.9 jit_solution(17755609564993800332)
XLA Ops:
  0.0 2.1 %pack_halo.1 = (f32[10,3,8,128]{3,2,1,0:T(8,128)S(1)}, f32[10,3,8,128]{3,2,1,0:T(8,128)S(1)}) custom-call(f32[3,10,64,128]{3,2,1,0:T(8,128)} %tracers_in.3), custom_call_target="tpu_custom_call" | custom-call | tf_op jit(solution)/shard_map/pack_halo/pallas_call | solution.py:70
  2.1 0.5 collective-permute-start
  2.6 5.0 %collective-permute-start.1 = (f32[10,3,8,128]{3,2,1,0:T(8,128)S(1)}, f32[10,3,8,128]{3,2,1,0:T(8,128)S(1)}, u32[]{:S(2)}, u32[]{:S(2)}) collective-permute-start(f32[10,3,8,128]{3,2,1,0:T(8,128)S(1)} %get-tuple-element.15), channel_id=1, source_target_pairs={{0,30},{2,0},{4,2},{6,4},{8,6},{10,8},{12,10},{14,12},{16,14},{18,... | collective-permute-start | bytes 368648 | tf_op jit(solution)/shard_map/ppermute | solution.py:503
  7.6 5.3 %advect_inside.1 = (f32[30,64,128]{2,1,0:T(8,128)}, s32[10,64,128]{2,1,0:T(8,128)}, f32[10,64,128]{2,1,0:T(8,128)}, f32[10,64,128]{2,1,0:T(8,128)}, f32[9,64,128...) custom-call(f32[3,10,64,128]{3,2,1,0:T(8,128)} %tracers_in.3, s32[10,64,128]{2,1,0:T(8,128)} %offsets_in.1, ...), custom_call_target="tpu_custom_call" | custom-call | bytes 20971520 | tf_op jit(solution)/shard_map/advect_inside/pallas_call | solution.py:178
  12.9 0.0 collective-permute-done
  12.9 0.0 collective-permute-done.1
  12.9 14.6 %solve_pick.1 = f32[32,120,128]{2,1,0:T(8,128)} custom-call(f32[30,8,128]{2,1,0:T(8,128)S(1)} %bitcast.7, f32[30,8,128]{2,1,0:T(8,128)S(1)} %bitcast.8, f32[30,64,128]{2,1,0:T(8,128)} %get-tuple-element.16.inside_in, s32[10,64,128]{2,1,0:T(8,128)} %get-tuple-element.17.left_cell_in, f32[10,64,128]{2,1,0:T(8,128)} %get-tuple-element.18.west_edge_in, ...), custom_call_target="tpu_custom_call" | custom-call | bytes 41943040 | tf_op jit(solution)/shard_map/solve_pick/pallas_call | solution.py:410
  27.5 3.6 %all-to-all-start = ((f32[32,15,8,128]{3,2,1,0:T(8,128)}), f32[32,15,8,128]{3,2,1,0:T(8,128)S(1)}, u32[]{:S(2)}, u32[]{:S(2)}) async-start(f32[32,15,8,128]{3,2,1,0:T(8,128)} %bitcast.9), calls=%async_computation | async-start | bytes 3932160 | tf_op jit(solution)/shard_map/all_to_all | solution.py:506
  31.1 45.9 %all-to-all-done = f32[32,15,8,128]{3,2,1,0:T(8,128)S(1)} async-done(((f32[32,15,8,128]{3,2,1,0:T(8,128)}), f32[32,15,8,128]{3,2,1,0:T(8,128)S(1)}, u32[]{:S(2)}, u32[]{:S(2)}) %all-to-all-start) | async-done | bytes 1966112 | tf_op jit(solution)/shard_map/all_to_all | solution.py:506
  77.0 1.9 %place_owned.1 = f32[10,3,8192]{2,1,0:T(4,128)} custom-call(s32[1]{0:T(128)} %bitcast.own, f32[32,120,128]{2,1,0:T(8,128)S(1)} %bitcast.6), custom_call_target="tpu_custom_call" | custom-call | tf_op jit(solution)/shard_map/place_owned/pallas_call | solution.py:478
Async XLA Ops:
  2.1 10.8 %collective-permute-start = (f32[10,3,8,128]{3,2,1,0:T(8,128)S(1)}, f32[10,3,8,128]{3,2,1,0:T(8,128)S(1)}, u32[]{:S(2)}, u32[]{:S(2)}) collective-permute-start(f32[10,3,8,128]{3,2,1,0:T(8,128)S(1)} %get-tuple-element.14), channel_id=1, source_target_pairs={{0,2},{2,4},{4,6},{6,8},{8,10},{10,12},{12,14},{14,16},{16,18},{18... | collective-permute-start | bytes 368648 | tf_op jit(solution)/shard_map/ppermute | solution.py:502
  2.6 10.3 %collective-permute-start.1 = (f32[10,3,8,128]{3,2,1,0:T(8,128)S(1)}, f32[10,3,8,128]{3,2,1,0:T(8,128)S(1)}, u32[]{:S(2)}, u32[]{:S(2)}) collective-permute-start(f32[10,3,8,128]{3,2,1,0:T(8,128)S(1)} %get-tuple-element.15), channel_id=1, source_target_pairs={{0,30},{2,0},{4,2},{6,4},{8,6},{10,8},{12,10},{14,12},{16,14},{18,... | collective-permute-start | bytes 368648 | tf_op jit(solution)/shard_map/ppermute | solution.py:503
  27.5 49.5 %all-to-all-start = ((f32[32,15,8,128]{3,2,1,0:T(8,128)}), f32[32,15,8,128]{3,2,1,0:T(8,128)S(1)}, u32[]{:S(2)}, u32[]{:S(2)}) async-start(f32[32,15,8,128]{3,2,1,0:T(8,128)} %bitcast.9), calls=%async_computation | async-start | bytes 3932160 | tf_op jit(solution)/shard_map/all_to_all | solution.py:506

commit v22 on v20

--- a/solution.py
+++ b/solution.py
@@ -11,7 +11,7 @@
 LANES = 128
 SUB = 8
 SLOT = 32
-FIRST = 32
+FIRST = 24
 MIB = 1024 * 1024
 LENGTH_BASE = 1000.0
 BIG = 60 * MIB

time: 79 us -> 79.4 us (level)
  no operation moved by 1% of the time
where the time goes in v22:
time: 79.4 us; the launch traced here: 79 us
  waiting for transfers between devices  45.9 us (58%)
  Pallas kernels  24 us (30%)
  starting transfers between devices  9.1 us (11%)
    all_to_all x1, waiting for transfers between devices, body(): lax.all_to_all(sent, ('lon', 'lat'), split_axis=0, concat_axis=0, tiled=T...  45.9 us
    pallas_call x1, Pallas kernels, make_sent(): pl.pallas_call(functools.partial(solve_kernel, parts), out_shape=jax.Shap...  14.7 us
    pallas_call x1, Pallas kernels, advect_inside(): pl.pallas_call(inside_kernel, out_shape=outputs, in_specs=[pl.BlockSpec(m...  5.26 us
    ppermute x1, starting transfers between devices, body(): from_east = lax.ppermute(west_cells, 'lon', ring('lon', -1))  5.03 us
    all_to_all x1, starting transfers between devices, body(): lax.all_to_all(sent, ('lon', 'lat'), split_axis=0, concat_axis=0, tiled=T...  3.57 us
    pallas_call x1, Pallas kernels, pack_halo(): pl.pallas_call(pack_halo_kernel, out_shape=(shape, shape), in_specs=[pl.B...  2.1 us
    pallas_call x1, Pallas kernels, place_owned(): pl.pallas_call(place_kernel, out_shape=jax.ShapeDtypeStruct((levels, ntr,...  1.9 us
  transfers between devices with their start and end apart: 3, of which 1 were waited for; matrix products, arithmetic and copies ran while one was open for 0% of the time, Pallas kernels for 7%

profile of v22, /device:TPU:0, one launch (start us, length us, event | category | flops | bytes accessed | tf_op | source)
XLA Modules:
  0.0 79.0 jit_solution(16834916602424376483)
XLA Ops:
  0.0 2.1 %pack_halo.1 = (f32[10,3,8,128]{3,2,1,0:T(8,128)S(1)}, f32[10,3,8,128]{3,2,1,0:T(8,128)S(1)}) custom-call(f32[3,10,64,128]{3,2,1,0:T(8,128)} %tracers_in.3), custom_call_target="tpu_custom_call" | custom-call | tf_op jit(solution)/shard_map/pack_halo/pallas_call | solution.py:70
  2.1 0.5 collective-permute-start
  2.6 5.0 %collective-permute-start.1 = (f32[10,3,8,128]{3,2,1,0:T(8,128)S(1)}, f32[10,3,8,128]{3,2,1,0:T(8,128)S(1)}, u32[]{:S(2)}, u32[]{:S(2)}) collective-permute-start(f32[10,3,8,128]{3,2,1,0:T(8,128)S(1)} %get-tuple-element.15), channel_id=1, source_target_pairs={{0,30},{2,0},{4,2},{6,4},{8,6},{10,8},{12,10},{14,12},{16,14},{18,... | collective-permute-start | bytes 368648 | tf_op jit(solution)/shard_map/ppermute | solution.py:492
  7.6 5.3 %advect_inside.1 = (f32[30,64,128]{2,1,0:T(8,128)}, s32[10,64,128]{2,1,0:T(8,128)}, f32[10,64,128]{2,1,0:T(8,128)}, f32[10,64,128]{2,1,0:T(8,128)}, f32[9,64,128...) custom-call(f32[3,10,64,128]{3,2,1,0:T(8,128)} %tracers_in.3, s32[10,64,128]{2,1,0:T(8,128)} %offsets_in.1, ...), custom_call_target="tpu_custom_call" | custom-call | bytes 20971520 | tf_op jit(solution)/shard_map/advect_inside/pallas_call | solution.py:178
  12.9 0.0 collective-permute-done
  12.9 0.0 collective-permute-done.1
  12.9 14.7 %solve_pick.1 = f32[32,120,128]{2,1,0:T(8,128)} custom-call(f32[30,8,128]{2,1,0:T(8,128)S(1)} %bitcast.7, f32[30,8,128]{2,1,0:T(8,128)S(1)} %bitcast.8, f32[30,64,128]{2,1,0:T(8,128)} %get-tuple-element.16.inside_in, s32[10,64,128]{2,1,0:T(8,128)} %get-tuple-element.17.left_cell_in, f32[10,64,128]{2,1,0:T(8,128)} %get-tuple-element.18.west_edge_in, ...), custom_call_target="tpu_custom_call" | custom-call | bytes 41943040 | tf_op jit(solution)/shard_map/solve_pick/pallas_call | solution.py:399
  27.7 3.6 %all-to-all-start = ((f32[32,15,8,128]{3,2,1,0:T(8,128)}), f32[32,15,8,128]{3,2,1,0:T(8,128)S(1)}, u32[]{:S(2)}, u32[]{:S(2)}) async-start(f32[32,15,8,128]{3,2,1,0:T(8,128)} %bitcast.9), calls=%async_computation | async-start | bytes 3932160 | tf_op jit(solution)/shard_map/all_to_all | solution.py:495
  31.3 45.9 %all-to-all-done = f32[32,15,8,128]{3,2,1,0:T(8,128)S(1)} async-done(((f32[32,15,8,128]{3,2,1,0:T(8,128)}), f32[32,15,8,128]{3,2,1,0:T(8,128)S(1)}, u32[]{:S(2)}, u32[]{:S(2)}) %all-to-all-start) | async-done | bytes 1966112 | tf_op jit(solution)/shard_map/all_to_all | solution.py:495
  77.1 1.9 %place_owned.1 = f32[10,3,8192]{2,1,0:T(4,128)} custom-call(s32[1]{0:T(128)} %bitcast.own, f32[32,120,128]{2,1,0:T(8,128)S(1)} %bitcast.6), custom_call_target="tpu_custom_call" | custom-call | tf_op jit(solution)/shard_map/place_owned/pallas_call | solution.py:467
Async XLA Ops:
  2.1 10.8 %collective-permute-start = (f32[10,3,8,128]{3,2,1,0:T(8,128)S(1)}, f32[10,3,8,128]{3,2,1,0:T(8,128)S(1)}, u32[]{:S(2)}, u32[]{:S(2)}) collective-permute-start(f32[10,3,8,128]{3,2,1,0:T(8,128)S(1)} %get-tuple-element.14), channel_id=1, source_target_pairs={{0,2},{2,4},{4,6},{6,8},{8,10},{10,12},{12,14},{14,16},{16,18},{18... | collective-permute-start | bytes 368648 | tf_op jit(solution)/shard_map/ppermute | solution.py:491
  2.6 10.3 %collective-permute-start.1 = (f32[10,3,8,128]{3,2,1,0:T(8,128)S(1)}, f32[10,3,8,128]{3,2,1,0:T(8,128)S(1)}, u32[]{:S(2)}, u32[]{:S(2)}) collective-permute-start(f32[10,3,8,128]{3,2,1,0:T(8,128)S(1)} %get-tuple-element.15), channel_id=1, source_target_pairs={{0,30},{2,0},{4,2},{6,4},{8,6},{10,8},{12,10},{14,12},{16,14},{18,... | collective-permute-start | bytes 368648 | tf_op jit(solution)/shard_map/ppermute | solution.py:492
  27.7 49.5 %all-to-all-start = ((f32[32,15,8,128]{3,2,1,0:T(8,128)}), f32[32,15,8,128]{3,2,1,0:T(8,128)S(1)}, u32[]{:S(2)}, u32[]{:S(2)}) async-start(f32[32,15,8,128]{3,2,1,0:T(8,128)} %bitcast.9), calls=%async_computation | async-start | bytes 3932160 | tf_op jit(solution)/shard_map/all_to_all | solution.py:495

commit v23 on v22

--- a/solution.py
+++ b/solution.py
@@ -11,7 +11,7 @@
 LANES = 128
 SUB = 8
 SLOT = 32
-FIRST = 24
+FIRST = 40
 MIB = 1024 * 1024
 LENGTH_BASE = 1000.0
 BIG = 60 * MIB

time: 79.4 us -> 78.7 us (level)
  no operation moved by 1% of the time
where the time goes in v23:
time: 78.7 us; the launch traced here: 78.5 us
  waiting for transfers between devices  45.9 us (58%)
  Pallas kernels  23.5 us (30%)
  starting transfers between devices  9.1 us (12%)
    all_to_all x1, waiting for transfers between devices, body(): lax.all_to_all(sent, ('lon', 'lat'), split_axis=0, concat_axis=0, tiled=T...  45.9 us
    pallas_call x1, Pallas kernels, make_sent(): pl.pallas_call(functools.partial(solve_kernel, parts), out_shape=jax.Shap...  14.2 us
    pallas_call x1, Pallas kernels, advect_inside(): pl.pallas_call(inside_kernel, out_shape=outputs, in_specs=[pl.BlockSpec(m...  5.26 us
    ppermute x1, starting transfers between devices, body(): from_east = lax.ppermute(west_cells, 'lon', ring('lon', -1))  5.03 us
    all_to_all x1, starting transfers between devices, body(): lax.all_to_all(sent, ('lon', 'lat'), split_axis=0, concat_axis=0, tiled=T...  3.57 us
    pallas_call x1, Pallas kernels, pack_halo(): pl.pallas_call(pack_halo_kernel, out_shape=(shape, shape), in_specs=[pl.B...  2.1 us
    pallas_call x1, Pallas kernels, place_owned(): pl.pallas_call(place_kernel, out_shape=jax.ShapeDtypeStruct((levels, ntr,...  1.9 us
  transfers between devices with their start and end apart: 3, of which 1 were waited for; matrix products, arithmetic and copies ran while one was open for 0% of the time, Pallas kernels for 7%

profile of v23, /device:TPU:0, one launch (start us, length us, event | category | flops | bytes accessed | tf_op | source)
XLA Modules:
  0.0 78.5 jit_solution(18026654932559116362)
XLA Ops:
  0.0 2.1 %pack_halo.1 = (f32[10,3,8,128]{3,2,1,0:T(8,128)S(1)}, f32[10,3,8,128]{3,2,1,0:T(8,128)S(1)}) custom-call(f32[3,10,64,128]{3,2,1,0:T(8,128)} %tracers_in.3), custom_call_target="tpu_custom_call" | custom-call | tf_op jit(solution)/shard_map/pack_halo/pallas_call | solution.py:70
  2.1 0.5 collective-permute-start
  2.6 5.0 %collective-permute-start.1 = (f32[10,3,8,128]{3,2,1,0:T(8,128)S(1)}, f32[10,3,8,128]{3,2,1,0:T(8,128)S(1)}, u32[]{:S(2)}, u32[]{:S(2)}) collective-permute-start(f32[10,3,8,128]{3,2,1,0:T(8,128)S(1)} %get-tuple-element.15), channel_id=1, source_target_pairs={{0,30},{2,0},{4,2},{6,4},{8,6},{10,8},{12,10},{14,12},{16,14},{18,... | collective-permute-start | bytes 368648 | tf_op jit(solution)/shard_map/ppermute | solution.py:492
  7.6 5.3 %advect_inside.1 = (f32[30,64,128]{2,1,0:T(8,128)}, s32[10,64,128]{2,1,0:T(8,128)}, f32[10,64,128]{2,1,0:T(8,128)}, f32[10,64,128]{2,1,0:T(8,128)}, f32[9,64,128...) custom-call(f32[3,10,64,128]{3,2,1,0:T(8,128)} %tracers_in.3, s32[10,64,128]{2,1,0:T(8,128)} %offsets_in.1, ...), custom_call_target="tpu_custom_call" | custom-call | bytes 20971520 | tf_op jit(solution)/shard_map/advect_inside/pallas_call | solution.py:178
  12.9 0.0 collective-permute-done
  12.9 0.0 collective-permute-done.1
  12.9 14.2 %solve_pick.1 = f32[32,120,128]{2,1,0:T(8,128)} custom-call(f32[30,8,128]{2,1,0:T(8,128)S(1)} %bitcast.7, f32[30,8,128]{2,1,0:T(8,128)S(1)} %bitcast.8, f32[30,64,128]{2,1,0:T(8,128)} %get-tuple-element.16.inside_in, s32[10,64,128]{2,1,0:T(8,128)} %get-tuple-element.17.left_cell_in, f32[10,64,128]{2,1,0:T(8,128)} %get-tuple-element.18.west_edge_in, ...), custom_call_target="tpu_custom_call" | custom-call | bytes 41943040 | tf_op jit(solution)/shard_map/solve_pick/pallas_call | solution.py:399
  27.1 3.6 %all-to-all-start = ((f32[32,15,8,128]{3,2,1,0:T(8,128)}), f32[32,15,8,128]{3,2,1,0:T(8,128)S(1)}, u32[]{:S(2)}, u32[]{:S(2)}) async-start(f32[32,15,8,128]{3,2,1,0:T(8,128)} %bitcast.9), calls=%async_computation | async-start | bytes 3932160 | tf_op jit(solution)/shard_map/all_to_all | solution.py:495
  30.7 45.9 %all-to-all-done = f32[32,15,8,128]{3,2,1,0:T(8,128)S(1)} async-done(((f32[32,15,8,128]{3,2,1,0:T(8,128)}), f32[32,15,8,128]{3,2,1,0:T(8,128)S(1)}, u32[]{:S(2)}, u32[]{:S(2)}) %all-to-all-start) | async-done | bytes 1966112 | tf_op jit(solution)/shard_map/all_to_all | solution.py:495
  76.6 1.9 %place_owned.1 = f32[10,3,8192]{2,1,0:T(4,128)} custom-call(s32[1]{0:T(128)} %bitcast.own, f32[32,120,128]{2,1,0:T(8,128)S(1)} %bitcast.6), custom_call_target="tpu_custom_call" | custom-call | tf_op jit(solution)/shard_map/place_owned/pallas_call | solution.py:467
Async XLA Ops:
  2.1 10.8 %collective-permute-start = (f32[10,3,8,128]{3,2,1,0:T(8,128)S(1)}, f32[10,3,8,128]{3,2,1,0:T(8,128)S(1)}, u32[]{:S(2)}, u32[]{:S(2)}) collective-permute-start(f32[10,3,8,128]{3,2,1,0:T(8,128)S(1)} %get-tuple-element.14), channel_id=1, source_target_pairs={{0,2},{2,4},{4,6},{6,8},{8,10},{10,12},{12,14},{14,16},{16,18},{18... | collective-permute-start | bytes 368648 | tf_op jit(solution)/shard_map/ppermute | solution.py:491
  2.6 10.3 %collective-permute-start.1 = (f32[10,3,8,128]{3,2,1,0:T(8,128)S(1)}, f32[10,3,8,128]{3,2,1,0:T(8,128)S(1)}, u32[]{:S(2)}, u32[]{:S(2)}) collective-permute-start(f32[10,3,8,128]{3,2,1,0:T(8,128)S(1)} %get-tuple-element.15), channel_id=1, source_target_pairs={{0,30},{2,0},{4,2},{6,4},{8,6},{10,8},{12,10},{14,12},{16,14},{18,... | collective-permute-start | bytes 368648 | tf_op jit(solution)/shard_map/ppermute | solution.py:492
  27.1 49.5 %all-to-all-start = ((f32[32,15,8,128]{3,2,1,0:T(8,128)}), f32[32,15,8,128]{3,2,1,0:T(8,128)S(1)}, u32[]{:S(2)}, u32[]{:S(2)}) async-start(f32[32,15,8,128]{3,2,1,0:T(8,128)} %bitcast.9), calls=%async_computation | async-start | bytes 3932160 | tf_op jit(solution)/shard_map/all_to_all | solution.py:495

commit v24 on v23

--- a/solution.py
+++ b/solution.py
@@ -11,7 +11,7 @@
 LANES = 128
 SUB = 8
 SLOT = 32
-FIRST = 40
+FIRST = 48
 MIB = 1024 * 1024
 LENGTH_BASE = 1000.0
 BIG = 60 * MIB

time: 78.7 us -> 79.2 us (level)
  no operation moved by 1% of the time
where the time goes in v24:
time: 79.2 us; the launch traced here: 79 us
  waiting for transfers between devices  45.9 us (58%)
  Pallas kernels  23.9 us (30%)
  starting transfers between devices  9.1 us (11%)
    all_to_all x1, waiting for transfers between devices, body(): lax.all_to_all(sent, ('lon', 'lat'), split_axis=0, concat_axis=0, tiled=T...  45.9 us
    pallas_call x1, Pallas kernels, make_sent(): pl.pallas_call(functools.partial(solve_kernel, parts), out_shape=jax.Shap...  14.6 us
    pallas_call x1, Pallas kernels, advect_inside(): pl.pallas_call(inside_kernel, out_shape=outputs, in_specs=[pl.BlockSpec(m...  5.26 us
    ppermute x1, starting transfers between devices, body(): from_east = lax.ppermute(west_cells, 'lon', ring('lon', -1))  5.03 us
    all_to_all x1, starting transfers between devices, body(): lax.all_to_all(sent, ('lon', 'lat'), split_axis=0, concat_axis=0, tiled=T...  3.57 us
    pallas_call x1, Pallas kernels, pack_halo(): pl.pallas_call(pack_halo_kernel, out_shape=(shape, shape), in_specs=[pl.B...  2.1 us
    pallas_call x1, Pallas kernels, place_owned(): pl.pallas_call(place_kernel, out_shape=jax.ShapeDtypeStruct((levels, ntr,...  1.9 us
  transfers between devices with their start and end apart: 3, of which 1 were waited for; matrix products, arithmetic and copies ran while one was open for 0% of the time, Pallas kernels for 7%

profile of v24, /device:TPU:0, one launch (start us, length us, event | category | flops | bytes accessed | tf_op | source)
XLA Modules:
  0.0 79.0 jit_solution(3620385082990393732)
XLA Ops:
  0.0 2.1 %pack_halo.1 = (f32[10,3,8,128]{3,2,1,0:T(8,128)S(1)}, f32[10,3,8,128]{3,2,1,0:T(8,128)S(1)}) custom-call(f32[3,10,64,128]{3,2,1,0:T(8,128)} %tracers_in.3), custom_call_target="tpu_custom_call" | custom-call | tf_op jit(solution)/shard_map/pack_halo/pallas_call | solution.py:70
  2.1 0.5 collective-permute-start
  2.6 5.0 %collective-permute-start.1 = (f32[10,3,8,128]{3,2,1,0:T(8,128)S(1)}, f32[10,3,8,128]{3,2,1,0:T(8,128)S(1)}, u32[]{:S(2)}, u32[]{:S(2)}) collective-permute-start(f32[10,3,8,128]{3,2,1,0:T(8,128)S(1)} %get-tuple-element.15), channel_id=1, source_target_pairs={{0,30},{2,0},{4,2},{6,4},{8,6},{10,8},{12,10},{14,12},{16,14},{18,... | collective-permute-start | bytes 368648 | tf_op jit(solution)/shard_map/ppermute | solution.py:492
  7.6 5.3 %advect_inside.1 = (f32[30,64,128]{2,1,0:T(8,128)}, s32[10,64,128]{2,1,0:T(8,128)}, f32[10,64,128]{2,1,0:T(8,128)}, f32[10,64,128]{2,1,0:T(8,128)}, f32[9,64,128...) custom-call(f32[3,10,64,128]{3,2,1,0:T(8,128)} %tracers_in.3, s32[10,64,128]{2,1,0:T(8,128)} %offsets_in.1, ...), custom_call_target="tpu_custom_call" | custom-call | bytes 20971520 | tf_op jit(solution)/shard_map/advect_inside/pallas_call | solution.py:178
  12.9 0.0 collective-permute-done
  12.9 0.0 collective-permute-done.1
  12.9 14.6 %solve_pick.1 = f32[32,120,128]{2,1,0:T(8,128)} custom-call(f32[30,8,128]{2,1,0:T(8,128)S(1)} %bitcast.7, f32[30,8,128]{2,1,0:T(8,128)S(1)} %bitcast.8, f32[30,64,128]{2,1,0:T(8,128)} %get-tuple-element.16.inside_in, s32[10,64,128]{2,1,0:T(8,128)} %get-tuple-element.17.left_cell_in, f32[10,64,128]{2,1,0:T(8,128)} %get-tuple-element.18.west_edge_in, ...), custom_call_target="tpu_custom_call" | custom-call | bytes 41943040 | tf_op jit(solution)/shard_map/solve_pick/pallas_call | solution.py:399
  27.6 3.6 %all-to-all-start = ((f32[32,15,8,128]{3,2,1,0:T(8,128)}), f32[32,15,8,128]{3,2,1,0:T(8,128)S(1)}, u32[]{:S(2)}, u32[]{:S(2)}) async-start(f32[32,15,8,128]{3,2,1,0:T(8,128)} %bitcast.9), calls=%async_computation | async-start | bytes 3932160 | tf_op jit(solution)/shard_map/all_to_all | solution.py:495
  31.2 45.9 %all-to-all-done = f32[32,15,8,128]{3,2,1,0:T(8,128)S(1)} async-done(((f32[32,15,8,128]{3,2,1,0:T(8,128)}), f32[32,15,8,128]{3,2,1,0:T(8,128)S(1)}, u32[]{:S(2)}, u32[]{:S(2)}) %all-to-all-start) | async-done | bytes 1966112 | tf_op jit(solution)/shard_map/all_to_all | solution.py:495
  77.1 1.9 %place_owned.1 = f32[10,3,8192]{2,1,0:T(4,128)} custom-call(s32[1]{0:T(128)} %bitcast.own, f32[32,120,128]{2,1,0:T(8,128)S(1)} %bitcast.6), custom_call_target="tpu_custom_call" | custom-call | tf_op jit(solution)/shard_map/place_owned/pallas_call | solution.py:467
Async XLA Ops:
  2.1 10.8 %collective-permute-start = (f32[10,3,8,128]{3,2,1,0:T(8,128)S(1)}, f32[10,3,8,128]{3,2,1,0:T(8,128)S(1)}, u32[]{:S(2)}, u32[]{:S(2)}) collective-permute-start(f32[10,3,8,128]{3,2,1,0:T(8,128)S(1)} %get-tuple-element.14), channel_id=1, source_target_pairs={{0,2},{2,4},{4,6},{6,8},{8,10},{10,12},{12,14},{14,16},{16,18},{18... | collective-permute-start | bytes 368648 | tf_op jit(solution)/shard_map/ppermute | solution.py:491
  2.6 10.3 %collective-permute-start.1 = (f32[10,3,8,128]{3,2,1,0:T(8,128)S(1)}, f32[10,3,8,128]{3,2,1,0:T(8,128)S(1)}, u32[]{:S(2)}, u32[]{:S(2)}) collective-permute-start(f32[10,3,8,128]{3,2,1,0:T(8,128)S(1)} %get-tuple-element.15), channel_id=1, source_target_pairs={{0,30},{2,0},{4,2},{6,4},{8,6},{10,8},{12,10},{14,12},{16,14},{18,... | collective-permute-start | bytes 368648 | tf_op jit(solution)/shard_map/ppermute | solution.py:492
  27.6 49.5 %all-to-all-start = ((f32[32,15,8,128]{3,2,1,0:T(8,128)}), f32[32,15,8,128]{3,2,1,0:T(8,128)S(1)}, u32[]{:S(2)}, u32[]{:S(2)}) async-start(f32[32,15,8,128]{3,2,1,0:T(8,128)} %bitcast.9), calls=%async_computation | async-start | bytes 3932160 | tf_op jit(solution)/shard_map/all_to_all | solution.py:495

commit v25 on v23

--- a/solution.py
+++ b/solution.py
@@ -191,7 +191,7 @@
 def add_edges_and_solve(inside, left_cell, west_edge, east_edge, lower, upper, halo, solved):
     levels, lats, _ = left_cell.shape
     ntr = inside.shape[0] // levels
-    together = 2
+    together = 4
 
     def solve_part(part):
         rows = pl.ds(pl.multiple_of(part * SUB, SUB), SUB)

time: 78.7 us -> 78.6 us (level)
  no operation moved by 1% of the time
where the time goes in v25:
time: 78.6 us; the launch traced here: 78.4 us
  waiting for transfers between devices  45.9 us (58%)
  Pallas kernels  23.4 us (30%)
  starting transfers between devices  9.1 us (12%)
    all_to_all x1, waiting for transfers between devices, body(): lax.all_to_all(sent, ('lon', 'lat'), split_axis=0, concat_axis=0, tiled=T...  45.9 us
    pallas_call x1, Pallas kernels, make_sent(): pl.pallas_call(functools.partial(solve_kernel, parts), out_shape=jax.Shap...  14.1 us
    pallas_call x1, Pallas kernels, advect_inside(): pl.pallas_call(inside_kernel, out_shape=outputs, in_specs=[pl.BlockSpec(m...  5.26 us
    ppermute x1, starting transfers between devices, body(): from_east = lax.ppermute(west_cells, 'lon', ring('lon', -1))  5.03 us
    all_to_all x1, starting transfers between devices, body(): lax.all_to_all(sent, ('lon', 'lat'), split_axis=0, concat_axis=0, tiled=T...  3.57 us
    pallas_call x1, Pallas kernels, pack_halo(): pl.pallas_call(pack_halo_kernel, out_shape=(shape, shape), in_specs=[pl.B...  2.1 us
    pallas_call x1, Pallas kernels, place_owned(): pl.pallas_call(place_kernel, out_shape=jax.ShapeDtypeStruct((levels, ntr,...  1.9 us
  transfers between devices with their start and end apart: 3, of which 1 were waited for; matrix products, arithmetic and copies ran while one was open for 0% of the time, Pallas kernels for 7%

profile of v25, /device:TPU:0, one launch (start us, length us, event | category | flops | bytes accessed | tf_op | source)
XLA Modules:
  0.0 78.4 jit_solution(7730370766997813080)
XLA Ops:
  0.0 2.1 %pack_halo.1 = (f32[10,3,8,128]{3,2,1,0:T(8,128)S(1)}, f32[10,3,8,128]{3,2,1,0:T(8,128)S(1)}) custom-call(f32[3,10,64,128]{3,2,1,0:T(8,128)} %tracers_in.3), custom_call_target="tpu_custom_call" | custom-call | tf_op jit(solution)/shard_map/pack_halo/pallas_call | solution.py:70
  2.1 0.5 collective-permute-start
  2.6 5.0 %collective-permute-start.1 = (f32[10,3,8,128]{3,2,1,0:T(8,128)S(1)}, f32[10,3,8,128]{3,2,1,0:T(8,128)S(1)}, u32[]{:S(2)}, u32[]{:S(2)}) collective-permute-start(f32[10,3,8,128]{3,2,1,0:T(8,128)S(1)} %get-tuple-element.15), channel_id=1, source_target_pairs={{0,30},{2,0},{4,2},{6,4},{8,6},{10,8},{12,10},{14,12},{16,14},{18,... | collective-permute-start | bytes 368648 | tf_op jit(solution)/shard_map/ppermute | solution.py:492
  7.6 5.3 %advect_inside.1 = (f32[30,64,128]{2,1,0:T(8,128)}, s32[10,64,128]{2,1,0:T(8,128)}, f32[10,64,128]{2,1,0:T(8,128)}, f32[10,64,128]{2,1,0:T(8,128)}, f32[9,64,128...) custom-call(f32[3,10,64,128]{3,2,1,0:T(8,128)} %tracers_in.3, s32[10,64,128]{2,1,0:T(8,128)} %offsets_in.1, ...), custom_call_target="tpu_custom_call" | custom-call | bytes 20971520 | tf_op jit(solution)/shard_map/advect_inside/pallas_call | solution.py:178
  12.9 0.0 collective-permute-done
  12.9 0.0 collective-permute-done.1
  12.9 14.1 %solve_pick.1 = f32[32,120,128]{2,1,0:T(8,128)} custom-call(f32[30,8,128]{2,1,0:T(8,128)S(1)} %bitcast.7, f32[30,8,128]{2,1,0:T(8,128)S(1)} %bitcast.8, f32[30,64,128]{2,1,0:T(8,128)} %get-tuple-element.16.inside_in, s32[10,64,128]{2,1,0:T(8,128)} %get-tuple-element.17.left_cell_in, f32[10,64,128]{2,1,0:T(8,128)} %get-tuple-element.18.west_edge_in, ...), custom_call_target="tpu_custom_call" | custom-call | bytes 41943040 | tf_op jit(solution)/shard_map/solve_pick/pallas_call | solution.py:399
  27.0 3.6 %all-to-all-start = ((f32[32,15,8,128]{3,2,1,0:T(8,128)}), f32[32,15,8,128]{3,2,1,0:T(8,128)S(1)}, u32[]{:S(2)}, u32[]{:S(2)}) async-start(f32[32,15,8,128]{3,2,1,0:T(8,128)} %bitcast.9), calls=%async_computation | async-start | bytes 3932160 | tf_op jit(solution)/shard_map/all_to_all | solution.py:495
  30.6 45.9 %all-to-all-done = f32[32,15,8,128]{3,2,1,0:T(8,128)S(1)} async-done(((f32[32,15,8,128]{3,2,1,0:T(8,128)}), f32[32,15,8,128]{3,2,1,0:T(8,128)S(1)}, u32[]{:S(2)}, u32[]{:S(2)}) %all-to-all-start) | async-done | bytes 1966112 | tf_op jit(solution)/shard_map/all_to_all | solution.py:495
  76.5 1.9 %place_owned.1 = f32[10,3,8192]{2,1,0:T(4,128)} custom-call(s32[1]{0:T(128)} %bitcast.own, f32[32,120,128]{2,1,0:T(8,128)S(1)} %bitcast.6), custom_call_target="tpu_custom_call" | custom-call | tf_op jit(solution)/shard_map/place_owned/pallas_call | solution.py:467
Async XLA Ops:
  2.1 10.8 %collective-permute-start = (f32[10,3,8,128]{3,2,1,0:T(8,128)S(1)}, f32[10,3,8,128]{3,2,1,0:T(8,128)S(1)}, u32[]{:S(2)}, u32[]{:S(2)}) collective-permute-start(f32[10,3,8,128]{3,2,1,0:T(8,128)S(1)} %get-tuple-element.14), channel_id=1, source_target_pairs={{0,2},{2,4},{4,6},{6,8},{8,10},{10,12},{12,14},{14,16},{16,18},{18... | collective-permute-start | bytes 368648 | tf_op jit(solution)/shard_map/ppermute | solution.py:491
  2.6 10.3 %collective-permute-start.1 = (f32[10,3,8,128]{3,2,1,0:T(8,128)S(1)}, f32[10,3,8,128]{3,2,1,0:T(8,128)S(1)}, u32[]{:S(2)}, u32[]{:S(2)}) collective-permute-start(f32[10,3,8,128]{3,2,1,0:T(8,128)S(1)} %get-tuple-element.15), channel_id=1, source_target_pairs={{0,30},{2,0},{4,2},{6,4},{8,6},{10,8},{12,10},{14,12},{16,14},{18,... | collective-permute-start | bytes 368648 | tf_op jit(solution)/shard_map/ppermute | solution.py:492
  27.0 49.5 %all-to-all-start = ((f32[32,15,8,128]{3,2,1,0:T(8,128)}), f32[32,15,8,128]{3,2,1,0:T(8,128)S(1)}, u32[]{:S(2)}, u32[]{:S(2)}) async-start(f32[32,15,8,128]{3,2,1,0:T(8,128)} %bitcast.9), calls=%async_computation | async-start | bytes 3932160 | tf_op jit(solution)/shard_map/all_to_all | solution.py:495
